TPU v7x, 256 devices: a whole 4x4x8 slice. The times are simulated.
256 devices in a mesh: ta: 8 (over x, y_lo), af: 32 (over y_hi, z, core).
Axes of the slice: x: 4, y: 4 (y_hi: 2, y_lo: 2; y = y_hi * 2 + y_lo), z: 8, core: 2. Of those that a mesh axis runs over, the one named last changes fastest.
Arguments:
- activations: bfloat16 [32768, 4096], P(('ta', 'af')), may hold values from -24 to 24
- cotangent: bfloat16 [32768, 4096], P(('ta', 'af')), may hold values from -6 to 6
- masked: int32 [32768], P(('ta', 'af')), may hold values 0 or 1
- ratios: int32 [256], P(('ta', 'af')), may hold values from 100 to 1000
- owners: int32 [32], replicated, may hold values from 0 to 31, as said below
Outputs:
- update: float32 [4096, 4096], P('af')
Inputs may be any that keep to these rules, and one draw needn't show every extreme that they name: `owners`: heads with the same value are orthogonalized together; no value is named by more than 2 heads, and one value by exactly 2.
All inputs are finite; a program needn't handle non-finite values. No bound on the sum of `masked` on one device may be relied on, other than what follows from the above.
Results may differ from a plain program's by a relative error of at most 0.03.
Values may be sent and summed in bfloat16 or wider, within the bound.
No kernel may reach another device: no remote copies, remote signals or barrier semaphores. Data moves between devices by JAX's collectives and lax.ppermute only.
A program may use at most 192 MiB of HBM per device.

v0:
```python
import math

import jax
import jax.numpy as jnp
from jax import lax
from jax.sharding import PartitionSpec as P

HEADS = 32
NS_ITERS = 5


quintic_a = 3.4445
quintic_b = -4.775
quintic_c = 2.0315
epsilon = 1e-07
highest = lax.Precision.HIGHEST


def owner_selection(owners, owner_count, head_count, slot_count):
    head_order = jnp.arange(head_count)
    same_owner = owners[:, None] == owners[None, :]
    earlier = head_order[None, :] < head_order[:, None]
    slot_rank = jnp.sum(jnp.logical_and(same_owner, earlier), axis=1)
    groups = jnp.arange(owner_count)[:, None, None]
    slot_ids = jnp.arange(slot_count)[None, :, None]
    return jnp.logical_and(owners[None, None, :] == groups, slot_rank[None, None, :] == slot_ids)


def products(left, right):
    return jnp.einsum("ri,rj->ij", left, right, precision=highest)


def polish(iterate, gram_now):
    polynomial = quintic_b * gram_now + quintic_c * jnp.dot(gram_now, gram_now, precision=highest)
    return quintic_a * iterate + jnp.dot(iterate, polynomial, precision=highest)


def newton_local(matrix):
    frob_norm = jnp.sqrt(jnp.sum(matrix * matrix)) + epsilon
    iterate = matrix / frob_norm
    for turn in range(NS_ITERS):
        iterate = polish(iterate, products(iterate, iterate))
    return iterate


def on_device(activations, cotangent, masked, ratios, owners):
    n_af = lax.axis_size("af")
    tok_rows, width = activations.shape
    columns = cotangent.shape[1]
    head_size = columns // HEADS
    slot_count = max(2, (HEADS + n_af - 1) // n_af)
    my_rows = width // n_af
    wide_slot = slot_count * head_size
    weight = masked.astype(jnp.float32) * 1000.0 / ratios[0].astype(jnp.float32)
    scaled = (cotangent.astype(jnp.float32) * weight[:, None]).astype(jnp.bfloat16)
    product = lax.dot_general(
        activations, scaled, (((0,), (0,)), ((), ())), preferred_element_type=jnp.float32
    )
    gradient = lax.psum_scatter(
        lax.optimization_barrier(product.astype(jnp.bfloat16))
        .astype(jnp.float32)
        .astype(jnp.bfloat16),
        "af",
        scatter_dimension=0,
        tiled=True,
    ).astype(jnp.float32)
    gradient = lax.psum(gradient, "ta")
    head_grad = gradient.astype(jnp.bfloat16).reshape(my_rows, HEADS, head_size)
    selection = owner_selection(owners, n_af, HEADS, slot_count)
    outgoing = jnp.einsum(
        "okh,rhd->orkd",
        selection.astype(jnp.bfloat16),
        head_grad,
        preferred_element_type=jnp.float32,
    )
    outgoing = outgoing.astype(jnp.bfloat16).reshape(n_af, my_rows, wide_slot)
    received = lax.all_to_all(outgoing, "af", split_axis=0, concat_axis=0, tiled=True)
    iterate = newton_local(received.reshape(width, wide_slot).astype(jnp.float32))
    returned = lax.all_to_all(
        iterate.reshape(n_af, my_rows, wide_slot), "af", split_axis=0, concat_axis=0, tiled=True
    )
    update = jnp.einsum(
        "okh,orkd->rhd",
        selection.astype(jnp.float32),
        returned.reshape(n_af, my_rows, slot_count, head_size),
        precision=highest,
    ) * math.sqrt(width)
    return update.reshape(my_rows, columns)


def solution(mesh):
    placed = (P(("ta", "af"), None), P(("ta", "af"), None), P(("ta", "af")), P(("ta", "af")), P())
    return jax.shard_map(
        on_device, mesh=mesh, in_specs=placed, out_specs=P("af", None), check_vma=False
    )
```

profile of v0, /device:TPU:1, one launch (start us, length us, event | category | flops | bytes accessed | tf_op | source)
XLA Modules:
  0.0 750.3 jit_solution(4188259880608419294)
XLA Ops:
  7.9 15.2 %convert_bitcast_fusion = bf16[4096,4096]{0,1:T(8,128)(2,1)} fusion(bf16[128,4096]{1,0:T(8,128)(2,1)S(1)} %copy-done, bf16[128,4096]{1,0:T(8,128)(2,1)} %param.6, f32[128]{0:T(128)S(1)} %multiply_divide_fusion), kind=kOutput, calls=%fused_computation | convolution fusion | flops 4313317376 | bytes 35652096 | tf_op jit(solution)/shard_map/dot_general | solution.py:56
  23.2 41.0 %copy.31 = bf16[4096,4096]{1,0:T(8,128)(2,1)} copy(bf16[4096,4096]{0,1:T(8,128)(2,1)} %convert_bitcast_fusion) | data formatting | bytes 67108864
  64.2 346.1 %reduce-scatter.4.cloned.1.call-done = bf16[128,4096]{1,0:T(8,128)(2,1)} async-done(((bf16[4096,4096]{1,0:T(8,128)(2,1)}), bf16[128,4096]{1,0:T(8,128)(2,1)}) %reduce-scatter.4.cloned.1.call-update) | async-done | bytes 1048592
  410.3 2.3 copy.32
  412.8 76.6 %all-reduce.2.cloned.1.call-done = bf16[128,4096]{0,1:T(8,128)(2,1)} async-done(((bf16[128,4096]{0,1:T(8,128)(2,1)}), bf16[128,4096]{0,1:T(8,128)(2,1)}) %all-reduce.2.cloned.1.call-update) | async-done | bytes 1048592 | tf_op jit(solution)/shard_map/psum | solution.py:67
  489.3 1.9 copy.23
  492.1 3.1 copy.18
  495.2 4.1 copy.19
  499.3 64.5 %all_to_all.10 = bf16[32,128,256]{2,1,0:T(8,128)(2,1)S(1)} all-to-all(bf16[32,128,256]{2,1,0:T(8,128)(2,1)} %copy.19), channel_id=1, replica_groups=mesh['ta'=8,'af'=32] {'af'}, dimensions={0} | all-to-all | bytes 4194304 | tf_op jit(solution)/shard_map/all_to_all | solution.py:77
  566.2 7.1 convolution_bitcast_fusion
  574.2 3.4 convolution_add_fusion.4
  577.6 7.2 fusion.16
  585.2 3.4 convolution_add_fusion.3
  588.6 6.9 fusion.17
  595.9 3.4 convolution_add_fusion.2
  599.4 7.0 fusion.18
  606.8 3.4 convolution_add_fusion.1
  610.2 7.0 fusion.19
  617.6 5.0 convolution_add_fusion
  622.6 5.6 copy.21
  628.2 102.1 %all_to_all.11 = f32[32,128,256]{1,2,0:T(8,128)} all-to-all(f32[32,128,256]{1,2,0:T(8,128)} %copy.21), channel_id=1, replica_groups=mesh['ta'=8,'af'=32] {'af'}, dimensions={0} | all-to-all | bytes 8388608 | tf_op jit(solution)/shard_map/all_to_all | solution.py:79
  730.3 5.6 copy.22
  735.9 4.1 bitcast_multiply_fusion
  740.0 3.0 copy.35
  (22 shorter events, 5.8 us)
Async XLA Ops:
  6.5 1.4 copy-start
  6.5 403.7 %reduce-scatter.4.cloned.1.call-start = ((), (), s32[]{:S(2)}) async-start(), calls=%async_computation.4 | async-start | bytes 34603008
  64.1 348.4 %copy-start.2 = (s32[32]{0:T(128)S(1)}, s32[32]{0:T(128)}, u32[]{:S(2)}) copy-start(s32[32]{0:T(128)} %param.9) | copy-start | bytes 388
  64.2 425.2 %all-reduce.2.cloned.1.call-start = ((), (), s32[]{:S(2)}) async-start(), calls=%async_computation.3 | async-start | bytes 2097152 | tf_op jit(solution)/shard_map/psum | solution.py:67
  730.3 12.7 %copy-start.1 = (bf16[128,4096]{1,0:T(8,128)(2,1)S(1)}, bf16[128,4096]{1,0:T(8,128)(2,1)}, u32[]{:S(2)}) copy-start(bf16[128,4096]{1,0:T(8,128)(2,1)} %param.5) | copy-start | bytes 3145732
Sparse Core Ops, SparseCore 0:
  64.3 345.9 reduce-scatter.3
  413.1 76.1 all-reduce.1
where the time goes:
time: 757 us; the launch traced here: 750 us
  waiting for transfers between devices  423 us (56%)
  blocking collectives  167 us (22%)
  matrix products  75.9 us (10%)
  local copies, waits for them, and re-layouts  66.5 us (9%)
  between operations  15.4 us (2%)
    unnamed x3, waiting for transfers between devices  346 us
    all_to_all x1, blocking collectives, on_device(): lax.all_to_all(iterate.reshape(n_af, my_rows, wide_slot), 'af', split_axi...  102 us
    psum x1, waiting for transfers between devices, on_device(): gradient = lax.psum(gradient, 'ta')  76.6 us
    all_to_all x1, blocking collectives, on_device(): lax.all_to_all(outgoing, 'af', split_axis=0, concat_axis=0, tiled=True)  64.5 us
    unnamed x9, local copies, waits for them, and re-layouts  46.2 us
    dot_general x5, matrix products, products(): return jnp.einsum('ri,rj->ij', left, right, precision=highest)  35.2 us
    dot_general x5, matrix products, polish(): return quintic_a * iterate + jnp.dot(iterate, polynomial, precision=highest)  18.7 us
    dot_general x1, matrix products, on_device(): lax.dot_general(activations, scaled, (((0,), (0,)), ((), ())), preferred_...  15.2 us
  transfers between devices with their start and end apart: 2, of which 2 were waited for; matrix products, arithmetic and copies ran while one was open for 0% of the time, Pallas kernels for 0%

commit v1 on v0

v1 whole, which is shorter than its diff:
```python
import jax
import jax.numpy as jnp
from jax import lax
from jax.experimental import pallas as pl
from jax.experimental.pallas import tpu as pltpu
from jax.sharding import Mesh
from jax.sharding import PartitionSpec as P

HEADS = 32
NS_ITERS = 5
quintic_a = 3.4445
quintic_b = -4.775
quintic_c = 2.0315
epsilon = 1e-07
highest = lax.Precision.HIGHEST

Y_AT, X_AT, ZH_AT, Z0_AT, CORE_AT, PAIRS_AT, PERM_AT = 0, 1, 2, 3, 4, 5, 8

HEAD = 128
SLOT = 2 * HEAD
BLOCK = 1024
HALF = 64

f32, bf16 = jnp.float32, jnp.bfloat16


def smem():
    return pl.BlockSpec(memory_space=pltpu.SMEM)


def vmem():
    return pl.BlockSpec(memory_space=pltpu.VMEM)


def local_kernel(body, outs, operands, mib, flops, name):
    moved = sum(o.size * o.dtype.itemsize for o in list(outs) + list(operands))
    return pl.pallas_call(
        body,
        out_shape=outs,
        in_specs=[smem()] + [vmem()] * (len(operands) - 1),
        out_specs=[vmem()] * len(outs),
        compiler_params=pltpu.CompilerParams(vmem_limit_bytes=mib * 2**20),
        cost_estimate=pl.CostEstimate(flops=flops, bytes_accessed=moved, transcendentals=0),
        name=name,
    )(*operands)


def shape(dims, dtype):
    return jax.ShapeDtypeStruct(dims, dtype)


def scalars(owners):
    order = jnp.arange(HEADS)
    same = owners[:, None] == owners[None, :]
    paired = jnp.sum(same, axis=1) > 1
    first = jnp.min(jnp.where(same, order[None, :], HEADS), axis=1)
    key = jnp.where(paired, 0, HEADS * HEADS) + first * HEADS + order
    place = jnp.sum(key[None, :] < key[:, None], axis=1)
    perm = jnp.sum(jnp.where(place[:, None] == order[None, :], order[:, None], 0), axis=0)
    pairs = jnp.sum(paired) // 2
    here = [
        lax.axis_index("yhi") * 2 + lax.axis_index("ylo"),
        lax.axis_index("x"),
        lax.axis_index("zh"),
        lax.axis_index("z0"),
        lax.axis_index("core"),
        pairs,
        pairs,
        pairs,
    ]
    return jnp.concatenate([jnp.stack([v.astype(jnp.int32) for v in here]), perm.astype(jnp.int32)])


def prepare(meta, act, cot, weight, *outs):
    rows_out, cols_out = outs[:4], outs[4:]
    width = act.shape[1]
    for k in range(4):
        y = (meta[Y_AT] + k) & 3
        base = (y >> 1) * (width // 2)
        low = (y & 1) * HALF
        for crel in range(2):
            for zrel in range(2):
                for zh in range(4):
                    block = zh * 4 + (meta[Z0_AT] ^ zrel) * 2 + (meta[CORE_AT] ^ crel)
                    at = pl.multiple_of(base + block * 128, 128)
                    turned = act[:, pl.ds(at, 128)].T
                    part = jnp.where(low == 0, turned[:HALF], turned[HALF:])
                    to = ((crel * 2 + zrel) * 4 + zh) * HALF
                    rows_out[k][to : to + HALF, :] = part
    w = weight[...]
    for k in range(4):
        x = (meta[X_AT] + k) & 3
        for j in range(8):
            slot = x * 4 + ((meta[ZH_AT] + j // 2) & 3)
            head = meta[PERM_AT + slot * 2 + j % 2]
            at = pl.multiple_of(head * HEAD, HEAD)
            cols_out[k][:, j * HEAD : (j + 1) * HEAD] = (cot[:, pl.ds(at, HEAD)].astype(f32) * w).astype(
                bf16
            )


def multiply(meta, r0, r1, r3, r2a, r2b, g0, g1, g3, g2a, g2b, keep, send):
    tok = r0.shape[2]

    def rows_of(dx, dy):
        if dx == 2:
            return (r2a if dy < 2 else r2b)[dy % 2]
        return {0: r0, 1: r1, 3: r3}[dx][dy]

    def cols_of(dx, dy, at):
        ref = (g2a if dx < 2 else g2b) if dy == 2 else {0: g0, 1: g1, 3: g3}[dy]
        return ref[dx % 2 if dy == 2 else dx, :, pl.ds(at, SLOT)]

    for n in range(BLOCK // SLOT):
        total = jnp.zeros((BLOCK, SLOT), f32)
        for dx in range(4):
            left = jnp.concatenate([rows_of(dx, dy) for dy in range(4)], axis=1)
            right = jnp.concatenate([cols_of(dx, dy, n * SLOT) for dy in range(4)], axis=0)
            total = total + jnp.dot(left, right, preferred_element_type=f32)
        total = total.astype(bf16)
        for zrel in range(2):
            keep[zrel * 4 + n] = total[zrel * 256 : (zrel + 1) * 256]
            send[zrel * 4 + n] = total[512 + zrel * 256 : 512 + (zrel + 1) * 256]


def add_cores(meta, mine, other, *outs):
    for i, out in enumerate(outs):
        out[...] = (mine[i].astype(f32) + other[i].astype(f32)).astype(bf16)


def gram_part(meta, *refs):
    terms, (head_grad, keep, send, whole) = refs[:8], refs[8:]
    total = terms[0][...].astype(f32)
    for term in terms[1:]:
        total = total + term[...].astype(f32)
    part = total.astype(bf16)
    head_grad[...] = part
    whole[...] = lax.dot_general(part, part, (((0,), (0,)), ((), ())), preferred_element_type=f32)
    core = meta[CORE_AT]
    keep[...] = whole[pl.ds(pl.multiple_of(core * HEAD, HEAD), HEAD), :]
    send[...] = whole[pl.ds(pl.multiple_of((1 - core) * HEAD, HEAD), HEAD), :]


def newton(meta, mine, other, head_grad, o0, o1, o2, o3, result):
    core = meta[CORE_AT]
    a, b = mine[...], other[...]
    gram = jnp.concatenate([jnp.where(core == 0, a, b), jnp.where(core == 0, b, a)], axis=0)
    slot = meta[X_AT] * 4 + meta[ZH_AT]
    pair = slot < meta[PAIRS_AT]
    row = lax.broadcasted_iota(jnp.int32, (SLOT, SLOT), 0)
    col = lax.broadcasted_iota(jnp.int32, (SLOT, SLOT), 1)
    together = jnp.logical_or((row < HEAD) == (col < HEAD), pair)
    gram = jnp.where(together, gram, 0.0)
    on_diagonal = jnp.where(row == col, gram, 0.0)
    down = jnp.sum(on_diagonal, axis=0, keepdims=True)
    across = jnp.sum(on_diagonal, axis=1, keepdims=True)
    lane, line = col[:1, :], row[:, :1]

    def factor(squares, at, axis):
        low = jnp.sum(jnp.where(at < HEAD, squares, 0.0), axis=axis, keepdims=True)
        high = jnp.sum(jnp.where(at < HEAD, 0.0, squares), axis=axis, keepdims=True)
        norm = jnp.where(pair, low + high, jnp.where(at < HEAD, low, high))
        return 1.0 / (jnp.sqrt(norm) + epsilon)

    by_col = factor(down, lane, 1)
    by_row = factor(across, line, 0)
    gram = gram * by_row * by_col
    unit = jnp.where(row == col, 1.0, 0.0)
    dot = lambda p, q: jnp.dot(p, q, precision=highest, preferred_element_type=f32)
    product = None
    for turn in range(NS_ITERS):
        step = quintic_a * unit + quintic_b * gram + quintic_c * dot(gram, gram)
        if turn < NS_ITERS - 1:
            gram = dot(dot(gram, step), step)
        product = step if product is None else dot(product, step)
    top = product.astype(bf16)
    rest = product - top.astype(f32)
    middle = rest.astype(bf16)
    bottom = (rest - middle.astype(f32)).astype(bf16)
    h = head_grad[...]
    update = jnp.dot(h, bottom, preferred_element_type=f32) + jnp.dot(h, middle, preferred_element_type=f32)
    update = update + jnp.dot(h, top, preferred_element_type=f32)
    result[...] = (update * (by_col * 64.0)).astype(bf16)
    for k, out in enumerate((o0, o1, o2, o3)):
        at = pl.multiple_of(((meta[ZH_AT] + k) & 3) * HALF, HALF)
        out[...] = result[pl.ds(at, HALF), :]


def place_heads(meta, p0, p1, p2, p3, q0, q1, q2, q3, out):
    ylo = meta[Y_AT] & 1
    for dx in range(4):
        for dzh in range(4):
            slot = ((meta[X_AT] - dx) & 3) * 4 + ((meta[ZH_AT] - dzh) & 3)
            for j in range(2):
                at = pl.multiple_of(meta[PERM_AT + slot * 2 + j] * HEAD, HEAD)
                for low, ref in ((ylo, (p0, p1, p2, p3)[dx]), (1 - ylo, (q0, q1, q2, q3)[dx])):
                    rows = pl.ds(pl.multiple_of(low * HALF, HALF), HALF)
                    out[rows, pl.ds(at, HEAD)] = ref[dzh, :, j * HEAD : (j + 1) * HEAD].astype(f32)


Y_INDEX = (0, 2, 1, 3)


def move_x(a, k):
    return lax.ppermute(a, "x", [(i, (i + k) % 4) for i in range(4)])


def move_y(a, k):
    return lax.ppermute(a, ("ylo", "yhi"), [(Y_INDEX[i], Y_INDEX[(i + k) % 4]) for i in range(4)])


def swap_y(a):
    return lax.ppermute(a, "ylo", [(0, 1), (1, 0)])


def swap_core(a):
    return lax.ppermute(a, "core", [(0, 1), (1, 0)])


def swap_z(a):
    return lax.ppermute(a, "z0", [(0, 1), (1, 0)])


def move_z(a, kh, k0):
    pairs = [(h * 2 + l, ((h + kh) % 4) * 2 + (l ^ k0)) for h in range(4) for l in range(2)]
    return lax.ppermute(a, ("zh", "z0"), pairs)


def on_device(activations, cotangent, masked, ratios, owners):
    tok, width = activations.shape
    meta = scalars(owners)
    weight = (masked.astype(f32) * 1000.0 / ratios[0].astype(f32))[:, None]
    blocks = local_kernel(
        prepare,
        [shape((BLOCK, tok), bf16)] * 4 + [shape((tok, BLOCK), bf16)] * 4,
        (meta, activations, cotangent, weight),
        24,
        2 * tok * width,
        "prepare",
    )
    rows, cols = blocks[:4], blocks[4:]
    rows = [rows[0]] + [move_y(rows[k], k) for k in (1, 2, 3)]
    cols = [cols[0]] + [move_x(cols[k], k) for k in (1, 2, 3)]
    r0, g0 = jnp.stack(rows), jnp.stack(cols)
    r1, r3 = move_x(r0, 1), move_x(r0, -1)
    g1, g3 = move_y(g0, 1), move_y(g0, -1)
    r2a, r2b = move_x(r1[:2], 1), move_x(r3[2:], -1)
    g2a, g2b = move_y(g1[:2], 1), move_y(g3[2:], -1)
    keep, send = local_kernel(
        multiply,
        [shape((8, 256, SLOT), bf16)] * 2,
        (meta, r0, r1, r3, r2a, r2b, g0, g1, g3, g2a, g2b),
        40,
        2 * BLOCK * BLOCK * 16 * tok,
        "multiply",
    )
    parts = local_kernel(
        add_cores,
        [shape((256, SLOT), bf16)] * 8,
        (meta, keep, swap_core(send)),
        8,
        8 * 256 * SLOT,
        "add_cores",
    )
    terms = [parts[0]] + [move_z(parts[k0 * 4 + kh], kh, k0) for kh, k0 in ((2, 0), (2, 1), (1, 1), (3, 1), (1, 0), (3, 0), (0, 1))]
    head_grad, mine, other, _ = local_kernel(
        gram_part,
        [shape((256, SLOT), bf16), shape((HEAD, SLOT), f32), shape((HEAD, SLOT), f32), shape((SLOT, SLOT), f32)],
        (meta, *terms),
        8,
        2 * 256 * SLOT * SLOT,
        "gram_part",
    )
    mine = mine + swap_core(other)
    mine = mine + swap_z(mine)
    mine = (mine + move_y(mine, 2)) + (move_y(mine, 1) + move_y(mine, 3))
    update = local_kernel(
        newton,
        [shape((HALF, SLOT), bf16)] * 4 + [shape((256, SLOT), bf16)],
        (meta, mine, swap_core(mine), head_grad),
        16,
        20 * 2 * SLOT**3 * 6,
        "newton",
    )
    p0 = jnp.stack([update[0]] + [lax.ppermute(update[k], "zh", [(i, (i + k) % 4) for i in range(4)]) for k in (1, 2, 3)])
    q0 = swap_y(p0)
    ps = [p0] + [move_x(p0, k) for k in (1, 2, 3)]
    qs = [q0] + [move_x(q0, k) for k in (1, 2, 3)]
    (out,) = local_kernel(
        place_heads, [shape((2 * HALF, width), f32)], (meta, *ps, *qs), 12, 0, "place_heads"
    )
    return out


def solution(mesh):
    axes = ("x", "ylo", "yhi", "zh", "z0", "core")
    fine = Mesh(mesh.devices.reshape(4, 2, 2, 4, 2, 2), axes)
    everywhere = P(axes)
    placed = (P(axes, None), P(axes, None), everywhere, everywhere, P())
    return jax.shard_map(
        on_device,
        mesh=fine,
        in_specs=placed,
        out_specs=P(("yhi", "zh", "z0", "core"), None),
        check_vma=False,
    )
```

time: 757 us -> 172 us (0.23)
  waiting for transfers between devices: 423 us -> 75.9 us
  blocking collectives: 167 us -> 0 us
  matrix products: 75.9 us -> 0 us
  starting transfers between devices: 0.04 us -> 67 us
  local copies, waits for them, and re-layouts: 66.5 us -> 2.8 us
  Pallas kernels: 0 us -> 19.7 us
  between operations: 15.4 us -> 3.39 us
    unnamed x3 -> x0, waiting for transfers between devices: 346 us -> none
    all_to_all x2 -> x0, blocking collectives: 167 us -> none  [the longest x1 102 us: on_device(): lax.all_to_all(iterate.reshape(n_af, my_rows, wide_slot), 'af', split_axi...]
    psum x1 -> x0, waiting for transfers between devices: 76.6 us -> none  [on_device(): gradient = lax.psum(gradient, 'ta')]
    dot_general x18 -> x0, matrix products: 75.9 us -> none  [the longest x5 35.2 us: products(): return jnp.einsum('ri,rj->ij', left, right, precision=highest)]
    ppermute x0 -> x38, waiting for transfers between devices: none -> 75.9 us  [the longest x10 36.8 us: move_y(): lax.ppermute(a, ('ylo', 'yhi'), [(Y_INDEX[i], Y_INDEX[(i + k) % 4]) for i...]
    ppermute x0 -> x38, starting transfers between devices: none -> 67 us  [the longest x7 20.8 us: move_z(): return lax.ppermute(a, ('zh', 'z0'), pairs)]
    unnamed x9 -> x4, local copies, waits for them, and re-layouts: 46.2 us -> 2.45 us
    pallas_call x0 -> x6, Pallas kernels: none -> 19.7 us  [local_kernel(): pl.pallas_call(body, out_shape=outs, in_specs=[smem()] + [vmem()] * (len(...]
  transfers between devices with their start and end apart: 2 -> 38, of which waited for: 2 -> 24; matrix products, arithmetic and copies ran while one was open for 0% -> 0% of each run, Pallas kernels for 0% -> 0%
where the time goes in v1:
time: 172 us
  waiting for transfers between devices  75.9 us (44%)
  starting transfers between devices  67 us (39%)
  Pallas kernels  19.7 us (11%)
  between operations  3.39 us (2%)
  other arithmetic  2.84 us (2%)
  local copies, waits for them, and re-layouts  2.8 us (2%)
    ppermute x10, waiting for transfers between devices, move_y(): lax.ppermute(a, ('ylo', 'yhi'), [(Y_INDEX[i], Y_INDEX[(i + k) % 4]) for i...  36.8 us
    ppermute x7, starting transfers between devices, move_z(): return lax.ppermute(a, ('zh', 'z0'), pairs)  20.8 us
    pallas_call x6, Pallas kernels, local_kernel(): pl.pallas_call(body, out_shape=outs, in_specs=[smem()] + [vmem()] * (len(...  19.7 us
    ppermute x10, starting transfers between devices, move_y(): lax.ppermute(a, ('ylo', 'yhi'), [(Y_INDEX[i], Y_INDEX[(i + k) % 4]) for i...  17.5 us
    ppermute x13, waiting for transfers between devices, move_x(): return lax.ppermute(a, 'x', [(i, (i + k) % 4) for i in range(4)])  15 us
    ppermute x13, starting transfers between devices, move_x(): return lax.ppermute(a, 'x', [(i, (i + k) % 4) for i in range(4)])  13.2 us
    ppermute x7, waiting for transfers between devices, move_z(): return lax.ppermute(a, ('zh', 'z0'), pairs)  10.5 us
    ppermute x3, starting transfers between devices, on_device(): lax.ppermute(update[k], 'zh', [(i, (i + k) % 4) for i in range(4)])  7.6 us
  transfers between devices with their start and end apart: 38, of which 24 were waited for; matrix products, arithmetic and copies ran while one was open for 0% of the time, Pallas kernels for 0%

profile of v1, /device:TPU:1, one launch (start us, length us, event | category | flops | bytes accessed | tf_op | source)
XLA Modules:
  0.0 171.6 jit_solution(15162633039398128655)
XLA Ops:
  12.0 2.5 %collective-permute-start.8 = (bf16[128,1024]{1,0:T(8,128)(2,1)S(1)}, bf16[128,1024]{1,0:T(8,128)(2,1)S(1)}, u32[]{:S(2)}, u32[]{:S(2)}) collective-permute-start(bf16[128,1024]{1,0:T(8,128)(2,1)S(1)} %get-tuple-element.36), channel_id=1, source_target_pairs={{0,128},{64,192},{128,0},{192,64},{1,129},{65,193},{129,1},{193,65... | collective-permute-start | bytes 786440 | tf_op jit(solution)/shard_map/ppermute | solution.py:205
  16.9 2.6 %collective-permute-start.1 = (bf16[1024,128]{1,0:T(8,128)(2,1)S(1)}, bf16[1024,128]{1,0:T(8,128)(2,1)S(1)}, u32[]{:S(2)}, u32[]{:S(2)}) collective-permute-start(bf16[1024,128]{1,0:T(8,128)(2,1)S(1)} %get-tuple-element.32), channel_id=1, source_target_pairs={{0,16},{32,48},{16,0},{48,32},{1,17},{33,49},{17,1},{49,33},{2,18}... | collective-permute-start | bytes 786440 | tf_op jit(solution)/shard_map/ppermute | solution.py:209
  21.9 3.9 %collective-permute-done.8 = bf16[128,1024]{1,0:T(8,128)(2,1)S(1)} collective-permute-done((bf16[128,1024]{1,0:T(8,128)(2,1)S(1)}, bf16[128,1024]{1,0:T(8,128)(2,1)S(1)}, u32[]{:S(2)}, u32[]{:S(2)}) %collective-permute-start.8) | collective-permute-done | bytes 262176 | tf_op jit(solution)/shard_map/ppermute | solution.py:205
  25.9 2.8 %collective-permute-start.11 = (bf16[4,128,1024]{2,1,0:T(8,128)(2,1)S(1)}, bf16[4,128,1024]{2,1,0:T(8,128)(2,1)S(1)}, u32[]{:S(2)}, u32[]{:S(2)}) collective-permute-start(bf16[4,128,1024]{2,1,0:T(8,128)(2,1)S(1)} %pad_maximum_fusion.1.g0), channel_id=1, source_target_pairs={{0,48},{32,0},{16,32},{48,16},{1,49},{33,1},{17,33},{49,17},{2,50}... | collective-permute-start | bytes 3145736 | tf_op jit(solution)/shard_map/ppermute | solution.py:209
  32.0 19.7 %collective-permute-done.11.g3 = bf16[4,128,1024]{2,1,0:T(8,128)(2,1)S(1)} collective-permute-done((bf16[4,128,1024]{2,1,0:T(8,128)(2,1)S(1)}, bf16[4,128,1024]{2,1,0:T(8,128)(2,1)S(1)}, u32[]{:S(2)}, u32[]{:S(2)}) %collective-permute-start.11) | collective-permute-done | bytes 1048608 | tf_op jit(solution)/shard_map/ppermute | solution.py:209
  51.8 3.5 %collective-permute-start.13 = (bf16[2,128,1024]{2,1,0:T(8,128)(2,1)S(1)}, bf16[2,128,1024]{2,1,0:T(8,128)(2,1)S(1)}, u32[]{:S(2)}, u32[]{:S(2)}) collective-permute-start(bf16[2,128,1024]{2,1,0:T(8,128)(2,1)S(1)} %slice.19), channel_id=1, source_target_pairs={{0,48},{32,0},{16,32},{48,16},{1,49},{33,1},{17,33},{49,17},{2,50}... | collective-permute-start | bytes 1572872 | tf_op jit(solution)/shard_map/ppermute | solution.py:209
  58.2 9.8 %collective-permute-done.13.g2b = bf16[2,128,1024]{2,1,0:T(8,128)(2,1)S(1)} collective-permute-done((bf16[2,128,1024]{2,1,0:T(8,128)(2,1)S(1)}, bf16[2,128,1024]{2,1,0:T(8,128)(2,1)S(1)}, u32[]{:S(2)}, u32[]{:S(2)}) %collective-permute-start.13) | collective-permute-done | bytes 524320 | tf_op jit(solution)/shard_map/ppermute | solution.py:209
  70.6 5.0 %multiply.1 = (bf16[8,256,256]{2,1,0:T(8,128)(2,1)S(1)}, bf16[8,256,256]{2,1,0:T(8,128)(2,1)S(1)}) custom-call(s32[40]{0:T(128)S(1)} %concatenate.3.meta, bf16[4,1024,128]{2,1,0:T(8,128)(2,1)S(1)} %pad_maximum_fusion.r0, bf16[4,1024,128]{2,1,0:T(8,128)(2,1)S(1)} %collective-permute-done.3.r1, bf16[4,1024,128]{2,1,0:T(8,128)(2,1)S(1)} %collective-permute-done.4.r3, ...), custom_call_target="tpu_custom_call" | custom-call | flops 4294967296 | bytes 10485920 | tf_op jit(solution)/shard_map/multiply/pallas_call | solution.py:37
  75.7 2.9 %collective-permute-start.14 = (bf16[8,256,256]{2,1,0:T(8,128)(2,1)S(1)}, bf16[8,256,256]{2,1,0:T(8,128)(2,1)S(1)}, u32[]{:S(2)}, u32[]{:S(2)}) collective-permute-start(bf16[8,256,256]{2,1,0:T(8,128)(2,1)S(1)} %get-tuple-element.39), channel_id=1, source_target_pairs={{0,1},{1,0},{2,3},{3,2},{4,5},{5,4},{6,7},{7,6},{8,9},{9,8},{10,11... | collective-permute-start | bytes 3145736 | tf_op jit(solution)/shard_map/ppermute | solution.py:217
  81.6 7.0 %collective-permute-start.15 = (bf16[256,256]{1,0:T(8,128)(2,1)S(1)}, bf16[256,256]{1,0:T(8,128)(2,1)S(1)}, u32[]{:S(2)}, u32[]{:S(2)}) collective-permute-start(bf16[256,256]{1,0:T(8,128)(2,1)S(1)} %get-tuple-element.41), channel_id=1, source_target_pairs={{0,8},{2,10},{4,12},{6,14},{8,0},{10,2},{12,4},{14,6},{1,9},{3,11}... | collective-permute-start | bytes 393224 | tf_op jit(solution)/shard_map/ppermute | solution.py:226
  94.3 5.0 %collective-permute-start.20 = (bf16[256,256]{1,0:T(8,128)(2,1)S(1)}, bf16[256,256]{1,0:T(8,128)(2,1)S(1)}, u32[]{:S(2)}, u32[]{:S(2)}) collective-permute-start(bf16[256,256]{1,0:T(8,128)(2,1)S(1)} %get-tuple-element.46), channel_id=1, source_target_pairs={{0,12},{2,14},{4,0},{6,2},{8,4},{10,6},{12,8},{14,10},{1,13},{3,15... | collective-permute-start | bytes 393224 | tf_op jit(solution)/shard_map/ppermute | solution.py:226
  99.3 3.3 %collective-permute-done.16.refs_2_ = bf16[256,256]{1,0:T(8,128)(2,1)S(1)} collective-permute-done((bf16[256,256]{1,0:T(8,128)(2,1)S(1)}, bf16[256,256]{1,0:T(8,128)(2,1)S(1)}, u32[]{:S(2)}, u32[]{:S(2)}) %collective-permute-start.16) | collective-permute-done | bytes 131104 | tf_op jit(solution)/shard_map/ppermute | solution.py:226
  102.7 3.1 %collective-permute-start.21 = (bf16[256,256]{1,0:T(8,128)(2,1)S(1)}, bf16[256,256]{1,0:T(8,128)(2,1)S(1)}, u32[]{:S(2)}, u32[]{:S(2)}) collective-permute-start(bf16[256,256]{1,0:T(8,128)(2,1)S(1)} %get-tuple-element.47), channel_id=1, source_target_pairs={{0,2},{2,0},{4,6},{6,4},{8,10},{10,8},{12,14},{14,12},{1,3},{3,1},... | collective-permute-start | bytes 393224 | tf_op jit(solution)/shard_map/ppermute | solution.py:226
  105.8 3.1 %collective-permute-done.17.refs_3_ = bf16[256,256]{1,0:T(8,128)(2,1)S(1)} collective-permute-done((bf16[256,256]{1,0:T(8,128)(2,1)S(1)}, bf16[256,256]{1,0:T(8,128)(2,1)S(1)}, u32[]{:S(2)}, u32[]{:S(2)}) %collective-permute-start.17) | collective-permute-done | bytes 131104 | tf_op jit(solution)/shard_map/ppermute | solution.py:226
  108.9 4.0 %collective-permute-done.20.refs_6_ = bf16[256,256]{1,0:T(8,128)(2,1)S(1)} collective-permute-done((bf16[256,256]{1,0:T(8,128)(2,1)S(1)}, bf16[256,256]{1,0:T(8,128)(2,1)S(1)}, u32[]{:S(2)}, u32[]{:S(2)}) %collective-permute-start.20) | collective-permute-done | bytes 131104 | tf_op jit(solution)/shard_map/ppermute | solution.py:226
  117.2 4.3 %collective-permute-done.23 = f32[128,256]{1,0:T(8,128)S(1)} collective-permute-done((f32[128,256]{1,0:T(8,128)S(1)}, f32[128,256]{1,0:T(8,128)S(1)}, u32[]{:S(2)}, u32[]{:S(2)}) %collective-permute-start.23) | collective-permute-done | bytes 131104 | tf_op jit(solution)/shard_map/ppermute | solution.py:221
  121.4 2.7 %collective-permute-start.26 = (f32[128,256]{1,0:T(8,128)S(1)}, f32[128,256]{1,0:T(8,128)S(1)}, u32[]{:S(2)}, u32[]{:S(2)}) collective-permute-start(f32[128,256]{1,0:T(8,128)S(1)} %add.45), channel_id=1, source_target_pairs={{0,48},{32,0},{16,32},{48,16},{1,49},{33,1},{17,33},{49,17},{2,50}... | collective-permute-start | bytes 393224 | tf_op jit(solution)/shard_map/ppermute | solution.py:209
  126.1 4.9 %collective-permute-done.25 = f32[128,256]{1,0:T(8,128)S(1)} collective-permute-done((f32[128,256]{1,0:T(8,128)S(1)}, f32[128,256]{1,0:T(8,128)S(1)}, u32[]{:S(2)}, u32[]{:S(2)}) %collective-permute-start.25) | collective-permute-done | bytes 131104 | tf_op jit(solution)/shard_map/ppermute | solution.py:209
  131.2 3.2 %collective-permute-start.27 = (f32[128,256]{1,0:T(8,128)S(1)}, f32[128,256]{1,0:T(8,128)S(1)}, u32[]{:S(2)}, u32[]{:S(2)}) collective-permute-start(f32[128,256]{1,0:T(8,128)S(1)} %add_add_fusion.mine), channel_id=1, source_target_pairs={{0,1},{1,0},{2,3},{3,2},{4,5},{5,4},{6,7},{7,6},{8,9},{9,8},{10,11... | collective-permute-start | bytes 393224 | tf_op jit(solution)/shard_map/ppermute | solution.py:217
  135.4 8.8 %newton.1 = (bf16[64,256]{1,0:T(8,128)(2,1)S(1)}, bf16[64,256]{1,0:T(8,128)(2,1)S(1)}, bf16[64,256]{1,0:T(8,128)(2,1)S(1)}, bf16[64,256]{1,0:T(8,128)(2,1)S(1)}, bf16[256,256]{1,0:T(8,128)(2,1)}) custom-call(s32[40]{0:T(128)S(1)} %concatenate.3.meta, f32[128,256]{1,0:T(8,128)S(1)} %add_add_fusion.mine, f32[128,256]{1,0:T(8,128)S(1)} %collective-permute-done.27.other, ...), custom_call_target="tpu_custom_call" | custom-call | flops 4026531840 | bytes 655520 | tf_op jit(solution)/shard_map/newton/pallas_call | solution.py:37
  146.5 3.5 %collective-permute-start.29 = (bf16[64,256]{1,0:T(8,128)(2,1)S(1)}, bf16[64,256]{1,0:T(8,128)(2,1)S(1)}, u32[]{:S(2)}, u32[]{:S(2)}) collective-permute-start(bf16[64,256]{1,0:T(8,128)(2,1)S(1)} %get-tuple-element.53), channel_id=1, source_target_pairs={{0,8},{4,12},{8,0},{12,4},{1,9},{5,13},{9,1},{13,5},{2,10},{6,14},... | collective-permute-start | bytes 98312 | tf_op jit(solution)/shard_map/ppermute | solution.py:285
  160.8 2.9 %collective-permute-done.31.p1 = bf16[4,64,256]{2,1,0:T(8,128)(2,1)S(1)} collective-permute-done((bf16[4,64,256]{2,1,0:T(8,128)(2,1)S(1)}, bf16[4,64,256]{2,1,0:T(8,128)(2,1)S(1)}, u32[]{:S(2)}, u32[]{:S(2)}) %collective-permute-start.31) | collective-permute-done | bytes 131104 | tf_op jit(solution)/shard_map/ppermute | solution.py:205
  164.2 2.6 %collective-permute-done.36.q2 = bf16[4,64,256]{2,1,0:T(8,128)(2,1)S(1)} collective-permute-done((bf16[4,64,256]{2,1,0:T(8,128)(2,1)S(1)}, bf16[4,64,256]{2,1,0:T(8,128)(2,1)S(1)}, u32[]{:S(2)}, u32[]{:S(2)}) %collective-permute-start.36) | collective-permute-done | bytes 131104 | tf_op jit(solution)/shard_map/ppermute | solution.py:205
  166.8 2.8 %collective-permute-done.35.q1 = bf16[4,64,256]{2,1,0:T(8,128)(2,1)S(1)} collective-permute-done((bf16[4,64,256]{2,1,0:T(8,128)(2,1)S(1)}, bf16[4,64,256]{2,1,0:T(8,128)(2,1)S(1)}, u32[]{:S(2)}, u32[]{:S(2)}) %collective-permute-start.35) | collective-permute-done | bytes 131104 | tf_op jit(solution)/shard_map/ppermute | solution.py:205
  (79 shorter events, 54.3 us)
Async XLA Ops:
  9.9 9.6 %collective-permute-start.7 = (bf16[128,1024]{1,0:T(8,128)(2,1)S(1)}, bf16[128,1024]{1,0:T(8,128)(2,1)S(1)}, u32[]{:S(2)}, u32[]{:S(2)}) collective-permute-start(bf16[128,1024]{1,0:T(8,128)(2,1)S(1)} %get-tuple-element.35), channel_id=1, source_target_pairs={{0,64},{64,128},{128,192},{192,0},{1,65},{65,129},{129,193},{193,1... | collective-permute-start | bytes 786440 | tf_op jit(solution)/shard_map/ppermute | solution.py:205
  12.0 13.8 %collective-permute-start.8 = (bf16[128,1024]{1,0:T(8,128)(2,1)S(1)}, bf16[128,1024]{1,0:T(8,128)(2,1)S(1)}, u32[]{:S(2)}, u32[]{:S(2)}) collective-permute-start(bf16[128,1024]{1,0:T(8,128)(2,1)S(1)} %get-tuple-element.36), channel_id=1, source_target_pairs={{0,128},{64,192},{128,0},{192,64},{1,129},{65,193},{129,1},{193,65... | collective-permute-start | bytes 786440 | tf_op jit(solution)/shard_map/ppermute | solution.py:205
  14.5 11.3 %collective-permute-start.9 = (bf16[128,1024]{1,0:T(8,128)(2,1)S(1)}, bf16[128,1024]{1,0:T(8,128)(2,1)S(1)}, u32[]{:S(2)}, u32[]{:S(2)}) collective-permute-start(bf16[128,1024]{1,0:T(8,128)(2,1)S(1)} %get-tuple-element.37), channel_id=1, source_target_pairs={{0,192},{64,0},{128,64},{192,128},{1,193},{65,1},{129,65},{193,129... | collective-permute-start | bytes 786440 | tf_op jit(solution)/shard_map/ppermute | solution.py:205
  15.6 13.1 %collective-permute-start = (bf16[1024,128]{1,0:T(8,128)(2,1)S(1)}, bf16[1024,128]{1,0:T(8,128)(2,1)S(1)}, u32[]{:S(2)}, u32[]{:S(2)}) collective-permute-start(bf16[1024,128]{1,0:T(8,128)(2,1)S(1)} %get-tuple-element.31), channel_id=1, source_target_pairs={{0,32},{32,16},{16,48},{48,0},{1,33},{33,17},{17,49},{49,1},{2,34}... | collective-permute-start | bytes 786440 | tf_op jit(solution)/shard_map/ppermute | solution.py:209
  16.9 13.1 %collective-permute-start.1 = (bf16[1024,128]{1,0:T(8,128)(2,1)S(1)}, bf16[1024,128]{1,0:T(8,128)(2,1)S(1)}, u32[]{:S(2)}, u32[]{:S(2)}) collective-permute-start(bf16[1024,128]{1,0:T(8,128)(2,1)S(1)} %get-tuple-element.32), channel_id=1, source_target_pairs={{0,16},{32,48},{16,0},{48,32},{1,17},{33,49},{17,1},{49,33},{2,18}... | collective-permute-start | bytes 786440 | tf_op jit(solution)/shard_map/ppermute | solution.py:209
  19.5 10.4 %collective-permute-start.2 = (bf16[1024,128]{1,0:T(8,128)(2,1)S(1)}, bf16[1024,128]{1,0:T(8,128)(2,1)S(1)}, u32[]{:S(2)}, u32[]{:S(2)}) collective-permute-start(bf16[1024,128]{1,0:T(8,128)(2,1)S(1)} %get-tuple-element.33), channel_id=1, source_target_pairs={{0,48},{32,0},{16,32},{48,16},{1,49},{33,1},{17,33},{49,17},{2,50}... | collective-permute-start | bytes 786440 | tf_op jit(solution)/shard_map/ppermute | solution.py:209
  25.9 25.8 %collective-permute-start.11 = (bf16[4,128,1024]{2,1,0:T(8,128)(2,1)S(1)}, bf16[4,128,1024]{2,1,0:T(8,128)(2,1)S(1)}, u32[]{:S(2)}, u32[]{:S(2)}) collective-permute-start(bf16[4,128,1024]{2,1,0:T(8,128)(2,1)S(1)} %pad_maximum_fusion.1.g0), channel_id=1, source_target_pairs={{0,48},{32,0},{16,32},{48,16},{1,49},{33,1},{17,33},{49,17},{2,50}... | collective-permute-start | bytes 3145736 | tf_op jit(solution)/shard_map/ppermute | solution.py:209
  28.7 26.5 %collective-permute-start.10 = (bf16[4,128,1024]{2,1,0:T(8,128)(2,1)S(1)}, bf16[4,128,1024]{2,1,0:T(8,128)(2,1)S(1)}, u32[]{:S(2)}, u32[]{:S(2)}) collective-permute-start(bf16[4,128,1024]{2,1,0:T(8,128)(2,1)S(1)} %pad_maximum_fusion.1.g0), channel_id=1, source_target_pairs={{0,32},{32,16},{16,48},{48,0},{1,33},{33,17},{17,49},{49,1},{2,34}... | collective-permute-start | bytes 3145736 | tf_op jit(solution)/shard_map/ppermute | solution.py:209
  30.1 26.2 %collective-permute-start.4 = (bf16[4,1024,128]{2,1,0:T(8,128)(2,1)S(1)}, bf16[4,1024,128]{2,1,0:T(8,128)(2,1)S(1)}, u32[]{:S(2)}, u32[]{:S(2)}) collective-permute-start(bf16[4,1024,128]{2,1,0:T(8,128)(2,1)S(1)} %pad_maximum_fusion.r0), channel_id=1, source_target_pairs={{0,192},{64,0},{128,64},{192,128},{1,193},{65,1},{129,65},{193,129... | collective-permute-start | bytes 3145736 | tf_op jit(solution)/shard_map/ppermute | solution.py:205
  32.0 25.6 %collective-permute-start.3 = (bf16[4,1024,128]{2,1,0:T(8,128)(2,1)S(1)}, bf16[4,1024,128]{2,1,0:T(8,128)(2,1)S(1)}, u32[]{:S(2)}, u32[]{:S(2)}) collective-permute-start(bf16[4,1024,128]{2,1,0:T(8,128)(2,1)S(1)} %pad_maximum_fusion.r0), channel_id=1, source_target_pairs={{0,64},{64,128},{128,192},{192,0},{1,65},{65,129},{129,193},{193,1... | collective-permute-start | bytes 3145736 | tf_op jit(solution)/shard_map/ppermute | solution.py:205
  51.8 16.2 %collective-permute-start.13 = (bf16[2,128,1024]{2,1,0:T(8,128)(2,1)S(1)}, bf16[2,128,1024]{2,1,0:T(8,128)(2,1)S(1)}, u32[]{:S(2)}, u32[]{:S(2)}) collective-permute-start(bf16[2,128,1024]{2,1,0:T(8,128)(2,1)S(1)} %slice.19), channel_id=1, source_target_pairs={{0,48},{32,0},{16,32},{48,16},{1,49},{33,1},{17,33},{49,17},{2,50}... | collective-permute-start | bytes 1572872 | tf_op jit(solution)/shard_map/ppermute | solution.py:209
  55.3 12.9 %collective-permute-start.12 = (bf16[2,128,1024]{2,1,0:T(8,128)(2,1)S(1)}, bf16[2,128,1024]{2,1,0:T(8,128)(2,1)S(1)}, u32[]{:S(2)}, u32[]{:S(2)}) collective-permute-start(bf16[2,128,1024]{2,1,0:T(8,128)(2,1)S(1)} %slice.18), channel_id=1, source_target_pairs={{0,32},{32,16},{16,48},{48,0},{1,33},{33,17},{17,49},{49,1},{2,34}... | collective-permute-start | bytes 1572872 | tf_op jit(solution)/shard_map/ppermute | solution.py:209
  56.3 12.6 %collective-permute-start.6 = (bf16[2,1024,128]{2,1,0:T(8,128)(2,1)S(1)}, bf16[2,1024,128]{2,1,0:T(8,128)(2,1)S(1)}, u32[]{:S(2)}, u32[]{:S(2)}) collective-permute-start(bf16[2,1024,128]{2,1,0:T(8,128)(2,1)S(1)} %slice.17), channel_id=1, source_target_pairs={{0,192},{64,0},{128,64},{192,128},{1,193},{65,1},{129,65},{193,129... | collective-permute-start | bytes 1572872 | tf_op jit(solution)/shard_map/ppermute | solution.py:205
  57.6 13.0 %collective-permute-start.5 = (bf16[2,1024,128]{2,1,0:T(8,128)(2,1)S(1)}, bf16[2,1024,128]{2,1,0:T(8,128)(2,1)S(1)}, u32[]{:S(2)}, u32[]{:S(2)}) collective-permute-start(bf16[2,1024,128]{2,1,0:T(8,128)(2,1)S(1)} %slice.16), channel_id=1, source_target_pairs={{0,64},{64,128},{128,192},{192,0},{1,65},{65,129},{129,193},{193,1... | collective-permute-start | bytes 1572872 | tf_op jit(solution)/shard_map/ppermute | solution.py:205
  81.6 12.7 %collective-permute-start.15 = (bf16[256,256]{1,0:T(8,128)(2,1)S(1)}, bf16[256,256]{1,0:T(8,128)(2,1)S(1)}, u32[]{:S(2)}, u32[]{:S(2)}) collective-permute-start(bf16[256,256]{1,0:T(8,128)(2,1)S(1)} %get-tuple-element.41), channel_id=1, source_target_pairs={{0,8},{2,10},{4,12},{6,14},{8,0},{10,2},{12,4},{14,6},{1,9},{3,11}... | collective-permute-start | bytes 393224 | tf_op jit(solution)/shard_map/ppermute | solution.py:226
  88.6 14.0 %collective-permute-start.16 = (bf16[256,256]{1,0:T(8,128)(2,1)S(1)}, bf16[256,256]{1,0:T(8,128)(2,1)S(1)}, u32[]{:S(2)}, u32[]{:S(2)}) collective-permute-start(bf16[256,256]{1,0:T(8,128)(2,1)S(1)} %get-tuple-element.42), channel_id=1, source_target_pairs={{0,10},{2,8},{4,14},{6,12},{8,2},{10,0},{12,6},{14,4},{1,11},{3,9}... | collective-permute-start | bytes 393224 | tf_op jit(solution)/shard_map/ppermute | solution.py:226
  88.6 20.2 %collective-permute-start.17 = (bf16[256,256]{1,0:T(8,128)(2,1)S(1)}, bf16[256,256]{1,0:T(8,128)(2,1)S(1)}, u32[]{:S(2)}, u32[]{:S(2)}) collective-permute-start(bf16[256,256]{1,0:T(8,128)(2,1)S(1)} %get-tuple-element.43), channel_id=1, source_target_pairs={{0,6},{2,4},{4,10},{6,8},{8,14},{10,12},{12,2},{14,0},{1,7},{3,5},... | collective-permute-start | bytes 393224 | tf_op jit(solution)/shard_map/ppermute | solution.py:226
  90.3 18.6 %collective-permute-start.18 = (bf16[256,256]{1,0:T(8,128)(2,1)S(1)}, bf16[256,256]{1,0:T(8,128)(2,1)S(1)}, u32[]{:S(2)}, u32[]{:S(2)}) collective-permute-start(bf16[256,256]{1,0:T(8,128)(2,1)S(1)} %get-tuple-element.44), channel_id=1, source_target_pairs={{0,14},{2,12},{4,2},{6,0},{8,6},{10,4},{12,10},{14,8},{1,15},{3,13... | collective-permute-start | bytes 393224 | tf_op jit(solution)/shard_map/ppermute | solution.py:226
  92.2 16.6 %collective-permute-start.19 = (bf16[256,256]{1,0:T(8,128)(2,1)S(1)}, bf16[256,256]{1,0:T(8,128)(2,1)S(1)}, u32[]{:S(2)}, u32[]{:S(2)}) collective-permute-start(bf16[256,256]{1,0:T(8,128)(2,1)S(1)} %get-tuple-element.45), channel_id=1, source_target_pairs={{0,4},{2,6},{4,8},{6,10},{8,12},{10,14},{12,0},{14,2},{1,5},{3,7},... | collective-permute-start | bytes 393224 | tf_op jit(solution)/shard_map/ppermute | solution.py:226
  94.3 18.6 %collective-permute-start.20 = (bf16[256,256]{1,0:T(8,128)(2,1)S(1)}, bf16[256,256]{1,0:T(8,128)(2,1)S(1)}, u32[]{:S(2)}, u32[]{:S(2)}) collective-permute-start(bf16[256,256]{1,0:T(8,128)(2,1)S(1)} %get-tuple-element.46), channel_id=1, source_target_pairs={{0,12},{2,14},{4,0},{6,2},{8,4},{10,6},{12,8},{14,10},{1,13},{3,15... | collective-permute-start | bytes 393224 | tf_op jit(solution)/shard_map/ppermute | solution.py:226
  102.7 10.2 %collective-permute-start.21 = (bf16[256,256]{1,0:T(8,128)(2,1)S(1)}, bf16[256,256]{1,0:T(8,128)(2,1)S(1)}, u32[]{:S(2)}, u32[]{:S(2)}) collective-permute-start(bf16[256,256]{1,0:T(8,128)(2,1)S(1)} %get-tuple-element.47), channel_id=1, source_target_pairs={{0,2},{2,0},{4,6},{6,4},{8,10},{10,8},{12,14},{14,12},{1,3},{3,1},... | collective-permute-start | bytes 393224 | tf_op jit(solution)/shard_map/ppermute | solution.py:226
  155.5 8.2 %collective-permute-start.31 = (bf16[4,64,256]{2,1,0:T(8,128)(2,1)S(1)}, bf16[4,64,256]{2,1,0:T(8,128)(2,1)S(1)}, u32[]{:S(2)}, u32[]{:S(2)}) collective-permute-start(bf16[4,64,256]{2,1,0:T(8,128)(2,1)S(1)} %pad_maximum_fusion.2.p0), channel_id=1, source_target_pairs={{0,64},{64,128},{128,192},{192,0},{1,65},{65,129},{129,193},{193,1... | collective-permute-start | bytes 393224 | tf_op jit(solution)/shard_map/ppermute | solution.py:205
  158.8 8.0 %collective-permute-start.36 = (bf16[4,64,256]{2,1,0:T(8,128)(2,1)S(1)}, bf16[4,64,256]{2,1,0:T(8,128)(2,1)S(1)}, u32[]{:S(2)}, u32[]{:S(2)}) collective-permute-start(bf16[4,64,256]{2,1,0:T(8,128)(2,1)S(1)} %collective-permute-done.34.q0), channel_id=1, source_target_pairs={{0,128},{64,192},{128,0},{192,64},{1,129},{65,193},{129,1},{193,65... | collective-permute-start | bytes 393224 | tf_op jit(solution)/shard_map/ppermute | solution.py:205
  160.0 9.6 %collective-permute-start.35 = (bf16[4,64,256]{2,1,0:T(8,128)(2,1)S(1)}, bf16[4,64,256]{2,1,0:T(8,128)(2,1)S(1)}, u32[]{:S(2)}, u32[]{:S(2)}) collective-permute-start(bf16[4,64,256]{2,1,0:T(8,128)(2,1)S(1)} %collective-permute-done.34.q0), channel_id=1, source_target_pairs={{0,64},{64,128},{128,192},{192,0},{1,65},{65,129},{129,193},{193,1... | collective-permute-start | bytes 393224 | tf_op jit(solution)/shard_map/ppermute | solution.py:205
  (16 other events, 77.0 us)

commit v2 on v1

v2 whole, which is shorter than its diff:
```python
import functools

import jax
import jax.numpy as jnp
from jax import lax
from jax.experimental import pallas as pl
from jax.experimental.pallas import tpu as pltpu
from jax.sharding import Mesh
from jax.sharding import PartitionSpec as P

HEADS = 32
NS_ITERS = 5
quintic_a = 3.4445
quintic_b = -4.775
quintic_c = 2.0315
epsilon = 1e-07

PAIRS_AT, PERM_AT = 0, 8

HEAD = 128
SLOT = 2 * HEAD
BLOCK = 1024
HALF = 64
GRAM = HEAD + HALF

f32, bf16 = jnp.float32, jnp.bfloat16


def smem():
    return pl.BlockSpec(memory_space=pltpu.SMEM)


def vmem():
    return pl.BlockSpec(memory_space=pltpu.VMEM)


def anywhere():
    return pl.BlockSpec(memory_space=pl.ANY)


def local_kernel(body, outs, operands, mib, flops, name, in_specs=None, out_specs=None, scratch=()):
    moved = sum(o.size * o.dtype.itemsize for o in list(outs) + list(operands))
    return pl.pallas_call(
        body,
        out_shape=outs,
        in_specs=in_specs or [vmem()] * len(operands),
        out_specs=out_specs or [vmem()] * len(outs),
        scratch_shapes=list(scratch),
        compiler_params=pltpu.CompilerParams(vmem_limit_bytes=mib * 2**20),
        cost_estimate=pl.CostEstimate(flops=flops, bytes_accessed=moved, transcendentals=0),
        name=name,
    )(*operands)


def shape(dims, dtype):
    return jax.ShapeDtypeStruct(dims, dtype)


def y_place():
    return lax.axis_index("yhi") * 2 + lax.axis_index("ylo")


def prepare(owners, ratio, masked, act_far, cot_far, *refs):
    rows_out, cols_out, meta = refs[:4], refs[4:8], refs[8]
    act, cot, count, taken, sems = refs[9:]
    get_act = pltpu.make_async_copy(act_far, act, sems.at[0])
    get_cot = pltpu.make_async_copy(cot_far, cot, sems.at[1])
    get_act.start()
    get_cot.start()

    for v in range(HEADS):
        count[v] = 0
        taken[v] = 0
    for h in range(HEADS):
        count[owners[h]] = count[owners[h]] + 1
    in_pairs = jnp.int32(0)
    for v in range(HEADS):
        in_pairs = in_pairs + jnp.where(count[v] > 1, 2, 0)
    next_pair, next_alone = jnp.int32(0), in_pairs
    for i in range(PERM_AT):
        meta[i] = in_pairs // 2
    for h in range(HEADS):
        owner = owners[h]
        paired = count[owner] > 1
        seen = taken[owner]
        opens = jnp.logical_and(paired, seen == 0)
        place = jnp.where(paired, jnp.where(seen == 0, next_pair, seen), next_alone)
        taken[owner] = place + 1
        meta[PERM_AT + place] = h
        next_pair = next_pair + jnp.where(opens, 2, 0)
        next_alone = next_alone + jnp.where(paired, 0, 1)

    tok, width = act.shape
    here_y, z0, core = y_place(), lax.axis_index("z0"), lax.axis_index("core")
    get_act.wait()
    for k in range(4):
        y = (here_y + k) & 3
        base = (y >> 1) * (width // 2)
        low = (y & 1) * HALF
        for crel in range(2):
            for zrel in range(2):
                for zh in range(4):
                    block = zh * 4 + (z0 ^ zrel) * 2 + (core ^ crel)
                    at = pl.multiple_of(base + block * 128, 128)
                    turned = act[:, pl.ds(at, 128)].T
                    part = jnp.where(low == 0, turned[:HALF], turned[HALF:])
                    to = ((crel * 2 + zrel) * 4 + zh) * HALF
                    rows_out[k][to : to + HALF, :] = part
    along = masked[...].astype(f32) * 1000.0 / ratio[0].astype(f32)
    line = lax.broadcasted_iota(jnp.int32, (tok, tok), 0)
    lane = lax.broadcasted_iota(jnp.int32, (tok, tok), 1)
    weight = jnp.sum(jnp.where(line == lane, along, 0.0), axis=1, keepdims=True)
    get_cot.wait()
    for k in range(4):
        x = (lax.axis_index("x") + k) & 3
        for j in range(8):
            slot = x * 4 + ((lax.axis_index("zh") + j // 2) & 3)
            head = meta[PERM_AT + slot * 2 + j % 2]
            at = pl.multiple_of(head * HEAD, HEAD)
            piece = cot[:, pl.ds(at, HEAD)].astype(f32) * weight
            cols_out[k][:, j * HEAD : (j + 1) * HEAD] = piece.astype(bf16)


def multiply(offset, r0, r1, r3, r2a, r2b, g0, g1, g3, g2a, g2b, out):
    z0 = lax.axis_index("z0")
    half = BLOCK // 2

    def rows_of(dx, dy):
        ref, i = ((r2a if dy < 2 else r2b), dy % 2) if dx == 2 else ({0: r0, 1: r1, 3: r3}[dx], dy)
        return ref[i, offset : offset + half, :]

    def cols_of(dx, dy, at):
        ref, i = ((g2a if dx < 2 else g2b), dx % 2) if dy == 2 else ({0: g0, 1: g1, 3: g3}[dy], dx)
        return ref[i, :, at : at + SLOT]

    for n in range(BLOCK // SLOT):
        total = jnp.zeros((half, SLOT), f32)
        for dx in range(4):
            left = jnp.concatenate([rows_of(dx, dy) for dy in range(4)], axis=1)
            right = jnp.concatenate([cols_of(dx, dy, n * SLOT) for dy in range(4)], axis=0)
            total = total + jnp.dot(left, right, preferred_element_type=f32)
        total = total.astype(bf16)
        out[2 * n] = total[:128]
        out[2 * n + 1] = total[128:256]
        out[8 + ((n - z0) & 3)] = total[256:384]
        out[12 + ((n + 1 - z0) & 3)] = total[384:]


def add_odd(mine, other, up, down):
    for j in range(4):
        up[j] = (mine[8 + j].astype(f32) + other[8 + j].astype(f32)).astype(bf16)
        down[j] = (mine[12 + j].astype(f32) + other[12 + j].astype(f32)).astype(bf16)


def add_even(mine, other, up, down, *outs):
    for a, out in enumerate(outs):
        for h, ref in enumerate((up, down)):
            total = mine[2 * a + h].astype(f32) + other[2 * a + h].astype(f32) + ref[a].astype(f32)
            out[h * 128 : (h + 1) * 128, :] = total.astype(out.dtype)


def gram_part(t0, t1, t2, t3, head_grad, keep, send):
    total = (t0[...] + t1[...].astype(f32)) + (t2[...].astype(f32) + t3[...].astype(f32))
    part = total.astype(bf16)
    head_grad[...] = part
    gram = lax.dot_general(part, part, (((0,), (0,)), ((), ())), preferred_element_type=f32)
    first = jnp.concatenate([gram[:HEAD, :HEAD], gram[:HALF, HEAD:]], axis=0)
    second = jnp.concatenate([gram[HEAD:, HEAD:], gram[HALF:HEAD, HEAD:]], axis=0)
    core = lax.axis_index("core")
    keep[...] = jnp.where(core == 0, first, second)
    send[...] = jnp.where(core == 0, second, first)


def split(a):
    top = a.astype(bf16)
    rest = a - top.astype(f32)
    middle = rest.astype(bf16)
    return top, middle, (rest - middle.astype(f32)).astype(bf16)


def dot(a, b):
    left = jnp.concatenate([a[2], a[0], a[1], a[1], a[0], a[0]], axis=1)
    right = jnp.concatenate([b[0], b[2], b[1], b[0], b[1], b[0]], axis=0)
    return jnp.dot(left, right, preferred_element_type=f32)


def newton(meta, mine, other, head_grad, o0, o1, o2, o3, result):
    core = lax.axis_index("core")
    a, b = mine[...], other[...]
    first, second = jnp.where(core == 0, a, b), jnp.where(core == 0, b, a)
    corner = jnp.concatenate([first[HEAD:], second[HEAD:]], axis=0)
    gram = jnp.concatenate(
        [
            jnp.concatenate([first[:HEAD], corner], axis=1),
            jnp.concatenate([corner.T, second[:HEAD]], axis=1),
        ],
        axis=0,
    )
    zh = lax.axis_index("zh")
    pair = lax.axis_index("x") * 4 + zh < meta[PAIRS_AT]
    row = lax.broadcasted_iota(jnp.int32, (SLOT, SLOT), 0)
    col = lax.broadcasted_iota(jnp.int32, (SLOT, SLOT), 1)
    together = jnp.logical_or((row < HEAD) == (col < HEAD), pair)
    gram = jnp.where(together, gram, 0.0)
    on_diagonal = jnp.where(row == col, gram, 0.0)
    down = jnp.sum(on_diagonal, axis=0, keepdims=True)
    across = jnp.sum(on_diagonal, axis=1, keepdims=True)
    lane, line = col[:1, :], row[:, :1]

    def factor(squares, at, axis):
        low = jnp.sum(jnp.where(at < HEAD, squares, 0.0), axis=axis, keepdims=True)
        high = jnp.sum(jnp.where(at < HEAD, 0.0, squares), axis=axis, keepdims=True)
        norm = jnp.where(pair, low + high, jnp.where(at < HEAD, low, high))
        return 1.0 / (jnp.sqrt(norm) + epsilon)

    by_col = factor(down, lane, 1)
    by_row = factor(across, line, 0)
    gram = gram * by_row * by_col
    unit = jnp.where(row == col, 1.0, 0.0)
    product = None
    for turn in range(NS_ITERS):
        terms = split(gram)
        step = quintic_a * unit + quintic_b * gram + quintic_c * dot(terms, terms)
        by_step = split(step)
        if turn == 0:
            gram = dot(split(dot(terms, by_step)), by_step)
            product = step
        elif turn < NS_ITERS - 1:
            both = jnp.concatenate([product, dot(terms, by_step)], axis=0)
            both = dot(split(both), by_step)
            product, gram = both[:SLOT], both[SLOT:]
        else:
            product = dot(split(product), by_step)
    top, middle, bottom = split(product)
    h = head_grad[...]
    update = jnp.dot(h, bottom, preferred_element_type=f32) + jnp.dot(h, middle, preferred_element_type=f32)
    update = update + jnp.dot(h, top, preferred_element_type=f32)
    result[...] = (update * (by_col * 64.0)).astype(bf16)
    for k, out in enumerate((o0, o1, o2, o3)):
        at = pl.multiple_of(((zh + k) & 3) * HALF, HALF)
        out[...] = result[pl.ds(at, HALF), :]


def place_heads(meta, p0, p1, p2, p3, q0, q1, q2, q3, out):
    ylo, x, zh = lax.axis_index("ylo"), lax.axis_index("x"), lax.axis_index("zh")
    for dx in range(4):
        for dzh in range(4):
            slot = ((x - dx) & 3) * 4 + ((zh - dzh) & 3)
            for j in range(2):
                at = pl.multiple_of(meta[PERM_AT + slot * 2 + j] * HEAD, HEAD)
                for low, ref in ((ylo, (p0, p1, p2, p3)[dx]), (1 - ylo, (q0, q1, q2, q3)[dx])):
                    rows = pl.ds(pl.multiple_of(low * HALF, HALF), HALF)
                    out[rows, pl.ds(at, HEAD)] = ref[dzh, :, j * HEAD : (j + 1) * HEAD].astype(f32)


Y_INDEX = (0, 2, 1, 3)


def move_x(a, k):
    return lax.ppermute(a, "x", [(i, (i + k) % 4) for i in range(4)])


def move_y(a, k):
    return lax.ppermute(a, ("ylo", "yhi"), [(Y_INDEX[i], Y_INDEX[(i + k) % 4]) for i in range(4)])


def move_z(a, k):
    return lax.ppermute(a, ("zh", "z0"), [(i, (i + k) % 8) for i in range(8)])


def swap(a, axis):
    return lax.ppermute(a, axis, [(0, 1), (1, 0)])


def on_device(activations, cotangent, masked, ratios, owners):
    tok, width = activations.shape
    *blocks, meta = local_kernel(
        prepare,
        [shape((BLOCK, tok), bf16)] * 4 + [shape((tok, BLOCK), bf16)] * 4 + [shape((PERM_AT + HEADS,), jnp.int32)],
        (owners, ratios, masked[None, :], activations, cotangent),
        16,
        2 * tok * width,
        "prepare",
        in_specs=[smem(), smem(), vmem(), anywhere(), anywhere()],
        out_specs=[vmem()] * 8 + [smem()],
        scratch=[
            pltpu.VMEM((tok, width), bf16),
            pltpu.VMEM((tok, width), bf16),
            pltpu.SMEM((HEADS,), jnp.int32),
            pltpu.SMEM((HEADS,), jnp.int32),
            pltpu.SemaphoreType.DMA((2,)),
        ],
    )
    rows, cols = blocks[:4], blocks[4:]
    rows = [rows[0]] + [move_y(rows[k], k) for k in (1, 2, 3)]
    cols = [cols[0]] + [move_x(cols[k], k) for k in (1, 2, 3)]
    r0, g0 = jnp.stack(rows), jnp.stack(cols)
    r1, r3 = move_x(r0, 1), move_x(r0, -1)
    g1, g3 = move_y(g0, 1), move_y(g0, -1)
    r2a, r2b = move_x(r1[:2], 1), move_x(r3[2:], -1)
    g2a, g2b = move_y(g1[:2], 1), move_y(g3[2:], -1)
    gathered = (r0, r1, r3, r2a, r2b, g0, g1, g3, g2a, g2b)

    def product(offset, name):
        (out,) = local_kernel(
            functools.partial(multiply, offset),
            [shape((16, 128, SLOT), bf16)],
            gathered,
            32,
            BLOCK * BLOCK * 16 * tok,
            name,
        )
        return out

    send = product(BLOCK // 2, "multiply_other")
    other = swap(send, "core")
    keep = product(0, "multiply_own")
    half_chunks = shape((4, 128, SLOT), bf16)
    up, down = local_kernel(
        add_odd, [half_chunks] * 2, (keep, other), 8, 8 * 128 * SLOT, "add_odd"
    )
    up, down = move_z(up, 1), move_z(down, -1)
    t0, t1, t2, t3 = local_kernel(
        add_even,
        [shape((256, SLOT), f32)] + [shape((256, SLOT), bf16)] * 3,
        (keep, other, up, down),
        8,
        16 * 128 * SLOT,
        "add_even",
    )
    head_grad, mine, theirs = local_kernel(
        gram_part,
        [shape((256, SLOT), bf16), shape((GRAM, HEAD), f32), shape((GRAM, HEAD), f32)],
        (t0, move_z(t1, 2), move_z(t2, 4), move_z(t3, 6)),
        8,
        2 * 256 * SLOT * SLOT,
        "gram_part",
    )
    mine = mine + swap(theirs, "core")
    mine = mine + swap(mine, "z0")
    mine = (mine + move_y(mine, 2)) + (move_y(mine, 1) + move_y(mine, 3))
    update = local_kernel(
        newton,
        [shape((HALF, SLOT), bf16)] * 4 + [shape((256, SLOT), bf16)],
        (meta, mine, swap(mine, "core"), head_grad),
        16,
        20 * 2 * SLOT**3 * 6,
        "newton",
        in_specs=[smem()] + [vmem()] * 3,
    )
    ring = lambda a, k: lax.ppermute(a, "zh", [(i, (i + k) % 4) for i in range(4)])
    p0 = jnp.stack([update[0]] + [ring(update[k], k) for k in (1, 2, 3)])
    q0 = swap(p0, "ylo")
    ps = [p0] + [move_x(p0, k) for k in (1, 2, 3)]
    qs = [q0] + [move_x(q0, k) for k in (1, 2, 3)]
    (out,) = local_kernel(
        place_heads,
        [shape((2 * HALF, width), f32)],
        (meta, *ps, *qs),
        12,
        0,
        "place_heads",
        in_specs=[smem()] + [vmem()] * 8,
    )
    return out


def solution(mesh):
    axes = ("x", "ylo", "yhi", "zh", "z0", "core")
    fine = Mesh(mesh.devices.reshape(4, 2, 2, 4, 2, 2), axes)
    everywhere = P(axes)
    placed = (P(axes, None), P(axes, None), everywhere, everywhere, P())
    return jax.shard_map(
        on_device,
        mesh=fine,
        in_specs=placed,
        out_specs=P(("yhi", "zh", "z0", "core"), None),
        check_vma=False,
    )
```

time: 172 us -> 162 us (0.942)
  starting transfers between devices: 67 us -> 57.3 us
  waiting for transfers between devices: 75.9 us -> 79 us
  between operations: 3.39 us -> 0.81 us
  other arithmetic: 2.84 us -> 0.33 us
    ppermute x15 -> x13, starting transfers between devices: 36.3 us -> 26.6 us  [the longest x5 13.1 us: move_z(): return lax.ppermute(a, ('zh', 'z0'), [(i, (i + k) % 8) for i in range(8)])]
    ppermute x15 -> x13, waiting for transfers between devices: 24.1 us -> 28.4 us  [the longest x5 16.9 us: move_z(): return lax.ppermute(a, ('zh', 'z0'), [(i, (i + k) % 8) for i in range(8)])]
    unnamed x4 -> x8, local copies, waits for them, and re-layouts: 2.45 us -> 3.75 us
    pallas_call x6 -> x8, Pallas kernels: 19.7 us -> 19.7 us  [local_kernel(): pl.pallas_call(body, out_shape=outs, in_specs=in_specs or [vmem()] * len(...]
  transfers between devices with their start and end apart: 38 -> 36, of which waited for: 24 -> 22; matrix products, arithmetic and copies ran while one was open for 0% -> 0% of each run, Pallas kernels for 0% -> 1%
where the time goes in v2:
time: 162 us; the launch traced here: 161 us
  waiting for transfers between devices  79 us (49%)
  starting transfers between devices  57.3 us (35%)
  Pallas kernels  19.7 us (12%)
  local copies, waits for them, and re-layouts  3.89 us (2%)
    ppermute x10, waiting for transfers between devices, move_y(): lax.ppermute(a, ('ylo', 'yhi'), [(Y_INDEX[i], Y_INDEX[(i + k) % 4]) for i...  36.1 us
    pallas_call x8, Pallas kernels, local_kernel(): pl.pallas_call(body, out_shape=outs, in_specs=in_specs or [vmem()] * len(...  19.7 us
    ppermute x10, starting transfers between devices, move_y(): lax.ppermute(a, ('ylo', 'yhi'), [(Y_INDEX[i], Y_INDEX[(i + k) % 4]) for i...  17.6 us
    ppermute x5, waiting for transfers between devices, move_z(): return lax.ppermute(a, ('zh', 'z0'), [(i, (i + k) % 8) for i in range(8)])  16.9 us
    ppermute x13, waiting for transfers between devices, move_x(): return lax.ppermute(a, 'x', [(i, (i + k) % 4) for i in range(4)])  14.6 us
    ppermute x13, starting transfers between devices, move_x(): return lax.ppermute(a, 'x', [(i, (i + k) % 4) for i in range(4)])  13.2 us
    ppermute x5, starting transfers between devices, move_z(): return lax.ppermute(a, ('zh', 'z0'), [(i, (i + k) % 8) for i in range(8)])  13.1 us
    ppermute x5, waiting for transfers between devices, swap(): return lax.ppermute(a, axis, [(0, 1), (1, 0)])  8.16 us
  transfers between devices with their start and end apart: 36, of which 22 were waited for; matrix products, arithmetic and copies ran while one was open for 0% of the time, Pallas kernels for 1%

profile of v2, /device:TPU:1, one launch (start us, length us, event | category | flops | bytes accessed | tf_op | source)
XLA Modules:
  0.0 161.1 jit_solution(14578461458852451922)
XLA Ops:
  4.4 2.6 %prepare.1 = (bf16[1024,128]{1,0:T(8,128)(2,1)S(1)}, bf16[1024,128]{1,0:T(8,128)(2,1)S(1)}, bf16[1024,128]{1,0:T(8,128)(2,1)S(1)}, bf16[1024,128]{1,0:T(8,128)(2...) custom-call(s32[32]{0:T(128)S(1)} %copy-done.2, ...), custom_call_target="tpu_custom_call" | custom-call | flops 1048576 | bytes 4195108 | tf_op jit(solution)/shard_map/prepare/pallas_call | solution.py:43
  9.1 2.4 %collective-permute-start.8 = (bf16[128,1024]{1,0:T(8,128)(2,1)S(1)}, bf16[128,1024]{1,0:T(8,128)(2,1)S(1)}, u32[]{:S(2)}, u32[]{:S(2)}) collective-permute-start(bf16[128,1024]{1,0:T(8,128)(2,1)S(1)} %get-tuple-element.34), channel_id=1, source_target_pairs={{0,128},{64,192},{128,0},{192,64},{1,129},{65,193},{129,1},{193,65... | collective-permute-start | bytes 786440 | tf_op jit(solution)/shard_map/ppermute | solution.py:260
  14.0 2.6 %collective-permute-start.1 = (bf16[1024,128]{1,0:T(8,128)(2,1)S(1)}, bf16[1024,128]{1,0:T(8,128)(2,1)S(1)}, u32[]{:S(2)}, u32[]{:S(2)}) collective-permute-start(bf16[1024,128]{1,0:T(8,128)(2,1)S(1)} %get-tuple-element.30), channel_id=1, source_target_pairs={{0,16},{32,48},{16,0},{48,32},{1,17},{33,49},{17,1},{49,33},{2,18}... | collective-permute-start | bytes 786440 | tf_op jit(solution)/shard_map/ppermute | solution.py:264
  16.6 2.4 %collective-permute-start.2 = (bf16[1024,128]{1,0:T(8,128)(2,1)S(1)}, bf16[1024,128]{1,0:T(8,128)(2,1)S(1)}, u32[]{:S(2)}, u32[]{:S(2)}) collective-permute-start(bf16[1024,128]{1,0:T(8,128)(2,1)S(1)} %get-tuple-element.31), channel_id=1, source_target_pairs={{0,48},{32,0},{16,32},{48,16},{1,49},{33,1},{17,33},{49,17},{2,50}... | collective-permute-start | bytes 786440 | tf_op jit(solution)/shard_map/ppermute | solution.py:264
  19.0 3.9 %collective-permute-done.8 = bf16[128,1024]{1,0:T(8,128)(2,1)S(1)} collective-permute-done((bf16[128,1024]{1,0:T(8,128)(2,1)S(1)}, bf16[128,1024]{1,0:T(8,128)(2,1)S(1)}, u32[]{:S(2)}, u32[]{:S(2)}) %collective-permute-start.8) | collective-permute-done | bytes 262176 | tf_op jit(solution)/shard_map/ppermute | solution.py:260
  23.0 2.8 %collective-permute-start.11 = (bf16[4,128,1024]{2,1,0:T(8,128)(2,1)S(1)}, bf16[4,128,1024]{2,1,0:T(8,128)(2,1)S(1)}, u32[]{:S(2)}, u32[]{:S(2)}) collective-permute-start(bf16[4,128,1024]{2,1,0:T(8,128)(2,1)S(1)} %pad_maximum_fusion.1.g0), channel_id=1, source_target_pairs={{0,48},{32,0},{16,32},{48,16},{1,49},{33,1},{17,33},{49,17},{2,50}... | collective-permute-start | bytes 3145736 | tf_op jit(solution)/shard_map/ppermute | solution.py:264
  29.1 19.7 %collective-permute-done.11.g3 = bf16[4,128,1024]{2,1,0:T(8,128)(2,1)S(1)} collective-permute-done((bf16[4,128,1024]{2,1,0:T(8,128)(2,1)S(1)}, bf16[4,128,1024]{2,1,0:T(8,128)(2,1)S(1)}, u32[]{:S(2)}, u32[]{:S(2)}) %collective-permute-start.11) | collective-permute-done | bytes 1048608 | tf_op jit(solution)/shard_map/ppermute | solution.py:264
  48.9 3.5 %collective-permute-start.13 = (bf16[2,128,1024]{2,1,0:T(8,128)(2,1)S(1)}, bf16[2,128,1024]{2,1,0:T(8,128)(2,1)S(1)}, u32[]{:S(2)}, u32[]{:S(2)}) collective-permute-start(bf16[2,128,1024]{2,1,0:T(8,128)(2,1)S(1)} %slice.19), channel_id=1, source_target_pairs={{0,48},{32,0},{16,32},{48,16},{1,49},{33,1},{17,33},{49,17},{2,50}... | collective-permute-start | bytes 1572872 | tf_op jit(solution)/shard_map/ppermute | solution.py:264
  55.3 9.8 %collective-permute-done.13.g2b = bf16[2,128,1024]{2,1,0:T(8,128)(2,1)S(1)} collective-permute-done((bf16[2,128,1024]{2,1,0:T(8,128)(2,1)S(1)}, bf16[2,128,1024]{2,1,0:T(8,128)(2,1)S(1)}, u32[]{:S(2)}, u32[]{:S(2)}) %collective-permute-start.13) | collective-permute-done | bytes 524320 | tf_op jit(solution)/shard_map/ppermute | solution.py:264
  70.1 2.9 %collective-permute-start.14 = (bf16[16,128,256]{2,1,0:T(8,128)(2,1)S(1)}, bf16[16,128,256]{2,1,0:T(8,128)(2,1)S(1)}, u32[]{:S(2)}, u32[]{:S(2)}) collective-permute-start(bf16[16,128,256]{2,1,0:T(8,128)(2,1)S(1)} %multiply_other.1), channel_id=1, source_target_pairs={{0,1},{1,0},{2,3},{3,2},{4,5},{5,4},{6,7},{7,6},{8,9},{9,8},{10,11... | collective-permute-start | bytes 3145736 | tf_op jit(solution)/shard_map/ppermute | solution.py:272
  77.2 4.0 %collective-permute-start.16 = (bf16[4,128,256]{2,1,0:T(8,128)(2,1)S(1)}, bf16[4,128,256]{2,1,0:T(8,128)(2,1)S(1)}, u32[]{:S(2)}, u32[]{:S(2)}) collective-permute-start(bf16[4,128,256]{2,1,0:T(8,128)(2,1)S(1)} %get-tuple-element.37), channel_id=1, source_target_pairs={{0,14},{2,0},{4,2},{6,4},{8,6},{10,8},{12,10},{14,12},{1,15},{3,1}... | collective-permute-start | bytes 786440 | tf_op jit(solution)/shard_map/ppermute | solution.py:268
  81.2 6.4 %collective-permute-done.15.up = bf16[4,128,256]{2,1,0:T(8,128)(2,1)S(1)} collective-permute-done((bf16[4,128,256]{2,1,0:T(8,128)(2,1)S(1)}, bf16[4,128,256]{2,1,0:T(8,128)(2,1)S(1)}, u32[]{:S(2)}, u32[]{:S(2)}) %collective-permute-start.15) | collective-permute-done | bytes 262176 | tf_op jit(solution)/shard_map/ppermute | solution.py:268
  89.4 2.5 %collective-permute-start.18 = (bf16[256,256]{1,0:T(8,128)(2,1)S(1)}, bf16[256,256]{1,0:T(8,128)(2,1)S(1)}, u32[]{:S(2)}, u32[]{:S(2)}) collective-permute-start(bf16[256,256]{1,0:T(8,128)(2,1)S(1)} %get-tuple-element.40), channel_id=1, source_target_pairs={{0,8},{2,10},{4,12},{6,14},{8,0},{10,2},{12,4},{14,6},{1,9},{3,11}... | collective-permute-start | bytes 393224 | tf_op jit(solution)/shard_map/ppermute | solution.py:268
  91.9 3.2 %collective-permute-start.19 = (bf16[256,256]{1,0:T(8,128)(2,1)S(1)}, bf16[256,256]{1,0:T(8,128)(2,1)S(1)}, u32[]{:S(2)}, u32[]{:S(2)}) collective-permute-start(bf16[256,256]{1,0:T(8,128)(2,1)S(1)} %get-tuple-element.41), channel_id=1, source_target_pairs={{0,12},{2,14},{4,0},{6,2},{8,4},{10,6},{12,8},{14,10},{1,13},{3,15... | collective-permute-start | bytes 393224 | tf_op jit(solution)/shard_map/ppermute | solution.py:268
  95.1 5.8 %collective-permute-done.18.t2 = bf16[256,256]{1,0:T(8,128)(2,1)S(1)} collective-permute-done((bf16[256,256]{1,0:T(8,128)(2,1)S(1)}, bf16[256,256]{1,0:T(8,128)(2,1)S(1)}, u32[]{:S(2)}, u32[]{:S(2)}) %collective-permute-start.18) | collective-permute-done | bytes 131104 | tf_op jit(solution)/shard_map/ppermute | solution.py:268
  100.9 4.7 %collective-permute-done.19.t3 = bf16[256,256]{1,0:T(8,128)(2,1)S(1)} collective-permute-done((bf16[256,256]{1,0:T(8,128)(2,1)S(1)}, bf16[256,256]{1,0:T(8,128)(2,1)S(1)}, u32[]{:S(2)}, u32[]{:S(2)}) %collective-permute-start.19) | collective-permute-done | bytes 131104 | tf_op jit(solution)/shard_map/ppermute | solution.py:268
  107.7 4.0 %collective-permute-done.21 = f32[192,128]{1,0:T(8,128)S(1)} collective-permute-done((f32[192,128]{1,0:T(8,128)S(1)}, f32[192,128]{1,0:T(8,128)S(1)}, u32[]{:S(2)}, u32[]{:S(2)}) %collective-permute-start.21) | collective-permute-done | bytes 98336 | tf_op jit(solution)/shard_map/ppermute | solution.py:272
  111.7 2.7 %collective-permute-start.24 = (f32[192,128]{1,0:T(8,128)S(1)}, f32[192,128]{1,0:T(8,128)S(1)}, u32[]{:S(2)}, u32[]{:S(2)}) collective-permute-start(f32[192,128]{1,0:T(8,128)S(1)} %add.16), channel_id=1, source_target_pairs={{0,48},{32,0},{16,32},{48,16},{1,49},{33,1},{17,33},{49,17},{2,50}... | collective-permute-start | bytes 294920 | tf_op jit(solution)/shard_map/ppermute | solution.py:264
  116.0 3.8 %collective-permute-done.23 = f32[192,128]{1,0:T(8,128)S(1)} collective-permute-done((f32[192,128]{1,0:T(8,128)S(1)}, f32[192,128]{1,0:T(8,128)S(1)}, u32[]{:S(2)}, u32[]{:S(2)}) %collective-permute-start.23) | collective-permute-done | bytes 98336 | tf_op jit(solution)/shard_map/ppermute | solution.py:264
  120.8 2.6 %collective-permute-start.25 = (f32[192,128]{1,0:T(8,128)S(1)}, f32[192,128]{1,0:T(8,128)S(1)}, u32[]{:S(2)}, u32[]{:S(2)}) collective-permute-start(f32[192,128]{1,0:T(8,128)S(1)} %add_add_fusion.mine), channel_id=1, source_target_pairs={{0,1},{1,0},{2,3},{3,2},{4,5},{5,4},{6,7},{7,6},{8,9},{9,8},{10,11... | collective-permute-start | bytes 294920 | tf_op jit(solution)/shard_map/ppermute | solution.py:272
  124.3 9.8 %newton.1 = (bf16[64,256]{1,0:T(8,128)(2,1)S(1)}, bf16[64,256]{1,0:T(8,128)(2,1)S(1)}, bf16[64,256]{1,0:T(8,128)(2,1)S(1)}, bf16[64,256]{1,0:T(8,128)(2,1)S(1)}, bf16[256,256]{1,0:T(8,128)(2,1)}) custom-call(s32[40]{0:T(128)S(1)} %get-tuple-element.27.meta, f32[192,128]{1,0:T(8,128)S(1)} %add_add_fusion.mine, f32[192,128]{1,0:T(8,128)S(1)} %collective-permute-done.25.other, ...), custom_call_target="tpu_custom_call" | custom-call | flops 4026531840 | bytes 589984 | tf_op jit(solution)/shard_map/newton/pallas_call | solution.py:43
  134.1 3.6 %collective-permute-start.26 = (bf16[64,256]{1,0:T(8,128)(2,1)S(1)}, bf16[64,256]{1,0:T(8,128)(2,1)S(1)}, u32[]{:S(2)}, u32[]{:S(2)}) collective-permute-start(bf16[64,256]{1,0:T(8,128)(2,1)S(1)} %get-tuple-element.46), channel_id=1, source_target_pairs={{0,4},{4,8},{8,12},{12,0},{1,5},{5,9},{9,13},{13,1},{2,6},{6,10},{... | collective-permute-start | bytes 98312 | tf_op jit(solution)/shard_map/ppermute | solution.py:351
  141.3 3.3 %collective-permute-done.27 = bf16[64,256]{1,0:T(8,128)(2,1)S(1)} collective-permute-done((bf16[64,256]{1,0:T(8,128)(2,1)S(1)}, bf16[64,256]{1,0:T(8,128)(2,1)S(1)}, u32[]{:S(2)}, u32[]{:S(2)}) %collective-permute-start.27) | collective-permute-done | bytes 32800 | tf_op jit(solution)/shard_map/ppermute | solution.py:351
  156.2 2.8 %collective-permute-done.33.q1 = bf16[4,64,256]{2,1,0:T(8,128)(2,1)S(1)} collective-permute-done((bf16[4,64,256]{2,1,0:T(8,128)(2,1)S(1)}, bf16[4,64,256]{2,1,0:T(8,128)(2,1)S(1)}, u32[]{:S(2)}, u32[]{:S(2)}) %collective-permute-start.33) | collective-permute-done | bytes 131104 | tf_op jit(solution)/shard_map/ppermute | solution.py:260
  (74 shorter events, 48.4 us)
Async XLA Ops:
  7.0 9.6 %collective-permute-start.7 = (bf16[128,1024]{1,0:T(8,128)(2,1)S(1)}, bf16[128,1024]{1,0:T(8,128)(2,1)S(1)}, u32[]{:S(2)}, u32[]{:S(2)}) collective-permute-start(bf16[128,1024]{1,0:T(8,128)(2,1)S(1)} %get-tuple-element.33), channel_id=1, source_target_pairs={{0,64},{64,128},{128,192},{192,0},{1,65},{65,129},{129,193},{193,1... | collective-permute-start | bytes 786440 | tf_op jit(solution)/shard_map/ppermute | solution.py:260
  9.1 13.8 %collective-permute-start.8 = (bf16[128,1024]{1,0:T(8,128)(2,1)S(1)}, bf16[128,1024]{1,0:T(8,128)(2,1)S(1)}, u32[]{:S(2)}, u32[]{:S(2)}) collective-permute-start(bf16[128,1024]{1,0:T(8,128)(2,1)S(1)} %get-tuple-element.34), channel_id=1, source_target_pairs={{0,128},{64,192},{128,0},{192,64},{1,129},{65,193},{129,1},{193,65... | collective-permute-start | bytes 786440 | tf_op jit(solution)/shard_map/ppermute | solution.py:260
  11.6 11.3 %collective-permute-start.9 = (bf16[128,1024]{1,0:T(8,128)(2,1)S(1)}, bf16[128,1024]{1,0:T(8,128)(2,1)S(1)}, u32[]{:S(2)}, u32[]{:S(2)}) collective-permute-start(bf16[128,1024]{1,0:T(8,128)(2,1)S(1)} %get-tuple-element.35), channel_id=1, source_target_pairs={{0,192},{64,0},{128,64},{192,128},{1,193},{65,1},{129,65},{193,129... | collective-permute-start | bytes 786440 | tf_op jit(solution)/shard_map/ppermute | solution.py:260
  12.7 13.1 %collective-permute-start = (bf16[1024,128]{1,0:T(8,128)(2,1)S(1)}, bf16[1024,128]{1,0:T(8,128)(2,1)S(1)}, u32[]{:S(2)}, u32[]{:S(2)}) collective-permute-start(bf16[1024,128]{1,0:T(8,128)(2,1)S(1)} %get-tuple-element.29), channel_id=1, source_target_pairs={{0,32},{32,16},{16,48},{48,0},{1,33},{33,17},{17,49},{49,1},{2,34}... | collective-permute-start | bytes 786440 | tf_op jit(solution)/shard_map/ppermute | solution.py:264
  14.0 13.1 %collective-permute-start.1 = (bf16[1024,128]{1,0:T(8,128)(2,1)S(1)}, bf16[1024,128]{1,0:T(8,128)(2,1)S(1)}, u32[]{:S(2)}, u32[]{:S(2)}) collective-permute-start(bf16[1024,128]{1,0:T(8,128)(2,1)S(1)} %get-tuple-element.30), channel_id=1, source_target_pairs={{0,16},{32,48},{16,0},{48,32},{1,17},{33,49},{17,1},{49,33},{2,18}... | collective-permute-start | bytes 786440 | tf_op jit(solution)/shard_map/ppermute | solution.py:264
  16.6 10.4 %collective-permute-start.2 = (bf16[1024,128]{1,0:T(8,128)(2,1)S(1)}, bf16[1024,128]{1,0:T(8,128)(2,1)S(1)}, u32[]{:S(2)}, u32[]{:S(2)}) collective-permute-start(bf16[1024,128]{1,0:T(8,128)(2,1)S(1)} %get-tuple-element.31), channel_id=1, source_target_pairs={{0,48},{32,0},{16,32},{48,16},{1,49},{33,1},{17,33},{49,17},{2,50}... | collective-permute-start | bytes 786440 | tf_op jit(solution)/shard_map/ppermute | solution.py:264
  23.0 25.8 %collective-permute-start.11 = (bf16[4,128,1024]{2,1,0:T(8,128)(2,1)S(1)}, bf16[4,128,1024]{2,1,0:T(8,128)(2,1)S(1)}, u32[]{:S(2)}, u32[]{:S(2)}) collective-permute-start(bf16[4,128,1024]{2,1,0:T(8,128)(2,1)S(1)} %pad_maximum_fusion.1.g0), channel_id=1, source_target_pairs={{0,48},{32,0},{16,32},{48,16},{1,49},{33,1},{17,33},{49,17},{2,50}... | collective-permute-start | bytes 3145736 | tf_op jit(solution)/shard_map/ppermute | solution.py:264
  25.8 26.5 %collective-permute-start.10 = (bf16[4,128,1024]{2,1,0:T(8,128)(2,1)S(1)}, bf16[4,128,1024]{2,1,0:T(8,128)(2,1)S(1)}, u32[]{:S(2)}, u32[]{:S(2)}) collective-permute-start(bf16[4,128,1024]{2,1,0:T(8,128)(2,1)S(1)} %pad_maximum_fusion.1.g0), channel_id=1, source_target_pairs={{0,32},{32,16},{16,48},{48,0},{1,33},{33,17},{17,49},{49,1},{2,34}... | collective-permute-start | bytes 3145736 | tf_op jit(solution)/shard_map/ppermute | solution.py:264
  27.2 26.2 %collective-permute-start.4 = (bf16[4,1024,128]{2,1,0:T(8,128)(2,1)S(1)}, bf16[4,1024,128]{2,1,0:T(8,128)(2,1)S(1)}, u32[]{:S(2)}, u32[]{:S(2)}) collective-permute-start(bf16[4,1024,128]{2,1,0:T(8,128)(2,1)S(1)} %pad_maximum_fusion.r0), channel_id=1, source_target_pairs={{0,192},{64,0},{128,64},{192,128},{1,193},{65,1},{129,65},{193,129... | collective-permute-start | bytes 3145736 | tf_op jit(solution)/shard_map/ppermute | solution.py:260
  29.1 25.6 %collective-permute-start.3 = (bf16[4,1024,128]{2,1,0:T(8,128)(2,1)S(1)}, bf16[4,1024,128]{2,1,0:T(8,128)(2,1)S(1)}, u32[]{:S(2)}, u32[]{:S(2)}) collective-permute-start(bf16[4,1024,128]{2,1,0:T(8,128)(2,1)S(1)} %pad_maximum_fusion.r0), channel_id=1, source_target_pairs={{0,64},{64,128},{128,192},{192,0},{1,65},{65,129},{129,193},{193,1... | collective-permute-start | bytes 3145736 | tf_op jit(solution)/shard_map/ppermute | solution.py:260
  48.9 16.2 %collective-permute-start.13 = (bf16[2,128,1024]{2,1,0:T(8,128)(2,1)S(1)}, bf16[2,128,1024]{2,1,0:T(8,128)(2,1)S(1)}, u32[]{:S(2)}, u32[]{:S(2)}) collective-permute-start(bf16[2,128,1024]{2,1,0:T(8,128)(2,1)S(1)} %slice.19), channel_id=1, source_target_pairs={{0,48},{32,0},{16,32},{48,16},{1,49},{33,1},{17,33},{49,17},{2,50}... | collective-permute-start | bytes 1572872 | tf_op jit(solution)/shard_map/ppermute | solution.py:264
  52.4 12.9 %collective-permute-start.12 = (bf16[2,128,1024]{2,1,0:T(8,128)(2,1)S(1)}, bf16[2,128,1024]{2,1,0:T(8,128)(2,1)S(1)}, u32[]{:S(2)}, u32[]{:S(2)}) collective-permute-start(bf16[2,128,1024]{2,1,0:T(8,128)(2,1)S(1)} %slice.18), channel_id=1, source_target_pairs={{0,32},{32,16},{16,48},{48,0},{1,33},{33,17},{17,49},{49,1},{2,34}... | collective-permute-start | bytes 1572872 | tf_op jit(solution)/shard_map/ppermute | solution.py:264
  53.4 12.6 %collective-permute-start.6 = (bf16[2,1024,128]{2,1,0:T(8,128)(2,1)S(1)}, bf16[2,1024,128]{2,1,0:T(8,128)(2,1)S(1)}, u32[]{:S(2)}, u32[]{:S(2)}) collective-permute-start(bf16[2,1024,128]{2,1,0:T(8,128)(2,1)S(1)} %slice.17), channel_id=1, source_target_pairs={{0,192},{64,0},{128,64},{192,128},{1,193},{65,1},{129,65},{193,129... | collective-permute-start | bytes 1572872 | tf_op jit(solution)/shard_map/ppermute | solution.py:260
  54.7 13.0 %collective-permute-start.5 = (bf16[2,1024,128]{2,1,0:T(8,128)(2,1)S(1)}, bf16[2,1024,128]{2,1,0:T(8,128)(2,1)S(1)}, u32[]{:S(2)}, u32[]{:S(2)}) collective-permute-start(bf16[2,1024,128]{2,1,0:T(8,128)(2,1)S(1)} %slice.16), channel_id=1, source_target_pairs={{0,64},{64,128},{128,192},{192,0},{1,65},{65,129},{129,193},{193,1... | collective-permute-start | bytes 1572872 | tf_op jit(solution)/shard_map/ppermute | solution.py:260
  75.4 12.1 %collective-permute-start.15 = (bf16[4,128,256]{2,1,0:T(8,128)(2,1)S(1)}, bf16[4,128,256]{2,1,0:T(8,128)(2,1)S(1)}, u32[]{:S(2)}, u32[]{:S(2)}) collective-permute-start(bf16[4,128,256]{2,1,0:T(8,128)(2,1)S(1)} %get-tuple-element.36), channel_id=1, source_target_pairs={{0,2},{2,4},{4,6},{6,8},{8,10},{10,12},{12,14},{14,0},{1,3},{3,5},... | collective-permute-start | bytes 786440 | tf_op jit(solution)/shard_map/ppermute | solution.py:268
  77.2 10.4 %collective-permute-start.16 = (bf16[4,128,256]{2,1,0:T(8,128)(2,1)S(1)}, bf16[4,128,256]{2,1,0:T(8,128)(2,1)S(1)}, u32[]{:S(2)}, u32[]{:S(2)}) collective-permute-start(bf16[4,128,256]{2,1,0:T(8,128)(2,1)S(1)} %get-tuple-element.37), channel_id=1, source_target_pairs={{0,14},{2,0},{4,2},{6,4},{8,6},{10,8},{12,10},{14,12},{1,15},{3,1}... | collective-permute-start | bytes 786440 | tf_op jit(solution)/shard_map/ppermute | solution.py:268
  87.7 7.3 %collective-permute-start.17 = (bf16[256,256]{1,0:T(8,128)(2,1)S(1)}, bf16[256,256]{1,0:T(8,128)(2,1)S(1)}, u32[]{:S(2)}, u32[]{:S(2)}) collective-permute-start(bf16[256,256]{1,0:T(8,128)(2,1)S(1)} %get-tuple-element.39), channel_id=1, source_target_pairs={{0,4},{2,6},{4,8},{6,10},{8,12},{10,14},{12,0},{14,2},{1,5},{3,7},... | collective-permute-start | bytes 393224 | tf_op jit(solution)/shard_map/ppermute | solution.py:268
  89.4 11.5 %collective-permute-start.18 = (bf16[256,256]{1,0:T(8,128)(2,1)S(1)}, bf16[256,256]{1,0:T(8,128)(2,1)S(1)}, u32[]{:S(2)}, u32[]{:S(2)}) collective-permute-start(bf16[256,256]{1,0:T(8,128)(2,1)S(1)} %get-tuple-element.40), channel_id=1, source_target_pairs={{0,8},{2,10},{4,12},{6,14},{8,0},{10,2},{12,4},{14,6},{1,9},{3,11}... | collective-permute-start | bytes 393224 | tf_op jit(solution)/shard_map/ppermute | solution.py:268
  91.9 13.8 %collective-permute-start.19 = (bf16[256,256]{1,0:T(8,128)(2,1)S(1)}, bf16[256,256]{1,0:T(8,128)(2,1)S(1)}, u32[]{:S(2)}, u32[]{:S(2)}) collective-permute-start(bf16[256,256]{1,0:T(8,128)(2,1)S(1)} %get-tuple-element.41), channel_id=1, source_target_pairs={{0,12},{2,14},{4,0},{6,2},{8,4},{10,6},{12,8},{14,10},{1,13},{3,15... | collective-permute-start | bytes 393224 | tf_op jit(solution)/shard_map/ppermute | solution.py:268
  134.1 7.2 %collective-permute-start.26 = (bf16[64,256]{1,0:T(8,128)(2,1)S(1)}, bf16[64,256]{1,0:T(8,128)(2,1)S(1)}, u32[]{:S(2)}, u32[]{:S(2)}) collective-permute-start(bf16[64,256]{1,0:T(8,128)(2,1)S(1)} %get-tuple-element.46), channel_id=1, source_target_pairs={{0,4},{4,8},{8,12},{12,0},{1,5},{5,9},{9,13},{13,1},{2,6},{6,10},{... | collective-permute-start | bytes 98312 | tf_op jit(solution)/shard_map/ppermute | solution.py:351
  137.7 6.8 %collective-permute-start.27 = (bf16[64,256]{1,0:T(8,128)(2,1)S(1)}, bf16[64,256]{1,0:T(8,128)(2,1)S(1)}, u32[]{:S(2)}, u32[]{:S(2)}) collective-permute-start(bf16[64,256]{1,0:T(8,128)(2,1)S(1)} %get-tuple-element.47), channel_id=1, source_target_pairs={{0,8},{4,12},{8,0},{12,4},{1,9},{5,13},{9,1},{13,5},{2,10},{6,14},... | collective-permute-start | bytes 98312 | tf_op jit(solution)/shard_map/ppermute | solution.py:351
  145.3 7.3 %collective-permute-start.29 = (bf16[4,64,256]{2,1,0:T(8,128)(2,1)S(1)}, bf16[4,64,256]{2,1,0:T(8,128)(2,1)S(1)}, u32[]{:S(2)}, u32[]{:S(2)}) collective-permute-start(bf16[4,64,256]{2,1,0:T(8,128)(2,1)S(1)} %pad_maximum_fusion.2.p0), channel_id=1, source_target_pairs={{0,64},{64,128},{128,192},{192,0},{1,65},{65,129},{129,193},{193,1... | collective-permute-start | bytes 393224 | tf_op jit(solution)/shard_map/ppermute | solution.py:260
  148.6 7.6 %collective-permute-start.34 = (bf16[4,64,256]{2,1,0:T(8,128)(2,1)S(1)}, bf16[4,64,256]{2,1,0:T(8,128)(2,1)S(1)}, u32[]{:S(2)}, u32[]{:S(2)}) collective-permute-start(bf16[4,64,256]{2,1,0:T(8,128)(2,1)S(1)} %collective-permute-done.32.q0), channel_id=1, source_target_pairs={{0,128},{64,192},{128,0},{192,64},{1,129},{65,193},{129,1},{193,65... | collective-permute-start | bytes 393224 | tf_op jit(solution)/shard_map/ppermute | solution.py:260
  149.8 9.2 %collective-permute-start.33 = (bf16[4,64,256]{2,1,0:T(8,128)(2,1)S(1)}, bf16[4,64,256]{2,1,0:T(8,128)(2,1)S(1)}, u32[]{:S(2)}, u32[]{:S(2)}) collective-permute-start(bf16[4,64,256]{2,1,0:T(8,128)(2,1)S(1)} %collective-permute-done.32.q0), channel_id=1, source_target_pairs={{0,64},{64,128},{128,192},{192,0},{1,65},{65,129},{129,193},{193,1... | collective-permute-start | bytes 393224 | tf_op jit(solution)/shard_map/ppermute | solution.py:260
  (16 other events, 59.8 us)

commit v3 on v2

v3 whole, which is shorter than its diff:
```python
import functools

import jax
import jax.numpy as jnp
from jax import lax
from jax.experimental import pallas as pl
from jax.experimental.pallas import tpu as pltpu
from jax.sharding import Mesh
from jax.sharding import PartitionSpec as P

HEADS = 32
NS_ITERS = 5
quintic_a = 3.4445
quintic_b = -4.775
quintic_c = 2.0315
epsilon = 1e-07

PAIRS_AT, PERM_AT = 0, 8

HEAD = 128
SLOT = 2 * HEAD
BLOCK = 1024
HALF = 64
GRAM = HEAD + HALF

PREPARE_MIB = 56

f32, bf16 = jnp.float32, jnp.bfloat16


def smem():
    return pl.BlockSpec(memory_space=pltpu.SMEM)


def vmem():
    return pl.BlockSpec(memory_space=pltpu.VMEM)


def anywhere():
    return pl.BlockSpec(memory_space=pl.ANY)


def local_kernel(body, outs, operands, mib, flops, name, in_specs=None, out_specs=None, scratch=()):
    moved = sum(o.size * o.dtype.itemsize for o in list(outs) + list(operands))
    return pl.pallas_call(
        body,
        out_shape=outs,
        in_specs=in_specs or [vmem()] * len(operands),
        out_specs=out_specs or [vmem()] * len(outs),
        scratch_shapes=list(scratch),
        compiler_params=pltpu.CompilerParams(vmem_limit_bytes=mib * 2**20),
        cost_estimate=pl.CostEstimate(flops=flops, bytes_accessed=moved, transcendentals=0),
        name=name,
    )(*operands)


def shape(dims, dtype):
    return jax.ShapeDtypeStruct(dims, dtype)


def y_place():
    return lax.axis_index("yhi") * 2 + lax.axis_index("ylo")


def gray(place):
    return place ^ (place >> 1)


def partner(place, core, i):
    flip = jnp.where(core == 0, i, (i >> 1) | ((i & 1) << 1))
    return gray(gray(place) ^ flip)


def prepare(owners_far, ratio_far, masked, act_far, cot_far, *refs):
    rows_out, cols_out, meta = refs[:2], refs[2:4], refs[4]
    act, cot, owners, ratio, count, taken, sems = refs[5:]
    copies = [
        pltpu.make_async_copy(far, near, sems.at[i])
        for i, (far, near) in enumerate(
            ((owners_far, owners), (ratio_far, ratio), (act_far, act), (cot_far, cot))
        )
    ]
    for copy in copies:
        copy.start()
    for v in range(HEADS):
        count[v] = 0
        taken[v] = 0
    copies[0].wait()

    for h in range(HEADS):
        count[owners[h]] = count[owners[h]] + 1
    in_pairs = jnp.int32(0)
    for v in range(HEADS):
        in_pairs = in_pairs + jnp.where(count[v] > 1, 2, 0)
    next_pair, next_alone = jnp.int32(0), in_pairs
    for i in range(PERM_AT):
        meta[i] = in_pairs // 2
    for h in range(HEADS):
        owner = owners[h]
        paired = count[owner] > 1
        seen = taken[owner]
        opens = jnp.logical_and(paired, seen == 0)
        place = jnp.where(paired, jnp.where(seen == 0, next_pair, seen), next_alone)
        taken[owner] = place + 1
        meta[PERM_AT + place] = h
        next_pair = next_pair + jnp.where(opens, 2, 0)
        next_alone = next_alone + jnp.where(paired, 0, 1)

    tok, width = act.shape
    here_y, z0, core = y_place(), lax.axis_index("z0"), lax.axis_index("core")
    copies[1].wait()
    copies[2].wait()
    for i in range(4):
        y = partner(here_y, core, i)
        base = (y >> 1) * (width // 2)
        low = (y & 1) * HALF
        for crel in range(2):
            for zrel in range(2):
                for zh in range(4):
                    block = zh * 4 + (z0 ^ zrel) * 2 + (core ^ crel)
                    at = pl.multiple_of(base + block * 128, 128)
                    turned = act[:, pl.ds(at, 128)].T
                    part = jnp.where(low == 0, turned[:HALF], turned[HALF:])
                    to = ((crel * 2 + zrel) * 4 + zh) * HALF
                    rows_out[i & 1][i >> 1, to : to + HALF, :] = part
    along = masked[...].astype(f32) * 1000.0 / ratio[0].astype(f32)
    line = lax.broadcasted_iota(jnp.int32, (tok, tok), 0)
    lane = lax.broadcasted_iota(jnp.int32, (tok, tok), 1)
    weight = jnp.sum(jnp.where(line == lane, along, 0.0), axis=1, keepdims=True)
    copies[3].wait()
    for i in range(4):
        x = partner(lax.axis_index("x"), core, i)
        for j in range(8):
            slot = x * 4 + ((lax.axis_index("zh") + j // 2) & 3)
            head = meta[PERM_AT + slot * 2 + j % 2]
            at = pl.multiple_of(head * HEAD, HEAD)
            piece = cot[:, pl.ds(at, HEAD)].astype(f32) * weight
            cols_out[i & 1][i >> 1, :, j * HEAD : (j + 1) * HEAD] = piece.astype(bf16)


def multiply(other_core, *refs):
    rows, cols, out = refs[:4], refs[4:8], refs[8]
    z0, core = lax.axis_index("z0"), lax.axis_index("core") ^ other_core
    half = BLOCK // 2
    offset = other_core * half
    for n in range(BLOCK // SLOT):
        total = jnp.zeros((half, SLOT), f32)
        for i in range(4):
            left = jnp.concatenate([rows[i][j, offset : offset + half, :] for j in range(4)], axis=1)
            right = jnp.concatenate([cols[j][i, :, n * SLOT : (n + 1) * SLOT] for j in range(4)], axis=0)
            total = total + jnp.dot(left, right, preferred_element_type=f32)
        total = total.astype(bf16)
        out[jnp.where(core == 0, n, -n) & 3] = total[:256]
        out[4 + (jnp.where(core == 0, n - z0, z0 - n - 1) & 3)] = total[256:]


def add_odd(mine, other, out):
    for j in range(4):
        out[j] = (mine[4 + j].astype(f32) + other[4 + j].astype(f32)).astype(bf16)


def add_even(mine, other, arrived, stay, move):
    for a in range(4):
        total = mine[a].astype(f32) + other[a].astype(f32) + arrived[a].astype(f32)
        if a % 2:
            move[a // 2] = total.astype(bf16)
        else:
            stay[a // 2] = total


def add_far(stay, arrived, near, far):
    near[...] = stay[0] + arrived[0].astype(f32)
    far[...] = (stay[1] + arrived[1].astype(f32)).astype(bf16)


def gram_part(near, arrived, head_grad, keep, send):
    part = (near[...] + arrived[...].astype(f32)).astype(bf16)
    head_grad[...] = part
    gram = lax.dot_general(part, part, (((0,), (0,)), ((), ())), preferred_element_type=f32)
    first = jnp.concatenate([gram[:HEAD, :HEAD], gram[:HALF, HEAD:]], axis=0)
    second = jnp.concatenate([gram[HEAD:, HEAD:], gram[HALF:HEAD, HEAD:]], axis=0)
    core = lax.axis_index("core")
    keep[...] = jnp.where(core == 0, first, second)
    send[...] = jnp.where(core == 0, second, first)


def product(a, b):
    return jnp.dot(a, b, precision=lax.Precision.HIGHEST, preferred_element_type=f32)


def two_terms(a):
    top = a.astype(bf16)
    return top, (a - top.astype(f32)).astype(bf16)


def short_product(a, b):
    dot = functools.partial(jnp.dot, preferred_element_type=f32)
    return (dot(a[1], b[0]) + dot(a[0], b[1])) + dot(a[0], b[0])


def newton(meta, mine, other, head_grad, keep, send, result):
    core = lax.axis_index("core")
    a, b = mine[...], other[...]
    first, second = jnp.where(core == 0, a, b), jnp.where(core == 0, b, a)
    corner = jnp.concatenate([first[HEAD:], second[HEAD:]], axis=0)
    gram = jnp.concatenate(
        [
            jnp.concatenate([first[:HEAD], corner], axis=1),
            jnp.concatenate([corner.T, second[:HEAD]], axis=1),
        ],
        axis=0,
    )
    zh = lax.axis_index("zh")
    pair = lax.axis_index("x") * 4 + zh < meta[PAIRS_AT]
    row = lax.broadcasted_iota(jnp.int32, (SLOT, SLOT), 0)
    col = lax.broadcasted_iota(jnp.int32, (SLOT, SLOT), 1)
    together = jnp.logical_or((row < HEAD) == (col < HEAD), pair)
    gram = jnp.where(together, gram, 0.0)
    on_diagonal = jnp.where(row == col, gram, 0.0)
    down = jnp.sum(on_diagonal, axis=0, keepdims=True)
    across = jnp.sum(on_diagonal, axis=1, keepdims=True)
    lane, line = col[:1, :], row[:, :1]

    def factor(squares, at, axis):
        low = jnp.sum(jnp.where(at < HEAD, squares, 0.0), axis=axis, keepdims=True)
        high = jnp.sum(jnp.where(at < HEAD, 0.0, squares), axis=axis, keepdims=True)
        norm = jnp.where(pair, low + high, jnp.where(at < HEAD, low, high))
        return 1.0 / (jnp.sqrt(norm) + epsilon)

    by_col = factor(down, lane, 1)
    by_row = factor(across, line, 0)
    gram = gram * by_row * by_col
    unit = jnp.where(row == col, 1.0, 0.0)
    factors = None
    for turn in range(NS_ITERS):
        multiplied = product if turn < 2 else lambda p, q: short_product(two_terms(p), two_terms(q))
        step = quintic_a * unit + quintic_b * gram + quintic_c * multiplied(gram, gram)
        if turn < NS_ITERS - 1:
            gram = multiplied(multiplied(gram, step), step)
        factors = step if factors is None else product(factors, step)
    top, middle = two_terms(factors)
    bottom = (factors - top.astype(f32) - middle.astype(f32)).astype(bf16)
    h = head_grad[...]
    update = jnp.dot(h, bottom, preferred_element_type=f32) + jnp.dot(h, middle, preferred_element_type=f32)
    update = update + jnp.dot(h, top, preferred_element_type=f32)
    result[...] = (update * (by_col * 64.0)).astype(bf16)
    for i in range(4):
        at = pl.multiple_of(partner(zh, core, i) * HALF, HALF)
        (send if i & 1 else keep)[i >> 1] = result[pl.ds(at, HALF), :]


def place_heads(meta, p0, p1, p2, p3, q0, q1, q2, q3, out):
    ylo, x, zh = lax.axis_index("ylo"), lax.axis_index("x"), lax.axis_index("zh")
    core = lax.axis_index("core")
    for dx in range(4):
        for i in range(4):
            slot = ((x - dx) & 3) * 4 + partner(zh, core, i)
            for j in range(2):
                at = pl.multiple_of(meta[PERM_AT + slot * 2 + j] * HEAD, HEAD)
                for low, ref in ((ylo, (p0, p1, p2, p3)[dx]), (1 - ylo, (q0, q1, q2, q3)[dx])):
                    rows = pl.ds(pl.multiple_of(low * HALF, HALF), HALF)
                    out[rows, pl.ds(at, HEAD)] = ref[i, :, j * HEAD : (j + 1) * HEAD].astype(f32)


RINGS = {"x": ("x",), "y": ("ylo", "yhi"), "zh": ("zh",)}


def ring_index(ring, place):
    return (place & 1) * 2 + (place >> 1) if ring == "y" else place


def exchange(a, ring, second):
    pairs = []
    for place in range(4):
        for core in range(2):
            to = gray(gray(place) ^ (1 << (core ^ second)))
            pairs.append((ring_index(ring, place) * 2 + core, ring_index(ring, to) * 2 + core))
    return lax.ppermute(a, RINGS[ring] + ("core",), pairs)


def move_x(a, k):
    return lax.ppermute(a, "x", [(i, (i + k) % 4) for i in range(4)])


def move_z(a, k):
    pairs = [(i * 2 + core, (i + (k, -k)[core]) % 8 * 2 + core) for i in range(8) for core in range(2)]
    return lax.ppermute(a, ("zh", "z0", "core"), pairs)


def swap(a, axis):
    return lax.ppermute(a, axis, [(0, 1), (1, 0)])


def each_to_each(keep, send, ring):
    first = exchange(send, ring, 0)
    second = exchange(jnp.stack([keep[1], first[1]]), ring, 1)
    return jnp.stack([keep[0], first[0], second[0], second[1]])


def on_device(activations, cotangent, masked, ratios, owners):
    tok, width = activations.shape
    row_blocks, col_blocks = shape((2, BLOCK, tok), bf16), shape((2, tok, BLOCK), bf16)
    keep_r, send_r, keep_g, send_g, meta = local_kernel(
        prepare,
        [row_blocks, row_blocks, col_blocks, col_blocks, shape((PERM_AT + HEADS,), jnp.int32)],
        (owners, ratios, masked[None, :], activations, cotangent),
        PREPARE_MIB,
        2 * tok * width,
        "prepare",
        in_specs=[anywhere(), anywhere(), vmem(), anywhere(), anywhere()],
        out_specs=[vmem()] * 4 + [smem()],
        scratch=[
            pltpu.VMEM((tok, width), bf16),
            pltpu.VMEM((tok, width), bf16),
            pltpu.SMEM((HEADS,), jnp.int32),
            pltpu.SMEM((1,), jnp.int32),
            pltpu.SMEM((HEADS,), jnp.int32),
            pltpu.SMEM((HEADS,), jnp.int32),
            pltpu.SemaphoreType.DMA((4,)),
        ],
    )
    r0, g0 = each_to_each(keep_r, send_r, "y"), each_to_each(keep_g, send_g, "x")
    r1, r2 = exchange(r0, "x", 0), exchange(r0, "x", 1)
    g1, g2 = exchange(g0, "y", 0), exchange(g0, "y", 1)
    r3, g3 = exchange(r1, "x", 1), exchange(g1, "y", 1)
    gathered = (r0, r1, r2, r3, g0, g1, g2, g3)

    def part(other_core, name):
        (out,) = local_kernel(
            functools.partial(multiply, other_core),
            [shape((8, 256, SLOT), bf16)],
            gathered,
            32,
            BLOCK * BLOCK * 16 * tok,
            name,
        )
        return out

    other = swap(part(1, "multiply_other"), "core")
    own = part(0, "multiply_own")
    (odd,) = local_kernel(add_odd, [shape((4, 256, SLOT), bf16)], (own, other), 8, 4 * 256 * SLOT, "add_odd")
    stay, move = local_kernel(
        add_even,
        [shape((2, 256, SLOT), f32), shape((2, 256, SLOT), bf16)],
        (own, other, move_z(odd, 1)),
        8,
        8 * 256 * SLOT,
        "add_even",
    )
    near, far = local_kernel(
        add_far,
        [shape((256, SLOT), f32), shape((256, SLOT), bf16)],
        (stay, move_z(move, 2)),
        8,
        2 * 256 * SLOT,
        "add_far",
    )
    head_grad, mine, theirs = local_kernel(
        gram_part,
        [shape((256, SLOT), bf16), shape((GRAM, HEAD), f32), shape((GRAM, HEAD), f32)],
        (near, move_z(far, 4)),
        8,
        2 * 256 * SLOT * SLOT,
        "gram_part",
    )
    mine = mine + swap(theirs, "core")
    mine = mine + swap(mine, "z0")
    mine = mine + exchange(mine, "y", 0)
    mine = mine + exchange(mine, "y", 1)
    keep, send = local_kernel(
        newton,
        [shape((2, HALF, SLOT), bf16)] * 2,
        (meta, mine, swap(mine, "core"), head_grad),
        16,
        20 * 2 * SLOT**3 * 6,
        "newton",
        in_specs=[smem()] + [vmem()] * 3,
        scratch=[pltpu.VMEM((256, SLOT), bf16)],
    )
    p0 = each_to_each(keep, send, "zh")
    q0 = swap(p0, "ylo")
    ps = [p0] + [move_x(p0, k) for k in (1, 2, 3)]
    qs = [q0] + [move_x(q0, k) for k in (1, 2, 3)]
    (out,) = local_kernel(
        place_heads,
        [shape((2 * HALF, width), f32)],
        (meta, *ps, *qs),
        12,
        0,
        "place_heads",
        in_specs=[smem()] + [vmem()] * 8,
    )
    return out


def solution(mesh):
    axes = ("x", "ylo", "yhi", "zh", "z0", "core")
    fine = Mesh(mesh.devices.reshape(4, 2, 2, 4, 2, 2), axes)
    everywhere = P(axes)
    placed = (P(axes, None), P(axes, None), everywhere, everywhere, P())
    return jax.shard_map(
        on_device,
        mesh=fine,
        in_specs=placed,
        out_specs=P(("yhi", "zh", "z0", "core"), None),
        check_vma=False,
    )
```

time: 162 us -> 167 us (1.031)
  waiting for transfers between devices: 79 us -> 94.5 us
  starting transfers between devices: 57.3 us -> 49 us
  local copies, waits for them, and re-layouts: 3.89 us -> 2.21 us
    ppermute x18 -> x17, waiting for transfers between devices: 56.3 us -> 78.4 us  [the longest x14 59.5 us: exchange(): return lax.ppermute(a, RINGS[ring] + ('core',), pairs)]
    ppermute x5, starting transfers between devices: 6.34 us -> 15.9 us  [swap(): return lax.ppermute(a, axis, [(0, 1), (1, 0)])]
    ppermute x18 -> x17, starting transfers between devices: 37.8 us -> 28.7 us  [the longest x14 17.3 us: exchange(): return lax.ppermute(a, RINGS[ring] + ('core',), pairs)]
    ppermute x13 -> x6, starting transfers between devices: 13.2 us -> 4.36 us  [move_x(): return lax.ppermute(a, 'x', [(i, (i + k) % 4) for i in range(4)])]
    ppermute x13 -> x6, waiting for transfers between devices: 14.6 us -> 8.59 us  [move_x(): return lax.ppermute(a, 'x', [(i, (i + k) % 4) for i in range(4)])]
    unnamed x8 -> x2, local copies, waits for them, and re-layouts: 3.75 us -> 0.01 us
    slice x4 -> x6, local copies, waits for them, and re-layouts: 0.14 us -> 2.21 us  [each_to_each(): return jnp.stack([keep[0], first[0], second[0], second[1]])]
    pallas_call x8 -> x9, Pallas kernels: 19.7 us -> 18.2 us  [local_kernel(): pl.pallas_call(body, out_shape=outs, in_specs=in_specs or [vmem()] * len(...]
  transfers between devices with their start and end apart: 36 -> 28, of which waited for: 22 -> 24; matrix products, arithmetic and copies ran while one was open for 0% -> 2% of each run, Pallas kernels for 1% -> 1%
where the time goes in v3:
time: 167 us; the launch traced here: 165 us
  waiting for transfers between devices  94.5 us (57%)
  starting transfers between devices  49 us (29%)
  Pallas kernels  18.2 us (11%)
  local copies, waits for them, and re-layouts  2.21 us (1%)
    ppermute x14, waiting for transfers between devices, exchange(): return lax.ppermute(a, RINGS[ring] + ('core',), pairs)  59.5 us
    ppermute x3, waiting for transfers between devices, move_z(): return lax.ppermute(a, ('zh', 'z0', 'core'), pairs)  18.9 us
    pallas_call x9, Pallas kernels, local_kernel(): pl.pallas_call(body, out_shape=outs, in_specs=in_specs or [vmem()] * len(...  18.2 us
    ppermute x14, starting transfers between devices, exchange(): return lax.ppermute(a, RINGS[ring] + ('core',), pairs)  17.3 us
    ppermute x5, starting transfers between devices, swap(): return lax.ppermute(a, axis, [(0, 1), (1, 0)])  15.9 us
    ppermute x3, starting transfers between devices, move_z(): return lax.ppermute(a, ('zh', 'z0', 'core'), pairs)  11.4 us
    ppermute x6, waiting for transfers between devices, move_x(): return lax.ppermute(a, 'x', [(i, (i + k) % 4) for i in range(4)])  8.59 us
    ppermute x5, waiting for transfers between devices, swap(): return lax.ppermute(a, axis, [(0, 1), (1, 0)])  7.52 us
  transfers between devices with their start and end apart: 28, of which 24 were waited for; matrix products, arithmetic and copies ran while one was open for 2% of the time, Pallas kernels for 1%

profile of v3, /device:TPU:1, one launch (start us, length us, event | category | flops | bytes accessed | tf_op | source)
XLA Modules:
  0.0 165.1 jit_solution(17771732637567586033)
XLA Ops:
  0.7 4.1 %prepare.1 = (bf16[2,1024,128]{2,1,0:T(8,128)(2,1)}, bf16[2,1024,128]{2,1,0:T(8,128)(2,1)}, bf16[2,128,1024]{2,1,0:T(8,128)(2,1)}, bf16[2,128,1024]{2,1,0:T(8,128)(2,1)}, s32[40]{0:T(128)}) custom-call(s32[32]{0:T(128)} %owners_far.1, s32[1]{0:T(128)S(6)} %copy.6.ratio_far, s32[1,128]{1,0:T(1,128)} %bitcast.1, bf16[128,4096]{1,0:T(8,128)(2,1)} %act_far.1, ...), custom_call_target="tpu_custom_call" | custom-call | flops 1048576 | bytes 4195108 | tf_op jit(solution)/shard_map/prepare/pallas_call | solution.py:45
  4.8 3.4 %collective-permute-start.5 = (bf16[2,128,1024]{2,1,0:T(8,128)(2,1)}, bf16[2,128,1024]{2,1,0:T(8,128)(2,1)S(1)}, u32[]{:S(2)}, u32[]{:S(2)}) collective-permute-start(bf16[2,128,1024]{2,1,0:T(8,128)(2,1)} %get-tuple-element.23), channel_id=1, source_target_pairs={{0,64},{1,193},{64,0},{65,129},{128,192},{129,65},{192,128},{193,1... | collective-permute-start | bytes 1572872 | tf_op jit(solution)/shard_map/ppermute | solution.py:278
  8.1 2.7 %collective-permute-start = (bf16[2,1024,128]{2,1,0:T(8,128)(2,1)}, bf16[2,1024,128]{2,1,0:T(8,128)(2,1)S(1)}, u32[]{:S(2)}, u32[]{:S(2)}) collective-permute-start(bf16[2,1024,128]{2,1,0:T(8,128)(2,1)} %get-tuple-element.21), channel_id=1, source_target_pairs={{0,32},{1,49},{32,0},{33,17},{16,48},{17,33},{48,16},{49,1},{2,34}... | collective-permute-start | bytes 1572872 | tf_op jit(solution)/shard_map/ppermute | solution.py:278
  18.2 5.3 %collective-permute-done.6 = bf16[2,128,1024]{2,1,0:T(8,128)(2,1)S(1)} collective-permute-done((bf16[2,128,1024]{2,1,0:T(8,128)(2,1)S(1)}, bf16[2,128,1024]{2,1,0:T(8,128)(2,1)S(1)}, u32[]{:S(2)}, u32[]{:S(2)}) %collective-permute-start.6) | collective-permute-done | bytes 524320 | tf_op jit(solution)/shard_map/ppermute | solution.py:278
  23.5 3.0 %collective-permute-start.7 = (bf16[4,128,1024]{2,1,0:T(8,128)(2,1)S(1)}, bf16[4,128,1024]{2,1,0:T(8,128)(2,1)S(1)}, u32[]{:S(2)}, u32[]{:S(2)}) collective-permute-start(bf16[4,128,1024]{2,1,0:T(8,128)(2,1)S(1)} %pad_maximum_fusion.1.refs_4_), channel_id=1, source_target_pairs={{0,32},{1,49},{32,0},{33,17},{16,48},{17,33},{48,16},{49,1},{2,34}... | collective-permute-start | bytes 3145736 | tf_op jit(solution)/shard_map/ppermute | solution.py:278
  29.2 15.2 %collective-permute-done.7.refs_5_ = bf16[4,128,1024]{2,1,0:T(8,128)(2,1)S(1)} collective-permute-done((bf16[4,128,1024]{2,1,0:T(8,128)(2,1)S(1)}, bf16[4,128,1024]{2,1,0:T(8,128)(2,1)S(1)}, u32[]{:S(2)}, u32[]{:S(2)}) %collective-permute-start.7) | collective-permute-done | bytes 1048608 | tf_op jit(solution)/shard_map/ppermute | solution.py:278
  46.9 7.0 %collective-permute-done.8.refs_6_ = bf16[4,128,1024]{2,1,0:T(8,128)(2,1)S(1)} collective-permute-done((bf16[4,128,1024]{2,1,0:T(8,128)(2,1)S(1)}, bf16[4,128,1024]{2,1,0:T(8,128)(2,1)S(1)}, u32[]{:S(2)}, u32[]{:S(2)}) %collective-permute-start.8) | collective-permute-done | bytes 1048608 | tf_op jit(solution)/shard_map/ppermute | solution.py:278
  53.9 11.2 %collective-permute-done.9.refs_7_ = bf16[4,128,1024]{2,1,0:T(8,128)(2,1)S(1)} collective-permute-done((bf16[4,128,1024]{2,1,0:T(8,128)(2,1)S(1)}, bf16[4,128,1024]{2,1,0:T(8,128)(2,1)S(1)}, u32[]{:S(2)}, u32[]{:S(2)}) %collective-permute-start.9) | collective-permute-done | bytes 1048608 | tf_op jit(solution)/shard_map/ppermute | solution.py:278
  68.0 7.0 %collective-permute-start.10 = (bf16[8,256,256]{2,1,0:T(8,128)(2,1)S(1)}, bf16[8,256,256]{2,1,0:T(8,128)(2,1)S(1)}, u32[]{:S(2)}, u32[]{:S(2)}) collective-permute-start(bf16[8,256,256]{2,1,0:T(8,128)(2,1)S(1)} %multiply_other.1), channel_id=1, source_target_pairs={{0,1},{1,0},{2,3},{3,2},{4,5},{5,4},{6,7},{7,6},{8,9},{9,8},{10,11... | collective-permute-start | bytes 3145736 | tf_op jit(solution)/shard_map/ppermute | solution.py:291
  77.5 5.7 %collective-permute-start.11 = (bf16[4,256,256]{2,1,0:T(8,128)(2,1)S(1)}, bf16[4,256,256]{2,1,0:T(8,128)(2,1)S(1)}, u32[]{:S(2)}, u32[]{:S(2)}) collective-permute-start(bf16[4,256,256]{2,1,0:T(8,128)(2,1)S(1)} %add_odd.1), channel_id=1, source_target_pairs={{0,2},{1,15},{2,4},{3,1},{4,6},{5,3},{6,8},{7,5},{8,10},{9,7},{10,... | collective-permute-start | bytes 1572872 | tf_op jit(solution)/shard_map/ppermute | solution.py:287
  83.1 6.1 %collective-permute-done.11.arrived = bf16[4,256,256]{2,1,0:T(8,128)(2,1)S(1)} collective-permute-done((bf16[4,256,256]{2,1,0:T(8,128)(2,1)S(1)}, bf16[4,256,256]{2,1,0:T(8,128)(2,1)S(1)}, u32[]{:S(2)}, u32[]{:S(2)}) %collective-permute-start.11) | collective-permute-done | bytes 524320 | tf_op jit(solution)/shard_map/ppermute | solution.py:287
  89.4 2.9 %collective-permute-start.12 = (bf16[2,256,256]{2,1,0:T(8,128)(2,1)S(1)}, bf16[2,256,256]{2,1,0:T(8,128)(2,1)S(1)}, u32[]{:S(2)}, u32[]{:S(2)}) collective-permute-start(bf16[2,256,256]{2,1,0:T(8,128)(2,1)S(1)} %get-tuple-element.25), channel_id=1, source_target_pairs={{0,4},{1,13},{2,6},{3,15},{4,8},{5,1},{6,10},{7,3},{8,12},{9,5},{1... | collective-permute-start | bytes 786440 | tf_op jit(solution)/shard_map/ppermute | solution.py:287
  92.3 6.3 %collective-permute-done.12.arrived = bf16[2,256,256]{2,1,0:T(8,128)(2,1)S(1)} collective-permute-done((bf16[2,256,256]{2,1,0:T(8,128)(2,1)S(1)}, bf16[2,256,256]{2,1,0:T(8,128)(2,1)S(1)}, u32[]{:S(2)}, u32[]{:S(2)}) %collective-permute-start.12) | collective-permute-done | bytes 262176 | tf_op jit(solution)/shard_map/ppermute | solution.py:287
  98.7 2.9 %collective-permute-start.13 = (bf16[256,256]{1,0:T(8,128)(2,1)S(1)}, bf16[256,256]{1,0:T(8,128)(2,1)S(1)}, u32[]{:S(2)}, u32[]{:S(2)}) collective-permute-start(bf16[256,256]{1,0:T(8,128)(2,1)S(1)} %get-tuple-element.27), channel_id=1, source_target_pairs={{0,8},{1,9},{2,10},{3,11},{4,12},{5,13},{6,14},{7,15},{8,0},{9,1},... | collective-permute-start | bytes 393224 | tf_op jit(solution)/shard_map/ppermute | solution.py:287
  101.5 6.4 %collective-permute-done.13.arrived = bf16[256,256]{1,0:T(8,128)(2,1)S(1)} collective-permute-done((bf16[256,256]{1,0:T(8,128)(2,1)S(1)}, bf16[256,256]{1,0:T(8,128)(2,1)S(1)}, u32[]{:S(2)}, u32[]{:S(2)}) %collective-permute-start.13) | collective-permute-done | bytes 131104 | tf_op jit(solution)/shard_map/ppermute | solution.py:287
  108.2 5.1 %collective-permute-start.14 = (f32[192,128]{1,0:T(8,128)S(1)}, f32[192,128]{1,0:T(8,128)S(1)}, u32[]{:S(2)}, u32[]{:S(2)}) collective-permute-start(f32[192,128]{1,0:T(8,128)S(1)} %get-tuple-element.29), channel_id=1, source_target_pairs={{0,1},{1,0},{2,3},{3,2},{4,5},{5,4},{6,7},{7,6},{8,9},{9,8},{10,11... | collective-permute-start | bytes 294920 | tf_op jit(solution)/shard_map/ppermute | solution.py:291
  114.4 4.0 %collective-permute-done.15 = f32[192,128]{1,0:T(8,128)S(1)} collective-permute-done((f32[192,128]{1,0:T(8,128)S(1)}, f32[192,128]{1,0:T(8,128)S(1)}, u32[]{:S(2)}, u32[]{:S(2)}) %collective-permute-start.15) | collective-permute-done | bytes 98336 | tf_op jit(solution)/shard_map/ppermute | solution.py:291
  119.3 3.9 %collective-permute-done.16 = f32[192,128]{1,0:T(8,128)S(1)} collective-permute-done((f32[192,128]{1,0:T(8,128)S(1)}, f32[192,128]{1,0:T(8,128)S(1)}, u32[]{:S(2)}, u32[]{:S(2)}) %collective-permute-start.16) | collective-permute-done | bytes 98336 | tf_op jit(solution)/shard_map/ppermute | solution.py:278
  123.3 3.5 %collective-permute-done.17 = f32[192,128]{1,0:T(8,128)S(1)} collective-permute-done((f32[192,128]{1,0:T(8,128)S(1)}, f32[192,128]{1,0:T(8,128)S(1)}, u32[]{:S(2)}, u32[]{:S(2)}) %collective-permute-start.17) | collective-permute-done | bytes 98336 | tf_op jit(solution)/shard_map/ppermute | solution.py:278
  126.8 3.6 %collective-permute-start.18 = (f32[192,128]{1,0:T(8,128)S(1)}, f32[192,128]{1,0:T(8,128)S(1)}, u32[]{:S(2)}, u32[]{:S(2)}) collective-permute-start(f32[192,128]{1,0:T(8,128)S(1)} %add.15.mine), channel_id=1, source_target_pairs={{0,1},{1,0},{2,3},{3,2},{4,5},{5,4},{6,7},{7,6},{8,9},{9,8},{10,11... | collective-permute-start | bytes 294920 | tf_op jit(solution)/shard_map/ppermute | solution.py:291
  131.3 6.8 %newton.1 = (bf16[2,64,256]{2,1,0:T(8,128)(2,1)S(1)}, bf16[2,64,256]{2,1,0:T(8,128)(2,1)S(1)}) custom-call(s32[40]{0:T(128)S(1)} %copy-done, f32[192,128]{1,0:T(8,128)S(1)} %add.15.mine, f32[192,128]{1,0:T(8,128)S(1)} %collective-permute-done.18.other, bf16[256,256]{1,0:T(8,128)(2,1)S(1)} %get-tuple-element.30.head_grad), custom_call_target="tpu_custom_call" | custom-call | flops 4026531840 | bytes 458912 | tf_op jit(solution)/shard_map/newton/pallas_call | solution.py:45
  139.2 4.2 %collective-permute-done.19 = bf16[2,64,256]{2,1,0:T(8,128)(2,1)S(1)} collective-permute-done((bf16[2,64,256]{2,1,0:T(8,128)(2,1)S(1)}, bf16[2,64,256]{2,1,0:T(8,128)(2,1)S(1)}, u32[]{:S(2)}, u32[]{:S(2)}) %collective-permute-start.19) | collective-permute-done | bytes 65568 | tf_op jit(solution)/shard_map/ppermute | solution.py:278
  144.0 4.3 %collective-permute-done.20 = bf16[2,64,256]{2,1,0:T(8,128)(2,1)S(1)} collective-permute-done((bf16[2,64,256]{2,1,0:T(8,128)(2,1)S(1)}, bf16[2,64,256]{2,1,0:T(8,128)(2,1)S(1)}, u32[]{:S(2)}, u32[]{:S(2)}) %collective-permute-start.20) | collective-permute-done | bytes 65568 | tf_op jit(solution)/shard_map/ppermute | solution.py:278
  157.7 2.6 %collective-permute-done.26.q2 = bf16[4,64,256]{2,1,0:T(8,128)(2,1)S(1)} collective-permute-done((bf16[4,64,256]{2,1,0:T(8,128)(2,1)S(1)}, bf16[4,64,256]{2,1,0:T(8,128)(2,1)S(1)}, u32[]{:S(2)}, u32[]{:S(2)}) %collective-permute-start.26) | collective-permute-done | bytes 131104 | tf_op jit(solution)/shard_map/ppermute | solution.py:282
  (59 shorter events, 37.1 us)
Async XLA Ops:
  4.8 10.2 %collective-permute-start.5 = (bf16[2,128,1024]{2,1,0:T(8,128)(2,1)}, bf16[2,128,1024]{2,1,0:T(8,128)(2,1)S(1)}, u32[]{:S(2)}, u32[]{:S(2)}) collective-permute-start(bf16[2,128,1024]{2,1,0:T(8,128)(2,1)} %get-tuple-element.23), channel_id=1, source_target_pairs={{0,64},{1,193},{64,0},{65,129},{128,192},{129,65},{192,128},{193,1... | collective-permute-start | bytes 1572872 | tf_op jit(solution)/shard_map/ppermute | solution.py:278
  8.1 9.5 %collective-permute-start = (bf16[2,1024,128]{2,1,0:T(8,128)(2,1)}, bf16[2,1024,128]{2,1,0:T(8,128)(2,1)S(1)}, u32[]{:S(2)}, u32[]{:S(2)}) collective-permute-start(bf16[2,1024,128]{2,1,0:T(8,128)(2,1)} %get-tuple-element.21), channel_id=1, source_target_pairs={{0,32},{1,49},{32,0},{33,17},{16,48},{17,33},{48,16},{49,1},{2,34}... | collective-permute-start | bytes 1572872 | tf_op jit(solution)/shard_map/ppermute | solution.py:278
  15.0 8.4 %collective-permute-start.6 = (bf16[2,128,1024]{2,1,0:T(8,128)(2,1)S(1)}, bf16[2,128,1024]{2,1,0:T(8,128)(2,1)S(1)}, u32[]{:S(2)}, u32[]{:S(2)}) collective-permute-start(bf16[2,128,1024]{2,1,0:T(8,128)(2,1)S(1)} %pad_maximum_fusion.3), channel_id=1, source_target_pairs={{0,192},{1,65},{64,128},{65,1},{128,64},{129,193},{192,0},{193,129... | collective-permute-start | bytes 1572872 | tf_op jit(solution)/shard_map/ppermute | solution.py:278
  17.8 8.8 %collective-permute-start.1 = (bf16[2,1024,128]{2,1,0:T(8,128)(2,1)S(1)}, bf16[2,1024,128]{2,1,0:T(8,128)(2,1)S(1)}, u32[]{:S(2)}, u32[]{:S(2)}) collective-permute-start(bf16[2,1024,128]{2,1,0:T(8,128)(2,1)S(1)} %pad_maximum_fusion.2), channel_id=1, source_target_pairs={{0,48},{1,33},{32,16},{33,1},{16,32},{17,49},{48,0},{49,17},{2,50}... | collective-permute-start | bytes 1572872 | tf_op jit(solution)/shard_map/ppermute | solution.py:278
  23.5 20.9 %collective-permute-start.7 = (bf16[4,128,1024]{2,1,0:T(8,128)(2,1)S(1)}, bf16[4,128,1024]{2,1,0:T(8,128)(2,1)S(1)}, u32[]{:S(2)}, u32[]{:S(2)}) collective-permute-start(bf16[4,128,1024]{2,1,0:T(8,128)(2,1)S(1)} %pad_maximum_fusion.1.refs_4_), channel_id=1, source_target_pairs={{0,32},{1,49},{32,0},{33,17},{16,48},{17,33},{48,16},{49,1},{2,34}... | collective-permute-start | bytes 3145736 | tf_op jit(solution)/shard_map/ppermute | solution.py:278
  26.7 20.2 %collective-permute-start.2 = (bf16[4,1024,128]{2,1,0:T(8,128)(2,1)S(1)}, bf16[4,1024,128]{2,1,0:T(8,128)(2,1)S(1)}, u32[]{:S(2)}, u32[]{:S(2)}) collective-permute-start(bf16[4,1024,128]{2,1,0:T(8,128)(2,1)S(1)} %pad_maximum_fusion.refs_0_), channel_id=1, source_target_pairs={{0,64},{1,193},{64,0},{65,129},{128,192},{129,65},{192,128},{193,1... | collective-permute-start | bytes 3145736 | tf_op jit(solution)/shard_map/ppermute | solution.py:278
  29.2 24.6 %collective-permute-start.8 = (bf16[4,128,1024]{2,1,0:T(8,128)(2,1)S(1)}, bf16[4,128,1024]{2,1,0:T(8,128)(2,1)S(1)}, u32[]{:S(2)}, u32[]{:S(2)}) collective-permute-start(bf16[4,128,1024]{2,1,0:T(8,128)(2,1)S(1)} %pad_maximum_fusion.1.refs_4_), channel_id=1, source_target_pairs={{0,48},{1,33},{32,16},{33,1},{16,32},{17,49},{48,0},{49,17},{2,50}... | collective-permute-start | bytes 3145736 | tf_op jit(solution)/shard_map/ppermute | solution.py:278
  29.2 24.6 %collective-permute-start.3 = (bf16[4,1024,128]{2,1,0:T(8,128)(2,1)S(1)}, bf16[4,1024,128]{2,1,0:T(8,128)(2,1)S(1)}, u32[]{:S(2)}, u32[]{:S(2)}) collective-permute-start(bf16[4,1024,128]{2,1,0:T(8,128)(2,1)S(1)} %pad_maximum_fusion.refs_0_), channel_id=1, source_target_pairs={{0,192},{1,65},{64,128},{65,1},{128,64},{129,193},{192,0},{193,129... | collective-permute-start | bytes 3145736 | tf_op jit(solution)/shard_map/ppermute | solution.py:278
  44.5 20.6 %collective-permute-start.9 = (bf16[4,128,1024]{2,1,0:T(8,128)(2,1)S(1)}, bf16[4,128,1024]{2,1,0:T(8,128)(2,1)S(1)}, u32[]{:S(2)}, u32[]{:S(2)}) collective-permute-start(bf16[4,128,1024]{2,1,0:T(8,128)(2,1)S(1)} %collective-permute-done.7.refs_5_), channel_id=1, source_target_pairs={{0,48},{1,33},{32,16},{33,1},{16,32},{17,49},{48,0},{49,17},{2,50}... | collective-permute-start | bytes 3145736 | tf_op jit(solution)/shard_map/ppermute | solution.py:278
  46.9 18.8 %collective-permute-start.4 = (bf16[4,1024,128]{2,1,0:T(8,128)(2,1)S(1)}, bf16[4,1024,128]{2,1,0:T(8,128)(2,1)S(1)}, u32[]{:S(2)}, u32[]{:S(2)}) collective-permute-start(bf16[4,1024,128]{2,1,0:T(8,128)(2,1)S(1)} %collective-permute-done.2.refs_1_), channel_id=1, source_target_pairs={{0,192},{1,65},{64,128},{65,1},{128,64},{129,193},{192,0},{193,129... | collective-permute-start | bytes 3145736 | tf_op jit(solution)/shard_map/ppermute | solution.py:278
  68.0 9.3 %collective-permute-start.10 = (bf16[8,256,256]{2,1,0:T(8,128)(2,1)S(1)}, bf16[8,256,256]{2,1,0:T(8,128)(2,1)S(1)}, u32[]{:S(2)}, u32[]{:S(2)}) collective-permute-start(bf16[8,256,256]{2,1,0:T(8,128)(2,1)S(1)} %multiply_other.1), channel_id=1, source_target_pairs={{0,1},{1,0},{2,3},{3,2},{4,5},{5,4},{6,7},{7,6},{8,9},{9,8},{10,11... | collective-permute-start | bytes 3145736 | tf_op jit(solution)/shard_map/ppermute | solution.py:291
  77.5 11.8 %collective-permute-start.11 = (bf16[4,256,256]{2,1,0:T(8,128)(2,1)S(1)}, bf16[4,256,256]{2,1,0:T(8,128)(2,1)S(1)}, u32[]{:S(2)}, u32[]{:S(2)}) collective-permute-start(bf16[4,256,256]{2,1,0:T(8,128)(2,1)S(1)} %add_odd.1), channel_id=1, source_target_pairs={{0,2},{1,15},{2,4},{3,1},{4,6},{5,3},{6,8},{7,5},{8,10},{9,7},{10,... | collective-permute-start | bytes 1572872 | tf_op jit(solution)/shard_map/ppermute | solution.py:287
  89.4 9.2 %collective-permute-start.12 = (bf16[2,256,256]{2,1,0:T(8,128)(2,1)S(1)}, bf16[2,256,256]{2,1,0:T(8,128)(2,1)S(1)}, u32[]{:S(2)}, u32[]{:S(2)}) collective-permute-start(bf16[2,256,256]{2,1,0:T(8,128)(2,1)S(1)} %get-tuple-element.25), channel_id=1, source_target_pairs={{0,4},{1,13},{2,6},{3,15},{4,8},{5,1},{6,10},{7,3},{8,12},{9,5},{1... | collective-permute-start | bytes 786440 | tf_op jit(solution)/shard_map/ppermute | solution.py:287
  98.7 9.3 %collective-permute-start.13 = (bf16[256,256]{1,0:T(8,128)(2,1)S(1)}, bf16[256,256]{1,0:T(8,128)(2,1)S(1)}, u32[]{:S(2)}, u32[]{:S(2)}) collective-permute-start(bf16[256,256]{1,0:T(8,128)(2,1)S(1)} %get-tuple-element.27), channel_id=1, source_target_pairs={{0,8},{1,9},{2,10},{3,11},{4,12},{5,13},{6,14},{7,15},{8,0},{9,1},... | collective-permute-start | bytes 393224 | tf_op jit(solution)/shard_map/ppermute | solution.py:287
  108.2 6.1 %collective-permute-start.14 = (f32[192,128]{1,0:T(8,128)S(1)}, f32[192,128]{1,0:T(8,128)S(1)}, u32[]{:S(2)}, u32[]{:S(2)}) collective-permute-start(f32[192,128]{1,0:T(8,128)S(1)} %get-tuple-element.29), channel_id=1, source_target_pairs={{0,1},{1,0},{2,3},{3,2},{4,5},{5,4},{6,7},{7,6},{8,9},{9,8},{10,11... | collective-permute-start | bytes 294920 | tf_op jit(solution)/shard_map/ppermute | solution.py:291
  118.4 4.8 %collective-permute-start.16 = (f32[192,128]{1,0:T(8,128)S(1)}, f32[192,128]{1,0:T(8,128)S(1)}, u32[]{:S(2)}, u32[]{:S(2)}) collective-permute-start(f32[192,128]{1,0:T(8,128)S(1)} %add.13), channel_id=1, source_target_pairs={{0,32},{1,49},{32,0},{33,17},{16,48},{17,33},{48,16},{49,1},{2,34}... | collective-permute-start | bytes 294920 | tf_op jit(solution)/shard_map/ppermute | solution.py:278
  138.1 5.3 %collective-permute-start.19 = (bf16[2,64,256]{2,1,0:T(8,128)(2,1)S(1)}, bf16[2,64,256]{2,1,0:T(8,128)(2,1)S(1)}, u32[]{:S(2)}, u32[]{:S(2)}) collective-permute-start(bf16[2,64,256]{2,1,0:T(8,128)(2,1)S(1)} %get-tuple-element.32), channel_id=1, source_target_pairs={{0,4},{1,13},{4,0},{5,9},{8,12},{9,5},{12,8},{13,1},{2,6},{3,15},{... | collective-permute-start | bytes 196616 | tf_op jit(solution)/shard_map/ppermute | solution.py:278
  143.4 4.8 %collective-permute-start.20 = (bf16[2,64,256]{2,1,0:T(8,128)(2,1)S(1)}, bf16[2,64,256]{2,1,0:T(8,128)(2,1)S(1)}, u32[]{:S(2)}, u32[]{:S(2)}) collective-permute-start(bf16[2,64,256]{2,1,0:T(8,128)(2,1)S(1)} %pad_maximum_fusion.5), channel_id=1, source_target_pairs={{0,12},{1,5},{4,8},{5,1},{8,4},{9,13},{12,0},{13,9},{2,14},{3,7},{... | collective-permute-start | bytes 196616 | tf_op jit(solution)/shard_map/ppermute | solution.py:278
  148.4 6.0 %collective-permute-start.23 = (bf16[4,64,256]{2,1,0:T(8,128)(2,1)S(1)}, bf16[4,64,256]{2,1,0:T(8,128)(2,1)S(1)}, u32[]{:S(2)}, u32[]{:S(2)}) collective-permute-start(bf16[4,64,256]{2,1,0:T(8,128)(2,1)S(1)} %pad_maximum_fusion.4.p0), channel_id=1, source_target_pairs={{0,192},{64,0},{128,64},{192,128},{1,193},{65,1},{129,65},{193,129... | collective-permute-start | bytes 393224 | tf_op jit(solution)/shard_map/ppermute | solution.py:282
  149.9 5.4 %collective-permute-start.22 = (bf16[4,64,256]{2,1,0:T(8,128)(2,1)S(1)}, bf16[4,64,256]{2,1,0:T(8,128)(2,1)S(1)}, u32[]{:S(2)}, u32[]{:S(2)}) collective-permute-start(bf16[4,64,256]{2,1,0:T(8,128)(2,1)S(1)} %pad_maximum_fusion.4.p0), channel_id=1, source_target_pairs={{0,128},{64,192},{128,0},{192,64},{1,129},{65,193},{129,1},{193,65... | collective-permute-start | bytes 393224 | tf_op jit(solution)/shard_map/ppermute | solution.py:282
  149.9 6.4 %collective-permute-start.21 = (bf16[4,64,256]{2,1,0:T(8,128)(2,1)S(1)}, bf16[4,64,256]{2,1,0:T(8,128)(2,1)S(1)}, u32[]{:S(2)}, u32[]{:S(2)}) collective-permute-start(bf16[4,64,256]{2,1,0:T(8,128)(2,1)S(1)} %pad_maximum_fusion.4.p0), channel_id=1, source_target_pairs={{0,64},{64,128},{128,192},{192,0},{1,65},{65,129},{129,193},{193,1... | collective-permute-start | bytes 393224 | tf_op jit(solution)/shard_map/ppermute | solution.py:282
  152.2 5.5 %collective-permute-start.27 = (bf16[4,64,256]{2,1,0:T(8,128)(2,1)S(1)}, bf16[4,64,256]{2,1,0:T(8,128)(2,1)S(1)}, u32[]{:S(2)}, u32[]{:S(2)}) collective-permute-start(bf16[4,64,256]{2,1,0:T(8,128)(2,1)S(1)} %collective-permute-done.24.q0), channel_id=1, source_target_pairs={{0,192},{64,0},{128,64},{192,128},{1,193},{65,1},{129,65},{193,129... | collective-permute-start | bytes 393224 | tf_op jit(solution)/shard_map/ppermute | solution.py:282
  153.6 6.7 %collective-permute-start.26 = (bf16[4,64,256]{2,1,0:T(8,128)(2,1)S(1)}, bf16[4,64,256]{2,1,0:T(8,128)(2,1)S(1)}, u32[]{:S(2)}, u32[]{:S(2)}) collective-permute-start(bf16[4,64,256]{2,1,0:T(8,128)(2,1)S(1)} %collective-permute-done.24.q0), channel_id=1, source_target_pairs={{0,128},{64,192},{128,0},{192,64},{1,129},{65,193},{129,1},{193,65... | collective-permute-start | bytes 393224 | tf_op jit(solution)/shard_map/ppermute | solution.py:282
  154.3 8.6 %collective-permute-start.25 = (bf16[4,64,256]{2,1,0:T(8,128)(2,1)S(1)}, bf16[4,64,256]{2,1,0:T(8,128)(2,1)S(1)}, u32[]{:S(2)}, u32[]{:S(2)}) collective-permute-start(bf16[4,64,256]{2,1,0:T(8,128)(2,1)S(1)} %collective-permute-done.24.q0), channel_id=1, source_target_pairs={{0,64},{64,128},{128,192},{192,0},{1,65},{65,129},{129,193},{193,1... | collective-permute-start | bytes 393224 | tf_op jit(solution)/shard_map/ppermute | solution.py:282
  (5 other events, 69.9 us)

commit v4 on v2

--- a/solution.py
+++ b/solution.py
@@ -22,6 +22,8 @@
 BLOCK = 1024
 HALF = 64
 GRAM = HEAD + HALF
+
+PREPARE_MIB = 56
 
 f32, bf16 = jnp.float32, jnp.bfloat16
 
@@ -60,17 +62,22 @@
     return lax.axis_index("yhi") * 2 + lax.axis_index("ylo")
 
 
-def prepare(owners, ratio, masked, act_far, cot_far, *refs):
+def prepare(owners_far, ratio_far, masked, act_far, cot_far, *refs):
     rows_out, cols_out, meta = refs[:4], refs[4:8], refs[8]
-    act, cot, count, taken, sems = refs[9:]
-    get_act = pltpu.make_async_copy(act_far, act, sems.at[0])
-    get_cot = pltpu.make_async_copy(cot_far, cot, sems.at[1])
-    get_act.start()
-    get_cot.start()
-
+    act, cot, owners, ratio, count, taken, sems = refs[9:]
+    copies = [
+        pltpu.make_async_copy(far, near, sems.at[i])
+        for i, (far, near) in enumerate(
+            ((owners_far, owners), (ratio_far, ratio), (act_far, act), (cot_far, cot))
+        )
+    ]
+    for copy in copies:
+        copy.start()
     for v in range(HEADS):
         count[v] = 0
         taken[v] = 0
+    copies[0].wait()
+
     for h in range(HEADS):
         count[owners[h]] = count[owners[h]] + 1
     in_pairs = jnp.int32(0)
@@ -92,25 +99,26 @@
 
     tok, width = act.shape
     here_y, z0, core = y_place(), lax.axis_index("z0"), lax.axis_index("core")
-    get_act.wait()
+    copies[1].wait()
+    copies[2].wait()
     for k in range(4):
         y = (here_y + k) & 3
         base = (y >> 1) * (width // 2)
         low = (y & 1) * HALF
-        for crel in range(2):
-            for zrel in range(2):
+        for zrel in range(2):
+            for crel in range(2):
                 for zh in range(4):
                     block = zh * 4 + (z0 ^ zrel) * 2 + (core ^ crel)
                     at = pl.multiple_of(base + block * 128, 128)
                     turned = act[:, pl.ds(at, 128)].T
                     part = jnp.where(low == 0, turned[:HALF], turned[HALF:])
-                    to = ((crel * 2 + zrel) * 4 + zh) * HALF
+                    to = ((zrel * 2 + crel) * 4 + zh) * HALF
                     rows_out[k][to : to + HALF, :] = part
     along = masked[...].astype(f32) * 1000.0 / ratio[0].astype(f32)
     line = lax.broadcasted_iota(jnp.int32, (tok, tok), 0)
     lane = lax.broadcasted_iota(jnp.int32, (tok, tok), 1)
     weight = jnp.sum(jnp.where(line == lane, along, 0.0), axis=1, keepdims=True)
-    get_cot.wait()
+    copies[3].wait()
     for k in range(4):
         x = (lax.axis_index("x") + k) & 3
         for j in range(8):
@@ -121,35 +129,52 @@
             cols_out[k][:, j * HEAD : (j + 1) * HEAD] = piece.astype(bf16)
 
 
-def multiply(offset, r0, r1, r3, r2a, r2b, g0, g1, g3, g2a, g2b, out):
+def piece(near, opposite, i, j):
+    return (opposite[j // 2], j % 2) if i == 2 else (near[i], j)
+
+
+def operands(refs, pairs, rows, at):
+    r0, r1, r3, r2a, r2b, g0, g1, g3, g2a, g2b = refs
+    left, right = [], []
+    for dx, dy in pairs:
+        ref, i = piece({0: r0, 1: r1, 3: r3}, (r2a, r2b), dx, dy)
+        left.append(ref[i, rows[0] : rows[1], :])
+        ref, i = piece({0: g0, 1: g1, 3: g3}, (g2a, g2b), dy, dx)
+        right.append(ref[i, :, at : at + SLOT])
+    return jnp.concatenate(left, axis=1), jnp.concatenate(right, axis=0)
+
+
+def multiply_near(r0, r1, r3, g0, g1, g3, out):
+    refs = (r0, r1, r3, None, None, g0, g1, g3, None, None)
+    pairs = [(dx, dy) for dx in (0, 1, 3) for dy in (0, 1, 3)]
+    for n in range(BLOCK // SLOT):
+        left, right = operands(refs, pairs, (0, BLOCK), n * SLOT)
+        out[:, n * SLOT : (n + 1) * SLOT] = jnp.dot(left, right, preferred_element_type=f32)
+
+
+def multiply_rest(odd, near, *refs):
+    refs, outs = refs[:10], refs[10:]
     z0 = lax.axis_index("z0")
     half = BLOCK // 2
-
-    def rows_of(dx, dy):
-        ref, i = ((r2a if dy < 2 else r2b), dy % 2) if dx == 2 else ({0: r0, 1: r1, 3: r3}[dx], dy)
-        return ref[i, offset : offset + half, :]
-
-    def cols_of(dx, dy, at):
-        ref, i = ((g2a if dx < 2 else g2b), dx % 2) if dy == 2 else ({0: g0, 1: g1, 3: g3}[dy], dx)
-        return ref[i, :, at : at + SLOT]
-
+    rows = (odd * half, (odd + 1) * half)
+    pairs = [(dx, dy) for dx in range(4) for dy in range(4) if dx == 2 or dy == 2]
     for n in range(BLOCK // SLOT):
-        total = jnp.zeros((half, SLOT), f32)
-        for dx in range(4):
-            left = jnp.concatenate([rows_of(dx, dy) for dy in range(4)], axis=1)
-            right = jnp.concatenate([cols_of(dx, dy, n * SLOT) for dy in range(4)], axis=0)
-            total = total + jnp.dot(left, right, preferred_element_type=f32)
-        total = total.astype(bf16)
-        out[2 * n] = total[:128]
-        out[2 * n + 1] = total[128:256]
-        out[8 + ((n - z0) & 3)] = total[256:384]
-        out[12 + ((n + 1 - z0) & 3)] = total[384:]
+        left, right = operands(refs, pairs, rows, n * SLOT)
+        total = near[rows[0] : rows[1], n * SLOT : (n + 1) * SLOT]
+        total = (total + jnp.dot(left, right, preferred_element_type=f32)).astype(bf16)
+        for out, part in zip(outs, (total[: half // 2], total[half // 2 :])):
+            if odd:
+                out[(n - z0) & 3] = part[:128]
+                out[4 + ((n + 1 - z0) & 3)] = part[128:]
+            else:
+                out[2 * n] = part[:128]
+                out[2 * n + 1] = part[128:]
 
 
 def add_odd(mine, other, up, down):
     for j in range(4):
-        up[j] = (mine[8 + j].astype(f32) + other[8 + j].astype(f32)).astype(bf16)
-        down[j] = (mine[12 + j].astype(f32) + other[12 + j].astype(f32)).astype(bf16)
+        up[j] = (mine[j].astype(f32) + other[j].astype(f32)).astype(bf16)
+        down[j] = (mine[4 + j].astype(f32) + other[4 + j].astype(f32)).astype(bf16)
 
 
 def add_even(mine, other, up, down, *outs):
@@ -171,17 +196,18 @@
     send[...] = jnp.where(core == 0, second, first)
 
 
-def split(a):
+def product(a, b):
+    return jnp.dot(a, b, precision=lax.Precision.HIGHEST, preferred_element_type=f32)
+
+
+def two_terms(a):
     top = a.astype(bf16)
-    rest = a - top.astype(f32)
-    middle = rest.astype(bf16)
-    return top, middle, (rest - middle.astype(f32)).astype(bf16)
-
-
-def dot(a, b):
-    left = jnp.concatenate([a[2], a[0], a[1], a[1], a[0], a[0]], axis=1)
-    right = jnp.concatenate([b[0], b[2], b[1], b[0], b[1], b[0]], axis=0)
-    return jnp.dot(left, right, preferred_element_type=f32)
+    return top, (a - top.astype(f32)).astype(bf16)
+
+
+def short_product(a, b):
+    dot = functools.partial(jnp.dot, preferred_element_type=f32)
+    return (dot(a[1], b[0]) + dot(a[0], b[1])) + dot(a[0], b[0])
 
 
 def newton(meta, mine, other, head_grad, o0, o1, o2, o3, result):
@@ -217,21 +243,15 @@
     by_row = factor(across, line, 0)
     gram = gram * by_row * by_col
     unit = jnp.where(row == col, 1.0, 0.0)
-    product = None
+    factors = None
     for turn in range(NS_ITERS):
-        terms = split(gram)
-        step = quintic_a * unit + quintic_b * gram + quintic_c * dot(terms, terms)
-        by_step = split(step)
-        if turn == 0:
-            gram = dot(split(dot(terms, by_step)), by_step)
-            product = step
-        elif turn < NS_ITERS - 1:
-            both = jnp.concatenate([product, dot(terms, by_step)], axis=0)
-            both = dot(split(both), by_step)
-            product, gram = both[:SLOT], both[SLOT:]
-        else:
-            product = dot(split(product), by_step)
-    top, middle, bottom = split(product)
+        multiplied = product if turn < 2 else lambda p, q: short_product(two_terms(p), two_terms(q))
+        step = quintic_a * unit + quintic_b * gram + quintic_c * multiplied(gram, gram)
+        if turn < NS_ITERS - 1:
+            gram = multiplied(multiplied(gram, step), step)
+        factors = step if factors is None else product(factors, step)
+    top, middle = two_terms(factors)
+    bottom = (factors - top.astype(f32) - middle.astype(f32)).astype(bf16)
     h = head_grad[...]
     update = jnp.dot(h, bottom, preferred_element_type=f32) + jnp.dot(h, middle, preferred_element_type=f32)
     update = update + jnp.dot(h, top, preferred_element_type=f32)
@@ -278,17 +298,19 @@
         prepare,
         [shape((BLOCK, tok), bf16)] * 4 + [shape((tok, BLOCK), bf16)] * 4 + [shape((PERM_AT + HEADS,), jnp.int32)],
         (owners, ratios, masked[None, :], activations, cotangent),
-        16,
+        PREPARE_MIB,
         2 * tok * width,
         "prepare",
-        in_specs=[smem(), smem(), vmem(), anywhere(), anywhere()],
+        in_specs=[anywhere(), anywhere(), vmem(), anywhere(), anywhere()],
         out_specs=[vmem()] * 8 + [smem()],
         scratch=[
             pltpu.VMEM((tok, width), bf16),
             pltpu.VMEM((tok, width), bf16),
             pltpu.SMEM((HEADS,), jnp.int32),
+            pltpu.SMEM((1,), jnp.int32),
             pltpu.SMEM((HEADS,), jnp.int32),
-            pltpu.SemaphoreType.DMA((2,)),
+            pltpu.SMEM((HEADS,), jnp.int32),
+            pltpu.SemaphoreType.DMA((4,)),
         ],
     )
     rows, cols = blocks[:4], blocks[4:]
@@ -301,29 +323,34 @@
     g2a, g2b = move_y(g1[:2], 1), move_y(g3[2:], -1)
     gathered = (r0, r1, r3, r2a, r2b, g0, g1, g3, g2a, g2b)
 
-    def product(offset, name):
-        (out,) = local_kernel(
-            functools.partial(multiply, offset),
-            [shape((16, 128, SLOT), bf16)],
-            gathered,
+    flops = 2 * BLOCK * BLOCK * tok
+    (near,) = local_kernel(
+        multiply_near, [shape((BLOCK, BLOCK), f32)], (r0, r1, r3, g0, g1, g3), 32, 9 * flops, "multiply_near"
+    )
+
+    def rest(odd, name):
+        return local_kernel(
+            functools.partial(multiply_rest, odd),
+            [shape((8, 128, SLOT), bf16)] * 2,
+            (near, *gathered),
             32,
-            BLOCK * BLOCK * 16 * tok,
+            7 * flops // 2,
             name,
         )
-        return out
-
-    send = product(BLOCK // 2, "multiply_other")
-    other = swap(send, "core")
-    keep = product(0, "multiply_own")
+
+    own_odd, odd = rest(1, "multiply_odd")
+    odd = swap(odd, "core")
+    own_even, even = rest(0, "multiply_even")
+    even = swap(even, "core")
     half_chunks = shape((4, 128, SLOT), bf16)
     up, down = local_kernel(
-        add_odd, [half_chunks] * 2, (keep, other), 8, 8 * 128 * SLOT, "add_odd"
+        add_odd, [half_chunks] * 2, (own_odd, odd), 8, 8 * 128 * SLOT, "add_odd"
     )
     up, down = move_z(up, 1), move_z(down, -1)
     t0, t1, t2, t3 = local_kernel(
         add_even,
         [shape((256, SLOT), f32)] + [shape((256, SLOT), bf16)] * 3,
-        (keep, other, up, down),
+        (own_even, even, up, down),
         8,
         16 * 128 * SLOT,
         "add_even",
@@ -341,12 +368,13 @@
     mine = (mine + move_y(mine, 2)) + (move_y(mine, 1) + move_y(mine, 3))
     update = local_kernel(
         newton,
-        [shape((HALF, SLOT), bf16)] * 4 + [shape((256, SLOT), bf16)],
+        [shape((HALF, SLOT), bf16)] * 4,
         (meta, mine, swap(mine, "core"), head_grad),
         16,
         20 * 2 * SLOT**3 * 6,
         "newton",
         in_specs=[smem()] + [vmem()] * 3,
+        scratch=[pltpu.VMEM((256, SLOT), bf16)],
     )
     ring = lambda a, k: lax.ppermute(a, "zh", [(i, (i + k) % 4) for i in range(4)])
     p0 = jnp.stack([update[0]] + [ring(update[k], k) for k in (1, 2, 3)])

time: 162 us -> 155 us (0.957)
  waiting for transfers between devices: 79 us -> 65.5 us
  starting transfers between devices: 57.3 us -> 67 us
  local copies, waits for them, and re-layouts: 3.89 us -> 0.15 us
  other arithmetic: 0.33 us -> 2.23 us
    ppermute x10, waiting for transfers between devices: 36.1 us -> 26.2 us  [move_y(): lax.ppermute(a, ('ylo', 'yhi'), [(Y_INDEX[i], Y_INDEX[(i + k) % 4]) for i...]
    ppermute x13, starting transfers between devices: 13.2 us -> 19.8 us  [move_x(): return lax.ppermute(a, 'x', [(i, (i + k) % 4) for i in range(4)])]
    unnamed x8 -> x2, local copies, waits for them, and re-layouts: 3.75 us -> 0.01 us
    ppermute x5 -> x6, starting transfers between devices: 6.34 us -> 8.69 us  [swap(): return lax.ppermute(a, axis, [(0, 1), (1, 0)])]
    ppermute x5 -> x6, waiting for transfers between devices: 8.16 us -> 6.07 us  [swap(): return lax.ppermute(a, axis, [(0, 1), (1, 0)])]
    another operation x2, other arithmetic: 0.26 us -> 2.17 us  [on_device(): r0, g0 = (jnp.stack(rows), jnp.stack(cols))]
    pallas_call x8 -> x9, Pallas kernels: 19.7 us -> 18.9 us  [local_kernel(): pl.pallas_call(body, out_shape=outs, in_specs=in_specs or [vmem()] * len(...]
  transfers between devices with their start and end apart: 36 -> 37, of which waited for: 22 -> 19; matrix products, arithmetic and copies ran while one was open for 0% -> 1% of each run, Pallas kernels for 1% -> 3%
where the time goes in v4:
time: 155 us
  starting transfers between devices  67 us (43%)
  waiting for transfers between devices  65.5 us (42%)
  Pallas kernels  18.9 us (12%)
  other arithmetic  2.23 us (1%)
    ppermute x10, waiting for transfers between devices, move_y(): lax.ppermute(a, ('ylo', 'yhi'), [(Y_INDEX[i], Y_INDEX[(i + k) % 4]) for i...  26.2 us
    ppermute x13, starting transfers between devices, move_x(): return lax.ppermute(a, 'x', [(i, (i + k) % 4) for i in range(4)])  19.8 us
    pallas_call x9, Pallas kernels, local_kernel(): pl.pallas_call(body, out_shape=outs, in_specs=in_specs or [vmem()] * len(...  18.9 us
    ppermute x10, starting transfers between devices, move_y(): lax.ppermute(a, ('ylo', 'yhi'), [(Y_INDEX[i], Y_INDEX[(i + k) % 4]) for i...  18.3 us
    ppermute x5, waiting for transfers between devices, move_z(): return lax.ppermute(a, ('zh', 'z0'), [(i, (i + k) % 8) for i in range(8)])  16.8 us
    ppermute x13, waiting for transfers between devices, move_x(): return lax.ppermute(a, 'x', [(i, (i + k) % 4) for i in range(4)])  13.2 us
    ppermute x5, starting transfers between devices, move_z(): return lax.ppermute(a, ('zh', 'z0'), [(i, (i + k) % 8) for i in range(8)])  13.1 us
    ppermute x6, starting transfers between devices, swap(): return lax.ppermute(a, axis, [(0, 1), (1, 0)])  8.69 us
  transfers between devices with their start and end apart: 37, of which 19 were waited for; matrix products, arithmetic and copies ran while one was open for 1% of the time, Pallas kernels for 3%

profile of v4, /device:TPU:1, one launch (start us, length us, event | category | flops | bytes accessed | tf_op | source)
XLA Modules:
  0.0 154.7 jit_solution(16973732856420655928)
XLA Ops:
  0.7 4.1 %prepare.1 = (bf16[1024,128]{1,0:T(8,128)(2,1)}, bf16[1024,128]{1,0:T(8,128)(2,1)}, bf16[1024,128]{1,0:T(8,128)(2,1)}, bf16[1024,128]{1,0:T(8,128)(2,1)}, bf16[1...) custom-call(s32[32]{0:T(128)} %owners_far.1, ...), custom_call_target="tpu_custom_call" | custom-call | flops 1048576 | bytes 4195108 | tf_op jit(solution)/shard_map/prepare/pallas_call | solution.py:45
  6.9 2.4 %collective-permute-start.6 = (bf16[128,1024]{1,0:T(8,128)(2,1)}, bf16[128,1024]{1,0:T(8,128)(2,1)S(1)}, u32[]{:S(2)}, u32[]{:S(2)}) collective-permute-start(bf16[128,1024]{1,0:T(8,128)(2,1)} %get-tuple-element.38), channel_id=1, source_target_pairs={{0,128},{64,192},{128,0},{192,64},{1,129},{65,193},{129,1},{193,65... | collective-permute-start | bytes 786440 | tf_op jit(solution)/shard_map/ppermute | solution.py:280
  11.8 2.6 %collective-permute-start.1 = (bf16[1024,128]{1,0:T(8,128)(2,1)}, bf16[1024,128]{1,0:T(8,128)(2,1)S(1)}, u32[]{:S(2)}, u32[]{:S(2)}) collective-permute-start(bf16[1024,128]{1,0:T(8,128)(2,1)} %get-tuple-element.34), channel_id=1, source_target_pairs={{0,16},{32,48},{16,0},{48,32},{1,17},{33,49},{17,1},{49,33},{2,18}... | collective-permute-start | bytes 786440 | tf_op jit(solution)/shard_map/ppermute | solution.py:284
  14.4 2.6 %collective-permute-start.2 = (bf16[1024,128]{1,0:T(8,128)(2,1)}, bf16[1024,128]{1,0:T(8,128)(2,1)S(1)}, u32[]{:S(2)}, u32[]{:S(2)}) collective-permute-start(bf16[1024,128]{1,0:T(8,128)(2,1)} %get-tuple-element.35), channel_id=1, source_target_pairs={{0,48},{32,0},{16,32},{48,16},{1,49},{33,1},{17,33},{49,17},{2,50}... | collective-permute-start | bytes 786440 | tf_op jit(solution)/shard_map/ppermute | solution.py:284
  17.0 3.9 %collective-permute-done.6 = bf16[128,1024]{1,0:T(8,128)(2,1)S(1)} collective-permute-done((bf16[128,1024]{1,0:T(8,128)(2,1)}, bf16[128,1024]{1,0:T(8,128)(2,1)S(1)}, u32[]{:S(2)}, u32[]{:S(2)}) %collective-permute-start.6) | collective-permute-done | bytes 262176 | tf_op jit(solution)/shard_map/ppermute | solution.py:280
  29.1 19.5 %collective-permute-done.8.g1.refs_6_ = bf16[4,128,1024]{2,1,0:T(8,128)(2,1)S(1)} collective-permute-done((bf16[4,128,1024]{2,1,0:T(8,128)(2,1)S(1)}, bf16[4,128,1024]{2,1,0:T(8,128)(2,1)S(1)}, u32[]{:S(2)}, u32[]{:S(2)}) %collective-permute-start.8) | collective-permute-done | bytes 1048608 | tf_op jit(solution)/shard_map/ppermute | solution.py:284
  48.8 2.7 %collective-permute-start.13 = (bf16[2,128,1024]{2,1,0:T(8,128)(2,1)S(1)}, bf16[2,128,1024]{2,1,0:T(8,128)(2,1)S(1)}, u32[]{:S(2)}, u32[]{:S(2)}) collective-permute-start(bf16[2,128,1024]{2,1,0:T(8,128)(2,1)S(1)} %slice.19), channel_id=1, source_target_pairs={{0,48},{32,0},{16,32},{48,16},{1,49},{33,1},{17,33},{49,17},{2,50}... | collective-permute-start | bytes 1572872 | tf_op jit(solution)/shard_map/ppermute | solution.py:284
  51.7 2.9 %collective-permute-start.11 = (bf16[2,1024,128]{2,1,0:T(8,128)(2,1)S(1)}, bf16[2,1024,128]{2,1,0:T(8,128)(2,1)S(1)}, u32[]{:S(2)}, u32[]{:S(2)}) collective-permute-start(bf16[2,1024,128]{2,1,0:T(8,128)(2,1)S(1)} %slice.17), channel_id=1, source_target_pairs={{0,192},{64,0},{128,64},{192,128},{1,193},{65,1},{129,65},{193,129... | collective-permute-start | bytes 1572872 | tf_op jit(solution)/shard_map/ppermute | solution.py:280
  54.6 2.9 %multiply_near.1.near = f32[1024,1024]{1,0:T(8,128)S(1)} custom-call(bf16[4,1024,128]{2,1,0:T(8,128)(2,1)S(1)} %pad_maximum_fusion.r0.refs_0_, bf16[4,1024,128]{2,1,0:T(8,128)(2,1)S(1)} %collective-permute-done.3.r1.refs_1_, bf16[4,1024,128]{2,1,0:T(8,128)(2,1)S(1)} %collective-permute-done.4.r3.refs_2_, ...), custom_call_target="tpu_custom_call" | custom-call | flops 2415919104 | bytes 10485760 | tf_op jit(solution)/shard_map/multiply_near/pallas_call | solution.py:45
  57.5 4.5 %collective-permute-done.12.refs_8_ = bf16[2,128,1024]{2,1,0:T(8,128)(2,1)S(1)} collective-permute-done((bf16[2,128,1024]{2,1,0:T(8,128)(2,1)S(1)}, bf16[2,128,1024]{2,1,0:T(8,128)(2,1)S(1)}, u32[]{:S(2)}, u32[]{:S(2)}) %collective-permute-start.12) | collective-permute-done | bytes 524320 | tf_op jit(solution)/shard_map/ppermute | solution.py:284
  65.6 2.9 %collective-permute-start.15 = (bf16[8,128,256]{2,1,0:T(8,128)(2,1)S(1)}, bf16[8,128,256]{2,1,0:T(8,128)(2,1)S(1)}, u32[]{:S(2)}, u32[]{:S(2)}) collective-permute-start(bf16[8,128,256]{2,1,0:T(8,128)(2,1)S(1)} %get-tuple-element.43), channel_id=1, source_target_pairs={{0,1},{1,0},{2,3},{3,2},{4,5},{5,4},{6,7},{7,6},{8,9},{9,8},{10,11... | collective-permute-start | bytes 1572872 | tf_op jit(solution)/shard_map/ppermute | solution.py:292
  71.9 4.0 %collective-permute-start.17 = (bf16[4,128,256]{2,1,0:T(8,128)(2,1)S(1)}, bf16[4,128,256]{2,1,0:T(8,128)(2,1)S(1)}, u32[]{:S(2)}, u32[]{:S(2)}) collective-permute-start(bf16[4,128,256]{2,1,0:T(8,128)(2,1)S(1)} %get-tuple-element.45), channel_id=1, source_target_pairs={{0,14},{2,0},{4,2},{6,4},{8,6},{10,8},{12,10},{14,12},{1,15},{3,1}... | collective-permute-start | bytes 786440 | tf_op jit(solution)/shard_map/ppermute | solution.py:288
  75.9 6.3 %collective-permute-done.16.up = bf16[4,128,256]{2,1,0:T(8,128)(2,1)S(1)} collective-permute-done((bf16[4,128,256]{2,1,0:T(8,128)(2,1)S(1)}, bf16[4,128,256]{2,1,0:T(8,128)(2,1)S(1)}, u32[]{:S(2)}, u32[]{:S(2)}) %collective-permute-start.16) | collective-permute-done | bytes 262176 | tf_op jit(solution)/shard_map/ppermute | solution.py:288
  84.1 2.5 %collective-permute-start.19 = (bf16[256,256]{1,0:T(8,128)(2,1)S(1)}, bf16[256,256]{1,0:T(8,128)(2,1)S(1)}, u32[]{:S(2)}, u32[]{:S(2)}) collective-permute-start(bf16[256,256]{1,0:T(8,128)(2,1)S(1)} %get-tuple-element.48), channel_id=1, source_target_pairs={{0,8},{2,10},{4,12},{6,14},{8,0},{10,2},{12,4},{14,6},{1,9},{3,11}... | collective-permute-start | bytes 393224 | tf_op jit(solution)/shard_map/ppermute | solution.py:288
  86.6 3.2 %collective-permute-start.20 = (bf16[256,256]{1,0:T(8,128)(2,1)S(1)}, bf16[256,256]{1,0:T(8,128)(2,1)S(1)}, u32[]{:S(2)}, u32[]{:S(2)}) collective-permute-start(bf16[256,256]{1,0:T(8,128)(2,1)S(1)} %get-tuple-element.49), channel_id=1, source_target_pairs={{0,12},{2,14},{4,0},{6,2},{8,4},{10,6},{12,8},{14,10},{1,13},{3,15... | collective-permute-start | bytes 393224 | tf_op jit(solution)/shard_map/ppermute | solution.py:288
  89.8 5.8 %collective-permute-done.19.t2 = bf16[256,256]{1,0:T(8,128)(2,1)S(1)} collective-permute-done((bf16[256,256]{1,0:T(8,128)(2,1)S(1)}, bf16[256,256]{1,0:T(8,128)(2,1)S(1)}, u32[]{:S(2)}, u32[]{:S(2)}) %collective-permute-start.19) | collective-permute-done | bytes 131104 | tf_op jit(solution)/shard_map/ppermute | solution.py:288
  95.6 4.7 %collective-permute-done.20.t3 = bf16[256,256]{1,0:T(8,128)(2,1)S(1)} collective-permute-done((bf16[256,256]{1,0:T(8,128)(2,1)S(1)}, bf16[256,256]{1,0:T(8,128)(2,1)S(1)}, u32[]{:S(2)}, u32[]{:S(2)}) %collective-permute-start.20) | collective-permute-done | bytes 131104 | tf_op jit(solution)/shard_map/ppermute | solution.py:288
  102.3 4.0 %collective-permute-done.22 = f32[192,128]{1,0:T(8,128)S(1)} collective-permute-done((f32[192,128]{1,0:T(8,128)S(1)}, f32[192,128]{1,0:T(8,128)S(1)}, u32[]{:S(2)}, u32[]{:S(2)}) %collective-permute-start.22) | collective-permute-done | bytes 98336 | tf_op jit(solution)/shard_map/ppermute | solution.py:292
  114.5 2.6 %collective-permute-start.26 = (f32[192,128]{1,0:T(8,128)S(1)}, f32[192,128]{1,0:T(8,128)S(1)}, u32[]{:S(2)}, u32[]{:S(2)}) collective-permute-start(f32[192,128]{1,0:T(8,128)S(1)} %add_add_fusion.mine), channel_id=1, source_target_pairs={{0,1},{1,0},{2,3},{3,2},{4,5},{5,4},{6,7},{7,6},{8,9},{9,8},{10,11... | collective-permute-start | bytes 294920 | tf_op jit(solution)/shard_map/ppermute | solution.py:292
  118.1 6.8 %newton.1 = (bf16[64,256]{1,0:T(8,128)(2,1)S(1)}, bf16[64,256]{1,0:T(8,128)(2,1)S(1)}, bf16[64,256]{1,0:T(8,128)(2,1)S(1)}, bf16[64,256]{1,0:T(8,128)(2,1)S(1)}) custom-call(s32[40]{0:T(128)S(1)} %copy-done, f32[192,128]{1,0:T(8,128)S(1)} %add_add_fusion.mine, f32[192,128]{1,0:T(8,128)S(1)} %collective-permute-done.26.other, ...), custom_call_target="tpu_custom_call" | custom-call | flops 4026531840 | bytes 458912 | tf_op jit(solution)/shard_map/newton/pallas_call | solution.py:45
  124.9 3.6 %collective-permute-start.27 = (bf16[64,256]{1,0:T(8,128)(2,1)S(1)}, bf16[64,256]{1,0:T(8,128)(2,1)S(1)}, u32[]{:S(2)}, u32[]{:S(2)}) collective-permute-start(bf16[64,256]{1,0:T(8,128)(2,1)S(1)} %get-tuple-element.54), channel_id=1, source_target_pairs={{0,4},{4,8},{8,12},{12,0},{1,5},{5,9},{9,13},{13,1},{2,6},{6,10},{... | collective-permute-start | bytes 98312 | tf_op jit(solution)/shard_map/ppermute | solution.py:379
  132.1 3.2 %collective-permute-done.28 = bf16[64,256]{1,0:T(8,128)(2,1)S(1)} collective-permute-done((bf16[64,256]{1,0:T(8,128)(2,1)S(1)}, bf16[64,256]{1,0:T(8,128)(2,1)S(1)}, u32[]{:S(2)}, u32[]{:S(2)}) %collective-permute-start.28) | collective-permute-done | bytes 32800 | tf_op jit(solution)/shard_map/ppermute | solution.py:379
  137.5 4.2 %collective-permute-start.31 = (bf16[4,64,256]{2,1,0:T(8,128)(2,1)S(1)}, bf16[4,64,256]{2,1,0:T(8,128)(2,1)S(1)}, u32[]{:S(2)}, u32[]{:S(2)}) collective-permute-start(bf16[4,64,256]{2,1,0:T(8,128)(2,1)S(1)} %pad_maximum_fusion.2.p0), channel_id=1, source_target_pairs={{0,128},{64,192},{128,0},{192,64},{1,129},{65,193},{129,1},{193,65... | collective-permute-start | bytes 393224 | tf_op jit(solution)/shard_map/ppermute | solution.py:280
  147.8 3.7 %collective-permute-done.35.q2 = bf16[4,64,256]{2,1,0:T(8,128)(2,1)S(1)} collective-permute-done((bf16[4,64,256]{2,1,0:T(8,128)(2,1)S(1)}, bf16[4,64,256]{2,1,0:T(8,128)(2,1)S(1)}, u32[]{:S(2)}, u32[]{:S(2)}) %collective-permute-start.35) | collective-permute-done | bytes 131104 | tf_op jit(solution)/shard_map/ppermute | solution.py:280
  (71 shorter events, 48.3 us)
Async XLA Ops:
  4.7 9.6 %collective-permute-start.5 = (bf16[128,1024]{1,0:T(8,128)(2,1)}, bf16[128,1024]{1,0:T(8,128)(2,1)S(1)}, u32[]{:S(2)}, u32[]{:S(2)}) collective-permute-start(bf16[128,1024]{1,0:T(8,128)(2,1)} %get-tuple-element.37), channel_id=1, source_target_pairs={{0,64},{64,128},{128,192},{192,0},{1,65},{65,129},{129,193},{193,1... | collective-permute-start | bytes 786440 | tf_op jit(solution)/shard_map/ppermute | solution.py:280
  6.9 14.0 %collective-permute-start.6 = (bf16[128,1024]{1,0:T(8,128)(2,1)}, bf16[128,1024]{1,0:T(8,128)(2,1)S(1)}, u32[]{:S(2)}, u32[]{:S(2)}) collective-permute-start(bf16[128,1024]{1,0:T(8,128)(2,1)} %get-tuple-element.38), channel_id=1, source_target_pairs={{0,128},{64,192},{128,0},{192,64},{1,129},{65,193},{129,1},{193,65... | collective-permute-start | bytes 786440 | tf_op jit(solution)/shard_map/ppermute | solution.py:280
  9.3 11.5 %collective-permute-start.7 = (bf16[128,1024]{1,0:T(8,128)(2,1)}, bf16[128,1024]{1,0:T(8,128)(2,1)S(1)}, u32[]{:S(2)}, u32[]{:S(2)}) collective-permute-start(bf16[128,1024]{1,0:T(8,128)(2,1)} %get-tuple-element.39), channel_id=1, source_target_pairs={{0,192},{64,0},{128,64},{192,128},{1,193},{65,1},{129,65},{193,129... | collective-permute-start | bytes 786440 | tf_op jit(solution)/shard_map/ppermute | solution.py:280
  10.5 14.4 %collective-permute-start = (bf16[1024,128]{1,0:T(8,128)(2,1)}, bf16[1024,128]{1,0:T(8,128)(2,1)S(1)}, u32[]{:S(2)}, u32[]{:S(2)}) collective-permute-start(bf16[1024,128]{1,0:T(8,128)(2,1)} %get-tuple-element.33), channel_id=1, source_target_pairs={{0,32},{32,16},{16,48},{48,0},{1,33},{33,17},{17,49},{49,1},{2,34}... | collective-permute-start | bytes 786440 | tf_op jit(solution)/shard_map/ppermute | solution.py:284
  11.8 13.3 %collective-permute-start.1 = (bf16[1024,128]{1,0:T(8,128)(2,1)}, bf16[1024,128]{1,0:T(8,128)(2,1)S(1)}, u32[]{:S(2)}, u32[]{:S(2)}) collective-permute-start(bf16[1024,128]{1,0:T(8,128)(2,1)} %get-tuple-element.34), channel_id=1, source_target_pairs={{0,16},{32,48},{16,0},{48,32},{1,17},{33,49},{17,1},{49,33},{2,18}... | collective-permute-start | bytes 786440 | tf_op jit(solution)/shard_map/ppermute | solution.py:284
  14.4 10.6 %collective-permute-start.2 = (bf16[1024,128]{1,0:T(8,128)(2,1)}, bf16[1024,128]{1,0:T(8,128)(2,1)S(1)}, u32[]{:S(2)}, u32[]{:S(2)}) collective-permute-start(bf16[1024,128]{1,0:T(8,128)(2,1)} %get-tuple-element.35), channel_id=1, source_target_pairs={{0,48},{32,0},{16,32},{48,16},{1,49},{33,1},{17,33},{49,17},{2,50}... | collective-permute-start | bytes 786440 | tf_op jit(solution)/shard_map/ppermute | solution.py:284
  21.9 26.7 %collective-permute-start.8 = (bf16[4,128,1024]{2,1,0:T(8,128)(2,1)S(1)}, bf16[4,128,1024]{2,1,0:T(8,128)(2,1)S(1)}, u32[]{:S(2)}, u32[]{:S(2)}) collective-permute-start(bf16[4,128,1024]{2,1,0:T(8,128)(2,1)S(1)} %pad_maximum_fusion.1.g0.refs_5_), channel_id=1, source_target_pairs={{0,32},{32,16},{16,48},{48,0},{1,33},{33,17},{17,49},{49,1},{2,34}... | collective-permute-start | bytes 3145736 | tf_op jit(solution)/shard_map/ppermute | solution.py:284
  23.3 25.4 %collective-permute-start.9 = (bf16[4,128,1024]{2,1,0:T(8,128)(2,1)S(1)}, bf16[4,128,1024]{2,1,0:T(8,128)(2,1)S(1)}, u32[]{:S(2)}, u32[]{:S(2)}) collective-permute-start(bf16[4,128,1024]{2,1,0:T(8,128)(2,1)S(1)} %pad_maximum_fusion.1.g0.refs_5_), channel_id=1, source_target_pairs={{0,48},{32,0},{16,32},{48,16},{1,49},{33,1},{17,33},{49,17},{2,50}... | collective-permute-start | bytes 3145736 | tf_op jit(solution)/shard_map/ppermute | solution.py:284
  26.1 25.4 %collective-permute-start.3 = (bf16[4,1024,128]{2,1,0:T(8,128)(2,1)S(1)}, bf16[4,1024,128]{2,1,0:T(8,128)(2,1)S(1)}, u32[]{:S(2)}, u32[]{:S(2)}) collective-permute-start(bf16[4,1024,128]{2,1,0:T(8,128)(2,1)S(1)} %pad_maximum_fusion.r0.refs_0_), channel_id=1, source_target_pairs={{0,64},{64,128},{128,192},{192,0},{1,65},{65,129},{129,193},{193,1... | collective-permute-start | bytes 3145736 | tf_op jit(solution)/shard_map/ppermute | solution.py:280
  27.4 24.3 %collective-permute-start.4 = (bf16[4,1024,128]{2,1,0:T(8,128)(2,1)S(1)}, bf16[4,1024,128]{2,1,0:T(8,128)(2,1)S(1)}, u32[]{:S(2)}, u32[]{:S(2)}) collective-permute-start(bf16[4,1024,128]{2,1,0:T(8,128)(2,1)S(1)} %pad_maximum_fusion.r0.refs_0_), channel_id=1, source_target_pairs={{0,192},{64,0},{128,64},{192,128},{1,193},{65,1},{129,65},{193,129... | collective-permute-start | bytes 3145736 | tf_op jit(solution)/shard_map/ppermute | solution.py:280
  48.6 13.4 %collective-permute-start.12 = (bf16[2,128,1024]{2,1,0:T(8,128)(2,1)S(1)}, bf16[2,128,1024]{2,1,0:T(8,128)(2,1)S(1)}, u32[]{:S(2)}, u32[]{:S(2)}) collective-permute-start(bf16[2,128,1024]{2,1,0:T(8,128)(2,1)S(1)} %slice.18), channel_id=1, source_target_pairs={{0,32},{32,16},{16,48},{48,0},{1,33},{33,17},{17,49},{49,1},{2,34}... | collective-permute-start | bytes 1572872 | tf_op jit(solution)/shard_map/ppermute | solution.py:284
  48.8 13.2 %collective-permute-start.13 = (bf16[2,128,1024]{2,1,0:T(8,128)(2,1)S(1)}, bf16[2,128,1024]{2,1,0:T(8,128)(2,1)S(1)}, u32[]{:S(2)}, u32[]{:S(2)}) collective-permute-start(bf16[2,128,1024]{2,1,0:T(8,128)(2,1)S(1)} %slice.19), channel_id=1, source_target_pairs={{0,48},{32,0},{16,32},{48,16},{1,49},{33,1},{17,33},{49,17},{2,50}... | collective-permute-start | bytes 1572872 | tf_op jit(solution)/shard_map/ppermute | solution.py:284
  51.6 12.8 %collective-permute-start.10 = (bf16[2,1024,128]{2,1,0:T(8,128)(2,1)S(1)}, bf16[2,1024,128]{2,1,0:T(8,128)(2,1)S(1)}, u32[]{:S(2)}, u32[]{:S(2)}) collective-permute-start(bf16[2,1024,128]{2,1,0:T(8,128)(2,1)S(1)} %slice.16), channel_id=1, source_target_pairs={{0,64},{64,128},{128,192},{192,0},{1,65},{65,129},{129,193},{193,1... | collective-permute-start | bytes 1572872 | tf_op jit(solution)/shard_map/ppermute | solution.py:280
  51.7 12.7 %collective-permute-start.11 = (bf16[2,1024,128]{2,1,0:T(8,128)(2,1)S(1)}, bf16[2,1024,128]{2,1,0:T(8,128)(2,1)S(1)}, u32[]{:S(2)}, u32[]{:S(2)}) collective-permute-start(bf16[2,1024,128]{2,1,0:T(8,128)(2,1)S(1)} %slice.17), channel_id=1, source_target_pairs={{0,192},{64,0},{128,64},{192,128},{1,193},{65,1},{129,65},{193,129... | collective-permute-start | bytes 1572872 | tf_op jit(solution)/shard_map/ppermute | solution.py:280
  70.2 12.0 %collective-permute-start.16 = (bf16[4,128,256]{2,1,0:T(8,128)(2,1)S(1)}, bf16[4,128,256]{2,1,0:T(8,128)(2,1)S(1)}, u32[]{:S(2)}, u32[]{:S(2)}) collective-permute-start(bf16[4,128,256]{2,1,0:T(8,128)(2,1)S(1)} %get-tuple-element.44), channel_id=1, source_target_pairs={{0,2},{2,4},{4,6},{6,8},{8,10},{10,12},{12,14},{14,0},{1,3},{3,5},... | collective-permute-start | bytes 786440 | tf_op jit(solution)/shard_map/ppermute | solution.py:288
  71.9 10.3 %collective-permute-start.17 = (bf16[4,128,256]{2,1,0:T(8,128)(2,1)S(1)}, bf16[4,128,256]{2,1,0:T(8,128)(2,1)S(1)}, u32[]{:S(2)}, u32[]{:S(2)}) collective-permute-start(bf16[4,128,256]{2,1,0:T(8,128)(2,1)S(1)} %get-tuple-element.45), channel_id=1, source_target_pairs={{0,14},{2,0},{4,2},{6,4},{8,6},{10,8},{12,10},{14,12},{1,15},{3,1}... | collective-permute-start | bytes 786440 | tf_op jit(solution)/shard_map/ppermute | solution.py:288
  82.4 7.4 %collective-permute-start.18 = (bf16[256,256]{1,0:T(8,128)(2,1)S(1)}, bf16[256,256]{1,0:T(8,128)(2,1)S(1)}, u32[]{:S(2)}, u32[]{:S(2)}) collective-permute-start(bf16[256,256]{1,0:T(8,128)(2,1)S(1)} %get-tuple-element.47), channel_id=1, source_target_pairs={{0,4},{2,6},{4,8},{6,10},{8,12},{10,14},{12,0},{14,2},{1,5},{3,7},... | collective-permute-start | bytes 393224 | tf_op jit(solution)/shard_map/ppermute | solution.py:288
  84.1 11.5 %collective-permute-start.19 = (bf16[256,256]{1,0:T(8,128)(2,1)S(1)}, bf16[256,256]{1,0:T(8,128)(2,1)S(1)}, u32[]{:S(2)}, u32[]{:S(2)}) collective-permute-start(bf16[256,256]{1,0:T(8,128)(2,1)S(1)} %get-tuple-element.48), channel_id=1, source_target_pairs={{0,8},{2,10},{4,12},{6,14},{8,0},{10,2},{12,4},{14,6},{1,9},{3,11}... | collective-permute-start | bytes 393224 | tf_op jit(solution)/shard_map/ppermute | solution.py:288
  86.6 13.7 %collective-permute-start.20 = (bf16[256,256]{1,0:T(8,128)(2,1)S(1)}, bf16[256,256]{1,0:T(8,128)(2,1)S(1)}, u32[]{:S(2)}, u32[]{:S(2)}) collective-permute-start(bf16[256,256]{1,0:T(8,128)(2,1)S(1)} %get-tuple-element.49), channel_id=1, source_target_pairs={{0,12},{2,14},{4,0},{6,2},{8,4},{10,6},{12,8},{14,10},{1,13},{3,15... | collective-permute-start | bytes 393224 | tf_op jit(solution)/shard_map/ppermute | solution.py:288
  124.9 7.2 %collective-permute-start.27 = (bf16[64,256]{1,0:T(8,128)(2,1)S(1)}, bf16[64,256]{1,0:T(8,128)(2,1)S(1)}, u32[]{:S(2)}, u32[]{:S(2)}) collective-permute-start(bf16[64,256]{1,0:T(8,128)(2,1)S(1)} %get-tuple-element.54), channel_id=1, source_target_pairs={{0,4},{4,8},{8,12},{12,0},{1,5},{5,9},{9,13},{13,1},{2,6},{6,10},{... | collective-permute-start | bytes 98312 | tf_op jit(solution)/shard_map/ppermute | solution.py:379
  128.5 6.8 %collective-permute-start.28 = (bf16[64,256]{1,0:T(8,128)(2,1)S(1)}, bf16[64,256]{1,0:T(8,128)(2,1)S(1)}, u32[]{:S(2)}, u32[]{:S(2)}) collective-permute-start(bf16[64,256]{1,0:T(8,128)(2,1)S(1)} %get-tuple-element.55), channel_id=1, source_target_pairs={{0,8},{4,12},{8,0},{12,4},{1,9},{5,13},{9,1},{13,5},{2,10},{6,14},... | collective-permute-start | bytes 98312 | tf_op jit(solution)/shard_map/ppermute | solution.py:379
  137.5 8.3 %collective-permute-start.31 = (bf16[4,64,256]{2,1,0:T(8,128)(2,1)S(1)}, bf16[4,64,256]{2,1,0:T(8,128)(2,1)S(1)}, u32[]{:S(2)}, u32[]{:S(2)}) collective-permute-start(bf16[4,64,256]{2,1,0:T(8,128)(2,1)S(1)} %pad_maximum_fusion.2.p0), channel_id=1, source_target_pairs={{0,128},{64,192},{128,0},{192,64},{1,129},{65,193},{129,1},{193,65... | collective-permute-start | bytes 393224 | tf_op jit(solution)/shard_map/ppermute | solution.py:280
  143.2 8.3 %collective-permute-start.35 = (bf16[4,64,256]{2,1,0:T(8,128)(2,1)S(1)}, bf16[4,64,256]{2,1,0:T(8,128)(2,1)S(1)}, u32[]{:S(2)}, u32[]{:S(2)}) collective-permute-start(bf16[4,64,256]{2,1,0:T(8,128)(2,1)S(1)} %collective-permute-done.33.q0), channel_id=1, source_target_pairs={{0,128},{64,192},{128,0},{192,64},{1,129},{65,193},{129,1},{193,65... | collective-permute-start | bytes 393224 | tf_op jit(solution)/shard_map/ppermute | solution.py:280
  144.1 8.5 %collective-permute-start.36 = (bf16[4,64,256]{2,1,0:T(8,128)(2,1)S(1)}, bf16[4,64,256]{2,1,0:T(8,128)(2,1)S(1)}, u32[]{:S(2)}, u32[]{:S(2)}) collective-permute-start(bf16[4,64,256]{2,1,0:T(8,128)(2,1)S(1)} %collective-permute-done.33.q0), channel_id=1, source_target_pairs={{0,192},{64,0},{128,64},{192,128},{1,193},{65,1},{129,65},{193,129... | collective-permute-start | bytes 393224 | tf_op jit(solution)/shard_map/ppermute | solution.py:280
  (14 other events, 113.9 us)

commit v5 on v4

--- a/solution.py
+++ b/solution.py
@@ -23,8 +23,6 @@
 HALF = 64
 GRAM = HEAD + HALF
 
-PREPARE_MIB = 56
-
 f32, bf16 = jnp.float32, jnp.bfloat16
 
 
@@ -36,8 +34,8 @@
     return pl.BlockSpec(memory_space=pltpu.VMEM)
 
 
-def anywhere():
-    return pl.BlockSpec(memory_space=pl.ANY)
+def hbm():
+    return pl.BlockSpec(memory_space=pltpu.HBM)
 
 
 def local_kernel(body, outs, operands, mib, flops, name, in_specs=None, out_specs=None, scratch=()):
@@ -261,16 +259,21 @@
         out[...] = result[pl.ds(at, HALF), :]
 
 
-def place_heads(meta, p0, p1, p2, p3, q0, q1, q2, q3, out):
+def place_heads(meta, p0, p1, p2, p3, q0, q1, q2, q3, out, rows, sems):
     ylo, x, zh = lax.axis_index("ylo"), lax.axis_index("x"), lax.axis_index("zh")
-    for dx in range(4):
-        for dzh in range(4):
-            slot = ((x - dx) & 3) * 4 + ((zh - dzh) & 3)
-            for j in range(2):
-                at = pl.multiple_of(meta[PERM_AT + slot * 2 + j] * HEAD, HEAD)
-                for low, ref in ((ylo, (p0, p1, p2, p3)[dx]), (1 - ylo, (q0, q1, q2, q3)[dx])):
-                    rows = pl.ds(pl.multiple_of(low * HALF, HALF), HALF)
-                    out[rows, pl.ds(at, HEAD)] = ref[dzh, :, j * HEAD : (j + 1) * HEAD].astype(f32)
+    copies = []
+    for i, refs in enumerate(((p0, p1, p2, p3), (q0, q1, q2, q3))):
+        for dx in range(4):
+            for dzh in range(4):
+                slot = ((x - dx) & 3) * 4 + ((zh - dzh) & 3)
+                for j in range(2):
+                    at = pl.multiple_of(meta[PERM_AT + slot * 2 + j] * HEAD, HEAD)
+                    rows[i, :, pl.ds(at, HEAD)] = refs[dx][dzh, :, j * HEAD : (j + 1) * HEAD].astype(f32)
+        half = pl.ds(pl.multiple_of((ylo ^ i) * HALF, HALF), HALF)
+        copies.append(pltpu.make_async_copy(rows.at[i], out.at[half, :], sems.at[i]))
+        copies[i].start()
+    for copy in copies:
+        copy.wait()
 
 
 Y_INDEX = (0, 2, 1, 3)
@@ -290,6 +293,11 @@
 
 def swap(a, axis):
     return lax.ppermute(a, axis, [(0, 1), (1, 0)])
+
+
+def farthest_first(arrays, move):
+    opposite = move(arrays[2], 2)
+    return [arrays[0], move(arrays[1], 1), opposite, move(arrays[3], 3)]
 
 
 def on_device(activations, cotangent, masked, ratios, owners):
@@ -298,10 +306,10 @@
         prepare,
         [shape((BLOCK, tok), bf16)] * 4 + [shape((tok, BLOCK), bf16)] * 4 + [shape((PERM_AT + HEADS,), jnp.int32)],
         (owners, ratios, masked[None, :], activations, cotangent),
-        PREPARE_MIB,
+        16,
         2 * tok * width,
         "prepare",
-        in_specs=[anywhere(), anywhere(), vmem(), anywhere(), anywhere()],
+        in_specs=[hbm(), hbm(), vmem(), hbm(), hbm()],
         out_specs=[vmem()] * 8 + [smem()],
         scratch=[
             pltpu.VMEM((tok, width), bf16),
@@ -314,9 +322,8 @@
         ],
     )
     rows, cols = blocks[:4], blocks[4:]
-    rows = [rows[0]] + [move_y(rows[k], k) for k in (1, 2, 3)]
-    cols = [cols[0]] + [move_x(cols[k], k) for k in (1, 2, 3)]
-    r0, g0 = jnp.stack(rows), jnp.stack(cols)
+    r0, g0 = farthest_first(rows, move_y), farthest_first(cols, move_x)
+    r0, g0 = jnp.stack(r0), jnp.stack(g0)
     r1, r3 = move_x(r0, 1), move_x(r0, -1)
     g1, g3 = move_y(g0, 1), move_y(g0, -1)
     r2a, r2b = move_x(r1[:2], 1), move_x(r3[2:], -1)
@@ -355,10 +362,12 @@
         16 * 128 * SLOT,
         "add_even",
     )
+    t2 = move_z(t2, 4)
+    t1, t3 = move_z(t1, 2), move_z(t3, 6)
     head_grad, mine, theirs = local_kernel(
         gram_part,
         [shape((256, SLOT), bf16), shape((GRAM, HEAD), f32), shape((GRAM, HEAD), f32)],
-        (t0, move_z(t1, 2), move_z(t2, 4), move_z(t3, 6)),
+        (t0, t1, t2, t3),
         8,
         2 * 256 * SLOT * SLOT,
         "gram_part",
@@ -377,10 +386,9 @@
         scratch=[pltpu.VMEM((256, SLOT), bf16)],
     )
     ring = lambda a, k: lax.ppermute(a, "zh", [(i, (i + k) % 4) for i in range(4)])
-    p0 = jnp.stack([update[0]] + [ring(update[k], k) for k in (1, 2, 3)])
+    p0 = jnp.stack(farthest_first(update, ring))
     q0 = swap(p0, "ylo")
-    ps = [p0] + [move_x(p0, k) for k in (1, 2, 3)]
-    qs = [q0] + [move_x(q0, k) for k in (1, 2, 3)]
+    ps, qs = farthest_first([p0] * 4, move_x), farthest_first([q0] * 4, move_x)
     (out,) = local_kernel(
         place_heads,
         [shape((2 * HALF, width), f32)],
@@ -389,6 +397,8 @@
         0,
         "place_heads",
         in_specs=[smem()] + [vmem()] * 8,
+        out_specs=[hbm()],
+        scratch=[pltpu.VMEM((2, HALF, width), f32), pltpu.SemaphoreType.DMA((2,))],
     )
     return out
 

time: 155 us -> 156 us (level)
  waiting for transfers between devices: 65.5 us -> 70.5 us
  starting transfers between devices: 67 us -> 62.9 us
  local copies, waits for them, and re-layouts: 0.15 us -> 3.89 us
  other arithmetic: 2.23 us -> 0.33 us
  Pallas kernels: 18.9 us -> 17.1 us
    ppermute x10, waiting for transfers between devices: 26.2 us -> 31.2 us  [move_y(): lax.ppermute(a, ('ylo', 'yhi'), [(Y_INDEX[i], Y_INDEX[(i + k) % 4]) for i...]
    unnamed x2 -> x8, local copies, waits for them, and re-layouts: 0.01 us -> 3.75 us
    ppermute x6, starting transfers between devices: 8.69 us -> 6.41 us  [swap(): return lax.ppermute(a, axis, [(0, 1), (1, 0)])]
    another operation x3, other arithmetic: 2.18 us -> 0.28 us  [the longest x2 0.26 us: on_device(): r0, g0 = (jnp.stack(r0), jnp.stack(g0))]
    pallas_call x9, Pallas kernels: 18.9 us -> 17.1 us  [local_kernel(): pl.pallas_call(body, out_shape=outs, in_specs=in_specs or [vmem()] * len(...]
    ppermute x10, starting transfers between devices: 18.3 us -> 16.6 us  [move_y(): lax.ppermute(a, ('ylo', 'yhi'), [(Y_INDEX[i], Y_INDEX[(i + k) % 4]) for i...]
  transfers between devices with their start and end apart: 37 -> 37, of which waited for: 19 -> 20; matrix products, arithmetic and copies ran while one was open for 1% -> 0% of each run, Pallas kernels for 3% -> 3%
where the time goes in v5:
time: 156 us
  waiting for transfers between devices  70.5 us (45%)
  starting transfers between devices  62.9 us (40%)
  Pallas kernels  17.1 us (11%)
  local copies, waits for them, and re-layouts  3.89 us (2%)
    ppermute x10, waiting for transfers between devices, move_y(): lax.ppermute(a, ('ylo', 'yhi'), [(Y_INDEX[i], Y_INDEX[(i + k) % 4]) for i...  31.2 us
    ppermute x13, starting transfers between devices, move_x(): return lax.ppermute(a, 'x', [(i, (i + k) % 4) for i in range(4)])  19.5 us
    pallas_call x9, Pallas kernels, local_kernel(): pl.pallas_call(body, out_shape=outs, in_specs=in_specs or [vmem()] * len(...  17.1 us
    ppermute x5, waiting for transfers between devices, move_z(): return lax.ppermute(a, ('zh', 'z0'), [(i, (i + k) % 8) for i in range(8)])  16.8 us
    ppermute x10, starting transfers between devices, move_y(): lax.ppermute(a, ('ylo', 'yhi'), [(Y_INDEX[i], Y_INDEX[(i + k) % 4]) for i...  16.6 us
    ppermute x13, waiting for transfers between devices, move_x(): return lax.ppermute(a, 'x', [(i, (i + k) % 4) for i in range(4)])  13.2 us
    ppermute x5, starting transfers between devices, move_z(): return lax.ppermute(a, ('zh', 'z0'), [(i, (i + k) % 8) for i in range(8)])  13.1 us
    ppermute x3, starting transfers between devices, on_device(): lax.ppermute(a, 'zh', [(i, (i + k) % 4) for i in range(4)])  7.22 us
  transfers between devices with their start and end apart: 37, of which 20 were waited for; matrix products, arithmetic and copies ran while one was open for 0% of the time, Pallas kernels for 3%

profile of v5, /device:TPU:1, one launch (start us, length us, event | category | flops | bytes accessed | tf_op | source)
XLA Modules:
  0.0 155.7 jit_solution(15158312244929538761)
XLA Ops:
  4.4 2.4 %prepare.1 = (bf16[1024,128]{1,0:T(8,128)(2,1)S(1)}, bf16[1024,128]{1,0:T(8,128)(2,1)S(1)}, bf16[1024,128]{1,0:T(8,128)(2,1)S(1)}, bf16[1024,128]{1,0:T(8,128)(2...) custom-call(s32[32]{0:T(128)S(1)} %copy-done.2, ...), custom_call_target="tpu_custom_call" | custom-call | flops 1048576 | bytes 4195108 | tf_op jit(solution)/shard_map/prepare/pallas_call | solution.py:43
  9.0 2.4 %collective-permute-start.6 = (bf16[128,1024]{1,0:T(8,128)(2,1)S(1)}, bf16[128,1024]{1,0:T(8,128)(2,1)S(1)}, u32[]{:S(2)}, u32[]{:S(2)}) collective-permute-start(bf16[128,1024]{1,0:T(8,128)(2,1)S(1)} %get-tuple-element.38), channel_id=1, source_target_pairs={{0,128},{64,192},{128,0},{192,64},{1,129},{65,193},{129,1},{193,65... | collective-permute-start | bytes 786440 | tf_op jit(solution)/shard_map/ppermute | solution.py:283
  13.9 2.6 %collective-permute-start.1 = (bf16[1024,128]{1,0:T(8,128)(2,1)S(1)}, bf16[1024,128]{1,0:T(8,128)(2,1)S(1)}, u32[]{:S(2)}, u32[]{:S(2)}) collective-permute-start(bf16[1024,128]{1,0:T(8,128)(2,1)S(1)} %get-tuple-element.34), channel_id=1, source_target_pairs={{0,16},{32,48},{16,0},{48,32},{1,17},{33,49},{17,1},{49,33},{2,18}... | collective-permute-start | bytes 786440 | tf_op jit(solution)/shard_map/ppermute | solution.py:287
  16.5 2.4 %collective-permute-start.2 = (bf16[1024,128]{1,0:T(8,128)(2,1)S(1)}, bf16[1024,128]{1,0:T(8,128)(2,1)S(1)}, u32[]{:S(2)}, u32[]{:S(2)}) collective-permute-start(bf16[1024,128]{1,0:T(8,128)(2,1)S(1)} %get-tuple-element.35), channel_id=1, source_target_pairs={{0,48},{32,0},{16,32},{48,16},{1,49},{33,1},{17,33},{49,17},{2,50}... | collective-permute-start | bytes 786440 | tf_op jit(solution)/shard_map/ppermute | solution.py:287
  18.9 3.9 %collective-permute-done.6 = bf16[128,1024]{1,0:T(8,128)(2,1)S(1)} collective-permute-done((bf16[128,1024]{1,0:T(8,128)(2,1)S(1)}, bf16[128,1024]{1,0:T(8,128)(2,1)S(1)}, u32[]{:S(2)}, u32[]{:S(2)}) %collective-permute-start.6) | collective-permute-done | bytes 262176 | tf_op jit(solution)/shard_map/ppermute | solution.py:283
  29.8 21.2 %collective-permute-done.8.g1.refs_6_ = bf16[4,128,1024]{2,1,0:T(8,128)(2,1)S(1)} collective-permute-done((bf16[4,128,1024]{2,1,0:T(8,128)(2,1)S(1)}, bf16[4,128,1024]{2,1,0:T(8,128)(2,1)S(1)}, u32[]{:S(2)}, u32[]{:S(2)}) %collective-permute-start.8) | collective-permute-done | bytes 1048608 | tf_op jit(solution)/shard_map/ppermute | solution.py:287
  51.2 2.7 %collective-permute-start.13 = (bf16[2,128,1024]{2,1,0:T(8,128)(2,1)S(1)}, bf16[2,128,1024]{2,1,0:T(8,128)(2,1)S(1)}, u32[]{:S(2)}, u32[]{:S(2)}) collective-permute-start(bf16[2,128,1024]{2,1,0:T(8,128)(2,1)S(1)} %slice.19), channel_id=1, source_target_pairs={{0,48},{32,0},{16,32},{48,16},{1,49},{33,1},{17,33},{49,17},{2,50}... | collective-permute-start | bytes 1572872 | tf_op jit(solution)/shard_map/ppermute | solution.py:287
  54.2 2.8 %collective-permute-start.11 = (bf16[2,1024,128]{2,1,0:T(8,128)(2,1)S(1)}, bf16[2,1024,128]{2,1,0:T(8,128)(2,1)S(1)}, u32[]{:S(2)}, u32[]{:S(2)}) collective-permute-start(bf16[2,1024,128]{2,1,0:T(8,128)(2,1)S(1)} %slice.17), channel_id=1, source_target_pairs={{0,192},{64,0},{128,64},{192,128},{1,193},{65,1},{129,65},{193,129... | collective-permute-start | bytes 1572872 | tf_op jit(solution)/shard_map/ppermute | solution.py:283
  57.0 2.9 %multiply_near.1.near = f32[1024,1024]{1,0:T(8,128)S(1)} custom-call(bf16[4,1024,128]{2,1,0:T(8,128)(2,1)S(1)} %pad_maximum_fusion.r0.refs_0_, bf16[4,1024,128]{2,1,0:T(8,128)(2,1)S(1)} %collective-permute-done.3.r1.refs_1_, bf16[4,1024,128]{2,1,0:T(8,128)(2,1)S(1)} %collective-permute-done.4.r3.refs_2_, ...), custom_call_target="tpu_custom_call" | custom-call | flops 2415919104 | bytes 10485760 | tf_op jit(solution)/shard_map/multiply_near/pallas_call | solution.py:43
  59.9 5.1 %collective-permute-done.12.refs_8_ = bf16[2,128,1024]{2,1,0:T(8,128)(2,1)S(1)} collective-permute-done((bf16[2,128,1024]{2,1,0:T(8,128)(2,1)S(1)}, bf16[2,128,1024]{2,1,0:T(8,128)(2,1)S(1)}, u32[]{:S(2)}, u32[]{:S(2)}) %collective-permute-start.12) | collective-permute-done | bytes 524320 | tf_op jit(solution)/shard_map/ppermute | solution.py:287
  68.6 2.4 %collective-permute-start.15 = (bf16[8,128,256]{2,1,0:T(8,128)(2,1)S(1)}, bf16[8,128,256]{2,1,0:T(8,128)(2,1)S(1)}, u32[]{:S(2)}, u32[]{:S(2)}) collective-permute-start(bf16[8,128,256]{2,1,0:T(8,128)(2,1)S(1)} %get-tuple-element.43), channel_id=1, source_target_pairs={{0,1},{1,0},{2,3},{3,2},{4,5},{5,4},{6,7},{7,6},{8,9},{9,8},{10,11... | collective-permute-start | bytes 1572872 | tf_op jit(solution)/shard_map/ppermute | solution.py:295
  74.3 4.0 %collective-permute-start.17 = (bf16[4,128,256]{2,1,0:T(8,128)(2,1)S(1)}, bf16[4,128,256]{2,1,0:T(8,128)(2,1)S(1)}, u32[]{:S(2)}, u32[]{:S(2)}) collective-permute-start(bf16[4,128,256]{2,1,0:T(8,128)(2,1)S(1)} %get-tuple-element.45), channel_id=1, source_target_pairs={{0,14},{2,0},{4,2},{6,4},{8,6},{10,8},{12,10},{14,12},{1,15},{3,1}... | collective-permute-start | bytes 786440 | tf_op jit(solution)/shard_map/ppermute | solution.py:291
  78.3 6.3 %collective-permute-done.16.up = bf16[4,128,256]{2,1,0:T(8,128)(2,1)S(1)} collective-permute-done((bf16[4,128,256]{2,1,0:T(8,128)(2,1)S(1)}, bf16[4,128,256]{2,1,0:T(8,128)(2,1)S(1)}, u32[]{:S(2)}, u32[]{:S(2)}) %collective-permute-start.16) | collective-permute-done | bytes 262176 | tf_op jit(solution)/shard_map/ppermute | solution.py:291
  86.5 2.5 %collective-permute-start.19 = (bf16[256,256]{1,0:T(8,128)(2,1)S(1)}, bf16[256,256]{1,0:T(8,128)(2,1)S(1)}, u32[]{:S(2)}, u32[]{:S(2)}) collective-permute-start(bf16[256,256]{1,0:T(8,128)(2,1)S(1)} %get-tuple-element.48), channel_id=1, source_target_pairs={{0,8},{2,10},{4,12},{6,14},{8,0},{10,2},{12,4},{14,6},{1,9},{3,11}... | collective-permute-start | bytes 393224 | tf_op jit(solution)/shard_map/ppermute | solution.py:291
  89.0 3.2 %collective-permute-start.20 = (bf16[256,256]{1,0:T(8,128)(2,1)S(1)}, bf16[256,256]{1,0:T(8,128)(2,1)S(1)}, u32[]{:S(2)}, u32[]{:S(2)}) collective-permute-start(bf16[256,256]{1,0:T(8,128)(2,1)S(1)} %get-tuple-element.49), channel_id=1, source_target_pairs={{0,12},{2,14},{4,0},{6,2},{8,4},{10,6},{12,8},{14,10},{1,13},{3,15... | collective-permute-start | bytes 393224 | tf_op jit(solution)/shard_map/ppermute | solution.py:291
  92.2 5.8 %collective-permute-done.19.t2 = bf16[256,256]{1,0:T(8,128)(2,1)S(1)} collective-permute-done((bf16[256,256]{1,0:T(8,128)(2,1)S(1)}, bf16[256,256]{1,0:T(8,128)(2,1)S(1)}, u32[]{:S(2)}, u32[]{:S(2)}) %collective-permute-start.19) | collective-permute-done | bytes 131104 | tf_op jit(solution)/shard_map/ppermute | solution.py:291
  98.0 4.7 %collective-permute-done.20.t3 = bf16[256,256]{1,0:T(8,128)(2,1)S(1)} collective-permute-done((bf16[256,256]{1,0:T(8,128)(2,1)S(1)}, bf16[256,256]{1,0:T(8,128)(2,1)S(1)}, u32[]{:S(2)}, u32[]{:S(2)}) %collective-permute-start.20) | collective-permute-done | bytes 131104 | tf_op jit(solution)/shard_map/ppermute | solution.py:291
  104.7 4.0 %collective-permute-done.22 = f32[192,128]{1,0:T(8,128)S(1)} collective-permute-done((f32[192,128]{1,0:T(8,128)S(1)}, f32[192,128]{1,0:T(8,128)S(1)}, u32[]{:S(2)}, u32[]{:S(2)}) %collective-permute-start.22) | collective-permute-done | bytes 98336 | tf_op jit(solution)/shard_map/ppermute | solution.py:295
  113.8 3.3 %collective-permute-done.24 = f32[192,128]{1,0:T(8,128)S(1)} collective-permute-done((f32[192,128]{1,0:T(8,128)S(1)}, f32[192,128]{1,0:T(8,128)S(1)}, u32[]{:S(2)}, u32[]{:S(2)}) %collective-permute-start.24) | collective-permute-done | bytes 98336 | tf_op jit(solution)/shard_map/ppermute | solution.py:287
  119.5 6.8 %newton.1 = (bf16[64,256]{1,0:T(8,128)(2,1)S(1)}, bf16[64,256]{1,0:T(8,128)(2,1)S(1)}, bf16[64,256]{1,0:T(8,128)(2,1)S(1)}, bf16[64,256]{1,0:T(8,128)(2,1)S(1)}) custom-call(s32[40]{0:T(128)S(1)} %get-tuple-element.31.meta, f32[192,128]{1,0:T(8,128)S(1)} %add_add_fusion.mine, f32[192,128]{1,0:T(8,128)S(1)} %collective-permute-done.26.other, ...), custom_call_target="tpu_custom_call" | custom-call | flops 4026531840 | bytes 458912 | tf_op jit(solution)/shard_map/newton/pallas_call | solution.py:43
  126.3 3.6 %collective-permute-start.27 = (bf16[64,256]{1,0:T(8,128)(2,1)S(1)}, bf16[64,256]{1,0:T(8,128)(2,1)S(1)}, u32[]{:S(2)}, u32[]{:S(2)}) collective-permute-start(bf16[64,256]{1,0:T(8,128)(2,1)S(1)} %get-tuple-element.54), channel_id=1, source_target_pairs={{0,4},{4,8},{8,12},{12,0},{1,5},{5,9},{9,13},{13,1},{2,6},{6,10},{... | collective-permute-start | bytes 98312 | tf_op jit(solution)/shard_map/ppermute | solution.py:388
  133.5 3.2 %collective-permute-done.28 = bf16[64,256]{1,0:T(8,128)(2,1)S(1)} collective-permute-done((bf16[64,256]{1,0:T(8,128)(2,1)S(1)}, bf16[64,256]{1,0:T(8,128)(2,1)S(1)}, u32[]{:S(2)}, u32[]{:S(2)}) %collective-permute-start.28) | collective-permute-done | bytes 32800 | tf_op jit(solution)/shard_map/ppermute | solution.py:388
  138.5 4.2 %collective-permute-start.31 = (bf16[4,64,256]{2,1,0:T(8,128)(2,1)S(1)}, bf16[4,64,256]{2,1,0:T(8,128)(2,1)S(1)}, u32[]{:S(2)}, u32[]{:S(2)}) collective-permute-start(bf16[4,64,256]{2,1,0:T(8,128)(2,1)S(1)} %pad_maximum_fusion.2.p0), channel_id=1, source_target_pairs={{0,128},{64,192},{128,0},{192,64},{1,129},{65,193},{129,1},{193,65... | collective-permute-start | bytes 393224 | tf_op jit(solution)/shard_map/ppermute | solution.py:283
  148.8 3.7 %collective-permute-done.35.q2 = bf16[4,64,256]{2,1,0:T(8,128)(2,1)S(1)} collective-permute-done((bf16[4,64,256]{2,1,0:T(8,128)(2,1)S(1)}, bf16[4,64,256]{2,1,0:T(8,128)(2,1)S(1)}, u32[]{:S(2)}, u32[]{:S(2)}) %collective-permute-start.35) | collective-permute-done | bytes 131104 | tf_op jit(solution)/shard_map/ppermute | solution.py:283
  (77 shorter events, 48.5 us)
Async XLA Ops:
  6.8 9.6 %collective-permute-start.5 = (bf16[128,1024]{1,0:T(8,128)(2,1)S(1)}, bf16[128,1024]{1,0:T(8,128)(2,1)S(1)}, u32[]{:S(2)}, u32[]{:S(2)}) collective-permute-start(bf16[128,1024]{1,0:T(8,128)(2,1)S(1)} %get-tuple-element.37), channel_id=1, source_target_pairs={{0,64},{64,128},{128,192},{192,0},{1,65},{65,129},{129,193},{193,1... | collective-permute-start | bytes 786440 | tf_op jit(solution)/shard_map/ppermute | solution.py:283
  9.0 13.8 %collective-permute-start.6 = (bf16[128,1024]{1,0:T(8,128)(2,1)S(1)}, bf16[128,1024]{1,0:T(8,128)(2,1)S(1)}, u32[]{:S(2)}, u32[]{:S(2)}) collective-permute-start(bf16[128,1024]{1,0:T(8,128)(2,1)S(1)} %get-tuple-element.38), channel_id=1, source_target_pairs={{0,128},{64,192},{128,0},{192,64},{1,129},{65,193},{129,1},{193,65... | collective-permute-start | bytes 786440 | tf_op jit(solution)/shard_map/ppermute | solution.py:283
  11.4 11.3 %collective-permute-start.7 = (bf16[128,1024]{1,0:T(8,128)(2,1)S(1)}, bf16[128,1024]{1,0:T(8,128)(2,1)S(1)}, u32[]{:S(2)}, u32[]{:S(2)}) collective-permute-start(bf16[128,1024]{1,0:T(8,128)(2,1)S(1)} %get-tuple-element.39), channel_id=1, source_target_pairs={{0,192},{64,0},{128,64},{192,128},{1,193},{65,1},{129,65},{193,129... | collective-permute-start | bytes 786440 | tf_op jit(solution)/shard_map/ppermute | solution.py:283
  12.6 13.2 %collective-permute-start = (bf16[1024,128]{1,0:T(8,128)(2,1)S(1)}, bf16[1024,128]{1,0:T(8,128)(2,1)S(1)}, u32[]{:S(2)}, u32[]{:S(2)}) collective-permute-start(bf16[1024,128]{1,0:T(8,128)(2,1)S(1)} %get-tuple-element.33), channel_id=1, source_target_pairs={{0,32},{32,16},{16,48},{48,0},{1,33},{33,17},{17,49},{49,1},{2,34}... | collective-permute-start | bytes 786440 | tf_op jit(solution)/shard_map/ppermute | solution.py:287
  13.9 13.1 %collective-permute-start.1 = (bf16[1024,128]{1,0:T(8,128)(2,1)S(1)}, bf16[1024,128]{1,0:T(8,128)(2,1)S(1)}, u32[]{:S(2)}, u32[]{:S(2)}) collective-permute-start(bf16[1024,128]{1,0:T(8,128)(2,1)S(1)} %get-tuple-element.34), channel_id=1, source_target_pairs={{0,16},{32,48},{16,0},{48,32},{1,17},{33,49},{17,1},{49,33},{2,18}... | collective-permute-start | bytes 786440 | tf_op jit(solution)/shard_map/ppermute | solution.py:287
  16.5 10.4 %collective-permute-start.2 = (bf16[1024,128]{1,0:T(8,128)(2,1)S(1)}, bf16[1024,128]{1,0:T(8,128)(2,1)S(1)}, u32[]{:S(2)}, u32[]{:S(2)}) collective-permute-start(bf16[1024,128]{1,0:T(8,128)(2,1)S(1)} %get-tuple-element.35), channel_id=1, source_target_pairs={{0,48},{32,0},{16,32},{48,16},{1,49},{33,1},{17,33},{49,17},{2,50}... | collective-permute-start | bytes 786440 | tf_op jit(solution)/shard_map/ppermute | solution.py:287
  22.9 28.1 %collective-permute-start.8 = (bf16[4,128,1024]{2,1,0:T(8,128)(2,1)S(1)}, bf16[4,128,1024]{2,1,0:T(8,128)(2,1)S(1)}, u32[]{:S(2)}, u32[]{:S(2)}) collective-permute-start(bf16[4,128,1024]{2,1,0:T(8,128)(2,1)S(1)} %pad_maximum_fusion.1.g0.refs_5_), channel_id=1, source_target_pairs={{0,32},{32,16},{16,48},{48,0},{1,33},{33,17},{17,49},{49,1},{2,34}... | collective-permute-start | bytes 3145736 | tf_op jit(solution)/shard_map/ppermute | solution.py:287
  24.3 26.9 %collective-permute-start.9 = (bf16[4,128,1024]{2,1,0:T(8,128)(2,1)S(1)}, bf16[4,128,1024]{2,1,0:T(8,128)(2,1)S(1)}, u32[]{:S(2)}, u32[]{:S(2)}) collective-permute-start(bf16[4,128,1024]{2,1,0:T(8,128)(2,1)S(1)} %pad_maximum_fusion.1.g0.refs_5_), channel_id=1, source_target_pairs={{0,48},{32,0},{16,32},{48,16},{1,49},{33,1},{17,33},{49,17},{2,50}... | collective-permute-start | bytes 3145736 | tf_op jit(solution)/shard_map/ppermute | solution.py:287
  27.1 26.9 %collective-permute-start.3 = (bf16[4,1024,128]{2,1,0:T(8,128)(2,1)S(1)}, bf16[4,1024,128]{2,1,0:T(8,128)(2,1)S(1)}, u32[]{:S(2)}, u32[]{:S(2)}) collective-permute-start(bf16[4,1024,128]{2,1,0:T(8,128)(2,1)S(1)} %pad_maximum_fusion.r0.refs_0_), channel_id=1, source_target_pairs={{0,64},{64,128},{128,192},{192,0},{1,65},{65,129},{129,193},{193,1... | collective-permute-start | bytes 3145736 | tf_op jit(solution)/shard_map/ppermute | solution.py:283
  27.4 26.7 %collective-permute-start.4 = (bf16[4,1024,128]{2,1,0:T(8,128)(2,1)S(1)}, bf16[4,1024,128]{2,1,0:T(8,128)(2,1)S(1)}, u32[]{:S(2)}, u32[]{:S(2)}) collective-permute-start(bf16[4,1024,128]{2,1,0:T(8,128)(2,1)S(1)} %pad_maximum_fusion.r0.refs_0_), channel_id=1, source_target_pairs={{0,192},{64,0},{128,64},{192,128},{1,193},{65,1},{129,65},{193,129... | collective-permute-start | bytes 3145736 | tf_op jit(solution)/shard_map/ppermute | solution.py:283
  51.1 13.9 %collective-permute-start.12 = (bf16[2,128,1024]{2,1,0:T(8,128)(2,1)S(1)}, bf16[2,128,1024]{2,1,0:T(8,128)(2,1)S(1)}, u32[]{:S(2)}, u32[]{:S(2)}) collective-permute-start(bf16[2,128,1024]{2,1,0:T(8,128)(2,1)S(1)} %slice.18), channel_id=1, source_target_pairs={{0,32},{32,16},{16,48},{48,0},{1,33},{33,17},{17,49},{49,1},{2,34}... | collective-permute-start | bytes 1572872 | tf_op jit(solution)/shard_map/ppermute | solution.py:287
  51.2 13.8 %collective-permute-start.13 = (bf16[2,128,1024]{2,1,0:T(8,128)(2,1)S(1)}, bf16[2,128,1024]{2,1,0:T(8,128)(2,1)S(1)}, u32[]{:S(2)}, u32[]{:S(2)}) collective-permute-start(bf16[2,128,1024]{2,1,0:T(8,128)(2,1)S(1)} %slice.19), channel_id=1, source_target_pairs={{0,48},{32,0},{16,32},{48,16},{1,49},{33,1},{17,33},{49,17},{2,50}... | collective-permute-start | bytes 1572872 | tf_op jit(solution)/shard_map/ppermute | solution.py:287
  54.0 13.3 %collective-permute-start.10 = (bf16[2,1024,128]{2,1,0:T(8,128)(2,1)S(1)}, bf16[2,1024,128]{2,1,0:T(8,128)(2,1)S(1)}, u32[]{:S(2)}, u32[]{:S(2)}) collective-permute-start(bf16[2,1024,128]{2,1,0:T(8,128)(2,1)S(1)} %slice.16), channel_id=1, source_target_pairs={{0,64},{64,128},{128,192},{192,0},{1,65},{65,129},{129,193},{193,1... | collective-permute-start | bytes 1572872 | tf_op jit(solution)/shard_map/ppermute | solution.py:283
  54.2 13.1 %collective-permute-start.11 = (bf16[2,1024,128]{2,1,0:T(8,128)(2,1)S(1)}, bf16[2,1024,128]{2,1,0:T(8,128)(2,1)S(1)}, u32[]{:S(2)}, u32[]{:S(2)}) collective-permute-start(bf16[2,1024,128]{2,1,0:T(8,128)(2,1)S(1)} %slice.17), channel_id=1, source_target_pairs={{0,192},{64,0},{128,64},{192,128},{1,193},{65,1},{129,65},{193,129... | collective-permute-start | bytes 1572872 | tf_op jit(solution)/shard_map/ppermute | solution.py:283
  72.6 12.0 %collective-permute-start.16 = (bf16[4,128,256]{2,1,0:T(8,128)(2,1)S(1)}, bf16[4,128,256]{2,1,0:T(8,128)(2,1)S(1)}, u32[]{:S(2)}, u32[]{:S(2)}) collective-permute-start(bf16[4,128,256]{2,1,0:T(8,128)(2,1)S(1)} %get-tuple-element.44), channel_id=1, source_target_pairs={{0,2},{2,4},{4,6},{6,8},{8,10},{10,12},{12,14},{14,0},{1,3},{3,5},... | collective-permute-start | bytes 786440 | tf_op jit(solution)/shard_map/ppermute | solution.py:291
  74.3 10.3 %collective-permute-start.17 = (bf16[4,128,256]{2,1,0:T(8,128)(2,1)S(1)}, bf16[4,128,256]{2,1,0:T(8,128)(2,1)S(1)}, u32[]{:S(2)}, u32[]{:S(2)}) collective-permute-start(bf16[4,128,256]{2,1,0:T(8,128)(2,1)S(1)} %get-tuple-element.45), channel_id=1, source_target_pairs={{0,14},{2,0},{4,2},{6,4},{8,6},{10,8},{12,10},{14,12},{1,15},{3,1}... | collective-permute-start | bytes 786440 | tf_op jit(solution)/shard_map/ppermute | solution.py:291
  84.8 7.4 %collective-permute-start.18 = (bf16[256,256]{1,0:T(8,128)(2,1)S(1)}, bf16[256,256]{1,0:T(8,128)(2,1)S(1)}, u32[]{:S(2)}, u32[]{:S(2)}) collective-permute-start(bf16[256,256]{1,0:T(8,128)(2,1)S(1)} %get-tuple-element.47), channel_id=1, source_target_pairs={{0,4},{2,6},{4,8},{6,10},{8,12},{10,14},{12,0},{14,2},{1,5},{3,7},... | collective-permute-start | bytes 393224 | tf_op jit(solution)/shard_map/ppermute | solution.py:291
  86.5 11.5 %collective-permute-start.19 = (bf16[256,256]{1,0:T(8,128)(2,1)S(1)}, bf16[256,256]{1,0:T(8,128)(2,1)S(1)}, u32[]{:S(2)}, u32[]{:S(2)}) collective-permute-start(bf16[256,256]{1,0:T(8,128)(2,1)S(1)} %get-tuple-element.48), channel_id=1, source_target_pairs={{0,8},{2,10},{4,12},{6,14},{8,0},{10,2},{12,4},{14,6},{1,9},{3,11}... | collective-permute-start | bytes 393224 | tf_op jit(solution)/shard_map/ppermute | solution.py:291
  89.0 13.7 %collective-permute-start.20 = (bf16[256,256]{1,0:T(8,128)(2,1)S(1)}, bf16[256,256]{1,0:T(8,128)(2,1)S(1)}, u32[]{:S(2)}, u32[]{:S(2)}) collective-permute-start(bf16[256,256]{1,0:T(8,128)(2,1)S(1)} %get-tuple-element.49), channel_id=1, source_target_pairs={{0,12},{2,14},{4,0},{6,2},{8,4},{10,6},{12,8},{14,10},{1,13},{3,15... | collective-permute-start | bytes 393224 | tf_op jit(solution)/shard_map/ppermute | solution.py:291
  109.8 7.3 %collective-permute-start.24 = (f32[192,128]{1,0:T(8,128)S(1)}, f32[192,128]{1,0:T(8,128)S(1)}, u32[]{:S(2)}, u32[]{:S(2)}) collective-permute-start(f32[192,128]{1,0:T(8,128)S(1)} %add.16), channel_id=1, source_target_pairs={{0,32},{32,16},{16,48},{48,0},{1,33},{33,17},{17,49},{49,1},{2,34}... | collective-permute-start | bytes 294920 | tf_op jit(solution)/shard_map/ppermute | solution.py:287
  126.3 7.2 %collective-permute-start.27 = (bf16[64,256]{1,0:T(8,128)(2,1)S(1)}, bf16[64,256]{1,0:T(8,128)(2,1)S(1)}, u32[]{:S(2)}, u32[]{:S(2)}) collective-permute-start(bf16[64,256]{1,0:T(8,128)(2,1)S(1)} %get-tuple-element.54), channel_id=1, source_target_pairs={{0,4},{4,8},{8,12},{12,0},{1,5},{5,9},{9,13},{13,1},{2,6},{6,10},{... | collective-permute-start | bytes 98312 | tf_op jit(solution)/shard_map/ppermute | solution.py:388
  138.5 8.3 %collective-permute-start.31 = (bf16[4,64,256]{2,1,0:T(8,128)(2,1)S(1)}, bf16[4,64,256]{2,1,0:T(8,128)(2,1)S(1)}, u32[]{:S(2)}, u32[]{:S(2)}) collective-permute-start(bf16[4,64,256]{2,1,0:T(8,128)(2,1)S(1)} %pad_maximum_fusion.2.p0), channel_id=1, source_target_pairs={{0,128},{64,192},{128,0},{192,64},{1,129},{65,193},{129,1},{193,65... | collective-permute-start | bytes 393224 | tf_op jit(solution)/shard_map/ppermute | solution.py:283
  144.1 8.4 %collective-permute-start.35 = (bf16[4,64,256]{2,1,0:T(8,128)(2,1)S(1)}, bf16[4,64,256]{2,1,0:T(8,128)(2,1)S(1)}, u32[]{:S(2)}, u32[]{:S(2)}) collective-permute-start(bf16[4,64,256]{2,1,0:T(8,128)(2,1)S(1)} %collective-permute-done.33.q0), channel_id=1, source_target_pairs={{0,128},{64,192},{128,0},{192,64},{1,129},{65,193},{129,1},{193,65... | collective-permute-start | bytes 393224 | tf_op jit(solution)/shard_map/ppermute | solution.py:283
  145.0 8.5 %collective-permute-start.36 = (bf16[4,64,256]{2,1,0:T(8,128)(2,1)S(1)}, bf16[4,64,256]{2,1,0:T(8,128)(2,1)S(1)}, u32[]{:S(2)}, u32[]{:S(2)}) collective-permute-start(bf16[4,64,256]{2,1,0:T(8,128)(2,1)S(1)} %collective-permute-done.33.q0), channel_id=1, source_target_pairs={{0,192},{64,0},{128,64},{192,128},{1,193},{65,1},{129,65},{193,129... | collective-permute-start | bytes 393224 | tf_op jit(solution)/shard_map/ppermute | solution.py:283
  (17 other events, 68.5 us)

commit v6 on v5

--- a/solution.py
+++ b/solution.py
@@ -182,7 +182,7 @@
             out[h * 128 : (h + 1) * 128, :] = total.astype(out.dtype)
 
 
-def gram_part(t0, t1, t2, t3, head_grad, keep, send):
+def gram_part(t2, t1, t3, t0, head_grad, keep, send):
     total = (t0[...] + t1[...].astype(f32)) + (t2[...].astype(f32) + t3[...].astype(f32))
     part = total.astype(bf16)
     head_grad[...] = part
@@ -208,7 +208,7 @@
     return (dot(a[1], b[0]) + dot(a[0], b[1])) + dot(a[0], b[0])
 
 
-def newton(meta, mine, other, head_grad, o0, o1, o2, o3, result):
+def newton(meta, mine, other, head_grad, out):
     core = lax.axis_index("core")
     a, b = mine[...], other[...]
     first, second = jnp.where(core == 0, a, b), jnp.where(core == 0, b, a)
@@ -253,25 +253,22 @@
     h = head_grad[...]
     update = jnp.dot(h, bottom, preferred_element_type=f32) + jnp.dot(h, middle, preferred_element_type=f32)
     update = update + jnp.dot(h, top, preferred_element_type=f32)
-    result[...] = (update * (by_col * 64.0)).astype(bf16)
-    for k, out in enumerate((o0, o1, o2, o3)):
-        at = pl.multiple_of(((zh + k) & 3) * HALF, HALF)
-        out[...] = result[pl.ds(at, HALF), :]
-
-
-def place_heads(meta, p0, p1, p2, p3, q0, q1, q2, q3, out, rows, sems):
-    ylo, x, zh = lax.axis_index("ylo"), lax.axis_index("x"), lax.axis_index("zh")
+    update = (update * (by_col * 64.0)).astype(bf16)
+    for to in range(32):
+        rows = to % 4 * HALF
+        out[to] = update[rows : rows + HALF]
+
+
+def place_heads(meta, update, out, rows, sems):
     copies = []
-    for i, refs in enumerate(((p0, p1, p2, p3), (q0, q1, q2, q3))):
-        for dx in range(4):
-            for dzh in range(4):
-                slot = ((x - dx) & 3) * 4 + ((zh - dzh) & 3)
-                for j in range(2):
-                    at = pl.multiple_of(meta[PERM_AT + slot * 2 + j] * HEAD, HEAD)
-                    rows[i, :, pl.ds(at, HEAD)] = refs[dx][dzh, :, j * HEAD : (j + 1) * HEAD].astype(f32)
-        half = pl.ds(pl.multiple_of((ylo ^ i) * HALF, HALF), HALF)
-        copies.append(pltpu.make_async_copy(rows.at[i], out.at[half, :], sems.at[i]))
-        copies[i].start()
+    for low in range(2):
+        for slot in range(16):
+            for j in range(2):
+                at = pl.multiple_of(meta[PERM_AT + slot * 2 + j] * HEAD, HEAD)
+                block = update[(slot // 4 * 2 + low) * 4 + slot % 4, :, j * HEAD : (j + 1) * HEAD]
+                rows[low, :, pl.ds(at, HEAD)] = block.astype(f32)
+        copies.append(pltpu.make_async_copy(rows.at[low], out.at[pl.ds(low * HALF, HALF), :], sems.at[low]))
+        copies[low].start()
     for copy in copies:
         copy.wait()
 
@@ -367,7 +364,7 @@
     head_grad, mine, theirs = local_kernel(
         gram_part,
         [shape((256, SLOT), bf16), shape((GRAM, HEAD), f32), shape((GRAM, HEAD), f32)],
-        (t0, t1, t2, t3),
+        (t2, t1, t3, t0),
         8,
         2 * 256 * SLOT * SLOT,
         "gram_part",
@@ -375,28 +372,24 @@
     mine = mine + swap(theirs, "core")
     mine = mine + swap(mine, "z0")
     mine = (mine + move_y(mine, 2)) + (move_y(mine, 1) + move_y(mine, 3))
-    update = local_kernel(
+    (update,) = local_kernel(
         newton,
-        [shape((HALF, SLOT), bf16)] * 4,
+        [shape((32, HALF, SLOT), bf16)],
         (meta, mine, swap(mine, "core"), head_grad),
         16,
         20 * 2 * SLOT**3 * 6,
         "newton",
         in_specs=[smem()] + [vmem()] * 3,
-        scratch=[pltpu.VMEM((256, SLOT), bf16)],
-    )
-    ring = lambda a, k: lax.ppermute(a, "zh", [(i, (i + k) % 4) for i in range(4)])
-    p0 = jnp.stack(farthest_first(update, ring))
-    q0 = swap(p0, "ylo")
-    ps, qs = farthest_first([p0] * 4, move_x), farthest_first([q0] * 4, move_x)
+    )
+    update = lax.all_to_all(update, ("x", "ylo", "zh"), split_axis=0, concat_axis=0, tiled=True)
     (out,) = local_kernel(
         place_heads,
         [shape((2 * HALF, width), f32)],
-        (meta, *ps, *qs),
+        (meta, update),
         12,
         0,
         "place_heads",
-        in_specs=[smem()] + [vmem()] * 8,
+        in_specs=[smem(), vmem()],
         out_specs=[hbm()],
         scratch=[pltpu.VMEM((2, HALF, width), f32), pltpu.SemaphoreType.DMA((2,))],
     )

time: 156 us -> 166 us (1.064)
  blocking collectives: 0 us -> 38.5 us
  starting transfers between devices: 62.9 us -> 47.6 us
  waiting for transfers between devices: 70.5 us -> 57.7 us
    all_to_all x0 -> x1, blocking collectives: none -> 38.5 us  [on_device(): lax.all_to_all(update, ('x', 'ylo', 'zh'), split_axis=0, concat_axis=0, t...]
    ppermute x13 -> x7, starting transfers between devices: 19.5 us -> 11.5 us  [move_x(): return lax.ppermute(a, 'x', [(i, (i + k) % 4) for i in range(4)])]
    ppermute x3 -> x0, starting transfers between devices: 7.22 us -> none  [on_device(): lax.ppermute(a, 'zh', [(i, (i + k) % 4) for i in range(4)])]
    ppermute x13 -> x7, waiting for transfers between devices: 13.2 us -> 6.2 us  [move_x(): return lax.ppermute(a, 'x', [(i, (i + k) % 4) for i in range(4)])]
    ppermute x3 -> x0, waiting for transfers between devices: 3.25 us -> none  [on_device(): lax.ppermute(a, 'zh', [(i, (i + k) % 4) for i in range(4)])]
    ppermute x6 -> x5, waiting for transfers between devices: 6.08 us -> 4.95 us  [swap(): return lax.ppermute(a, axis, [(0, 1), (1, 0)])]
    ppermute x6 -> x5, starting transfers between devices: 6.41 us -> 6.4 us  [swap(): return lax.ppermute(a, axis, [(0, 1), (1, 0)])]
  transfers between devices with their start and end apart: 37 -> 27, of which waited for: 20 -> 15; matrix products, arithmetic and copies ran while one was open for 0% -> 0% of each run, Pallas kernels for 3% -> 3%
where the time goes in v6:
time: 166 us
  waiting for transfers between devices  57.7 us (35%)
  starting transfers between devices  47.6 us (29%)
  blocking collectives  38.5 us (23%)
  Pallas kernels  17.1 us (10%)
  local copies, waits for them, and re-layouts  3.89 us (2%)
    all_to_all x1, blocking collectives, on_device(): lax.all_to_all(update, ('x', 'ylo', 'zh'), split_axis=0, concat_axis=0, t...  38.5 us
    ppermute x10, waiting for transfers between devices, move_y(): lax.ppermute(a, ('ylo', 'yhi'), [(Y_INDEX[i], Y_INDEX[(i + k) % 4]) for i...  31.1 us
    pallas_call x9, Pallas kernels, local_kernel(): pl.pallas_call(body, out_shape=outs, in_specs=in_specs or [vmem()] * len(...  17.1 us
    ppermute x10, starting transfers between devices, move_y(): lax.ppermute(a, ('ylo', 'yhi'), [(Y_INDEX[i], Y_INDEX[(i + k) % 4]) for i...  16.6 us
    ppermute x5, waiting for transfers between devices, move_z(): return lax.ppermute(a, ('zh', 'z0'), [(i, (i + k) % 8) for i in range(8)])  15.5 us
    ppermute x5, starting transfers between devices, move_z(): return lax.ppermute(a, ('zh', 'z0'), [(i, (i + k) % 8) for i in range(8)])  13.1 us
    ppermute x7, starting transfers between devices, move_x(): return lax.ppermute(a, 'x', [(i, (i + k) % 4) for i in range(4)])  11.5 us
    ppermute x5, starting transfers between devices, swap(): return lax.ppermute(a, axis, [(0, 1), (1, 0)])  6.4 us
  transfers between devices with their start and end apart: 27, of which 15 were waited for; matrix products, arithmetic and copies ran while one was open for 0% of the time, Pallas kernels for 3%

profile of v6, /device:TPU:1, one launch (start us, length us, event | category | flops | bytes accessed | tf_op | source)
XLA Modules:
  0.0 166.0 jit_solution(12529204073254814668)
XLA Ops:
  4.4 2.4 %prepare.1 = (bf16[1024,128]{1,0:T(8,128)(2,1)S(1)}, bf16[1024,128]{1,0:T(8,128)(2,1)S(1)}, bf16[1024,128]{1,0:T(8,128)(2,1)S(1)}, bf16[1024,128]{1,0:T(8,128)(2...) custom-call(s32[32]{0:T(128)S(1)} %copy-done.2, ...), custom_call_target="tpu_custom_call" | custom-call | flops 1048576 | bytes 4195108 | tf_op jit(solution)/shard_map/prepare/pallas_call | solution.py:43
  9.0 2.4 %collective-permute-start.6 = (bf16[128,1024]{1,0:T(8,128)(2,1)S(1)}, bf16[128,1024]{1,0:T(8,128)(2,1)S(1)}, u32[]{:S(2)}, u32[]{:S(2)}) collective-permute-start(bf16[128,1024]{1,0:T(8,128)(2,1)S(1)} %get-tuple-element.34), channel_id=1, source_target_pairs={{0,128},{64,192},{128,0},{192,64},{1,129},{65,193},{129,1},{193,65... | collective-permute-start | bytes 786440 | tf_op jit(solution)/shard_map/ppermute | solution.py:280
  13.9 2.6 %collective-permute-start.1 = (bf16[1024,128]{1,0:T(8,128)(2,1)S(1)}, bf16[1024,128]{1,0:T(8,128)(2,1)S(1)}, u32[]{:S(2)}, u32[]{:S(2)}) collective-permute-start(bf16[1024,128]{1,0:T(8,128)(2,1)S(1)} %get-tuple-element.30), channel_id=1, source_target_pairs={{0,16},{32,48},{16,0},{48,32},{1,17},{33,49},{17,1},{49,33},{2,18}... | collective-permute-start | bytes 786440 | tf_op jit(solution)/shard_map/ppermute | solution.py:284
  16.5 2.4 %collective-permute-start.2 = (bf16[1024,128]{1,0:T(8,128)(2,1)S(1)}, bf16[1024,128]{1,0:T(8,128)(2,1)S(1)}, u32[]{:S(2)}, u32[]{:S(2)}) collective-permute-start(bf16[1024,128]{1,0:T(8,128)(2,1)S(1)} %get-tuple-element.31), channel_id=1, source_target_pairs={{0,48},{32,0},{16,32},{48,16},{1,49},{33,1},{17,33},{49,17},{2,50}... | collective-permute-start | bytes 786440 | tf_op jit(solution)/shard_map/ppermute | solution.py:284
  18.9 3.9 %collective-permute-done.6 = bf16[128,1024]{1,0:T(8,128)(2,1)S(1)} collective-permute-done((bf16[128,1024]{1,0:T(8,128)(2,1)S(1)}, bf16[128,1024]{1,0:T(8,128)(2,1)S(1)}, u32[]{:S(2)}, u32[]{:S(2)}) %collective-permute-start.6) | collective-permute-done | bytes 262176 | tf_op jit(solution)/shard_map/ppermute | solution.py:280
  27.4 2.4 %collective-permute-start.4 = (bf16[4,1024,128]{2,1,0:T(8,128)(2,1)S(1)}, bf16[4,1024,128]{2,1,0:T(8,128)(2,1)S(1)}, u32[]{:S(2)}, u32[]{:S(2)}) collective-permute-start(bf16[4,1024,128]{2,1,0:T(8,128)(2,1)S(1)} %pad_maximum_fusion.r0.refs_0_), channel_id=1, source_target_pairs={{0,192},{64,0},{128,64},{192,128},{1,193},{65,1},{129,65},{193,129... | collective-permute-start | bytes 3145736 | tf_op jit(solution)/shard_map/ppermute | solution.py:280
  29.8 21.2 %collective-permute-done.8.g1.refs_6_ = bf16[4,128,1024]{2,1,0:T(8,128)(2,1)S(1)} collective-permute-done((bf16[4,128,1024]{2,1,0:T(8,128)(2,1)S(1)}, bf16[4,128,1024]{2,1,0:T(8,128)(2,1)S(1)}, u32[]{:S(2)}, u32[]{:S(2)}) %collective-permute-start.8) | collective-permute-done | bytes 1048608 | tf_op jit(solution)/shard_map/ppermute | solution.py:284
  51.2 2.7 %collective-permute-start.13 = (bf16[2,128,1024]{2,1,0:T(8,128)(2,1)S(1)}, bf16[2,128,1024]{2,1,0:T(8,128)(2,1)S(1)}, u32[]{:S(2)}, u32[]{:S(2)}) collective-permute-start(bf16[2,128,1024]{2,1,0:T(8,128)(2,1)S(1)} %slice.19), channel_id=1, source_target_pairs={{0,48},{32,0},{16,32},{48,16},{1,49},{33,1},{17,33},{49,17},{2,50}... | collective-permute-start | bytes 1572872 | tf_op jit(solution)/shard_map/ppermute | solution.py:284
  54.2 2.8 %collective-permute-start.11 = (bf16[2,1024,128]{2,1,0:T(8,128)(2,1)S(1)}, bf16[2,1024,128]{2,1,0:T(8,128)(2,1)S(1)}, u32[]{:S(2)}, u32[]{:S(2)}) collective-permute-start(bf16[2,1024,128]{2,1,0:T(8,128)(2,1)S(1)} %slice.17), channel_id=1, source_target_pairs={{0,192},{64,0},{128,64},{192,128},{1,193},{65,1},{129,65},{193,129... | collective-permute-start | bytes 1572872 | tf_op jit(solution)/shard_map/ppermute | solution.py:280
  57.0 2.9 %multiply_near.1.near = f32[1024,1024]{1,0:T(8,128)S(1)} custom-call(bf16[4,1024,128]{2,1,0:T(8,128)(2,1)S(1)} %pad_maximum_fusion.r0.refs_0_, bf16[4,1024,128]{2,1,0:T(8,128)(2,1)S(1)} %collective-permute-done.3.r1.refs_1_, bf16[4,1024,128]{2,1,0:T(8,128)(2,1)S(1)} %collective-permute-done.4.r3.refs_2_, ...), custom_call_target="tpu_custom_call" | custom-call | flops 2415919104 | bytes 10485760 | tf_op jit(solution)/shard_map/multiply_near/pallas_call | solution.py:43
  59.9 5.1 %collective-permute-done.12.refs_8_ = bf16[2,128,1024]{2,1,0:T(8,128)(2,1)S(1)} collective-permute-done((bf16[2,128,1024]{2,1,0:T(8,128)(2,1)S(1)}, bf16[2,128,1024]{2,1,0:T(8,128)(2,1)S(1)}, u32[]{:S(2)}, u32[]{:S(2)}) %collective-permute-start.12) | collective-permute-done | bytes 524320 | tf_op jit(solution)/shard_map/ppermute | solution.py:284
  65.0 2.3 %collective-permute-done.10.refs_3_ = bf16[2,1024,128]{2,1,0:T(8,128)(2,1)S(1)} collective-permute-done((bf16[2,1024,128]{2,1,0:T(8,128)(2,1)S(1)}, bf16[2,1024,128]{2,1,0:T(8,128)(2,1)S(1)}, u32[]{:S(2)}, u32[]{:S(2)}) %collective-permute-start.10) | collective-permute-done | bytes 524320 | tf_op jit(solution)/shard_map/ppermute | solution.py:280
  68.6 2.4 %collective-permute-start.15 = (bf16[8,128,256]{2,1,0:T(8,128)(2,1)S(1)}, bf16[8,128,256]{2,1,0:T(8,128)(2,1)S(1)}, u32[]{:S(2)}, u32[]{:S(2)}) collective-permute-start(bf16[8,128,256]{2,1,0:T(8,128)(2,1)S(1)} %get-tuple-element.39), channel_id=1, source_target_pairs={{0,1},{1,0},{2,3},{3,2},{4,5},{5,4},{6,7},{7,6},{8,9},{9,8},{10,11... | collective-permute-start | bytes 1572872 | tf_op jit(solution)/shard_map/ppermute | solution.py:292
  74.3 4.0 %collective-permute-start.17 = (bf16[4,128,256]{2,1,0:T(8,128)(2,1)S(1)}, bf16[4,128,256]{2,1,0:T(8,128)(2,1)S(1)}, u32[]{:S(2)}, u32[]{:S(2)}) collective-permute-start(bf16[4,128,256]{2,1,0:T(8,128)(2,1)S(1)} %get-tuple-element.41), channel_id=1, source_target_pairs={{0,14},{2,0},{4,2},{6,4},{8,6},{10,8},{12,10},{14,12},{1,15},{3,1}... | collective-permute-start | bytes 786440 | tf_op jit(solution)/shard_map/ppermute | solution.py:288
  78.3 6.3 %collective-permute-done.16.up = bf16[4,128,256]{2,1,0:T(8,128)(2,1)S(1)} collective-permute-done((bf16[4,128,256]{2,1,0:T(8,128)(2,1)S(1)}, bf16[4,128,256]{2,1,0:T(8,128)(2,1)S(1)}, u32[]{:S(2)}, u32[]{:S(2)}) %collective-permute-start.16) | collective-permute-done | bytes 262176 | tf_op jit(solution)/shard_map/ppermute | solution.py:288
  84.8 3.8 %collective-permute-start.18 = (bf16[256,256]{1,0:T(8,128)(2,1)S(1)}, bf16[256,256]{1,0:T(8,128)(2,1)S(1)}, u32[]{:S(2)}, u32[]{:S(2)}) collective-permute-start(bf16[256,256]{1,0:T(8,128)(2,1)S(1)} %get-tuple-element.42), channel_id=1, source_target_pairs={{0,8},{2,10},{4,12},{6,14},{8,0},{10,2},{12,4},{14,6},{1,9},{3,11}... | collective-permute-start | bytes 393224 | tf_op jit(solution)/shard_map/ppermute | solution.py:288
  89.0 3.2 %collective-permute-start.20 = (bf16[256,256]{1,0:T(8,128)(2,1)S(1)}, bf16[256,256]{1,0:T(8,128)(2,1)S(1)}, u32[]{:S(2)}, u32[]{:S(2)}) collective-permute-start(bf16[256,256]{1,0:T(8,128)(2,1)S(1)} %get-tuple-element.44), channel_id=1, source_target_pairs={{0,12},{2,14},{4,0},{6,2},{8,4},{10,6},{12,8},{14,10},{1,13},{3,15... | collective-permute-start | bytes 393224 | tf_op jit(solution)/shard_map/ppermute | solution.py:288
  93.0 6.1 %collective-permute-done.19.t1 = bf16[256,256]{1,0:T(8,128)(2,1)S(1)} collective-permute-done((bf16[256,256]{1,0:T(8,128)(2,1)S(1)}, bf16[256,256]{1,0:T(8,128)(2,1)S(1)}, u32[]{:S(2)}, u32[]{:S(2)}) %collective-permute-start.19) | collective-permute-done | bytes 131104 | tf_op jit(solution)/shard_map/ppermute | solution.py:288
  99.1 2.3 %collective-permute-done.20.t3 = bf16[256,256]{1,0:T(8,128)(2,1)S(1)} collective-permute-done((bf16[256,256]{1,0:T(8,128)(2,1)S(1)}, bf16[256,256]{1,0:T(8,128)(2,1)S(1)}, u32[]{:S(2)}, u32[]{:S(2)}) %collective-permute-start.20) | collective-permute-done | bytes 131104 | tf_op jit(solution)/shard_map/ppermute | solution.py:288
  105.2 2.9 %collective-permute-done.22 = f32[192,128]{1,0:T(8,128)S(1)} collective-permute-done((f32[192,128]{1,0:T(8,128)S(1)}, f32[192,128]{1,0:T(8,128)S(1)}, u32[]{:S(2)}, u32[]{:S(2)}) %collective-permute-start.22) | collective-permute-done | bytes 98336 | tf_op jit(solution)/shard_map/ppermute | solution.py:292
  110.4 2.3 %collective-permute-start.25 = (f32[192,128]{1,0:T(8,128)S(1)}, f32[192,128]{1,0:T(8,128)S(1)}, u32[]{:S(2)}, u32[]{:S(2)}) collective-permute-start(f32[192,128]{1,0:T(8,128)S(1)} %add.16), channel_id=1, source_target_pairs={{0,48},{32,0},{16,32},{48,16},{1,49},{33,1},{17,33},{49,17},{2,50}... | collective-permute-start | bytes 294920 | tf_op jit(solution)/shard_map/ppermute | solution.py:284
  113.2 3.2 %collective-permute-done.24 = f32[192,128]{1,0:T(8,128)S(1)} collective-permute-done((f32[192,128]{1,0:T(8,128)S(1)}, f32[192,128]{1,0:T(8,128)S(1)}, u32[]{:S(2)}, u32[]{:S(2)}) %collective-permute-start.24) | collective-permute-done | bytes 98336 | tf_op jit(solution)/shard_map/ppermute | solution.py:284
  118.6 6.8 %newton.1 = bf16[32,64,256]{2,1,0:T(8,128)(2,1)S(1)} custom-call(s32[40]{0:T(128)S(1)} %get-tuple-element.27.meta, f32[192,128]{1,0:T(8,128)S(1)} %add_add_fusion.mine, f32[192,128]{1,0:T(8,128)S(1)} %collective-permute-done.26.other, bf16[256,256]{1,0:T(8,128)(2,1)S(1)} %get-tuple-element.48.head_grad), custom_call_target="tpu_custom_call" | custom-call | flops 4026531840 | bytes 1376416 | tf_op jit(solution)/shard_map/newton/pallas_call | solution.py:43
  125.4 38.5 %all_to_all.5.update = bf16[32,64,256]{2,1,0:T(8,128)(2,1)S(1)} all-to-all(bf16[32,64,256]{2,1,0:T(8,128)(2,1)S(1)} %newton.1), channel_id=1, replica_groups=mesh['x'=4,'ylo'=2,'yhi'=2,'zh'=4,'z0'=2,'core'=2] {'x','ylo','zh'}, dimensions={0} | all-to-all | bytes 2097152 | tf_op jit(solution)/shard_map/all_to_all | solution.py:384
  (57 shorter events, 30.2 us)
Async XLA Ops:
  6.8 9.6 %collective-permute-start.5 = (bf16[128,1024]{1,0:T(8,128)(2,1)S(1)}, bf16[128,1024]{1,0:T(8,128)(2,1)S(1)}, u32[]{:S(2)}, u32[]{:S(2)}) collective-permute-start(bf16[128,1024]{1,0:T(8,128)(2,1)S(1)} %get-tuple-element.33), channel_id=1, source_target_pairs={{0,64},{64,128},{128,192},{192,0},{1,65},{65,129},{129,193},{193,1... | collective-permute-start | bytes 786440 | tf_op jit(solution)/shard_map/ppermute | solution.py:280
  9.0 13.8 %collective-permute-start.6 = (bf16[128,1024]{1,0:T(8,128)(2,1)S(1)}, bf16[128,1024]{1,0:T(8,128)(2,1)S(1)}, u32[]{:S(2)}, u32[]{:S(2)}) collective-permute-start(bf16[128,1024]{1,0:T(8,128)(2,1)S(1)} %get-tuple-element.34), channel_id=1, source_target_pairs={{0,128},{64,192},{128,0},{192,64},{1,129},{65,193},{129,1},{193,65... | collective-permute-start | bytes 786440 | tf_op jit(solution)/shard_map/ppermute | solution.py:280
  11.4 11.3 %collective-permute-start.7 = (bf16[128,1024]{1,0:T(8,128)(2,1)S(1)}, bf16[128,1024]{1,0:T(8,128)(2,1)S(1)}, u32[]{:S(2)}, u32[]{:S(2)}) collective-permute-start(bf16[128,1024]{1,0:T(8,128)(2,1)S(1)} %get-tuple-element.35), channel_id=1, source_target_pairs={{0,192},{64,0},{128,64},{192,128},{1,193},{65,1},{129,65},{193,129... | collective-permute-start | bytes 786440 | tf_op jit(solution)/shard_map/ppermute | solution.py:280
  12.6 13.2 %collective-permute-start = (bf16[1024,128]{1,0:T(8,128)(2,1)S(1)}, bf16[1024,128]{1,0:T(8,128)(2,1)S(1)}, u32[]{:S(2)}, u32[]{:S(2)}) collective-permute-start(bf16[1024,128]{1,0:T(8,128)(2,1)S(1)} %get-tuple-element.29), channel_id=1, source_target_pairs={{0,32},{32,16},{16,48},{48,0},{1,33},{33,17},{17,49},{49,1},{2,34}... | collective-permute-start | bytes 786440 | tf_op jit(solution)/shard_map/ppermute | solution.py:284
  13.9 13.1 %collective-permute-start.1 = (bf16[1024,128]{1,0:T(8,128)(2,1)S(1)}, bf16[1024,128]{1,0:T(8,128)(2,1)S(1)}, u32[]{:S(2)}, u32[]{:S(2)}) collective-permute-start(bf16[1024,128]{1,0:T(8,128)(2,1)S(1)} %get-tuple-element.30), channel_id=1, source_target_pairs={{0,16},{32,48},{16,0},{48,32},{1,17},{33,49},{17,1},{49,33},{2,18}... | collective-permute-start | bytes 786440 | tf_op jit(solution)/shard_map/ppermute | solution.py:284
  16.5 10.4 %collective-permute-start.2 = (bf16[1024,128]{1,0:T(8,128)(2,1)S(1)}, bf16[1024,128]{1,0:T(8,128)(2,1)S(1)}, u32[]{:S(2)}, u32[]{:S(2)}) collective-permute-start(bf16[1024,128]{1,0:T(8,128)(2,1)S(1)} %get-tuple-element.31), channel_id=1, source_target_pairs={{0,48},{32,0},{16,32},{48,16},{1,49},{33,1},{17,33},{49,17},{2,50}... | collective-permute-start | bytes 786440 | tf_op jit(solution)/shard_map/ppermute | solution.py:284
  22.9 28.1 %collective-permute-start.8 = (bf16[4,128,1024]{2,1,0:T(8,128)(2,1)S(1)}, bf16[4,128,1024]{2,1,0:T(8,128)(2,1)S(1)}, u32[]{:S(2)}, u32[]{:S(2)}) collective-permute-start(bf16[4,128,1024]{2,1,0:T(8,128)(2,1)S(1)} %pad_maximum_fusion.1.g0.refs_5_), channel_id=1, source_target_pairs={{0,32},{32,16},{16,48},{48,0},{1,33},{33,17},{17,49},{49,1},{2,34}... | collective-permute-start | bytes 3145736 | tf_op jit(solution)/shard_map/ppermute | solution.py:284
  24.3 26.9 %collective-permute-start.9 = (bf16[4,128,1024]{2,1,0:T(8,128)(2,1)S(1)}, bf16[4,128,1024]{2,1,0:T(8,128)(2,1)S(1)}, u32[]{:S(2)}, u32[]{:S(2)}) collective-permute-start(bf16[4,128,1024]{2,1,0:T(8,128)(2,1)S(1)} %pad_maximum_fusion.1.g0.refs_5_), channel_id=1, source_target_pairs={{0,48},{32,0},{16,32},{48,16},{1,49},{33,1},{17,33},{49,17},{2,50}... | collective-permute-start | bytes 3145736 | tf_op jit(solution)/shard_map/ppermute | solution.py:284
  27.1 26.9 %collective-permute-start.3 = (bf16[4,1024,128]{2,1,0:T(8,128)(2,1)S(1)}, bf16[4,1024,128]{2,1,0:T(8,128)(2,1)S(1)}, u32[]{:S(2)}, u32[]{:S(2)}) collective-permute-start(bf16[4,1024,128]{2,1,0:T(8,128)(2,1)S(1)} %pad_maximum_fusion.r0.refs_0_), channel_id=1, source_target_pairs={{0,64},{64,128},{128,192},{192,0},{1,65},{65,129},{129,193},{193,1... | collective-permute-start | bytes 3145736 | tf_op jit(solution)/shard_map/ppermute | solution.py:280
  27.4 26.7 %collective-permute-start.4 = (bf16[4,1024,128]{2,1,0:T(8,128)(2,1)S(1)}, bf16[4,1024,128]{2,1,0:T(8,128)(2,1)S(1)}, u32[]{:S(2)}, u32[]{:S(2)}) collective-permute-start(bf16[4,1024,128]{2,1,0:T(8,128)(2,1)S(1)} %pad_maximum_fusion.r0.refs_0_), channel_id=1, source_target_pairs={{0,192},{64,0},{128,64},{192,128},{1,193},{65,1},{129,65},{193,129... | collective-permute-start | bytes 3145736 | tf_op jit(solution)/shard_map/ppermute | solution.py:280
  51.1 13.9 %collective-permute-start.12 = (bf16[2,128,1024]{2,1,0:T(8,128)(2,1)S(1)}, bf16[2,128,1024]{2,1,0:T(8,128)(2,1)S(1)}, u32[]{:S(2)}, u32[]{:S(2)}) collective-permute-start(bf16[2,128,1024]{2,1,0:T(8,128)(2,1)S(1)} %slice.18), channel_id=1, source_target_pairs={{0,32},{32,16},{16,48},{48,0},{1,33},{33,17},{17,49},{49,1},{2,34}... | collective-permute-start | bytes 1572872 | tf_op jit(solution)/shard_map/ppermute | solution.py:284
  51.2 13.8 %collective-permute-start.13 = (bf16[2,128,1024]{2,1,0:T(8,128)(2,1)S(1)}, bf16[2,128,1024]{2,1,0:T(8,128)(2,1)S(1)}, u32[]{:S(2)}, u32[]{:S(2)}) collective-permute-start(bf16[2,128,1024]{2,1,0:T(8,128)(2,1)S(1)} %slice.19), channel_id=1, source_target_pairs={{0,48},{32,0},{16,32},{48,16},{1,49},{33,1},{17,33},{49,17},{2,50}... | collective-permute-start | bytes 1572872 | tf_op jit(solution)/shard_map/ppermute | solution.py:284
  54.0 13.3 %collective-permute-start.10 = (bf16[2,1024,128]{2,1,0:T(8,128)(2,1)S(1)}, bf16[2,1024,128]{2,1,0:T(8,128)(2,1)S(1)}, u32[]{:S(2)}, u32[]{:S(2)}) collective-permute-start(bf16[2,1024,128]{2,1,0:T(8,128)(2,1)S(1)} %slice.16), channel_id=1, source_target_pairs={{0,64},{64,128},{128,192},{192,0},{1,65},{65,129},{129,193},{193,1... | collective-permute-start | bytes 1572872 | tf_op jit(solution)/shard_map/ppermute | solution.py:280
  54.2 13.1 %collective-permute-start.11 = (bf16[2,1024,128]{2,1,0:T(8,128)(2,1)S(1)}, bf16[2,1024,128]{2,1,0:T(8,128)(2,1)S(1)}, u32[]{:S(2)}, u32[]{:S(2)}) collective-permute-start(bf16[2,1024,128]{2,1,0:T(8,128)(2,1)S(1)} %slice.17), channel_id=1, source_target_pairs={{0,192},{64,0},{128,64},{192,128},{1,193},{65,1},{129,65},{193,129... | collective-permute-start | bytes 1572872 | tf_op jit(solution)/shard_map/ppermute | solution.py:280
  72.2 6.1 %collective-permute-start.14 = (bf16[8,128,256]{2,1,0:T(8,128)(2,1)S(1)}, bf16[8,128,256]{2,1,0:T(8,128)(2,1)S(1)}, u32[]{:S(2)}, u32[]{:S(2)}) collective-permute-start(bf16[8,128,256]{2,1,0:T(8,128)(2,1)S(1)} %get-tuple-element.37), channel_id=1, source_target_pairs={{0,1},{1,0},{2,3},{3,2},{4,5},{5,4},{6,7},{7,6},{8,9},{9,8},{10,11... | collective-permute-start | bytes 1572872 | tf_op jit(solution)/shard_map/ppermute | solution.py:292
  72.6 12.0 %collective-permute-start.16 = (bf16[4,128,256]{2,1,0:T(8,128)(2,1)S(1)}, bf16[4,128,256]{2,1,0:T(8,128)(2,1)S(1)}, u32[]{:S(2)}, u32[]{:S(2)}) collective-permute-start(bf16[4,128,256]{2,1,0:T(8,128)(2,1)S(1)} %get-tuple-element.40), channel_id=1, source_target_pairs={{0,2},{2,4},{4,6},{6,8},{8,10},{10,12},{12,14},{14,0},{1,3},{3,5},... | collective-permute-start | bytes 786440 | tf_op jit(solution)/shard_map/ppermute | solution.py:288
  74.3 10.3 %collective-permute-start.17 = (bf16[4,128,256]{2,1,0:T(8,128)(2,1)S(1)}, bf16[4,128,256]{2,1,0:T(8,128)(2,1)S(1)}, u32[]{:S(2)}, u32[]{:S(2)}) collective-permute-start(bf16[4,128,256]{2,1,0:T(8,128)(2,1)S(1)} %get-tuple-element.41), channel_id=1, source_target_pairs={{0,14},{2,0},{4,2},{6,4},{8,6},{10,8},{12,10},{14,12},{1,15},{3,1}... | collective-permute-start | bytes 786440 | tf_op jit(solution)/shard_map/ppermute | solution.py:288
  84.8 8.1 %collective-permute-start.18 = (bf16[256,256]{1,0:T(8,128)(2,1)S(1)}, bf16[256,256]{1,0:T(8,128)(2,1)S(1)}, u32[]{:S(2)}, u32[]{:S(2)}) collective-permute-start(bf16[256,256]{1,0:T(8,128)(2,1)S(1)} %get-tuple-element.42), channel_id=1, source_target_pairs={{0,8},{2,10},{4,12},{6,14},{8,0},{10,2},{12,4},{14,6},{1,9},{3,11}... | collective-permute-start | bytes 393224 | tf_op jit(solution)/shard_map/ppermute | solution.py:288
  88.6 10.5 %collective-permute-start.19 = (bf16[256,256]{1,0:T(8,128)(2,1)S(1)}, bf16[256,256]{1,0:T(8,128)(2,1)S(1)}, u32[]{:S(2)}, u32[]{:S(2)}) collective-permute-start(bf16[256,256]{1,0:T(8,128)(2,1)S(1)} %get-tuple-element.43), channel_id=1, source_target_pairs={{0,4},{2,6},{4,8},{6,10},{8,12},{10,14},{12,0},{14,2},{1,5},{3,7},... | collective-permute-start | bytes 393224 | tf_op jit(solution)/shard_map/ppermute | solution.py:288
  89.0 12.4 %collective-permute-start.20 = (bf16[256,256]{1,0:T(8,128)(2,1)S(1)}, bf16[256,256]{1,0:T(8,128)(2,1)S(1)}, u32[]{:S(2)}, u32[]{:S(2)}) collective-permute-start(bf16[256,256]{1,0:T(8,128)(2,1)S(1)} %get-tuple-element.44), channel_id=1, source_target_pairs={{0,12},{2,14},{4,0},{6,2},{8,4},{10,6},{12,8},{14,10},{1,13},{3,15... | collective-permute-start | bytes 393224 | tf_op jit(solution)/shard_map/ppermute | solution.py:288
  103.2 5.0 %collective-permute-start.22 = (f32[192,128]{1,0:T(8,128)S(1)}, f32[192,128]{1,0:T(8,128)S(1)}, u32[]{:S(2)}, u32[]{:S(2)}) collective-permute-start(f32[192,128]{1,0:T(8,128)S(1)} %add.15), channel_id=1, source_target_pairs={{0,2},{2,0},{1,3},{3,1},{4,6},{6,4},{5,7},{7,5},{8,10},{10,8},{9,1... | collective-permute-start | bytes 294920 | tf_op jit(solution)/shard_map/ppermute | solution.py:292
  108.1 5.1 %collective-permute-start.23 = (f32[192,128]{1,0:T(8,128)S(1)}, f32[192,128]{1,0:T(8,128)S(1)}, u32[]{:S(2)}, u32[]{:S(2)}) collective-permute-start(f32[192,128]{1,0:T(8,128)S(1)} %add.16), channel_id=1, source_target_pairs={{0,16},{32,48},{16,0},{48,32},{1,17},{33,49},{17,1},{49,33},{2,18}... | collective-permute-start | bytes 294920 | tf_op jit(solution)/shard_map/ppermute | solution.py:284
  109.2 7.2 %collective-permute-start.24 = (f32[192,128]{1,0:T(8,128)S(1)}, f32[192,128]{1,0:T(8,128)S(1)}, u32[]{:S(2)}, u32[]{:S(2)}) collective-permute-start(f32[192,128]{1,0:T(8,128)S(1)} %add.16), channel_id=1, source_target_pairs={{0,32},{32,16},{16,48},{48,0},{1,33},{33,17},{17,49},{49,1},{2,34}... | collective-permute-start | bytes 294920 | tf_op jit(solution)/shard_map/ppermute | solution.py:284
  110.4 5.9 %collective-permute-start.25 = (f32[192,128]{1,0:T(8,128)S(1)}, f32[192,128]{1,0:T(8,128)S(1)}, u32[]{:S(2)}, u32[]{:S(2)}) collective-permute-start(f32[192,128]{1,0:T(8,128)S(1)} %add.16), channel_id=1, source_target_pairs={{0,48},{32,0},{16,32},{48,16},{1,49},{33,1},{17,33},{49,17},{2,50}... | collective-permute-start | bytes 294920 | tf_op jit(solution)/shard_map/ppermute | solution.py:284
  (7 other events, 11.4 us)

commit v7 on v5

--- a/solution.py
+++ b/solution.py
@@ -99,26 +99,25 @@
     here_y, z0, core = y_place(), lax.axis_index("z0"), lax.axis_index("core")
     copies[1].wait()
     copies[2].wait()
-    for k in range(4):
-        y = (here_y + k) & 3
-        base = (y >> 1) * (width // 2)
-        low = (y & 1) * HALF
+    for high in range(2):
+        base = ((here_y >> 1) ^ high) * (width // 2)
         for zrel in range(2):
             for crel in range(2):
                 for zh in range(4):
                     block = zh * 4 + (z0 ^ zrel) * 2 + (core ^ crel)
                     at = pl.multiple_of(base + block * 128, 128)
                     turned = act[:, pl.ds(at, 128)].T
-                    part = jnp.where(low == 0, turned[:HALF], turned[HALF:])
                     to = ((zrel * 2 + crel) * 4 + zh) * HALF
-                    rows_out[k][to : to + HALF, :] = part
+                    for low in range(2):
+                        part = jnp.where((here_y & 1) == low, turned[:HALF], turned[HALF:])
+                        rows_out[high * 2 + low][to : to + HALF, :] = part
     along = masked[...].astype(f32) * 1000.0 / ratio[0].astype(f32)
     line = lax.broadcasted_iota(jnp.int32, (tok, tok), 0)
     lane = lax.broadcasted_iota(jnp.int32, (tok, tok), 1)
     weight = jnp.sum(jnp.where(line == lane, along, 0.0), axis=1, keepdims=True)
     copies[3].wait()
     for k in range(4):
-        x = (lax.axis_index("x") + k) & 3
+        x = lax.axis_index("x") ^ k
         for j in range(8):
             slot = x * 4 + ((lax.axis_index("zh") + j // 2) & 3)
             head = meta[PERM_AT + slot * 2 + j % 2]
@@ -142,7 +141,7 @@
     return jnp.concatenate(left, axis=1), jnp.concatenate(right, axis=0)
 
 
-def multiply_near(r0, r1, r3, g0, g1, g3, out):
+def multiply_near(g0, r0, g1, r1, g3, r3, out):
     refs = (r0, r1, r3, None, None, g0, g1, g3, None, None)
     pairs = [(dx, dy) for dx in (0, 1, 3) for dy in (0, 1, 3)]
     for n in range(BLOCK // SLOT):
@@ -182,7 +181,7 @@
             out[h * 128 : (h + 1) * 128, :] = total.astype(out.dtype)
 
 
-def gram_part(t0, t1, t2, t3, head_grad, keep, send):
+def gram_part(t2, t1, t3, t0, head_grad, keep, send):
     total = (t0[...] + t1[...].astype(f32)) + (t2[...].astype(f32) + t3[...].astype(f32))
     part = total.astype(bf16)
     head_grad[...] = part
@@ -255,7 +254,7 @@
     update = update + jnp.dot(h, top, preferred_element_type=f32)
     result[...] = (update * (by_col * 64.0)).astype(bf16)
     for k, out in enumerate((o0, o1, o2, o3)):
-        at = pl.multiple_of(((zh + k) & 3) * HALF, HALF)
+        at = pl.multiple_of((zh ^ k) * HALF, HALF)
         out[...] = result[pl.ds(at, HALF), :]
 
 
@@ -265,7 +264,7 @@
     for i, refs in enumerate(((p0, p1, p2, p3), (q0, q1, q2, q3))):
         for dx in range(4):
             for dzh in range(4):
-                slot = ((x - dx) & 3) * 4 + ((zh - dzh) & 3)
+                slot = (x ^ dx) * 4 + (zh ^ dzh)
                 for j in range(2):
                     at = pl.multiple_of(meta[PERM_AT + slot * 2 + j] * HEAD, HEAD)
                     rows[i, :, pl.ds(at, HEAD)] = refs[dx][dzh, :, j * HEAD : (j + 1) * HEAD].astype(f32)
@@ -280,11 +279,11 @@
 
 
 def move_x(a, k):
-    return lax.ppermute(a, "x", [(i, (i + k) % 4) for i in range(4)])
+    return lax.ppermute(a, "x", [(i, i ^ (k & 3)) for i in range(4)])
 
 
 def move_y(a, k):
-    return lax.ppermute(a, ("ylo", "yhi"), [(Y_INDEX[i], Y_INDEX[(i + k) % 4]) for i in range(4)])
+    return lax.ppermute(a, ("ylo", "yhi"), [(Y_INDEX[i], Y_INDEX[i ^ (k & 3)]) for i in range(4)])
 
 
 def move_z(a, k):
@@ -306,7 +305,7 @@
         prepare,
         [shape((BLOCK, tok), bf16)] * 4 + [shape((tok, BLOCK), bf16)] * 4 + [shape((PERM_AT + HEADS,), jnp.int32)],
         (owners, ratios, masked[None, :], activations, cotangent),
-        16,
+        52,
         2 * tok * width,
         "prepare",
         in_specs=[hbm(), hbm(), vmem(), hbm(), hbm()],
@@ -326,13 +325,13 @@
     r0, g0 = jnp.stack(r0), jnp.stack(g0)
     r1, r3 = move_x(r0, 1), move_x(r0, -1)
     g1, g3 = move_y(g0, 1), move_y(g0, -1)
-    r2a, r2b = move_x(r1[:2], 1), move_x(r3[2:], -1)
-    g2a, g2b = move_y(g1[:2], 1), move_y(g3[2:], -1)
+    r2a, r2b = move_x(r1[:2], 3), move_x(r3[2:], 1)
+    g2a, g2b = move_y(g1[:2], 3), move_y(g3[2:], 1)
     gathered = (r0, r1, r3, r2a, r2b, g0, g1, g3, g2a, g2b)
 
     flops = 2 * BLOCK * BLOCK * tok
     (near,) = local_kernel(
-        multiply_near, [shape((BLOCK, BLOCK), f32)], (r0, r1, r3, g0, g1, g3), 32, 9 * flops, "multiply_near"
+        multiply_near, [shape((BLOCK, BLOCK), f32)], (g0, r0, g1, r1, g3, r3), 32, 9 * flops, "multiply_near"
     )
 
     def rest(odd, name):
@@ -367,7 +366,7 @@
     head_grad, mine, theirs = local_kernel(
         gram_part,
         [shape((256, SLOT), bf16), shape((GRAM, HEAD), f32), shape((GRAM, HEAD), f32)],
-        (t0, t1, t2, t3),
+        (t2, t1, t3, t0),
         8,
         2 * 256 * SLOT * SLOT,
         "gram_part",
@@ -385,7 +384,7 @@
         in_specs=[smem()] + [vmem()] * 3,
         scratch=[pltpu.VMEM((256, SLOT), bf16)],
     )
-    ring = lambda a, k: lax.ppermute(a, "zh", [(i, (i + k) % 4) for i in range(4)])
+    ring = lambda a, k: lax.ppermute(a, "zh", [(i, i ^ (k & 3)) for i in range(4)])
     p0 = jnp.stack(farthest_first(update, ring))
     q0 = swap(p0, "ylo")
     ps, qs = farthest_first([p0] * 4, move_x), farthest_first([q0] * 4, move_x)

time: 156 us -> 152 us (0.974)
  local copies, waits for them, and re-layouts: 3.89 us -> 1.44 us
  waiting for transfers between devices: 70.5 us -> 68.1 us
    ppermute x6, starting transfers between devices: 6.41 us -> 10.1 us  [swap(): return lax.ppermute(a, axis, [(0, 1), (1, 0)])]
    ppermute x26, starting transfers between devices: 43.4 us -> 40.4 us  [the longest x13 19.3 us: move_x(): return lax.ppermute(a, 'x', [(i, i ^ k & 3) for i in range(4)])]
    unnamed x8 -> x4, local copies, waits for them, and re-layouts: 3.75 us -> 1.3 us
  transfers between devices with their start and end apart: 37 -> 37, of which waited for: 20 -> 23; matrix products, arithmetic and copies ran while one was open for 0% -> 0% of each run, Pallas kernels for 3% -> 3%
where the time goes in v7:
time: 152 us
  waiting for transfers between devices  68.1 us (45%)
  starting transfers between devices  63.6 us (42%)
  Pallas kernels  17.3 us (11%)
    ppermute x13, waiting for transfers between devices, move_x(): return lax.ppermute(a, 'x', [(i, i ^ k & 3) for i in range(4)])  30 us
    ppermute x13, starting transfers between devices, move_x(): return lax.ppermute(a, 'x', [(i, i ^ k & 3) for i in range(4)])  19.3 us
    pallas_call x9, Pallas kernels, local_kernel(): pl.pallas_call(body, out_shape=outs, in_specs=in_specs or [vmem()] * len(...  17.3 us
    ppermute x5, waiting for transfers between devices, move_z(): return lax.ppermute(a, ('zh', 'z0'), [(i, (i + k) % 8) for i in range(8)])  15.5 us
    ppermute x10, starting transfers between devices, move_y(): lax.ppermute(a, ('ylo', 'yhi'), [(Y_INDEX[i], Y_INDEX[i ^ k & 3]) for i i...  15.4 us
    ppermute x10, waiting for transfers between devices, move_y(): lax.ppermute(a, ('ylo', 'yhi'), [(Y_INDEX[i], Y_INDEX[i ^ k & 3]) for i i...  13.6 us
    ppermute x5, starting transfers between devices, move_z(): return lax.ppermute(a, ('zh', 'z0'), [(i, (i + k) % 8) for i in range(8)])  13.1 us
    ppermute x6, starting transfers between devices, swap(): return lax.ppermute(a, axis, [(0, 1), (1, 0)])  10.1 us
  transfers between devices with their start and end apart: 37, of which 23 were waited for; matrix products, arithmetic and copies ran while one was open for 0% of the time, Pallas kernels for 3%

profile of v7, /device:TPU:1, one launch (start us, length us, event | category | flops | bytes accessed | tf_op | source)
XLA Modules:
  0.0 151.8 jit_solution(6115654492889342723)
XLA Ops:
  2.0 2.6 %prepare.1 = (bf16[1024,128]{1,0:T(8,128)(2,1)S(1)}, bf16[1024,128]{1,0:T(8,128)(2,1)S(1)}, bf16[1024,128]{1,0:T(8,128)(2,1)S(1)}, bf16[1024,128]{1,0:T(8,128)(2...) custom-call(s32[32]{0:T(128)S(1)} %copy-done, ...), custom_call_target="tpu_custom_call" | custom-call | flops 1048576 | bytes 4195108 | tf_op jit(solution)/shard_map/prepare/pallas_call | solution.py:43
  4.5 2.2 %collective-permute-start.3 = (bf16[1024,128]{1,0:T(8,128)(2,1)S(1)}, bf16[1024,128]{1,0:T(8,128)(2,1)S(1)}, u32[]{:S(2)}, u32[]{:S(2)}) collective-permute-start(bf16[1024,128]{1,0:T(8,128)(2,1)S(1)} %get-tuple-element.37), channel_id=1, source_target_pairs={{0,32},{32,0},{16,48},{48,16},{1,33},{33,1},{17,49},{49,17},{2,34}... | collective-permute-start | bytes 786440 | tf_op jit(solution)/shard_map/ppermute | solution.py:286
  6.7 2.6 %collective-permute-start.4 = (bf16[1024,128]{1,0:T(8,128)(2,1)S(1)}, bf16[1024,128]{1,0:T(8,128)(2,1)S(1)}, u32[]{:S(2)}, u32[]{:S(2)}) collective-permute-start(bf16[1024,128]{1,0:T(8,128)(2,1)S(1)} %get-tuple-element.38), channel_id=1, source_target_pairs={{0,16},{32,48},{16,0},{48,32},{1,17},{33,49},{17,1},{49,33},{2,18}... | collective-permute-start | bytes 786440 | tf_op jit(solution)/shard_map/ppermute | solution.py:286
  10.6 2.5 %collective-permute-start.1 = (bf16[128,1024]{1,0:T(8,128)(2,1)S(1)}, bf16[128,1024]{1,0:T(8,128)(2,1)S(1)}, u32[]{:S(2)}, u32[]{:S(2)}) collective-permute-start(bf16[128,1024]{1,0:T(8,128)(2,1)S(1)} %get-tuple-element.34), channel_id=1, source_target_pairs={{0,128},{64,192},{128,0},{192,64},{1,129},{65,193},{129,1},{193,65... | collective-permute-start | bytes 786440 | tf_op jit(solution)/shard_map/ppermute | solution.py:282
  15.1 5.6 %collective-permute-done.4 = bf16[1024,128]{1,0:T(8,128)(2,1)S(1)} collective-permute-done((bf16[1024,128]{1,0:T(8,128)(2,1)S(1)}, bf16[1024,128]{1,0:T(8,128)(2,1)S(1)}, u32[]{:S(2)}, u32[]{:S(2)}) %collective-permute-start.4) | collective-permute-done | bytes 262176 | tf_op jit(solution)/shard_map/ppermute | solution.py:286
  27.5 2.2 %collective-permute-start.8 = (bf16[4,128,1024]{2,1,0:T(8,128)(2,1)S(1)}, bf16[4,128,1024]{2,1,0:T(8,128)(2,1)S(1)}, u32[]{:S(2)}, u32[]{:S(2)}) collective-permute-start(bf16[4,128,1024]{2,1,0:T(8,128)(2,1)S(1)} %pad_maximum_fusion.g0.refs_5_), channel_id=1, source_target_pairs={{0,48},{32,16},{16,32},{48,0},{1,49},{33,17},{17,33},{49,1},{2,50}... | collective-permute-start | bytes 3145736 | tf_op jit(solution)/shard_map/ppermute | solution.py:286
  29.7 15.8 %collective-permute-done.7.r1.refs_1_ = bf16[4,1024,128]{2,1,0:T(8,128)(2,1)S(1)} collective-permute-done((bf16[4,1024,128]{2,1,0:T(8,128)(2,1)S(1)}, bf16[4,1024,128]{2,1,0:T(8,128)(2,1)S(1)}, u32[]{:S(2)}, u32[]{:S(2)}) %collective-permute-start.7) | collective-permute-done | bytes 1048608 | tf_op jit(solution)/shard_map/ppermute | solution.py:282
  45.5 2.6 %collective-permute-start.10 = (bf16[2,1024,128]{2,1,0:T(8,128)(2,1)S(1)}, bf16[2,1024,128]{2,1,0:T(8,128)(2,1)S(1)}, u32[]{:S(2)}, u32[]{:S(2)}) collective-permute-start(bf16[2,1024,128]{2,1,0:T(8,128)(2,1)S(1)} %slice.16), channel_id=1, source_target_pairs={{0,192},{64,128},{128,64},{192,0},{1,193},{65,129},{129,65},{193,1... | collective-permute-start | bytes 1572872 | tf_op jit(solution)/shard_map/ppermute | solution.py:282
  48.4 3.6 %collective-permute-start.12 = (bf16[2,128,1024]{2,1,0:T(8,128)(2,1)S(1)}, bf16[2,128,1024]{2,1,0:T(8,128)(2,1)S(1)}, u32[]{:S(2)}, u32[]{:S(2)}) collective-permute-start(bf16[2,128,1024]{2,1,0:T(8,128)(2,1)S(1)} %slice.18), channel_id=1, source_target_pairs={{0,48},{32,16},{16,32},{48,0},{1,49},{33,17},{17,33},{49,1},{2,50}... | collective-permute-start | bytes 1572872 | tf_op jit(solution)/shard_map/ppermute | solution.py:286
  52.2 2.9 %multiply_near.1.near = f32[1024,1024]{1,0:T(8,128)S(1)} custom-call(bf16[4,128,1024]{2,1,0:T(8,128)(2,1)S(1)} %pad_maximum_fusion.g0.refs_5_, bf16[4,1024,128]{2,1,0:T(8,128)(2,1)S(1)} %pad_maximum_fusion.1.r0.refs_0_, bf16[4,128,1024]{2,1,0:T(8,128)(2,1)S(1)} %collective-permute-done.6.g1.refs_6_, ...), custom_call_target="tpu_custom_call" | custom-call | flops 2415919104 | bytes 10485760 | tf_op jit(solution)/shard_map/multiply_near/pallas_call | solution.py:43
  55.0 4.8 %collective-permute-done.10.refs_3_ = bf16[2,1024,128]{2,1,0:T(8,128)(2,1)S(1)} collective-permute-done((bf16[2,1024,128]{2,1,0:T(8,128)(2,1)S(1)}, bf16[2,1024,128]{2,1,0:T(8,128)(2,1)S(1)}, u32[]{:S(2)}, u32[]{:S(2)}) %collective-permute-start.10) | collective-permute-done | bytes 524320 | tf_op jit(solution)/shard_map/ppermute | solution.py:282
  62.5 5.5 %collective-permute-start.15 = (bf16[8,128,256]{2,1,0:T(8,128)(2,1)S(1)}, bf16[8,128,256]{2,1,0:T(8,128)(2,1)S(1)}, u32[]{:S(2)}, u32[]{:S(2)}) collective-permute-start(bf16[8,128,256]{2,1,0:T(8,128)(2,1)S(1)} %get-tuple-element.43), channel_id=1, source_target_pairs={{0,1},{1,0},{2,3},{3,2},{4,5},{5,4},{6,7},{7,6},{8,9},{9,8},{10,11... | collective-permute-start | bytes 1572872 | tf_op jit(solution)/shard_map/ppermute | solution.py:294
  71.4 4.0 %collective-permute-start.17 = (bf16[4,128,256]{2,1,0:T(8,128)(2,1)S(1)}, bf16[4,128,256]{2,1,0:T(8,128)(2,1)S(1)}, u32[]{:S(2)}, u32[]{:S(2)}) collective-permute-start(bf16[4,128,256]{2,1,0:T(8,128)(2,1)S(1)} %get-tuple-element.45), channel_id=1, source_target_pairs={{0,14},{2,0},{4,2},{6,4},{8,6},{10,8},{12,10},{14,12},{1,15},{3,1}... | collective-permute-start | bytes 786440 | tf_op jit(solution)/shard_map/ppermute | solution.py:290
  75.4 6.3 %collective-permute-done.16.up = bf16[4,128,256]{2,1,0:T(8,128)(2,1)S(1)} collective-permute-done((bf16[4,128,256]{2,1,0:T(8,128)(2,1)S(1)}, bf16[4,128,256]{2,1,0:T(8,128)(2,1)S(1)}, u32[]{:S(2)}, u32[]{:S(2)}) %collective-permute-start.16) | collective-permute-done | bytes 262176 | tf_op jit(solution)/shard_map/ppermute | solution.py:290
  81.9 3.8 %collective-permute-start.18 = (bf16[256,256]{1,0:T(8,128)(2,1)S(1)}, bf16[256,256]{1,0:T(8,128)(2,1)S(1)}, u32[]{:S(2)}, u32[]{:S(2)}) collective-permute-start(bf16[256,256]{1,0:T(8,128)(2,1)S(1)} %get-tuple-element.46), channel_id=1, source_target_pairs={{0,8},{2,10},{4,12},{6,14},{8,0},{10,2},{12,4},{14,6},{1,9},{3,11}... | collective-permute-start | bytes 393224 | tf_op jit(solution)/shard_map/ppermute | solution.py:290
  86.1 3.2 %collective-permute-start.20 = (bf16[256,256]{1,0:T(8,128)(2,1)S(1)}, bf16[256,256]{1,0:T(8,128)(2,1)S(1)}, u32[]{:S(2)}, u32[]{:S(2)}) collective-permute-start(bf16[256,256]{1,0:T(8,128)(2,1)S(1)} %get-tuple-element.48), channel_id=1, source_target_pairs={{0,12},{2,14},{4,0},{6,2},{8,4},{10,6},{12,8},{14,10},{1,13},{3,15... | collective-permute-start | bytes 393224 | tf_op jit(solution)/shard_map/ppermute | solution.py:290
  90.0 6.1 %collective-permute-done.19.t1 = bf16[256,256]{1,0:T(8,128)(2,1)S(1)} collective-permute-done((bf16[256,256]{1,0:T(8,128)(2,1)S(1)}, bf16[256,256]{1,0:T(8,128)(2,1)S(1)}, u32[]{:S(2)}, u32[]{:S(2)}) %collective-permute-start.19) | collective-permute-done | bytes 131104 | tf_op jit(solution)/shard_map/ppermute | solution.py:290
  96.1 2.3 %collective-permute-done.20.t3 = bf16[256,256]{1,0:T(8,128)(2,1)S(1)} collective-permute-done((bf16[256,256]{1,0:T(8,128)(2,1)S(1)}, bf16[256,256]{1,0:T(8,128)(2,1)S(1)}, u32[]{:S(2)}, u32[]{:S(2)}) %collective-permute-start.20) | collective-permute-done | bytes 131104 | tf_op jit(solution)/shard_map/ppermute | solution.py:290
  102.3 2.9 %collective-permute-done.22 = f32[192,128]{1,0:T(8,128)S(1)} collective-permute-done((f32[192,128]{1,0:T(8,128)S(1)}, f32[192,128]{1,0:T(8,128)S(1)}, u32[]{:S(2)}, u32[]{:S(2)}) %collective-permute-start.22) | collective-permute-done | bytes 98336 | tf_op jit(solution)/shard_map/ppermute | solution.py:294
  115.8 6.8 %newton.1 = (bf16[64,256]{1,0:T(8,128)(2,1)S(1)}, bf16[64,256]{1,0:T(8,128)(2,1)S(1)}, bf16[64,256]{1,0:T(8,128)(2,1)S(1)}, bf16[64,256]{1,0:T(8,128)(2,1)S(1)}) custom-call(s32[40]{0:T(128)S(1)} %get-tuple-element.31.meta, f32[192,128]{1,0:T(8,128)S(1)} %add_add_fusion.mine, f32[192,128]{1,0:T(8,128)S(1)} %collective-permute-done.26.other, ...), custom_call_target="tpu_custom_call" | custom-call | flops 4026531840 | bytes 458912 | tf_op jit(solution)/shard_map/newton/pallas_call | solution.py:43
  124.3 3.1 %collective-permute-start.28 = (bf16[64,256]{1,0:T(8,128)(2,1)S(1)}, bf16[64,256]{1,0:T(8,128)(2,1)S(1)}, u32[]{:S(2)}, u32[]{:S(2)}) collective-permute-start(bf16[64,256]{1,0:T(8,128)(2,1)S(1)} %get-tuple-element.55), channel_id=1, source_target_pairs={{0,8},{4,12},{8,0},{12,4},{1,9},{5,13},{9,1},{13,5},{2,10},{6,14},... | collective-permute-start | bytes 98312 | tf_op jit(solution)/shard_map/ppermute | solution.py:387
  128.3 2.8 %collective-permute-done.28 = bf16[64,256]{1,0:T(8,128)(2,1)S(1)} collective-permute-done((bf16[64,256]{1,0:T(8,128)(2,1)S(1)}, bf16[64,256]{1,0:T(8,128)(2,1)S(1)}, u32[]{:S(2)}, u32[]{:S(2)}) %collective-permute-start.28) | collective-permute-done | bytes 32800 | tf_op jit(solution)/shard_map/ppermute | solution.py:387
  142.9 3.4 %collective-permute-done.35.q2 = bf16[4,64,256]{2,1,0:T(8,128)(2,1)S(1)} collective-permute-done((bf16[4,64,256]{2,1,0:T(8,128)(2,1)S(1)}, bf16[4,64,256]{2,1,0:T(8,128)(2,1)S(1)}, u32[]{:S(2)}, u32[]{:S(2)}) %collective-permute-start.35) | collective-permute-done | bytes 131104 | tf_op jit(solution)/shard_map/ppermute | solution.py:282
  146.3 3.3 %collective-permute-done.36.q3 = bf16[4,64,256]{2,1,0:T(8,128)(2,1)S(1)} collective-permute-done((bf16[4,64,256]{2,1,0:T(8,128)(2,1)S(1)}, bf16[4,64,256]{2,1,0:T(8,128)(2,1)S(1)}, u32[]{:S(2)}, u32[]{:S(2)}) %collective-permute-start.36) | collective-permute-done | bytes 131104 | tf_op jit(solution)/shard_map/ppermute | solution.py:282
  (73 shorter events, 50.0 us)
Async XLA Ops:
  4.5 8.5 %collective-permute-start.3 = (bf16[1024,128]{1,0:T(8,128)(2,1)S(1)}, bf16[1024,128]{1,0:T(8,128)(2,1)S(1)}, u32[]{:S(2)}, u32[]{:S(2)}) collective-permute-start(bf16[1024,128]{1,0:T(8,128)(2,1)S(1)} %get-tuple-element.37), channel_id=1, source_target_pairs={{0,32},{32,0},{16,48},{48,16},{1,33},{33,1},{17,49},{49,17},{2,34}... | collective-permute-start | bytes 786440 | tf_op jit(solution)/shard_map/ppermute | solution.py:286
  6.7 14.0 %collective-permute-start.4 = (bf16[1024,128]{1,0:T(8,128)(2,1)S(1)}, bf16[1024,128]{1,0:T(8,128)(2,1)S(1)}, u32[]{:S(2)}, u32[]{:S(2)}) collective-permute-start(bf16[1024,128]{1,0:T(8,128)(2,1)S(1)} %get-tuple-element.38), channel_id=1, source_target_pairs={{0,16},{32,48},{16,0},{48,32},{1,17},{33,49},{17,1},{49,33},{2,18}... | collective-permute-start | bytes 786440 | tf_op jit(solution)/shard_map/ppermute | solution.py:286
  9.4 13.4 %collective-permute-start.5 = (bf16[1024,128]{1,0:T(8,128)(2,1)S(1)}, bf16[1024,128]{1,0:T(8,128)(2,1)S(1)}, u32[]{:S(2)}, u32[]{:S(2)}) collective-permute-start(bf16[1024,128]{1,0:T(8,128)(2,1)S(1)} %get-tuple-element.39), channel_id=1, source_target_pairs={{0,48},{32,16},{16,32},{48,0},{1,49},{33,17},{17,33},{49,1},{2,50}... | collective-permute-start | bytes 786440 | tf_op jit(solution)/shard_map/ppermute | solution.py:286
  9.4 16.6 %collective-permute-start = (bf16[128,1024]{1,0:T(8,128)(2,1)S(1)}, bf16[128,1024]{1,0:T(8,128)(2,1)S(1)}, u32[]{:S(2)}, u32[]{:S(2)}) collective-permute-start(bf16[128,1024]{1,0:T(8,128)(2,1)S(1)} %get-tuple-element.33), channel_id=1, source_target_pairs={{0,64},{64,0},{128,192},{192,128},{1,65},{65,1},{129,193},{193,129... | collective-permute-start | bytes 786440 | tf_op jit(solution)/shard_map/ppermute | solution.py:282
  10.6 15.4 %collective-permute-start.1 = (bf16[128,1024]{1,0:T(8,128)(2,1)S(1)}, bf16[128,1024]{1,0:T(8,128)(2,1)S(1)}, u32[]{:S(2)}, u32[]{:S(2)}) collective-permute-start(bf16[128,1024]{1,0:T(8,128)(2,1)S(1)} %get-tuple-element.34), channel_id=1, source_target_pairs={{0,128},{64,192},{128,0},{192,64},{1,129},{65,193},{129,1},{193,65... | collective-permute-start | bytes 786440 | tf_op jit(solution)/shard_map/ppermute | solution.py:282
  13.0 13.0 %collective-permute-start.2 = (bf16[128,1024]{1,0:T(8,128)(2,1)}, bf16[128,1024]{1,0:T(8,128)(2,1)S(1)}, u32[]{:S(2)}, u32[]{:S(2)}) collective-permute-start(bf16[128,1024]{1,0:T(8,128)(2,1)} %get-tuple-element.35), channel_id=1, source_target_pairs={{0,192},{64,128},{128,64},{192,0},{1,193},{65,129},{129,65},{193,1... | collective-permute-start | bytes 786440 | tf_op jit(solution)/shard_map/ppermute | solution.py:282
  22.9 22.6 %collective-permute-start.7 = (bf16[4,1024,128]{2,1,0:T(8,128)(2,1)S(1)}, bf16[4,1024,128]{2,1,0:T(8,128)(2,1)S(1)}, u32[]{:S(2)}, u32[]{:S(2)}) collective-permute-start(bf16[4,1024,128]{2,1,0:T(8,128)(2,1)S(1)} %pad_maximum_fusion.1.r0.refs_0_), channel_id=1, source_target_pairs={{0,64},{64,0},{128,192},{192,128},{1,65},{65,1},{129,193},{193,129... | collective-permute-start | bytes 3145736 | tf_op jit(solution)/shard_map/ppermute | solution.py:282
  24.2 24.0 %collective-permute-start.9 = (bf16[4,1024,128]{2,1,0:T(8,128)(2,1)S(1)}, bf16[4,1024,128]{2,1,0:T(8,128)(2,1)S(1)}, u32[]{:S(2)}, u32[]{:S(2)}) collective-permute-start(bf16[4,1024,128]{2,1,0:T(8,128)(2,1)S(1)} %pad_maximum_fusion.1.r0.refs_0_), channel_id=1, source_target_pairs={{0,192},{64,128},{128,64},{192,0},{1,193},{65,129},{129,65},{193,1... | collective-permute-start | bytes 3145736 | tf_op jit(solution)/shard_map/ppermute | solution.py:282
  26.2 22.2 %collective-permute-start.6 = (bf16[4,128,1024]{2,1,0:T(8,128)(2,1)S(1)}, bf16[4,128,1024]{2,1,0:T(8,128)(2,1)S(1)}, u32[]{:S(2)}, u32[]{:S(2)}) collective-permute-start(bf16[4,128,1024]{2,1,0:T(8,128)(2,1)S(1)} %pad_maximum_fusion.g0.refs_5_), channel_id=1, source_target_pairs={{0,32},{32,0},{16,48},{48,16},{1,33},{33,1},{17,49},{49,17},{2,34}... | collective-permute-start | bytes 3145736 | tf_op jit(solution)/shard_map/ppermute | solution.py:286
  27.5 24.5 %collective-permute-start.8 = (bf16[4,128,1024]{2,1,0:T(8,128)(2,1)S(1)}, bf16[4,128,1024]{2,1,0:T(8,128)(2,1)S(1)}, u32[]{:S(2)}, u32[]{:S(2)}) collective-permute-start(bf16[4,128,1024]{2,1,0:T(8,128)(2,1)S(1)} %pad_maximum_fusion.g0.refs_5_), channel_id=1, source_target_pairs={{0,48},{32,16},{16,32},{48,0},{1,49},{33,17},{17,33},{49,1},{2,50}... | collective-permute-start | bytes 3145736 | tf_op jit(solution)/shard_map/ppermute | solution.py:286
  45.5 14.3 %collective-permute-start.10 = (bf16[2,1024,128]{2,1,0:T(8,128)(2,1)S(1)}, bf16[2,1024,128]{2,1,0:T(8,128)(2,1)S(1)}, u32[]{:S(2)}, u32[]{:S(2)}) collective-permute-start(bf16[2,1024,128]{2,1,0:T(8,128)(2,1)S(1)} %slice.16), channel_id=1, source_target_pairs={{0,192},{64,128},{128,64},{192,0},{1,193},{65,129},{129,65},{193,1... | collective-permute-start | bytes 1572872 | tf_op jit(solution)/shard_map/ppermute | solution.py:282
  48.2 11.6 %collective-permute-start.11 = (bf16[2,1024,128]{2,1,0:T(8,128)(2,1)S(1)}, bf16[2,1024,128]{2,1,0:T(8,128)(2,1)S(1)}, u32[]{:S(2)}, u32[]{:S(2)}) collective-permute-start(bf16[2,1024,128]{2,1,0:T(8,128)(2,1)S(1)} %slice.17), channel_id=1, source_target_pairs={{0,64},{64,0},{128,192},{192,128},{1,65},{65,1},{129,193},{193,129... | collective-permute-start | bytes 1572872 | tf_op jit(solution)/shard_map/ppermute | solution.py:282
  48.4 12.8 %collective-permute-start.12 = (bf16[2,128,1024]{2,1,0:T(8,128)(2,1)S(1)}, bf16[2,128,1024]{2,1,0:T(8,128)(2,1)S(1)}, u32[]{:S(2)}, u32[]{:S(2)}) collective-permute-start(bf16[2,128,1024]{2,1,0:T(8,128)(2,1)S(1)} %slice.18), channel_id=1, source_target_pairs={{0,48},{32,16},{16,32},{48,0},{1,49},{33,17},{17,33},{49,1},{2,50}... | collective-permute-start | bytes 1572872 | tf_op jit(solution)/shard_map/ppermute | solution.py:286
  52.1 9.2 %collective-permute-start.13 = (bf16[2,128,1024]{2,1,0:T(8,128)(2,1)S(1)}, bf16[2,128,1024]{2,1,0:T(8,128)(2,1)S(1)}, u32[]{:S(2)}, u32[]{:S(2)}) collective-permute-start(bf16[2,128,1024]{2,1,0:T(8,128)(2,1)S(1)} %slice.19), channel_id=1, source_target_pairs={{0,32},{32,0},{16,48},{48,16},{1,33},{33,1},{17,49},{49,17},{2,34}... | collective-permute-start | bytes 1572872 | tf_op jit(solution)/shard_map/ppermute | solution.py:286
  62.5 7.1 %collective-permute-start.15 = (bf16[8,128,256]{2,1,0:T(8,128)(2,1)S(1)}, bf16[8,128,256]{2,1,0:T(8,128)(2,1)S(1)}, u32[]{:S(2)}, u32[]{:S(2)}) collective-permute-start(bf16[8,128,256]{2,1,0:T(8,128)(2,1)S(1)} %get-tuple-element.43), channel_id=1, source_target_pairs={{0,1},{1,0},{2,3},{3,2},{4,5},{5,4},{6,7},{7,6},{8,9},{9,8},{10,11... | collective-permute-start | bytes 1572872 | tf_op jit(solution)/shard_map/ppermute | solution.py:294
  69.7 12.0 %collective-permute-start.16 = (bf16[4,128,256]{2,1,0:T(8,128)(2,1)S(1)}, bf16[4,128,256]{2,1,0:T(8,128)(2,1)S(1)}, u32[]{:S(2)}, u32[]{:S(2)}) collective-permute-start(bf16[4,128,256]{2,1,0:T(8,128)(2,1)S(1)} %get-tuple-element.44), channel_id=1, source_target_pairs={{0,2},{2,4},{4,6},{6,8},{8,10},{10,12},{12,14},{14,0},{1,3},{3,5},... | collective-permute-start | bytes 786440 | tf_op jit(solution)/shard_map/ppermute | solution.py:290
  71.4 10.3 %collective-permute-start.17 = (bf16[4,128,256]{2,1,0:T(8,128)(2,1)S(1)}, bf16[4,128,256]{2,1,0:T(8,128)(2,1)S(1)}, u32[]{:S(2)}, u32[]{:S(2)}) collective-permute-start(bf16[4,128,256]{2,1,0:T(8,128)(2,1)S(1)} %get-tuple-element.45), channel_id=1, source_target_pairs={{0,14},{2,0},{4,2},{6,4},{8,6},{10,8},{12,10},{14,12},{1,15},{3,1}... | collective-permute-start | bytes 786440 | tf_op jit(solution)/shard_map/ppermute | solution.py:290
  81.9 8.1 %collective-permute-start.18 = (bf16[256,256]{1,0:T(8,128)(2,1)S(1)}, bf16[256,256]{1,0:T(8,128)(2,1)S(1)}, u32[]{:S(2)}, u32[]{:S(2)}) collective-permute-start(bf16[256,256]{1,0:T(8,128)(2,1)S(1)} %get-tuple-element.46), channel_id=1, source_target_pairs={{0,8},{2,10},{4,12},{6,14},{8,0},{10,2},{12,4},{14,6},{1,9},{3,11}... | collective-permute-start | bytes 393224 | tf_op jit(solution)/shard_map/ppermute | solution.py:290
  85.7 10.5 %collective-permute-start.19 = (bf16[256,256]{1,0:T(8,128)(2,1)S(1)}, bf16[256,256]{1,0:T(8,128)(2,1)S(1)}, u32[]{:S(2)}, u32[]{:S(2)}) collective-permute-start(bf16[256,256]{1,0:T(8,128)(2,1)S(1)} %get-tuple-element.47), channel_id=1, source_target_pairs={{0,4},{2,6},{4,8},{6,10},{8,12},{10,14},{12,0},{14,2},{1,5},{3,7},... | collective-permute-start | bytes 393224 | tf_op jit(solution)/shard_map/ppermute | solution.py:290
  86.1 12.4 %collective-permute-start.20 = (bf16[256,256]{1,0:T(8,128)(2,1)S(1)}, bf16[256,256]{1,0:T(8,128)(2,1)S(1)}, u32[]{:S(2)}, u32[]{:S(2)}) collective-permute-start(bf16[256,256]{1,0:T(8,128)(2,1)S(1)} %get-tuple-element.48), channel_id=1, source_target_pairs={{0,12},{2,14},{4,0},{6,2},{8,4},{10,6},{12,8},{14,10},{1,13},{3,15... | collective-permute-start | bytes 393224 | tf_op jit(solution)/shard_map/ppermute | solution.py:290
  124.3 6.8 %collective-permute-start.28 = (bf16[64,256]{1,0:T(8,128)(2,1)S(1)}, bf16[64,256]{1,0:T(8,128)(2,1)S(1)}, u32[]{:S(2)}, u32[]{:S(2)}) collective-permute-start(bf16[64,256]{1,0:T(8,128)(2,1)S(1)} %get-tuple-element.55), channel_id=1, source_target_pairs={{0,8},{4,12},{8,0},{12,4},{1,9},{5,13},{9,1},{13,5},{2,10},{6,14},... | collective-permute-start | bytes 98312 | tf_op jit(solution)/shard_map/ppermute | solution.py:387
  132.5 7.2 %collective-permute-start.30 = (bf16[4,64,256]{2,1,0:T(8,128)(2,1)S(1)}, bf16[4,64,256]{2,1,0:T(8,128)(2,1)S(1)}, u32[]{:S(2)}, u32[]{:S(2)}) collective-permute-start(bf16[4,64,256]{2,1,0:T(8,128)(2,1)S(1)} %pad_maximum_fusion.2.p0), channel_id=1, source_target_pairs={{0,64},{64,0},{128,192},{192,128},{1,65},{65,1},{129,193},{193,129... | collective-permute-start | bytes 393224 | tf_op jit(solution)/shard_map/ppermute | solution.py:282
  137.7 8.7 %collective-permute-start.35 = (bf16[4,64,256]{2,1,0:T(8,128)(2,1)S(1)}, bf16[4,64,256]{2,1,0:T(8,128)(2,1)S(1)}, u32[]{:S(2)}, u32[]{:S(2)}) collective-permute-start(bf16[4,64,256]{2,1,0:T(8,128)(2,1)S(1)} %collective-permute-done.33.q0), channel_id=1, source_target_pairs={{0,128},{64,192},{128,0},{192,64},{1,129},{65,193},{129,1},{193,65... | collective-permute-start | bytes 393224 | tf_op jit(solution)/shard_map/ppermute | solution.py:282
  139.7 9.9 %collective-permute-start.36 = (bf16[4,64,256]{2,1,0:T(8,128)(2,1)S(1)}, bf16[4,64,256]{2,1,0:T(8,128)(2,1)S(1)}, u32[]{:S(2)}, u32[]{:S(2)}) collective-permute-start(bf16[4,64,256]{2,1,0:T(8,128)(2,1)S(1)} %collective-permute-done.33.q0), channel_id=1, source_target_pairs={{0,192},{64,128},{128,64},{192,0},{1,193},{65,129},{129,65},{193,1... | collective-permute-start | bytes 393224 | tf_op jit(solution)/shard_map/ppermute | solution.py:282
  (15 other events, 65.5 us)

commit v8 on v7

--- a/solution.py
+++ b/solution.py
@@ -20,6 +20,7 @@
 HEAD = 128
 SLOT = 2 * HEAD
 BLOCK = 1024
+PLACE = (1, 2, 0, 3)
 HALF = 64
 GRAM = HEAD + HALF
 
@@ -127,6 +128,7 @@
 
 
 def piece(near, opposite, i, j):
+    j = PLACE[j]
     return (opposite[j // 2], j % 2) if i == 2 else (near[i], j)
 
 
@@ -299,6 +301,10 @@
     return [arrays[0], move(arrays[1], 1), opposite, move(arrays[3], 3)]
 
 
+def far_to_front(arrays):
+    return [arrays[2], arrays[0], arrays[1], arrays[3]]
+
+
 def on_device(activations, cotangent, masked, ratios, owners):
     tok, width = activations.shape
     *blocks, meta = local_kernel(
@@ -322,7 +328,7 @@
     )
     rows, cols = blocks[:4], blocks[4:]
     r0, g0 = farthest_first(rows, move_y), farthest_first(cols, move_x)
-    r0, g0 = jnp.stack(r0), jnp.stack(g0)
+    r0, g0 = jnp.stack(far_to_front(r0)), jnp.stack(far_to_front(g0))
     r1, r3 = move_x(r0, 1), move_x(r0, -1)
     g1, g3 = move_y(g0, 1), move_y(g0, -1)
     r2a, r2b = move_x(r1[:2], 3), move_x(r3[2:], 1)
@@ -387,7 +393,8 @@
     ring = lambda a, k: lax.ppermute(a, "zh", [(i, i ^ (k & 3)) for i in range(4)])
     p0 = jnp.stack(farthest_first(update, ring))
     q0 = swap(p0, "ylo")
-    ps, qs = farthest_first([p0] * 4, move_x), farthest_first([q0] * 4, move_x)
+    ps = farthest_first([p0] * 4, move_x)
+    qs = [q0, move_x(q0, 1), swap(ps[2], "ylo"), swap(ps[3], "ylo")]
     (out,) = local_kernel(
         place_heads,
         [shape((2 * HALF, width), f32)],

time: 152 us -> 149 us (0.980)
  starting transfers between devices: 63.6 us -> 60.6 us
    ppermute x6 -> x8, waiting for transfers between devices: 4.95 us -> 8.92 us  [swap(): return lax.ppermute(a, axis, [(0, 1), (1, 0)])]
    ppermute x13 -> x11, waiting for transfers between devices: 30 us -> 26.7 us  [move_x(): return lax.ppermute(a, 'x', [(i, i ^ k & 3) for i in range(4)])]
    ppermute x13 -> x11, starting transfers between devices: 19.3 us -> 17.1 us  [move_x(): return lax.ppermute(a, 'x', [(i, i ^ k & 3) for i in range(4)])]
    ppermute x6 -> x8, starting transfers between devices: 10.1 us -> 10.2 us  [swap(): return lax.ppermute(a, axis, [(0, 1), (1, 0)])]
  transfers between devices with their start and end apart: 37 -> 37, of which waited for: 23 -> 22; matrix products, arithmetic and copies ran while one was open for 0% -> 0% of each run, Pallas kernels for 3% -> 3%
where the time goes in v8:
time: 149 us; the launch traced here: 148 us
  waiting for transfers between devices  67.5 us (45%)
  starting transfers between devices  60.6 us (41%)
  Pallas kernels  17.3 us (12%)
    ppermute x11, waiting for transfers between devices, move_x(): return lax.ppermute(a, 'x', [(i, i ^ k & 3) for i in range(4)])  26.7 us
    pallas_call x9, Pallas kernels, local_kernel(): pl.pallas_call(body, out_shape=outs, in_specs=in_specs or [vmem()] * len(...  17.3 us
    ppermute x11, starting transfers between devices, move_x(): return lax.ppermute(a, 'x', [(i, i ^ k & 3) for i in range(4)])  17.1 us
    ppermute x5, waiting for transfers between devices, move_z(): return lax.ppermute(a, ('zh', 'z0'), [(i, (i + k) % 8) for i in range(8)])  15.4 us
    ppermute x10, starting transfers between devices, move_y(): lax.ppermute(a, ('ylo', 'yhi'), [(Y_INDEX[i], Y_INDEX[i ^ k & 3]) for i i...  14.5 us
    ppermute x5, starting transfers between devices, move_z(): return lax.ppermute(a, ('zh', 'z0'), [(i, (i + k) % 8) for i in range(8)])  13.1 us
    ppermute x10, waiting for transfers between devices, move_y(): lax.ppermute(a, ('ylo', 'yhi'), [(Y_INDEX[i], Y_INDEX[i ^ k & 3]) for i i...  12.4 us
    ppermute x8, starting transfers between devices, swap(): return lax.ppermute(a, axis, [(0, 1), (1, 0)])  10.2 us
  transfers between devices with their start and end apart: 37, of which 22 were waited for; matrix products, arithmetic and copies ran while one was open for 0% of the time, Pallas kernels for 3%

profile of v8, /device:TPU:1, one launch (start us, length us, event | category | flops | bytes accessed | tf_op | source)
XLA Modules:
  0.0 148.1 jit_solution(10552339901774848004)
XLA Ops:
  2.0 2.6 %prepare.1 = (bf16[1024,128]{1,0:T(8,128)(2,1)S(1)}, bf16[1024,128]{1,0:T(8,128)(2,1)S(1)}, bf16[1024,128]{1,0:T(8,128)(2,1)S(1)}, bf16[1024,128]{1,0:T(8,128)(2...) custom-call(s32[32]{0:T(128)S(1)} %copy-done, ...), custom_call_target="tpu_custom_call" | custom-call | flops 1048576 | bytes 4195108 | tf_op jit(solution)/shard_map/prepare/pallas_call | solution.py:44
  4.5 3.8 %collective-permute-start.3 = (bf16[1024,128]{1,0:T(8,128)(2,1)S(1)}, bf16[1024,128]{1,0:T(8,128)(2,1)S(1)}, u32[]{:S(2)}, u32[]{:S(2)}) collective-permute-start(bf16[1024,128]{1,0:T(8,128)(2,1)S(1)} %get-tuple-element.36), channel_id=1, source_target_pairs={{0,16},{32,48},{16,0},{48,32},{1,17},{33,49},{17,1},{49,33},{2,18}... | collective-permute-start | bytes 786440 | tf_op jit(solution)/shard_map/ppermute | solution.py:288
  9.1 2.7 %collective-permute-start = (bf16[128,1024]{1,0:T(8,128)(2,1)S(1)}, bf16[128,1024]{1,0:T(8,128)(2,1)S(1)}, u32[]{:S(2)}, u32[]{:S(2)}) collective-permute-start(bf16[128,1024]{1,0:T(8,128)(2,1)S(1)} %get-tuple-element.32), channel_id=1, source_target_pairs={{0,128},{64,192},{128,0},{192,64},{1,129},{65,193},{129,1},{193,65... | collective-permute-start | bytes 786440 | tf_op jit(solution)/shard_map/ppermute | solution.py:284
  13.4 3.2 %collective-permute-start.2 = (bf16[128,1024]{1,0:T(8,128)(2,1)}, bf16[128,1024]{1,0:T(8,128)(2,1)S(1)}, u32[]{:S(2)}, u32[]{:S(2)}) collective-permute-start(bf16[128,1024]{1,0:T(8,128)(2,1)} %get-tuple-element.35), channel_id=1, source_target_pairs={{0,192},{64,128},{128,64},{192,0},{1,193},{65,129},{129,65},{193,1... | collective-permute-start | bytes 786440 | tf_op jit(solution)/shard_map/ppermute | solution.py:284
  16.6 3.5 %collective-permute-done.4 = bf16[1024,128]{1,0:T(8,128)(2,1)S(1)} collective-permute-done((bf16[1024,128]{1,0:T(8,128)(2,1)S(1)}, bf16[1024,128]{1,0:T(8,128)(2,1)S(1)}, u32[]{:S(2)}, u32[]{:S(2)}) %collective-permute-start.4) | collective-permute-done | bytes 262176 | tf_op jit(solution)/shard_map/ppermute | solution.py:288
  27.5 18.5 %collective-permute-done.7.r1.refs_1_ = bf16[4,1024,128]{2,1,0:T(8,128)(2,1)S(1)} collective-permute-done((bf16[4,1024,128]{2,1,0:T(8,128)(2,1)S(1)}, bf16[4,1024,128]{2,1,0:T(8,128)(2,1)S(1)}, u32[]{:S(2)}, u32[]{:S(2)}) %collective-permute-start.7) | collective-permute-done | bytes 1048608 | tf_op jit(solution)/shard_map/ppermute | solution.py:284
  47.8 3.1 %collective-permute-start.12 = (bf16[2,128,1024]{2,1,0:T(8,128)(2,1)S(1)}, bf16[2,128,1024]{2,1,0:T(8,128)(2,1)S(1)}, u32[]{:S(2)}, u32[]{:S(2)}) collective-permute-start(bf16[2,128,1024]{2,1,0:T(8,128)(2,1)S(1)} %slice.18), channel_id=1, source_target_pairs={{0,48},{32,16},{16,32},{48,0},{1,49},{33,17},{17,33},{49,1},{2,50}... | collective-permute-start | bytes 1572872 | tf_op jit(solution)/shard_map/ppermute | solution.py:288
  51.0 2.9 %multiply_near.1.near = f32[1024,1024]{1,0:T(8,128)S(1)} custom-call(bf16[4,128,1024]{2,1,0:T(8,128)(2,1)S(1)} %pad_maximum_fusion.g0.refs_5_, bf16[4,1024,128]{2,1,0:T(8,128)(2,1)S(1)} %pad_maximum_fusion.1.r0.refs_0_, bf16[4,128,1024]{2,1,0:T(8,128)(2,1)S(1)} %collective-permute-done.6.g1.refs_6_, ...), custom_call_target="tpu_custom_call" | custom-call | flops 2415919104 | bytes 10485760 | tf_op jit(solution)/shard_map/multiply_near/pallas_call | solution.py:44
  53.9 5.3 %collective-permute-done.10.refs_3_ = bf16[2,1024,128]{2,1,0:T(8,128)(2,1)S(1)} collective-permute-done((bf16[2,1024,128]{2,1,0:T(8,128)(2,1)S(1)}, bf16[2,1024,128]{2,1,0:T(8,128)(2,1)S(1)}, u32[]{:S(2)}, u32[]{:S(2)}) %collective-permute-start.10) | collective-permute-done | bytes 524320 | tf_op jit(solution)/shard_map/ppermute | solution.py:284
  63.6 3.3 %collective-permute-start.15 = (bf16[8,128,256]{2,1,0:T(8,128)(2,1)S(1)}, bf16[8,128,256]{2,1,0:T(8,128)(2,1)S(1)}, u32[]{:S(2)}, u32[]{:S(2)}) collective-permute-start(bf16[8,128,256]{2,1,0:T(8,128)(2,1)S(1)} %get-tuple-element.43), channel_id=1, source_target_pairs={{0,1},{1,0},{2,3},{3,2},{4,5},{5,4},{6,7},{7,6},{8,9},{9,8},{10,11... | collective-permute-start | bytes 1572872 | tf_op jit(solution)/shard_map/ppermute | solution.py:296
  70.3 4.0 %collective-permute-start.17 = (bf16[4,128,256]{2,1,0:T(8,128)(2,1)S(1)}, bf16[4,128,256]{2,1,0:T(8,128)(2,1)S(1)}, u32[]{:S(2)}, u32[]{:S(2)}) collective-permute-start(bf16[4,128,256]{2,1,0:T(8,128)(2,1)S(1)} %get-tuple-element.45), channel_id=1, source_target_pairs={{0,14},{2,0},{4,2},{6,4},{8,6},{10,8},{12,10},{14,12},{1,15},{3,1}... | collective-permute-start | bytes 786440 | tf_op jit(solution)/shard_map/ppermute | solution.py:292
  74.3 6.3 %collective-permute-done.16.up = bf16[4,128,256]{2,1,0:T(8,128)(2,1)S(1)} collective-permute-done((bf16[4,128,256]{2,1,0:T(8,128)(2,1)S(1)}, bf16[4,128,256]{2,1,0:T(8,128)(2,1)S(1)}, u32[]{:S(2)}, u32[]{:S(2)}) %collective-permute-start.16) | collective-permute-done | bytes 262176 | tf_op jit(solution)/shard_map/ppermute | solution.py:292
  80.8 3.8 %collective-permute-start.18 = (bf16[256,256]{1,0:T(8,128)(2,1)S(1)}, bf16[256,256]{1,0:T(8,128)(2,1)S(1)}, u32[]{:S(2)}, u32[]{:S(2)}) collective-permute-start(bf16[256,256]{1,0:T(8,128)(2,1)S(1)} %get-tuple-element.46), channel_id=1, source_target_pairs={{0,8},{2,10},{4,12},{6,14},{8,0},{10,2},{12,4},{14,6},{1,9},{3,11}... | collective-permute-start | bytes 393224 | tf_op jit(solution)/shard_map/ppermute | solution.py:292
  84.9 3.2 %collective-permute-start.20 = (bf16[256,256]{1,0:T(8,128)(2,1)S(1)}, bf16[256,256]{1,0:T(8,128)(2,1)S(1)}, u32[]{:S(2)}, u32[]{:S(2)}) collective-permute-start(bf16[256,256]{1,0:T(8,128)(2,1)S(1)} %get-tuple-element.48), channel_id=1, source_target_pairs={{0,12},{2,14},{4,0},{6,2},{8,4},{10,6},{12,8},{14,10},{1,13},{3,15... | collective-permute-start | bytes 393224 | tf_op jit(solution)/shard_map/ppermute | solution.py:292
  88.9 6.1 %collective-permute-done.19.t1 = bf16[256,256]{1,0:T(8,128)(2,1)S(1)} collective-permute-done((bf16[256,256]{1,0:T(8,128)(2,1)S(1)}, bf16[256,256]{1,0:T(8,128)(2,1)S(1)}, u32[]{:S(2)}, u32[]{:S(2)}) %collective-permute-start.19) | collective-permute-done | bytes 131104 | tf_op jit(solution)/shard_map/ppermute | solution.py:292
  95.0 2.3 %collective-permute-done.20.t3 = bf16[256,256]{1,0:T(8,128)(2,1)S(1)} collective-permute-done((bf16[256,256]{1,0:T(8,128)(2,1)S(1)}, bf16[256,256]{1,0:T(8,128)(2,1)S(1)}, u32[]{:S(2)}, u32[]{:S(2)}) %collective-permute-start.20) | collective-permute-done | bytes 131104 | tf_op jit(solution)/shard_map/ppermute | solution.py:292
  99.1 2.1 %collective-permute-start.22 = (f32[192,128]{1,0:T(8,128)S(1)}, f32[192,128]{1,0:T(8,128)S(1)}, u32[]{:S(2)}, u32[]{:S(2)}) collective-permute-start(f32[192,128]{1,0:T(8,128)S(1)} %add.15), channel_id=1, source_target_pairs={{0,2},{2,0},{1,3},{3,1},{4,6},{6,4},{5,7},{7,5},{8,10},{10,8},{9,1... | collective-permute-start | bytes 294920 | tf_op jit(solution)/shard_map/ppermute | solution.py:296
  101.2 2.9 %collective-permute-done.22 = f32[192,128]{1,0:T(8,128)S(1)} collective-permute-done((f32[192,128]{1,0:T(8,128)S(1)}, f32[192,128]{1,0:T(8,128)S(1)}, u32[]{:S(2)}, u32[]{:S(2)}) %collective-permute-start.22) | collective-permute-done | bytes 98336 | tf_op jit(solution)/shard_map/ppermute | solution.py:296
  114.6 6.8 %newton.1 = (bf16[64,256]{1,0:T(8,128)(2,1)S(1)}, bf16[64,256]{1,0:T(8,128)(2,1)S(1)}, bf16[64,256]{1,0:T(8,128)(2,1)S(1)}, bf16[64,256]{1,0:T(8,128)(2,1)S(1)}) custom-call(s32[40]{0:T(128)S(1)} %get-tuple-element.31.meta, f32[192,128]{1,0:T(8,128)S(1)} %add_add_fusion.mine, f32[192,128]{1,0:T(8,128)S(1)} %collective-permute-done.26.other, ...), custom_call_target="tpu_custom_call" | custom-call | flops 4026531840 | bytes 458912 | tf_op jit(solution)/shard_map/newton/pallas_call | solution.py:44
  123.0 3.1 %collective-permute-start.28 = (bf16[64,256]{1,0:T(8,128)(2,1)S(1)}, bf16[64,256]{1,0:T(8,128)(2,1)S(1)}, u32[]{:S(2)}, u32[]{:S(2)}) collective-permute-start(bf16[64,256]{1,0:T(8,128)(2,1)S(1)} %get-tuple-element.55), channel_id=1, source_target_pairs={{0,8},{4,12},{8,0},{12,4},{1,9},{5,13},{9,1},{13,5},{2,10},{6,14},... | collective-permute-start | bytes 98312 | tf_op jit(solution)/shard_map/ppermute | solution.py:393
  127.1 2.7 %collective-permute-done.28 = bf16[64,256]{1,0:T(8,128)(2,1)S(1)} collective-permute-done((bf16[64,256]{1,0:T(8,128)(2,1)S(1)}, bf16[64,256]{1,0:T(8,128)(2,1)S(1)}, u32[]{:S(2)}, u32[]{:S(2)}) %collective-permute-start.28) | collective-permute-done | bytes 32800 | tf_op jit(solution)/shard_map/ppermute | solution.py:393
  131.3 2.5 %collective-permute-start.31 = (bf16[4,64,256]{2,1,0:T(8,128)(2,1)S(1)}, bf16[4,64,256]{2,1,0:T(8,128)(2,1)S(1)}, u32[]{:S(2)}, u32[]{:S(2)}) collective-permute-start(bf16[4,64,256]{2,1,0:T(8,128)(2,1)S(1)} %pad_maximum_fusion.2.p0), channel_id=1, source_target_pairs={{0,128},{64,192},{128,0},{192,64},{1,129},{65,193},{129,1},{193,65... | collective-permute-start | bytes 393224 | tf_op jit(solution)/shard_map/ppermute | solution.py:284
  138.1 2.6 %collective-permute-done.32.p3 = bf16[4,64,256]{2,1,0:T(8,128)(2,1)S(1)} collective-permute-done((bf16[4,64,256]{2,1,0:T(8,128)(2,1)S(1)}, bf16[4,64,256]{2,1,0:T(8,128)(2,1)S(1)}, u32[]{:S(2)}, u32[]{:S(2)}) %collective-permute-start.32) | collective-permute-done | bytes 131104 | tf_op jit(solution)/shard_map/ppermute | solution.py:284
  142.0 4.0 %collective-permute-done.36.q3 = bf16[4,64,256]{2,1,0:T(8,128)(2,1)S(1)} collective-permute-done((bf16[4,64,256]{2,1,0:T(8,128)(2,1)S(1)}, bf16[4,64,256]{2,1,0:T(8,128)(2,1)S(1)}, u32[]{:S(2)}, u32[]{:S(2)}) %collective-permute-start.36) | collective-permute-done | bytes 131104 | tf_op jit(solution)/shard_map/ppermute | solution.py:296
  (73 shorter events, 45.8 us)
Async XLA Ops:
  4.5 8.8 %collective-permute-start.3 = (bf16[1024,128]{1,0:T(8,128)(2,1)S(1)}, bf16[1024,128]{1,0:T(8,128)(2,1)S(1)}, u32[]{:S(2)}, u32[]{:S(2)}) collective-permute-start(bf16[1024,128]{1,0:T(8,128)(2,1)S(1)} %get-tuple-element.36), channel_id=1, source_target_pairs={{0,16},{32,48},{16,0},{48,32},{1,17},{33,49},{17,1},{49,33},{2,18}... | collective-permute-start | bytes 786440 | tf_op jit(solution)/shard_map/ppermute | solution.py:288
  8.4 11.8 %collective-permute-start.4 = (bf16[1024,128]{1,0:T(8,128)(2,1)S(1)}, bf16[1024,128]{1,0:T(8,128)(2,1)S(1)}, u32[]{:S(2)}, u32[]{:S(2)}) collective-permute-start(bf16[1024,128]{1,0:T(8,128)(2,1)S(1)} %get-tuple-element.38), channel_id=1, source_target_pairs={{0,32},{32,0},{16,48},{48,16},{1,33},{33,1},{17,49},{49,17},{2,34}... | collective-permute-start | bytes 786440 | tf_op jit(solution)/shard_map/ppermute | solution.py:288
  8.8 11.4 %collective-permute-start.5 = (bf16[1024,128]{1,0:T(8,128)(2,1)S(1)}, bf16[1024,128]{1,0:T(8,128)(2,1)S(1)}, u32[]{:S(2)}, u32[]{:S(2)}) collective-permute-start(bf16[1024,128]{1,0:T(8,128)(2,1)S(1)} %get-tuple-element.39), channel_id=1, source_target_pairs={{0,48},{32,16},{16,32},{48,0},{1,49},{33,17},{17,33},{49,1},{2,50}... | collective-permute-start | bytes 786440 | tf_op jit(solution)/shard_map/ppermute | solution.py:288
  9.1 14.9 %collective-permute-start = (bf16[128,1024]{1,0:T(8,128)(2,1)S(1)}, bf16[128,1024]{1,0:T(8,128)(2,1)S(1)}, u32[]{:S(2)}, u32[]{:S(2)}) collective-permute-start(bf16[128,1024]{1,0:T(8,128)(2,1)S(1)} %get-tuple-element.32), channel_id=1, source_target_pairs={{0,128},{64,192},{128,0},{192,64},{1,129},{65,193},{129,1},{193,65... | collective-permute-start | bytes 786440 | tf_op jit(solution)/shard_map/ppermute | solution.py:284
  11.9 12.1 %collective-permute-start.1 = (bf16[128,1024]{1,0:T(8,128)(2,1)S(1)}, bf16[128,1024]{1,0:T(8,128)(2,1)S(1)}, u32[]{:S(2)}, u32[]{:S(2)}) collective-permute-start(bf16[128,1024]{1,0:T(8,128)(2,1)S(1)} %get-tuple-element.34), channel_id=1, source_target_pairs={{0,64},{64,0},{128,192},{192,128},{1,65},{65,1},{129,193},{193,129... | collective-permute-start | bytes 786440 | tf_op jit(solution)/shard_map/ppermute | solution.py:284
  13.4 10.6 %collective-permute-start.2 = (bf16[128,1024]{1,0:T(8,128)(2,1)}, bf16[128,1024]{1,0:T(8,128)(2,1)S(1)}, u32[]{:S(2)}, u32[]{:S(2)}) collective-permute-start(bf16[128,1024]{1,0:T(8,128)(2,1)} %get-tuple-element.35), channel_id=1, source_target_pairs={{0,192},{64,128},{128,64},{192,0},{1,193},{65,129},{129,65},{193,1... | collective-permute-start | bytes 786440 | tf_op jit(solution)/shard_map/ppermute | solution.py:284
  20.3 25.7 %collective-permute-start.7 = (bf16[4,1024,128]{2,1,0:T(8,128)(2,1)S(1)}, bf16[4,1024,128]{2,1,0:T(8,128)(2,1)S(1)}, u32[]{:S(2)}, u32[]{:S(2)}) collective-permute-start(bf16[4,1024,128]{2,1,0:T(8,128)(2,1)S(1)} %pad_maximum_fusion.1.r0.refs_0_), channel_id=1, source_target_pairs={{0,64},{64,0},{128,192},{192,128},{1,65},{65,1},{129,193},{193,129... | collective-permute-start | bytes 3145736 | tf_op jit(solution)/shard_map/ppermute | solution.py:284
  22.2 25.2 %collective-permute-start.9 = (bf16[4,1024,128]{2,1,0:T(8,128)(2,1)S(1)}, bf16[4,1024,128]{2,1,0:T(8,128)(2,1)S(1)}, u32[]{:S(2)}, u32[]{:S(2)}) collective-permute-start(bf16[4,1024,128]{2,1,0:T(8,128)(2,1)S(1)} %pad_maximum_fusion.1.r0.refs_0_), channel_id=1, source_target_pairs={{0,192},{64,128},{128,64},{192,0},{1,193},{65,129},{129,65},{193,1... | collective-permute-start | bytes 3145736 | tf_op jit(solution)/shard_map/ppermute | solution.py:284
  24.2 23.6 %collective-permute-start.6 = (bf16[4,128,1024]{2,1,0:T(8,128)(2,1)S(1)}, bf16[4,128,1024]{2,1,0:T(8,128)(2,1)S(1)}, u32[]{:S(2)}, u32[]{:S(2)}) collective-permute-start(bf16[4,128,1024]{2,1,0:T(8,128)(2,1)S(1)} %pad_maximum_fusion.g0.refs_5_), channel_id=1, source_target_pairs={{0,32},{32,0},{16,48},{48,16},{1,33},{33,1},{17,49},{49,17},{2,34}... | collective-permute-start | bytes 3145736 | tf_op jit(solution)/shard_map/ppermute | solution.py:288
  25.6 25.3 %collective-permute-start.8 = (bf16[4,128,1024]{2,1,0:T(8,128)(2,1)S(1)}, bf16[4,128,1024]{2,1,0:T(8,128)(2,1)S(1)}, u32[]{:S(2)}, u32[]{:S(2)}) collective-permute-start(bf16[4,128,1024]{2,1,0:T(8,128)(2,1)S(1)} %pad_maximum_fusion.g0.refs_5_), channel_id=1, source_target_pairs={{0,48},{32,16},{16,32},{48,0},{1,49},{33,17},{17,33},{49,1},{2,50}... | collective-permute-start | bytes 3145736 | tf_op jit(solution)/shard_map/ppermute | solution.py:288
  46.0 13.2 %collective-permute-start.10 = (bf16[2,1024,128]{2,1,0:T(8,128)(2,1)S(1)}, bf16[2,1024,128]{2,1,0:T(8,128)(2,1)S(1)}, u32[]{:S(2)}, u32[]{:S(2)}) collective-permute-start(bf16[2,1024,128]{2,1,0:T(8,128)(2,1)S(1)} %slice.16), channel_id=1, source_target_pairs={{0,192},{64,128},{128,64},{192,0},{1,193},{65,129},{129,65},{193,1... | collective-permute-start | bytes 1572872 | tf_op jit(solution)/shard_map/ppermute | solution.py:284
  47.4 11.8 %collective-permute-start.11 = (bf16[2,1024,128]{2,1,0:T(8,128)(2,1)S(1)}, bf16[2,1024,128]{2,1,0:T(8,128)(2,1)S(1)}, u32[]{:S(2)}, u32[]{:S(2)}) collective-permute-start(bf16[2,1024,128]{2,1,0:T(8,128)(2,1)S(1)} %slice.17), channel_id=1, source_target_pairs={{0,64},{64,0},{128,192},{192,128},{1,65},{65,1},{129,193},{193,129... | collective-permute-start | bytes 1572872 | tf_op jit(solution)/shard_map/ppermute | solution.py:284
  47.8 13.3 %collective-permute-start.12 = (bf16[2,128,1024]{2,1,0:T(8,128)(2,1)S(1)}, bf16[2,128,1024]{2,1,0:T(8,128)(2,1)S(1)}, u32[]{:S(2)}, u32[]{:S(2)}) collective-permute-start(bf16[2,128,1024]{2,1,0:T(8,128)(2,1)S(1)} %slice.18), channel_id=1, source_target_pairs={{0,48},{32,16},{16,32},{48,0},{1,49},{33,17},{17,33},{49,1},{2,50}... | collective-permute-start | bytes 1572872 | tf_op jit(solution)/shard_map/ppermute | solution.py:288
  50.9 11.4 %collective-permute-start.13 = (bf16[2,128,1024]{2,1,0:T(8,128)(2,1)S(1)}, bf16[2,128,1024]{2,1,0:T(8,128)(2,1)S(1)}, u32[]{:S(2)}, u32[]{:S(2)}) collective-permute-start(bf16[2,128,1024]{2,1,0:T(8,128)(2,1)S(1)} %slice.19), channel_id=1, source_target_pairs={{0,32},{32,0},{16,48},{48,16},{1,33},{33,1},{17,49},{49,17},{2,34}... | collective-permute-start | bytes 1572872 | tf_op jit(solution)/shard_map/ppermute | solution.py:288
  68.5 12.0 %collective-permute-start.16 = (bf16[4,128,256]{2,1,0:T(8,128)(2,1)S(1)}, bf16[4,128,256]{2,1,0:T(8,128)(2,1)S(1)}, u32[]{:S(2)}, u32[]{:S(2)}) collective-permute-start(bf16[4,128,256]{2,1,0:T(8,128)(2,1)S(1)} %get-tuple-element.44), channel_id=1, source_target_pairs={{0,2},{2,4},{4,6},{6,8},{8,10},{10,12},{12,14},{14,0},{1,3},{3,5},... | collective-permute-start | bytes 786440 | tf_op jit(solution)/shard_map/ppermute | solution.py:292
  70.3 10.3 %collective-permute-start.17 = (bf16[4,128,256]{2,1,0:T(8,128)(2,1)S(1)}, bf16[4,128,256]{2,1,0:T(8,128)(2,1)S(1)}, u32[]{:S(2)}, u32[]{:S(2)}) collective-permute-start(bf16[4,128,256]{2,1,0:T(8,128)(2,1)S(1)} %get-tuple-element.45), channel_id=1, source_target_pairs={{0,14},{2,0},{4,2},{6,4},{8,6},{10,8},{12,10},{14,12},{1,15},{3,1}... | collective-permute-start | bytes 786440 | tf_op jit(solution)/shard_map/ppermute | solution.py:292
  80.8 8.1 %collective-permute-start.18 = (bf16[256,256]{1,0:T(8,128)(2,1)S(1)}, bf16[256,256]{1,0:T(8,128)(2,1)S(1)}, u32[]{:S(2)}, u32[]{:S(2)}) collective-permute-start(bf16[256,256]{1,0:T(8,128)(2,1)S(1)} %get-tuple-element.46), channel_id=1, source_target_pairs={{0,8},{2,10},{4,12},{6,14},{8,0},{10,2},{12,4},{14,6},{1,9},{3,11}... | collective-permute-start | bytes 393224 | tf_op jit(solution)/shard_map/ppermute | solution.py:292
  84.5 10.5 %collective-permute-start.19 = (bf16[256,256]{1,0:T(8,128)(2,1)S(1)}, bf16[256,256]{1,0:T(8,128)(2,1)S(1)}, u32[]{:S(2)}, u32[]{:S(2)}) collective-permute-start(bf16[256,256]{1,0:T(8,128)(2,1)S(1)} %get-tuple-element.47), channel_id=1, source_target_pairs={{0,4},{2,6},{4,8},{6,10},{8,12},{10,14},{12,0},{14,2},{1,5},{3,7},... | collective-permute-start | bytes 393224 | tf_op jit(solution)/shard_map/ppermute | solution.py:292
  84.9 12.4 %collective-permute-start.20 = (bf16[256,256]{1,0:T(8,128)(2,1)S(1)}, bf16[256,256]{1,0:T(8,128)(2,1)S(1)}, u32[]{:S(2)}, u32[]{:S(2)}) collective-permute-start(bf16[256,256]{1,0:T(8,128)(2,1)S(1)} %get-tuple-element.48), channel_id=1, source_target_pairs={{0,12},{2,14},{4,0},{6,2},{8,4},{10,6},{12,8},{14,10},{1,13},{3,15... | collective-permute-start | bytes 393224 | tf_op jit(solution)/shard_map/ppermute | solution.py:292
  105.8 6.2 %collective-permute-start.25 = (f32[192,128]{1,0:T(8,128)S(1)}, f32[192,128]{1,0:T(8,128)S(1)}, u32[]{:S(2)}, u32[]{:S(2)}) collective-permute-start(f32[192,128]{1,0:T(8,128)S(1)} %add.16), channel_id=1, source_target_pairs={{0,48},{32,16},{16,32},{48,0},{1,49},{33,17},{17,33},{49,1},{2,50}... | collective-permute-start | bytes 294920 | tf_op jit(solution)/shard_map/ppermute | solution.py:288
  123.0 6.8 %collective-permute-start.28 = (bf16[64,256]{1,0:T(8,128)(2,1)S(1)}, bf16[64,256]{1,0:T(8,128)(2,1)S(1)}, u32[]{:S(2)}, u32[]{:S(2)}) collective-permute-start(bf16[64,256]{1,0:T(8,128)(2,1)S(1)} %get-tuple-element.55), channel_id=1, source_target_pairs={{0,8},{4,12},{8,0},{12,4},{1,9},{5,13},{9,1},{13,5},{2,10},{6,14},... | collective-permute-start | bytes 98312 | tf_op jit(solution)/shard_map/ppermute | solution.py:393
  133.8 6.8 %collective-permute-start.32 = (bf16[4,64,256]{2,1,0:T(8,128)(2,1)S(1)}, bf16[4,64,256]{2,1,0:T(8,128)(2,1)S(1)}, u32[]{:S(2)}, u32[]{:S(2)}) collective-permute-start(bf16[4,64,256]{2,1,0:T(8,128)(2,1)S(1)} %pad_maximum_fusion.2.p0), channel_id=1, source_target_pairs={{0,192},{64,128},{128,64},{192,0},{1,193},{65,129},{129,65},{193,1... | collective-permute-start | bytes 393224 | tf_op jit(solution)/shard_map/ppermute | solution.py:284
  135.2 6.5 %collective-permute-start.30 = (bf16[4,64,256]{2,1,0:T(8,128)(2,1)S(1)}, bf16[4,64,256]{2,1,0:T(8,128)(2,1)S(1)}, u32[]{:S(2)}, u32[]{:S(2)}) collective-permute-start(bf16[4,64,256]{2,1,0:T(8,128)(2,1)S(1)} %pad_maximum_fusion.2.p0), channel_id=1, source_target_pairs={{0,64},{64,0},{128,192},{192,128},{1,65},{65,1},{129,193},{193,129... | collective-permute-start | bytes 393224 | tf_op jit(solution)/shard_map/ppermute | solution.py:284
  135.2 6.8 %collective-permute-start.34 = (bf16[4,64,256]{2,1,0:T(8,128)(2,1)S(1)}, bf16[4,64,256]{2,1,0:T(8,128)(2,1)S(1)}, u32[]{:S(2)}, u32[]{:S(2)}) collective-permute-start(bf16[4,64,256]{2,1,0:T(8,128)(2,1)S(1)} %collective-permute-done.33.q0), channel_id=1, source_target_pairs={{0,64},{64,0},{128,192},{192,128},{1,65},{65,1},{129,193},{193,129... | collective-permute-start | bytes 393224 | tf_op jit(solution)/shard_map/ppermute | solution.py:284
  (15 other events, 62.5 us)

commit v9 on v8

--- a/solution.py
+++ b/solution.py
@@ -39,7 +39,7 @@
     return pl.BlockSpec(memory_space=pltpu.HBM)
 
 
-def local_kernel(body, outs, operands, mib, flops, name, in_specs=None, out_specs=None, scratch=()):
+def local_kernel(body, outs, operands, mib, flops, name, in_specs=None, out_specs=None, scratch=(), aliases=None):
     moved = sum(o.size * o.dtype.itemsize for o in list(outs) + list(operands))
     return pl.pallas_call(
         body,
@@ -47,6 +47,7 @@
         in_specs=in_specs or [vmem()] * len(operands),
         out_specs=out_specs or [vmem()] * len(outs),
         scratch_shapes=list(scratch),
+        input_output_aliases=aliases or {},
         compiler_params=pltpu.CompilerParams(vmem_limit_bytes=mib * 2**20),
         cost_estimate=pl.CostEstimate(flops=flops, bytes_accessed=moved, transcendentals=0),
         name=name,
@@ -260,21 +261,19 @@
         out[...] = result[pl.ds(at, HALF), :]
 
 
-def place_heads(meta, p0, p1, p2, p3, q0, q1, q2, q3, out, rows, sems):
+def place_heads(other, meta, *refs):
+    blocks, (out, rows, sem) = refs[:4], refs[-3:]
     ylo, x, zh = lax.axis_index("ylo"), lax.axis_index("x"), lax.axis_index("zh")
-    copies = []
-    for i, refs in enumerate(((p0, p1, p2, p3), (q0, q1, q2, q3))):
-        for dx in range(4):
-            for dzh in range(4):
-                slot = (x ^ dx) * 4 + (zh ^ dzh)
-                for j in range(2):
-                    at = pl.multiple_of(meta[PERM_AT + slot * 2 + j] * HEAD, HEAD)
-                    rows[i, :, pl.ds(at, HEAD)] = refs[dx][dzh, :, j * HEAD : (j + 1) * HEAD].astype(f32)
-        half = pl.ds(pl.multiple_of((ylo ^ i) * HALF, HALF), HALF)
-        copies.append(pltpu.make_async_copy(rows.at[i], out.at[half, :], sems.at[i]))
-        copies[i].start()
-    for copy in copies:
-        copy.wait()
+    for dx in range(4):
+        for dzh in range(4):
+            slot = (x ^ dx) * 4 + (zh ^ dzh)
+            for j in range(2):
+                at = pl.multiple_of(meta[PERM_AT + slot * 2 + j] * HEAD, HEAD)
+                rows[:, pl.ds(at, HEAD)] = blocks[dx][dzh, :, j * HEAD : (j + 1) * HEAD].astype(f32)
+    half = pl.ds(pl.multiple_of((ylo ^ other) * HALF, HALF), HALF)
+    copy = pltpu.make_async_copy(rows, out.at[half, :], sem)
+    copy.start()
+    copy.wait()
 
 
 Y_INDEX = (0, 2, 1, 3)
@@ -395,17 +394,21 @@
     q0 = swap(p0, "ylo")
     ps = farthest_first([p0] * 4, move_x)
     qs = [q0, move_x(q0, 1), swap(ps[2], "ylo"), swap(ps[3], "ylo")]
-    (out,) = local_kernel(
-        place_heads,
-        [shape((2 * HALF, width), f32)],
-        (meta, *ps, *qs),
-        12,
-        0,
-        "place_heads",
-        in_specs=[smem()] + [vmem()] * 8,
-        out_specs=[hbm()],
-        scratch=[pltpu.VMEM((2, HALF, width), f32), pltpu.SemaphoreType.DMA((2,))],
-    )
+    out = None
+    for other, blocks in enumerate((ps, qs)):
+        earlier = [] if out is None else [out]
+        (out,) = local_kernel(
+            functools.partial(place_heads, other),
+            [shape((2 * HALF, width), f32)],
+            (meta, *blocks, *earlier),
+            12,
+            0,
+            "place_other" if other else "place_own",
+            in_specs=[smem()] + [vmem()] * 4 + [hbm()] * len(earlier),
+            out_specs=[hbm()],
+            scratch=[pltpu.VMEM((HALF, width), f32), pltpu.SemaphoreType.DMA],
+            aliases={5: 0} if earlier else {},
+        )
     return out
 
 

time: 149 us -> 149 us (level)
  waiting for transfers between devices: 67.5 us -> 65.9 us
    pallas_call x9 -> x10, Pallas kernels: 17.3 us -> 18.5 us  [local_kernel(): pl.pallas_call(body, out_shape=outs, in_specs=in_specs or [vmem()] * len(...]
  transfers between devices with their start and end apart: 37 -> 37, of which waited for: 22 -> 21; matrix products, arithmetic and copies ran while one was open for 0% -> 0% of each run, Pallas kernels for 3% -> 4%
where the time goes in v9:
time: 149 us; the launch traced here: 148 us
  waiting for transfers between devices  65.9 us (44%)
  starting transfers between devices  60.6 us (41%)
  Pallas kernels  18.5 us (12%)
    ppermute x11, waiting for transfers between devices, move_x(): return lax.ppermute(a, 'x', [(i, i ^ k & 3) for i in range(4)])  26.4 us
    pallas_call x10, Pallas kernels, local_kernel(): pl.pallas_call(body, out_shape=outs, in_specs=in_specs or [vmem()] * len(...  18.5 us
    ppermute x11, starting transfers between devices, move_x(): return lax.ppermute(a, 'x', [(i, i ^ k & 3) for i in range(4)])  17 us
    ppermute x5, waiting for transfers between devices, move_z(): return lax.ppermute(a, ('zh', 'z0'), [(i, (i + k) % 8) for i in range(8)])  15.5 us
    ppermute x10, starting transfers between devices, move_y(): lax.ppermute(a, ('ylo', 'yhi'), [(Y_INDEX[i], Y_INDEX[i ^ k & 3]) for i i...  14.5 us
    ppermute x5, starting transfers between devices, move_z(): return lax.ppermute(a, ('zh', 'z0'), [(i, (i + k) % 8) for i in range(8)])  13.1 us
    ppermute x10, waiting for transfers between devices, move_y(): lax.ppermute(a, ('ylo', 'yhi'), [(Y_INDEX[i], Y_INDEX[i ^ k & 3]) for i i...  12.4 us
    ppermute x8, starting transfers between devices, swap(): return lax.ppermute(a, axis, [(0, 1), (1, 0)])  10.2 us
  transfers between devices with their start and end apart: 37, of which 21 were waited for; matrix products, arithmetic and copies ran while one was open for 0% of the time, Pallas kernels for 4%

profile of v9, /device:TPU:1, one launch (start us, length us, event | category | flops | bytes accessed | tf_op | source)
XLA Modules:
  0.0 147.8 jit_solution(5688292775531268819)
XLA Ops:
  2.0 2.6 %prepare.1 = (bf16[1024,128]{1,0:T(8,128)(2,1)S(1)}, bf16[1024,128]{1,0:T(8,128)(2,1)S(1)}, bf16[1024,128]{1,0:T(8,128)(2,1)S(1)}, bf16[1024,128]{1,0:T(8,128)(2...) custom-call(s32[32]{0:T(128)S(1)} %copy-done, ...), custom_call_target="tpu_custom_call" | custom-call | flops 1048576 | bytes 4195108 | tf_op jit(solution)/shard_map/prepare/pallas_call | solution.py:44
  4.5 3.8 %collective-permute-start.3 = (bf16[1024,128]{1,0:T(8,128)(2,1)S(1)}, bf16[1024,128]{1,0:T(8,128)(2,1)S(1)}, u32[]{:S(2)}, u32[]{:S(2)}) collective-permute-start(bf16[1024,128]{1,0:T(8,128)(2,1)S(1)} %get-tuple-element.36), channel_id=1, source_target_pairs={{0,16},{32,48},{16,0},{48,32},{1,17},{33,49},{17,1},{49,33},{2,18}... | collective-permute-start | bytes 786440 | tf_op jit(solution)/shard_map/ppermute | solution.py:287
  9.1 2.7 %collective-permute-start = (bf16[128,1024]{1,0:T(8,128)(2,1)S(1)}, bf16[128,1024]{1,0:T(8,128)(2,1)S(1)}, u32[]{:S(2)}, u32[]{:S(2)}) collective-permute-start(bf16[128,1024]{1,0:T(8,128)(2,1)S(1)} %get-tuple-element.32), channel_id=1, source_target_pairs={{0,128},{64,192},{128,0},{192,64},{1,129},{65,193},{129,1},{193,65... | collective-permute-start | bytes 786440 | tf_op jit(solution)/shard_map/ppermute | solution.py:283
  13.4 3.2 %collective-permute-start.2 = (bf16[128,1024]{1,0:T(8,128)(2,1)}, bf16[128,1024]{1,0:T(8,128)(2,1)S(1)}, u32[]{:S(2)}, u32[]{:S(2)}) collective-permute-start(bf16[128,1024]{1,0:T(8,128)(2,1)} %get-tuple-element.35), channel_id=1, source_target_pairs={{0,192},{64,128},{128,64},{192,0},{1,193},{65,129},{129,65},{193,1... | collective-permute-start | bytes 786440 | tf_op jit(solution)/shard_map/ppermute | solution.py:283
  16.6 3.5 %collective-permute-done.4 = bf16[1024,128]{1,0:T(8,128)(2,1)S(1)} collective-permute-done((bf16[1024,128]{1,0:T(8,128)(2,1)S(1)}, bf16[1024,128]{1,0:T(8,128)(2,1)S(1)}, u32[]{:S(2)}, u32[]{:S(2)}) %collective-permute-start.4) | collective-permute-done | bytes 262176 | tf_op jit(solution)/shard_map/ppermute | solution.py:287
  27.5 18.5 %collective-permute-done.7.r1.refs_1_ = bf16[4,1024,128]{2,1,0:T(8,128)(2,1)S(1)} collective-permute-done((bf16[4,1024,128]{2,1,0:T(8,128)(2,1)S(1)}, bf16[4,1024,128]{2,1,0:T(8,128)(2,1)S(1)}, u32[]{:S(2)}, u32[]{:S(2)}) %collective-permute-start.7) | collective-permute-done | bytes 1048608 | tf_op jit(solution)/shard_map/ppermute | solution.py:283
  47.8 3.1 %collective-permute-start.12 = (bf16[2,128,1024]{2,1,0:T(8,128)(2,1)S(1)}, bf16[2,128,1024]{2,1,0:T(8,128)(2,1)S(1)}, u32[]{:S(2)}, u32[]{:S(2)}) collective-permute-start(bf16[2,128,1024]{2,1,0:T(8,128)(2,1)S(1)} %slice.18), channel_id=1, source_target_pairs={{0,48},{32,16},{16,32},{48,0},{1,49},{33,17},{17,33},{49,1},{2,50}... | collective-permute-start | bytes 1572872 | tf_op jit(solution)/shard_map/ppermute | solution.py:287
  51.0 2.9 %multiply_near.1.near = f32[1024,1024]{1,0:T(8,128)S(1)} custom-call(bf16[4,128,1024]{2,1,0:T(8,128)(2,1)S(1)} %pad_maximum_fusion.g0.refs_5_, bf16[4,1024,128]{2,1,0:T(8,128)(2,1)S(1)} %pad_maximum_fusion.1.r0.refs_0_, bf16[4,128,1024]{2,1,0:T(8,128)(2,1)S(1)} %collective-permute-done.6.g1.refs_6_, ...), custom_call_target="tpu_custom_call" | custom-call | flops 2415919104 | bytes 10485760 | tf_op jit(solution)/shard_map/multiply_near/pallas_call | solution.py:44
  53.9 5.3 %collective-permute-done.10.refs_3_ = bf16[2,1024,128]{2,1,0:T(8,128)(2,1)S(1)} collective-permute-done((bf16[2,1024,128]{2,1,0:T(8,128)(2,1)S(1)}, bf16[2,1024,128]{2,1,0:T(8,128)(2,1)S(1)}, u32[]{:S(2)}, u32[]{:S(2)}) %collective-permute-start.10) | collective-permute-done | bytes 524320 | tf_op jit(solution)/shard_map/ppermute | solution.py:283
  63.6 3.3 %collective-permute-start.15 = (bf16[8,128,256]{2,1,0:T(8,128)(2,1)S(1)}, bf16[8,128,256]{2,1,0:T(8,128)(2,1)S(1)}, u32[]{:S(2)}, u32[]{:S(2)}) collective-permute-start(bf16[8,128,256]{2,1,0:T(8,128)(2,1)S(1)} %get-tuple-element.43), channel_id=1, source_target_pairs={{0,1},{1,0},{2,3},{3,2},{4,5},{5,4},{6,7},{7,6},{8,9},{9,8},{10,11... | collective-permute-start | bytes 1572872 | tf_op jit(solution)/shard_map/ppermute | solution.py:295
  70.2 4.0 %collective-permute-start.17 = (bf16[4,128,256]{2,1,0:T(8,128)(2,1)S(1)}, bf16[4,128,256]{2,1,0:T(8,128)(2,1)S(1)}, u32[]{:S(2)}, u32[]{:S(2)}) collective-permute-start(bf16[4,128,256]{2,1,0:T(8,128)(2,1)S(1)} %get-tuple-element.45), channel_id=1, source_target_pairs={{0,14},{2,0},{4,2},{6,4},{8,6},{10,8},{12,10},{14,12},{1,15},{3,1}... | collective-permute-start | bytes 786440 | tf_op jit(solution)/shard_map/ppermute | solution.py:291
  74.3 6.3 %collective-permute-done.16.up = bf16[4,128,256]{2,1,0:T(8,128)(2,1)S(1)} collective-permute-done((bf16[4,128,256]{2,1,0:T(8,128)(2,1)S(1)}, bf16[4,128,256]{2,1,0:T(8,128)(2,1)S(1)}, u32[]{:S(2)}, u32[]{:S(2)}) %collective-permute-start.16) | collective-permute-done | bytes 262176 | tf_op jit(solution)/shard_map/ppermute | solution.py:291
  80.8 3.8 %collective-permute-start.18 = (bf16[256,256]{1,0:T(8,128)(2,1)S(1)}, bf16[256,256]{1,0:T(8,128)(2,1)S(1)}, u32[]{:S(2)}, u32[]{:S(2)}) collective-permute-start(bf16[256,256]{1,0:T(8,128)(2,1)S(1)} %get-tuple-element.46), channel_id=1, source_target_pairs={{0,8},{2,10},{4,12},{6,14},{8,0},{10,2},{12,4},{14,6},{1,9},{3,11}... | collective-permute-start | bytes 393224 | tf_op jit(solution)/shard_map/ppermute | solution.py:291
  84.9 3.2 %collective-permute-start.20 = (bf16[256,256]{1,0:T(8,128)(2,1)S(1)}, bf16[256,256]{1,0:T(8,128)(2,1)S(1)}, u32[]{:S(2)}, u32[]{:S(2)}) collective-permute-start(bf16[256,256]{1,0:T(8,128)(2,1)S(1)} %get-tuple-element.48), channel_id=1, source_target_pairs={{0,12},{2,14},{4,0},{6,2},{8,4},{10,6},{12,8},{14,10},{1,13},{3,15... | collective-permute-start | bytes 393224 | tf_op jit(solution)/shard_map/ppermute | solution.py:291
  88.9 6.1 %collective-permute-done.19.t1 = bf16[256,256]{1,0:T(8,128)(2,1)S(1)} collective-permute-done((bf16[256,256]{1,0:T(8,128)(2,1)S(1)}, bf16[256,256]{1,0:T(8,128)(2,1)S(1)}, u32[]{:S(2)}, u32[]{:S(2)}) %collective-permute-start.19) | collective-permute-done | bytes 131104 | tf_op jit(solution)/shard_map/ppermute | solution.py:291
  95.0 2.3 %collective-permute-done.20.t3 = bf16[256,256]{1,0:T(8,128)(2,1)S(1)} collective-permute-done((bf16[256,256]{1,0:T(8,128)(2,1)S(1)}, bf16[256,256]{1,0:T(8,128)(2,1)S(1)}, u32[]{:S(2)}, u32[]{:S(2)}) %collective-permute-start.20) | collective-permute-done | bytes 131104 | tf_op jit(solution)/shard_map/ppermute | solution.py:291
  101.2 2.9 %collective-permute-done.22 = f32[192,128]{1,0:T(8,128)S(1)} collective-permute-done((f32[192,128]{1,0:T(8,128)S(1)}, f32[192,128]{1,0:T(8,128)S(1)}, u32[]{:S(2)}, u32[]{:S(2)}) %collective-permute-start.22) | collective-permute-done | bytes 98336 | tf_op jit(solution)/shard_map/ppermute | solution.py:295
  109.9 2.1 %collective-permute-done.25 = f32[192,128]{1,0:T(8,128)S(1)} collective-permute-done((f32[192,128]{1,0:T(8,128)S(1)}, f32[192,128]{1,0:T(8,128)S(1)}, u32[]{:S(2)}, u32[]{:S(2)}) %collective-permute-start.25) | collective-permute-done | bytes 98336 | tf_op jit(solution)/shard_map/ppermute | solution.py:287
  114.6 6.8 %newton.1 = (bf16[64,256]{1,0:T(8,128)(2,1)S(1)}, bf16[64,256]{1,0:T(8,128)(2,1)S(1)}, bf16[64,256]{1,0:T(8,128)(2,1)S(1)}, bf16[64,256]{1,0:T(8,128)(2,1)S(1)}) custom-call(s32[40]{0:T(128)S(1)} %get-tuple-element.31.meta, f32[192,128]{1,0:T(8,128)S(1)} %add_add_fusion.mine, f32[192,128]{1,0:T(8,128)S(1)} %collective-permute-done.26.other, ...), custom_call_target="tpu_custom_call" | custom-call | flops 4026531840 | bytes 458912 | tf_op jit(solution)/shard_map/newton/pallas_call | solution.py:44
  123.0 3.1 %collective-permute-start.28 = (bf16[64,256]{1,0:T(8,128)(2,1)S(1)}, bf16[64,256]{1,0:T(8,128)(2,1)S(1)}, u32[]{:S(2)}, u32[]{:S(2)}) collective-permute-start(bf16[64,256]{1,0:T(8,128)(2,1)S(1)} %get-tuple-element.55), channel_id=1, source_target_pairs={{0,8},{4,12},{8,0},{12,4},{1,9},{5,13},{9,1},{13,5},{2,10},{6,14},... | collective-permute-start | bytes 98312 | tf_op jit(solution)/shard_map/ppermute | solution.py:392
  127.1 2.7 %collective-permute-done.28 = bf16[64,256]{1,0:T(8,128)(2,1)S(1)} collective-permute-done((bf16[64,256]{1,0:T(8,128)(2,1)S(1)}, bf16[64,256]{1,0:T(8,128)(2,1)S(1)}, u32[]{:S(2)}, u32[]{:S(2)}) %collective-permute-start.28) | collective-permute-done | bytes 32800 | tf_op jit(solution)/shard_map/ppermute | solution.py:392
  131.3 2.5 %collective-permute-start.32 = (bf16[4,64,256]{2,1,0:T(8,128)(2,1)S(1)}, bf16[4,64,256]{2,1,0:T(8,128)(2,1)S(1)}, u32[]{:S(2)}, u32[]{:S(2)}) collective-permute-start(bf16[4,64,256]{2,1,0:T(8,128)(2,1)S(1)} %pad_maximum_fusion.2.refs_0_), channel_id=1, source_target_pairs={{0,128},{64,192},{128,0},{192,64},{1,129},{65,193},{129,1},{193,65... | collective-permute-start | bytes 393224 | tf_op jit(solution)/shard_map/ppermute | solution.py:283
  138.1 2.6 %collective-permute-done.34.refs_3_ = bf16[4,64,256]{2,1,0:T(8,128)(2,1)S(1)} collective-permute-done((bf16[4,64,256]{2,1,0:T(8,128)(2,1)S(1)}, bf16[4,64,256]{2,1,0:T(8,128)(2,1)S(1)}, u32[]{:S(2)}, u32[]{:S(2)}) %collective-permute-start.34) | collective-permute-done | bytes 131104 | tf_op jit(solution)/shard_map/ppermute | solution.py:283
  143.4 2.6 %collective-permute-done.35.refs_3_ = bf16[4,64,256]{2,1,0:T(8,128)(2,1)S(1)} collective-permute-done((bf16[4,64,256]{2,1,0:T(8,128)(2,1)S(1)}, bf16[4,64,256]{2,1,0:T(8,128)(2,1)S(1)}, u32[]{:S(2)}, u32[]{:S(2)}) %collective-permute-start.35) | collective-permute-done | bytes 131104 | tf_op jit(solution)/shard_map/ppermute | solution.py:295
  (74 shorter events, 46.9 us)
Async XLA Ops:
  4.5 8.8 %collective-permute-start.3 = (bf16[1024,128]{1,0:T(8,128)(2,1)S(1)}, bf16[1024,128]{1,0:T(8,128)(2,1)S(1)}, u32[]{:S(2)}, u32[]{:S(2)}) collective-permute-start(bf16[1024,128]{1,0:T(8,128)(2,1)S(1)} %get-tuple-element.36), channel_id=1, source_target_pairs={{0,16},{32,48},{16,0},{48,32},{1,17},{33,49},{17,1},{49,33},{2,18}... | collective-permute-start | bytes 786440 | tf_op jit(solution)/shard_map/ppermute | solution.py:287
  8.4 11.8 %collective-permute-start.4 = (bf16[1024,128]{1,0:T(8,128)(2,1)S(1)}, bf16[1024,128]{1,0:T(8,128)(2,1)S(1)}, u32[]{:S(2)}, u32[]{:S(2)}) collective-permute-start(bf16[1024,128]{1,0:T(8,128)(2,1)S(1)} %get-tuple-element.38), channel_id=1, source_target_pairs={{0,32},{32,0},{16,48},{48,16},{1,33},{33,1},{17,49},{49,17},{2,34}... | collective-permute-start | bytes 786440 | tf_op jit(solution)/shard_map/ppermute | solution.py:287
  8.8 11.4 %collective-permute-start.5 = (bf16[1024,128]{1,0:T(8,128)(2,1)S(1)}, bf16[1024,128]{1,0:T(8,128)(2,1)S(1)}, u32[]{:S(2)}, u32[]{:S(2)}) collective-permute-start(bf16[1024,128]{1,0:T(8,128)(2,1)S(1)} %get-tuple-element.39), channel_id=1, source_target_pairs={{0,48},{32,16},{16,32},{48,0},{1,49},{33,17},{17,33},{49,1},{2,50}... | collective-permute-start | bytes 786440 | tf_op jit(solution)/shard_map/ppermute | solution.py:287
  9.1 14.9 %collective-permute-start = (bf16[128,1024]{1,0:T(8,128)(2,1)S(1)}, bf16[128,1024]{1,0:T(8,128)(2,1)S(1)}, u32[]{:S(2)}, u32[]{:S(2)}) collective-permute-start(bf16[128,1024]{1,0:T(8,128)(2,1)S(1)} %get-tuple-element.32), channel_id=1, source_target_pairs={{0,128},{64,192},{128,0},{192,64},{1,129},{65,193},{129,1},{193,65... | collective-permute-start | bytes 786440 | tf_op jit(solution)/shard_map/ppermute | solution.py:283
  11.9 12.1 %collective-permute-start.1 = (bf16[128,1024]{1,0:T(8,128)(2,1)S(1)}, bf16[128,1024]{1,0:T(8,128)(2,1)S(1)}, u32[]{:S(2)}, u32[]{:S(2)}) collective-permute-start(bf16[128,1024]{1,0:T(8,128)(2,1)S(1)} %get-tuple-element.34), channel_id=1, source_target_pairs={{0,64},{64,0},{128,192},{192,128},{1,65},{65,1},{129,193},{193,129... | collective-permute-start | bytes 786440 | tf_op jit(solution)/shard_map/ppermute | solution.py:283
  13.4 10.6 %collective-permute-start.2 = (bf16[128,1024]{1,0:T(8,128)(2,1)}, bf16[128,1024]{1,0:T(8,128)(2,1)S(1)}, u32[]{:S(2)}, u32[]{:S(2)}) collective-permute-start(bf16[128,1024]{1,0:T(8,128)(2,1)} %get-tuple-element.35), channel_id=1, source_target_pairs={{0,192},{64,128},{128,64},{192,0},{1,193},{65,129},{129,65},{193,1... | collective-permute-start | bytes 786440 | tf_op jit(solution)/shard_map/ppermute | solution.py:283
  20.3 25.7 %collective-permute-start.7 = (bf16[4,1024,128]{2,1,0:T(8,128)(2,1)S(1)}, bf16[4,1024,128]{2,1,0:T(8,128)(2,1)S(1)}, u32[]{:S(2)}, u32[]{:S(2)}) collective-permute-start(bf16[4,1024,128]{2,1,0:T(8,128)(2,1)S(1)} %pad_maximum_fusion.1.r0.refs_0_), channel_id=1, source_target_pairs={{0,64},{64,0},{128,192},{192,128},{1,65},{65,1},{129,193},{193,129... | collective-permute-start | bytes 3145736 | tf_op jit(solution)/shard_map/ppermute | solution.py:283
  22.2 25.1 %collective-permute-start.9 = (bf16[4,1024,128]{2,1,0:T(8,128)(2,1)S(1)}, bf16[4,1024,128]{2,1,0:T(8,128)(2,1)S(1)}, u32[]{:S(2)}, u32[]{:S(2)}) collective-permute-start(bf16[4,1024,128]{2,1,0:T(8,128)(2,1)S(1)} %pad_maximum_fusion.1.r0.refs_0_), channel_id=1, source_target_pairs={{0,192},{64,128},{128,64},{192,0},{1,193},{65,129},{129,65},{193,1... | collective-permute-start | bytes 3145736 | tf_op jit(solution)/shard_map/ppermute | solution.py:283
  24.2 23.6 %collective-permute-start.6 = (bf16[4,128,1024]{2,1,0:T(8,128)(2,1)S(1)}, bf16[4,128,1024]{2,1,0:T(8,128)(2,1)S(1)}, u32[]{:S(2)}, u32[]{:S(2)}) collective-permute-start(bf16[4,128,1024]{2,1,0:T(8,128)(2,1)S(1)} %pad_maximum_fusion.g0.refs_5_), channel_id=1, source_target_pairs={{0,32},{32,0},{16,48},{48,16},{1,33},{33,1},{17,49},{49,17},{2,34}... | collective-permute-start | bytes 3145736 | tf_op jit(solution)/shard_map/ppermute | solution.py:287
  25.6 25.3 %collective-permute-start.8 = (bf16[4,128,1024]{2,1,0:T(8,128)(2,1)S(1)}, bf16[4,128,1024]{2,1,0:T(8,128)(2,1)S(1)}, u32[]{:S(2)}, u32[]{:S(2)}) collective-permute-start(bf16[4,128,1024]{2,1,0:T(8,128)(2,1)S(1)} %pad_maximum_fusion.g0.refs_5_), channel_id=1, source_target_pairs={{0,48},{32,16},{16,32},{48,0},{1,49},{33,17},{17,33},{49,1},{2,50}... | collective-permute-start | bytes 3145736 | tf_op jit(solution)/shard_map/ppermute | solution.py:287
  46.0 13.2 %collective-permute-start.10 = (bf16[2,1024,128]{2,1,0:T(8,128)(2,1)S(1)}, bf16[2,1024,128]{2,1,0:T(8,128)(2,1)S(1)}, u32[]{:S(2)}, u32[]{:S(2)}) collective-permute-start(bf16[2,1024,128]{2,1,0:T(8,128)(2,1)S(1)} %slice.16), channel_id=1, source_target_pairs={{0,192},{64,128},{128,64},{192,0},{1,193},{65,129},{129,65},{193,1... | collective-permute-start | bytes 1572872 | tf_op jit(solution)/shard_map/ppermute | solution.py:283
  47.4 11.8 %collective-permute-start.11 = (bf16[2,1024,128]{2,1,0:T(8,128)(2,1)S(1)}, bf16[2,1024,128]{2,1,0:T(8,128)(2,1)S(1)}, u32[]{:S(2)}, u32[]{:S(2)}) collective-permute-start(bf16[2,1024,128]{2,1,0:T(8,128)(2,1)S(1)} %slice.17), channel_id=1, source_target_pairs={{0,64},{64,0},{128,192},{192,128},{1,65},{65,1},{129,193},{193,129... | collective-permute-start | bytes 1572872 | tf_op jit(solution)/shard_map/ppermute | solution.py:283
  47.8 13.3 %collective-permute-start.12 = (bf16[2,128,1024]{2,1,0:T(8,128)(2,1)S(1)}, bf16[2,128,1024]{2,1,0:T(8,128)(2,1)S(1)}, u32[]{:S(2)}, u32[]{:S(2)}) collective-permute-start(bf16[2,128,1024]{2,1,0:T(8,128)(2,1)S(1)} %slice.18), channel_id=1, source_target_pairs={{0,48},{32,16},{16,32},{48,0},{1,49},{33,17},{17,33},{49,1},{2,50}... | collective-permute-start | bytes 1572872 | tf_op jit(solution)/shard_map/ppermute | solution.py:287
  50.9 11.4 %collective-permute-start.13 = (bf16[2,128,1024]{2,1,0:T(8,128)(2,1)S(1)}, bf16[2,128,1024]{2,1,0:T(8,128)(2,1)S(1)}, u32[]{:S(2)}, u32[]{:S(2)}) collective-permute-start(bf16[2,128,1024]{2,1,0:T(8,128)(2,1)S(1)} %slice.19), channel_id=1, source_target_pairs={{0,32},{32,0},{16,48},{48,16},{1,33},{33,1},{17,49},{49,17},{2,34}... | collective-permute-start | bytes 1572872 | tf_op jit(solution)/shard_map/ppermute | solution.py:287
  68.5 12.0 %collective-permute-start.16 = (bf16[4,128,256]{2,1,0:T(8,128)(2,1)S(1)}, bf16[4,128,256]{2,1,0:T(8,128)(2,1)S(1)}, u32[]{:S(2)}, u32[]{:S(2)}) collective-permute-start(bf16[4,128,256]{2,1,0:T(8,128)(2,1)S(1)} %get-tuple-element.44), channel_id=1, source_target_pairs={{0,2},{2,4},{4,6},{6,8},{8,10},{10,12},{12,14},{14,0},{1,3},{3,5},... | collective-permute-start | bytes 786440 | tf_op jit(solution)/shard_map/ppermute | solution.py:291
  70.2 10.3 %collective-permute-start.17 = (bf16[4,128,256]{2,1,0:T(8,128)(2,1)S(1)}, bf16[4,128,256]{2,1,0:T(8,128)(2,1)S(1)}, u32[]{:S(2)}, u32[]{:S(2)}) collective-permute-start(bf16[4,128,256]{2,1,0:T(8,128)(2,1)S(1)} %get-tuple-element.45), channel_id=1, source_target_pairs={{0,14},{2,0},{4,2},{6,4},{8,6},{10,8},{12,10},{14,12},{1,15},{3,1}... | collective-permute-start | bytes 786440 | tf_op jit(solution)/shard_map/ppermute | solution.py:291
  80.8 8.1 %collective-permute-start.18 = (bf16[256,256]{1,0:T(8,128)(2,1)S(1)}, bf16[256,256]{1,0:T(8,128)(2,1)S(1)}, u32[]{:S(2)}, u32[]{:S(2)}) collective-permute-start(bf16[256,256]{1,0:T(8,128)(2,1)S(1)} %get-tuple-element.46), channel_id=1, source_target_pairs={{0,8},{2,10},{4,12},{6,14},{8,0},{10,2},{12,4},{14,6},{1,9},{3,11}... | collective-permute-start | bytes 393224 | tf_op jit(solution)/shard_map/ppermute | solution.py:291
  84.5 10.5 %collective-permute-start.19 = (bf16[256,256]{1,0:T(8,128)(2,1)S(1)}, bf16[256,256]{1,0:T(8,128)(2,1)S(1)}, u32[]{:S(2)}, u32[]{:S(2)}) collective-permute-start(bf16[256,256]{1,0:T(8,128)(2,1)S(1)} %get-tuple-element.47), channel_id=1, source_target_pairs={{0,4},{2,6},{4,8},{6,10},{8,12},{10,14},{12,0},{14,2},{1,5},{3,7},... | collective-permute-start | bytes 393224 | tf_op jit(solution)/shard_map/ppermute | solution.py:291
  84.9 12.4 %collective-permute-start.20 = (bf16[256,256]{1,0:T(8,128)(2,1)S(1)}, bf16[256,256]{1,0:T(8,128)(2,1)S(1)}, u32[]{:S(2)}, u32[]{:S(2)}) collective-permute-start(bf16[256,256]{1,0:T(8,128)(2,1)S(1)} %get-tuple-element.48), channel_id=1, source_target_pairs={{0,12},{2,14},{4,0},{6,2},{8,4},{10,6},{12,8},{14,10},{1,13},{3,15... | collective-permute-start | bytes 393224 | tf_op jit(solution)/shard_map/ppermute | solution.py:291
  123.0 6.8 %collective-permute-start.28 = (bf16[64,256]{1,0:T(8,128)(2,1)S(1)}, bf16[64,256]{1,0:T(8,128)(2,1)S(1)}, u32[]{:S(2)}, u32[]{:S(2)}) collective-permute-start(bf16[64,256]{1,0:T(8,128)(2,1)S(1)} %get-tuple-element.55), channel_id=1, source_target_pairs={{0,8},{4,12},{8,0},{12,4},{1,9},{5,13},{9,1},{13,5},{2,10},{6,14},... | collective-permute-start | bytes 98312 | tf_op jit(solution)/shard_map/ppermute | solution.py:392
  133.8 6.8 %collective-permute-start.34 = (bf16[4,64,256]{2,1,0:T(8,128)(2,1)S(1)}, bf16[4,64,256]{2,1,0:T(8,128)(2,1)S(1)}, u32[]{:S(2)}, u32[]{:S(2)}) collective-permute-start(bf16[4,64,256]{2,1,0:T(8,128)(2,1)S(1)} %pad_maximum_fusion.2.refs_0_), channel_id=1, source_target_pairs={{0,192},{64,128},{128,64},{192,0},{1,193},{65,129},{129,65},{193,1... | collective-permute-start | bytes 393224 | tf_op jit(solution)/shard_map/ppermute | solution.py:283
  135.2 6.5 %collective-permute-start.36 = (bf16[4,64,256]{2,1,0:T(8,128)(2,1)S(1)}, bf16[4,64,256]{2,1,0:T(8,128)(2,1)S(1)}, u32[]{:S(2)}, u32[]{:S(2)}) collective-permute-start(bf16[4,64,256]{2,1,0:T(8,128)(2,1)S(1)} %pad_maximum_fusion.2.refs_0_), channel_id=1, source_target_pairs={{0,64},{64,0},{128,192},{192,128},{1,65},{65,1},{129,193},{193,129... | collective-permute-start | bytes 393224 | tf_op jit(solution)/shard_map/ppermute | solution.py:283
  135.2 8.2 %collective-permute-start.31 = (bf16[4,64,256]{2,1,0:T(8,128)(2,1)S(1)}, bf16[4,64,256]{2,1,0:T(8,128)(2,1)S(1)}, u32[]{:S(2)}, u32[]{:S(2)}) collective-permute-start(bf16[4,64,256]{2,1,0:T(8,128)(2,1)S(1)} %collective-permute-done.30.refs_0_), channel_id=1, source_target_pairs={{0,64},{64,0},{128,192},{192,128},{1,65},{65,1},{129,193},{193,129... | collective-permute-start | bytes 393224 | tf_op jit(solution)/shard_map/ppermute | solution.py:283
  136.7 6.7 %collective-permute-start.33 = (bf16[4,64,256]{2,1,0:T(8,128)(2,1)S(1)}, bf16[4,64,256]{2,1,0:T(8,128)(2,1)S(1)}, u32[]{:S(2)}, u32[]{:S(2)}) collective-permute-start(bf16[4,64,256]{2,1,0:T(8,128)(2,1)S(1)} %collective-permute-done.32.refs_2_), channel_id=1, source_target_pairs={{0,32},{32,0},{1,33},{33,1},{2,34},{34,2},{3,35},{35,3},{4,36},{36... | collective-permute-start | bytes 393224 | tf_op jit(solution)/shard_map/ppermute | solution.py:295
  (15 other events, 63.3 us)

commit v10 on v9

--- a/solution.py
+++ b/solution.py
@@ -393,7 +393,7 @@
     p0 = jnp.stack(farthest_first(update, ring))
     q0 = swap(p0, "ylo")
     ps = farthest_first([p0] * 4, move_x)
-    qs = [q0, move_x(q0, 1), swap(ps[2], "ylo"), swap(ps[3], "ylo")]
+    qs = [q0, swap(ps[1], "ylo"), swap(ps[2], "ylo"), swap(ps[3], "ylo")]
     out = None
     for other, blocks in enumerate((ps, qs)):
         earlier = [] if out is None else [out]

time: 149 us -> 149 us (level)
  waiting for transfers between devices: 65.9 us -> 69.3 us
  starting transfers between devices: 60.6 us -> 58.2 us
    ppermute x11 -> x10, waiting for transfers between devices: 26.4 us -> 28.4 us  [move_x(): return lax.ppermute(a, 'x', [(i, i ^ k & 3) for i in range(4)])]
    ppermute x8 -> x9, waiting for transfers between devices: 7.52 us -> 8.95 us  [swap(): return lax.ppermute(a, axis, [(0, 1), (1, 0)])]
    ppermute x11 -> x10, starting transfers between devices: 17 us -> 15.7 us  [move_x(): return lax.ppermute(a, 'x', [(i, i ^ k & 3) for i in range(4)])]
    ppermute x8 -> x9, starting transfers between devices: 10.2 us -> 9.18 us  [swap(): return lax.ppermute(a, axis, [(0, 1), (1, 0)])]
  transfers between devices with their start and end apart: 37 -> 37, of which waited for: 21 -> 23; matrix products, arithmetic and copies ran while one was open for 0% -> 0% of each run, Pallas kernels for 4% -> 4%
where the time goes in v10:
time: 149 us
  waiting for transfers between devices  69.3 us (47%)
  starting transfers between devices  58.2 us (39%)
  Pallas kernels  18.5 us (12%)
    ppermute x10, waiting for transfers between devices, move_x(): return lax.ppermute(a, 'x', [(i, i ^ k & 3) for i in range(4)])  28.4 us
    pallas_call x10, Pallas kernels, local_kernel(): pl.pallas_call(body, out_shape=outs, in_specs=in_specs or [vmem()] * len(...  18.5 us
    ppermute x10, starting transfers between devices, move_x(): return lax.ppermute(a, 'x', [(i, i ^ k & 3) for i in range(4)])  15.7 us
    ppermute x5, waiting for transfers between devices, move_z(): return lax.ppermute(a, ('zh', 'z0'), [(i, (i + k) % 8) for i in range(8)])  15.4 us
    ppermute x10, starting transfers between devices, move_y(): lax.ppermute(a, ('ylo', 'yhi'), [(Y_INDEX[i], Y_INDEX[i ^ k & 3]) for i i...  14.5 us
    ppermute x5, starting transfers between devices, move_z(): return lax.ppermute(a, ('zh', 'z0'), [(i, (i + k) % 8) for i in range(8)])  13.1 us
    ppermute x10, waiting for transfers between devices, move_y(): lax.ppermute(a, ('ylo', 'yhi'), [(Y_INDEX[i], Y_INDEX[i ^ k & 3]) for i i...  12.4 us
    ppermute x9, starting transfers between devices, swap(): return lax.ppermute(a, axis, [(0, 1), (1, 0)])  9.18 us
  transfers between devices with their start and end apart: 37, of which 23 were waited for; matrix products, arithmetic and copies ran while one was open for 0% of the time, Pallas kernels for 4%

profile of v10, /device:TPU:1, one launch (start us, length us, event | category | flops | bytes accessed | tf_op | source)
XLA Modules:
  0.0 148.8 jit_solution(11221928946519702117)
XLA Ops:
  2.0 2.6 %prepare.1 = (bf16[1024,128]{1,0:T(8,128)(2,1)S(1)}, bf16[1024,128]{1,0:T(8,128)(2,1)S(1)}, bf16[1024,128]{1,0:T(8,128)(2,1)S(1)}, bf16[1024,128]{1,0:T(8,128)(2...) custom-call(s32[32]{0:T(128)S(1)} %copy-done, ...), custom_call_target="tpu_custom_call" | custom-call | flops 1048576 | bytes 4195108 | tf_op jit(solution)/shard_map/prepare/pallas_call | solution.py:44
  4.5 3.8 %collective-permute-start.3 = (bf16[1024,128]{1,0:T(8,128)(2,1)S(1)}, bf16[1024,128]{1,0:T(8,128)(2,1)S(1)}, u32[]{:S(2)}, u32[]{:S(2)}) collective-permute-start(bf16[1024,128]{1,0:T(8,128)(2,1)S(1)} %get-tuple-element.36), channel_id=1, source_target_pairs={{0,16},{32,48},{16,0},{48,32},{1,17},{33,49},{17,1},{49,33},{2,18}... | collective-permute-start | bytes 786440 | tf_op jit(solution)/shard_map/ppermute | solution.py:287
  9.1 2.7 %collective-permute-start = (bf16[128,1024]{1,0:T(8,128)(2,1)S(1)}, bf16[128,1024]{1,0:T(8,128)(2,1)S(1)}, u32[]{:S(2)}, u32[]{:S(2)}) collective-permute-start(bf16[128,1024]{1,0:T(8,128)(2,1)S(1)} %get-tuple-element.32), channel_id=1, source_target_pairs={{0,128},{64,192},{128,0},{192,64},{1,129},{65,193},{129,1},{193,65... | collective-permute-start | bytes 786440 | tf_op jit(solution)/shard_map/ppermute | solution.py:283
  13.4 3.2 %collective-permute-start.2 = (bf16[128,1024]{1,0:T(8,128)(2,1)}, bf16[128,1024]{1,0:T(8,128)(2,1)S(1)}, u32[]{:S(2)}, u32[]{:S(2)}) collective-permute-start(bf16[128,1024]{1,0:T(8,128)(2,1)} %get-tuple-element.35), channel_id=1, source_target_pairs={{0,192},{64,128},{128,64},{192,0},{1,193},{65,129},{129,65},{193,1... | collective-permute-start | bytes 786440 | tf_op jit(solution)/shard_map/ppermute | solution.py:283
  16.6 3.5 %collective-permute-done.4 = bf16[1024,128]{1,0:T(8,128)(2,1)S(1)} collective-permute-done((bf16[1024,128]{1,0:T(8,128)(2,1)S(1)}, bf16[1024,128]{1,0:T(8,128)(2,1)S(1)}, u32[]{:S(2)}, u32[]{:S(2)}) %collective-permute-start.4) | collective-permute-done | bytes 262176 | tf_op jit(solution)/shard_map/ppermute | solution.py:287
  27.5 18.5 %collective-permute-done.7.r1.refs_1_ = bf16[4,1024,128]{2,1,0:T(8,128)(2,1)S(1)} collective-permute-done((bf16[4,1024,128]{2,1,0:T(8,128)(2,1)S(1)}, bf16[4,1024,128]{2,1,0:T(8,128)(2,1)S(1)}, u32[]{:S(2)}, u32[]{:S(2)}) %collective-permute-start.7) | collective-permute-done | bytes 1048608 | tf_op jit(solution)/shard_map/ppermute | solution.py:283
  47.8 3.1 %collective-permute-start.12 = (bf16[2,128,1024]{2,1,0:T(8,128)(2,1)S(1)}, bf16[2,128,1024]{2,1,0:T(8,128)(2,1)S(1)}, u32[]{:S(2)}, u32[]{:S(2)}) collective-permute-start(bf16[2,128,1024]{2,1,0:T(8,128)(2,1)S(1)} %slice.18), channel_id=1, source_target_pairs={{0,48},{32,16},{16,32},{48,0},{1,49},{33,17},{17,33},{49,1},{2,50}... | collective-permute-start | bytes 1572872 | tf_op jit(solution)/shard_map/ppermute | solution.py:287
  51.0 2.9 %multiply_near.1.near = f32[1024,1024]{1,0:T(8,128)S(1)} custom-call(bf16[4,128,1024]{2,1,0:T(8,128)(2,1)S(1)} %pad_maximum_fusion.g0.refs_5_, bf16[4,1024,128]{2,1,0:T(8,128)(2,1)S(1)} %pad_maximum_fusion.1.r0.refs_0_, bf16[4,128,1024]{2,1,0:T(8,128)(2,1)S(1)} %collective-permute-done.6.g1.refs_6_, ...), custom_call_target="tpu_custom_call" | custom-call | flops 2415919104 | bytes 10485760 | tf_op jit(solution)/shard_map/multiply_near/pallas_call | solution.py:44
  53.9 5.3 %collective-permute-done.10.refs_3_ = bf16[2,1024,128]{2,1,0:T(8,128)(2,1)S(1)} collective-permute-done((bf16[2,1024,128]{2,1,0:T(8,128)(2,1)S(1)}, bf16[2,1024,128]{2,1,0:T(8,128)(2,1)S(1)}, u32[]{:S(2)}, u32[]{:S(2)}) %collective-permute-start.10) | collective-permute-done | bytes 524320 | tf_op jit(solution)/shard_map/ppermute | solution.py:283
  63.6 3.3 %collective-permute-start.15 = (bf16[8,128,256]{2,1,0:T(8,128)(2,1)S(1)}, bf16[8,128,256]{2,1,0:T(8,128)(2,1)S(1)}, u32[]{:S(2)}, u32[]{:S(2)}) collective-permute-start(bf16[8,128,256]{2,1,0:T(8,128)(2,1)S(1)} %get-tuple-element.43), channel_id=1, source_target_pairs={{0,1},{1,0},{2,3},{3,2},{4,5},{5,4},{6,7},{7,6},{8,9},{9,8},{10,11... | collective-permute-start | bytes 1572872 | tf_op jit(solution)/shard_map/ppermute | solution.py:295
  70.3 4.0 %collective-permute-start.17 = (bf16[4,128,256]{2,1,0:T(8,128)(2,1)S(1)}, bf16[4,128,256]{2,1,0:T(8,128)(2,1)S(1)}, u32[]{:S(2)}, u32[]{:S(2)}) collective-permute-start(bf16[4,128,256]{2,1,0:T(8,128)(2,1)S(1)} %get-tuple-element.45), channel_id=1, source_target_pairs={{0,14},{2,0},{4,2},{6,4},{8,6},{10,8},{12,10},{14,12},{1,15},{3,1}... | collective-permute-start | bytes 786440 | tf_op jit(solution)/shard_map/ppermute | solution.py:291
  74.3 6.3 %collective-permute-done.16.up = bf16[4,128,256]{2,1,0:T(8,128)(2,1)S(1)} collective-permute-done((bf16[4,128,256]{2,1,0:T(8,128)(2,1)S(1)}, bf16[4,128,256]{2,1,0:T(8,128)(2,1)S(1)}, u32[]{:S(2)}, u32[]{:S(2)}) %collective-permute-start.16) | collective-permute-done | bytes 262176 | tf_op jit(solution)/shard_map/ppermute | solution.py:291
  80.7 3.8 %collective-permute-start.18 = (bf16[256,256]{1,0:T(8,128)(2,1)S(1)}, bf16[256,256]{1,0:T(8,128)(2,1)S(1)}, u32[]{:S(2)}, u32[]{:S(2)}) collective-permute-start(bf16[256,256]{1,0:T(8,128)(2,1)S(1)} %get-tuple-element.46), channel_id=1, source_target_pairs={{0,8},{2,10},{4,12},{6,14},{8,0},{10,2},{12,4},{14,6},{1,9},{3,11}... | collective-permute-start | bytes 393224 | tf_op jit(solution)/shard_map/ppermute | solution.py:291
  84.9 3.2 %collective-permute-start.20 = (bf16[256,256]{1,0:T(8,128)(2,1)S(1)}, bf16[256,256]{1,0:T(8,128)(2,1)S(1)}, u32[]{:S(2)}, u32[]{:S(2)}) collective-permute-start(bf16[256,256]{1,0:T(8,128)(2,1)S(1)} %get-tuple-element.48), channel_id=1, source_target_pairs={{0,12},{2,14},{4,0},{6,2},{8,4},{10,6},{12,8},{14,10},{1,13},{3,15... | collective-permute-start | bytes 393224 | tf_op jit(solution)/shard_map/ppermute | solution.py:291
  88.9 6.1 %collective-permute-done.19.t1 = bf16[256,256]{1,0:T(8,128)(2,1)S(1)} collective-permute-done((bf16[256,256]{1,0:T(8,128)(2,1)S(1)}, bf16[256,256]{1,0:T(8,128)(2,1)S(1)}, u32[]{:S(2)}, u32[]{:S(2)}) %collective-permute-start.19) | collective-permute-done | bytes 131104 | tf_op jit(solution)/shard_map/ppermute | solution.py:291
  95.0 2.3 %collective-permute-done.20.t3 = bf16[256,256]{1,0:T(8,128)(2,1)S(1)} collective-permute-done((bf16[256,256]{1,0:T(8,128)(2,1)S(1)}, bf16[256,256]{1,0:T(8,128)(2,1)S(1)}, u32[]{:S(2)}, u32[]{:S(2)}) %collective-permute-start.20) | collective-permute-done | bytes 131104 | tf_op jit(solution)/shard_map/ppermute | solution.py:291
  99.1 2.1 %collective-permute-start.22 = (f32[192,128]{1,0:T(8,128)S(1)}, f32[192,128]{1,0:T(8,128)S(1)}, u32[]{:S(2)}, u32[]{:S(2)}) collective-permute-start(f32[192,128]{1,0:T(8,128)S(1)} %add.15), channel_id=1, source_target_pairs={{0,2},{2,0},{1,3},{3,1},{4,6},{6,4},{5,7},{7,5},{8,10},{10,8},{9,1... | collective-permute-start | bytes 294920 | tf_op jit(solution)/shard_map/ppermute | solution.py:295
  101.2 2.9 %collective-permute-done.22 = f32[192,128]{1,0:T(8,128)S(1)} collective-permute-done((f32[192,128]{1,0:T(8,128)S(1)}, f32[192,128]{1,0:T(8,128)S(1)}, u32[]{:S(2)}, u32[]{:S(2)}) %collective-permute-start.22) | collective-permute-done | bytes 98336 | tf_op jit(solution)/shard_map/ppermute | solution.py:295
  109.9 2.1 %collective-permute-done.25 = f32[192,128]{1,0:T(8,128)S(1)} collective-permute-done((f32[192,128]{1,0:T(8,128)S(1)}, f32[192,128]{1,0:T(8,128)S(1)}, u32[]{:S(2)}, u32[]{:S(2)}) %collective-permute-start.25) | collective-permute-done | bytes 98336 | tf_op jit(solution)/shard_map/ppermute | solution.py:287
  114.6 6.8 %newton.1 = (bf16[64,256]{1,0:T(8,128)(2,1)S(1)}, bf16[64,256]{1,0:T(8,128)(2,1)S(1)}, bf16[64,256]{1,0:T(8,128)(2,1)S(1)}, bf16[64,256]{1,0:T(8,128)(2,1)S(1)}) custom-call(s32[40]{0:T(128)S(1)} %get-tuple-element.31.meta, f32[192,128]{1,0:T(8,128)S(1)} %add_add_fusion.mine, f32[192,128]{1,0:T(8,128)S(1)} %collective-permute-done.26.other, ...), custom_call_target="tpu_custom_call" | custom-call | flops 4026531840 | bytes 458912 | tf_op jit(solution)/shard_map/newton/pallas_call | solution.py:44
  123.0 3.1 %collective-permute-start.28 = (bf16[64,256]{1,0:T(8,128)(2,1)S(1)}, bf16[64,256]{1,0:T(8,128)(2,1)S(1)}, u32[]{:S(2)}, u32[]{:S(2)}) collective-permute-start(bf16[64,256]{1,0:T(8,128)(2,1)S(1)} %get-tuple-element.55), channel_id=1, source_target_pairs={{0,8},{4,12},{8,0},{12,4},{1,9},{5,13},{9,1},{13,5},{2,10},{6,14},... | collective-permute-start | bytes 98312 | tf_op jit(solution)/shard_map/ppermute | solution.py:392
  127.1 2.7 %collective-permute-done.28 = bf16[64,256]{1,0:T(8,128)(2,1)S(1)} collective-permute-done((bf16[64,256]{1,0:T(8,128)(2,1)S(1)}, bf16[64,256]{1,0:T(8,128)(2,1)S(1)}, u32[]{:S(2)}, u32[]{:S(2)}) %collective-permute-start.28) | collective-permute-done | bytes 32800 | tf_op jit(solution)/shard_map/ppermute | solution.py:392
  138.6 2.7 %collective-permute-done.35.refs_3_ = bf16[4,64,256]{2,1,0:T(8,128)(2,1)S(1)} collective-permute-done((bf16[4,64,256]{2,1,0:T(8,128)(2,1)S(1)}, bf16[4,64,256]{2,1,0:T(8,128)(2,1)S(1)}, u32[]{:S(2)}, u32[]{:S(2)}) %collective-permute-start.35) | collective-permute-done | bytes 131104 | tf_op jit(solution)/shard_map/ppermute | solution.py:283
  144.2 2.8 %collective-permute-done.36.refs_3_ = bf16[4,64,256]{2,1,0:T(8,128)(2,1)S(1)} collective-permute-done((bf16[4,64,256]{2,1,0:T(8,128)(2,1)S(1)}, bf16[4,64,256]{2,1,0:T(8,128)(2,1)S(1)}, u32[]{:S(2)}, u32[]{:S(2)}) %collective-permute-start.36) | collective-permute-done | bytes 131104 | tf_op jit(solution)/shard_map/ppermute | solution.py:295
  (74 shorter events, 48.0 us)
Async XLA Ops:
  4.5 8.8 %collective-permute-start.3 = (bf16[1024,128]{1,0:T(8,128)(2,1)S(1)}, bf16[1024,128]{1,0:T(8,128)(2,1)S(1)}, u32[]{:S(2)}, u32[]{:S(2)}) collective-permute-start(bf16[1024,128]{1,0:T(8,128)(2,1)S(1)} %get-tuple-element.36), channel_id=1, source_target_pairs={{0,16},{32,48},{16,0},{48,32},{1,17},{33,49},{17,1},{49,33},{2,18}... | collective-permute-start | bytes 786440 | tf_op jit(solution)/shard_map/ppermute | solution.py:287
  8.4 11.8 %collective-permute-start.4 = (bf16[1024,128]{1,0:T(8,128)(2,1)S(1)}, bf16[1024,128]{1,0:T(8,128)(2,1)S(1)}, u32[]{:S(2)}, u32[]{:S(2)}) collective-permute-start(bf16[1024,128]{1,0:T(8,128)(2,1)S(1)} %get-tuple-element.38), channel_id=1, source_target_pairs={{0,32},{32,0},{16,48},{48,16},{1,33},{33,1},{17,49},{49,17},{2,34}... | collective-permute-start | bytes 786440 | tf_op jit(solution)/shard_map/ppermute | solution.py:287
  8.8 11.4 %collective-permute-start.5 = (bf16[1024,128]{1,0:T(8,128)(2,1)S(1)}, bf16[1024,128]{1,0:T(8,128)(2,1)S(1)}, u32[]{:S(2)}, u32[]{:S(2)}) collective-permute-start(bf16[1024,128]{1,0:T(8,128)(2,1)S(1)} %get-tuple-element.39), channel_id=1, source_target_pairs={{0,48},{32,16},{16,32},{48,0},{1,49},{33,17},{17,33},{49,1},{2,50}... | collective-permute-start | bytes 786440 | tf_op jit(solution)/shard_map/ppermute | solution.py:287
  9.1 14.9 %collective-permute-start = (bf16[128,1024]{1,0:T(8,128)(2,1)S(1)}, bf16[128,1024]{1,0:T(8,128)(2,1)S(1)}, u32[]{:S(2)}, u32[]{:S(2)}) collective-permute-start(bf16[128,1024]{1,0:T(8,128)(2,1)S(1)} %get-tuple-element.32), channel_id=1, source_target_pairs={{0,128},{64,192},{128,0},{192,64},{1,129},{65,193},{129,1},{193,65... | collective-permute-start | bytes 786440 | tf_op jit(solution)/shard_map/ppermute | solution.py:283
  11.9 12.1 %collective-permute-start.1 = (bf16[128,1024]{1,0:T(8,128)(2,1)S(1)}, bf16[128,1024]{1,0:T(8,128)(2,1)S(1)}, u32[]{:S(2)}, u32[]{:S(2)}) collective-permute-start(bf16[128,1024]{1,0:T(8,128)(2,1)S(1)} %get-tuple-element.34), channel_id=1, source_target_pairs={{0,64},{64,0},{128,192},{192,128},{1,65},{65,1},{129,193},{193,129... | collective-permute-start | bytes 786440 | tf_op jit(solution)/shard_map/ppermute | solution.py:283
  13.4 10.7 %collective-permute-start.2 = (bf16[128,1024]{1,0:T(8,128)(2,1)}, bf16[128,1024]{1,0:T(8,128)(2,1)S(1)}, u32[]{:S(2)}, u32[]{:S(2)}) collective-permute-start(bf16[128,1024]{1,0:T(8,128)(2,1)} %get-tuple-element.35), channel_id=1, source_target_pairs={{0,192},{64,128},{128,64},{192,0},{1,193},{65,129},{129,65},{193,1... | collective-permute-start | bytes 786440 | tf_op jit(solution)/shard_map/ppermute | solution.py:283
  20.3 25.7 %collective-permute-start.7 = (bf16[4,1024,128]{2,1,0:T(8,128)(2,1)S(1)}, bf16[4,1024,128]{2,1,0:T(8,128)(2,1)S(1)}, u32[]{:S(2)}, u32[]{:S(2)}) collective-permute-start(bf16[4,1024,128]{2,1,0:T(8,128)(2,1)S(1)} %pad_maximum_fusion.1.r0.refs_0_), channel_id=1, source_target_pairs={{0,64},{64,0},{128,192},{192,128},{1,65},{65,1},{129,193},{193,129... | collective-permute-start | bytes 3145736 | tf_op jit(solution)/shard_map/ppermute | solution.py:283
  22.2 25.2 %collective-permute-start.9 = (bf16[4,1024,128]{2,1,0:T(8,128)(2,1)S(1)}, bf16[4,1024,128]{2,1,0:T(8,128)(2,1)S(1)}, u32[]{:S(2)}, u32[]{:S(2)}) collective-permute-start(bf16[4,1024,128]{2,1,0:T(8,128)(2,1)S(1)} %pad_maximum_fusion.1.r0.refs_0_), channel_id=1, source_target_pairs={{0,192},{64,128},{128,64},{192,0},{1,193},{65,129},{129,65},{193,1... | collective-permute-start | bytes 3145736 | tf_op jit(solution)/shard_map/ppermute | solution.py:283
  24.2 23.6 %collective-permute-start.6 = (bf16[4,128,1024]{2,1,0:T(8,128)(2,1)S(1)}, bf16[4,128,1024]{2,1,0:T(8,128)(2,1)S(1)}, u32[]{:S(2)}, u32[]{:S(2)}) collective-permute-start(bf16[4,128,1024]{2,1,0:T(8,128)(2,1)S(1)} %pad_maximum_fusion.g0.refs_5_), channel_id=1, source_target_pairs={{0,32},{32,0},{16,48},{48,16},{1,33},{33,1},{17,49},{49,17},{2,34}... | collective-permute-start | bytes 3145736 | tf_op jit(solution)/shard_map/ppermute | solution.py:287
  25.6 25.3 %collective-permute-start.8 = (bf16[4,128,1024]{2,1,0:T(8,128)(2,1)S(1)}, bf16[4,128,1024]{2,1,0:T(8,128)(2,1)S(1)}, u32[]{:S(2)}, u32[]{:S(2)}) collective-permute-start(bf16[4,128,1024]{2,1,0:T(8,128)(2,1)S(1)} %pad_maximum_fusion.g0.refs_5_), channel_id=1, source_target_pairs={{0,48},{32,16},{16,32},{48,0},{1,49},{33,17},{17,33},{49,1},{2,50}... | collective-permute-start | bytes 3145736 | tf_op jit(solution)/shard_map/ppermute | solution.py:287
  46.0 13.2 %collective-permute-start.10 = (bf16[2,1024,128]{2,1,0:T(8,128)(2,1)S(1)}, bf16[2,1024,128]{2,1,0:T(8,128)(2,1)S(1)}, u32[]{:S(2)}, u32[]{:S(2)}) collective-permute-start(bf16[2,1024,128]{2,1,0:T(8,128)(2,1)S(1)} %slice.16), channel_id=1, source_target_pairs={{0,192},{64,128},{128,64},{192,0},{1,193},{65,129},{129,65},{193,1... | collective-permute-start | bytes 1572872 | tf_op jit(solution)/shard_map/ppermute | solution.py:283
  47.4 11.8 %collective-permute-start.11 = (bf16[2,1024,128]{2,1,0:T(8,128)(2,1)S(1)}, bf16[2,1024,128]{2,1,0:T(8,128)(2,1)S(1)}, u32[]{:S(2)}, u32[]{:S(2)}) collective-permute-start(bf16[2,1024,128]{2,1,0:T(8,128)(2,1)S(1)} %slice.17), channel_id=1, source_target_pairs={{0,64},{64,0},{128,192},{192,128},{1,65},{65,1},{129,193},{193,129... | collective-permute-start | bytes 1572872 | tf_op jit(solution)/shard_map/ppermute | solution.py:283
  47.8 13.3 %collective-permute-start.12 = (bf16[2,128,1024]{2,1,0:T(8,128)(2,1)S(1)}, bf16[2,128,1024]{2,1,0:T(8,128)(2,1)S(1)}, u32[]{:S(2)}, u32[]{:S(2)}) collective-permute-start(bf16[2,128,1024]{2,1,0:T(8,128)(2,1)S(1)} %slice.18), channel_id=1, source_target_pairs={{0,48},{32,16},{16,32},{48,0},{1,49},{33,17},{17,33},{49,1},{2,50}... | collective-permute-start | bytes 1572872 | tf_op jit(solution)/shard_map/ppermute | solution.py:287
  50.9 11.4 %collective-permute-start.13 = (bf16[2,128,1024]{2,1,0:T(8,128)(2,1)S(1)}, bf16[2,128,1024]{2,1,0:T(8,128)(2,1)S(1)}, u32[]{:S(2)}, u32[]{:S(2)}) collective-permute-start(bf16[2,128,1024]{2,1,0:T(8,128)(2,1)S(1)} %slice.19), channel_id=1, source_target_pairs={{0,32},{32,0},{16,48},{48,16},{1,33},{33,1},{17,49},{49,17},{2,34}... | collective-permute-start | bytes 1572872 | tf_op jit(solution)/shard_map/ppermute | solution.py:287
  68.5 12.0 %collective-permute-start.16 = (bf16[4,128,256]{2,1,0:T(8,128)(2,1)S(1)}, bf16[4,128,256]{2,1,0:T(8,128)(2,1)S(1)}, u32[]{:S(2)}, u32[]{:S(2)}) collective-permute-start(bf16[4,128,256]{2,1,0:T(8,128)(2,1)S(1)} %get-tuple-element.44), channel_id=1, source_target_pairs={{0,2},{2,4},{4,6},{6,8},{8,10},{10,12},{12,14},{14,0},{1,3},{3,5},... | collective-permute-start | bytes 786440 | tf_op jit(solution)/shard_map/ppermute | solution.py:291
  70.3 10.3 %collective-permute-start.17 = (bf16[4,128,256]{2,1,0:T(8,128)(2,1)S(1)}, bf16[4,128,256]{2,1,0:T(8,128)(2,1)S(1)}, u32[]{:S(2)}, u32[]{:S(2)}) collective-permute-start(bf16[4,128,256]{2,1,0:T(8,128)(2,1)S(1)} %get-tuple-element.45), channel_id=1, source_target_pairs={{0,14},{2,0},{4,2},{6,4},{8,6},{10,8},{12,10},{14,12},{1,15},{3,1}... | collective-permute-start | bytes 786440 | tf_op jit(solution)/shard_map/ppermute | solution.py:291
  80.7 8.1 %collective-permute-start.18 = (bf16[256,256]{1,0:T(8,128)(2,1)S(1)}, bf16[256,256]{1,0:T(8,128)(2,1)S(1)}, u32[]{:S(2)}, u32[]{:S(2)}) collective-permute-start(bf16[256,256]{1,0:T(8,128)(2,1)S(1)} %get-tuple-element.46), channel_id=1, source_target_pairs={{0,8},{2,10},{4,12},{6,14},{8,0},{10,2},{12,4},{14,6},{1,9},{3,11}... | collective-permute-start | bytes 393224 | tf_op jit(solution)/shard_map/ppermute | solution.py:291
  84.5 10.5 %collective-permute-start.19 = (bf16[256,256]{1,0:T(8,128)(2,1)S(1)}, bf16[256,256]{1,0:T(8,128)(2,1)S(1)}, u32[]{:S(2)}, u32[]{:S(2)}) collective-permute-start(bf16[256,256]{1,0:T(8,128)(2,1)S(1)} %get-tuple-element.47), channel_id=1, source_target_pairs={{0,4},{2,6},{4,8},{6,10},{8,12},{10,14},{12,0},{14,2},{1,5},{3,7},... | collective-permute-start | bytes 393224 | tf_op jit(solution)/shard_map/ppermute | solution.py:291
  84.9 12.4 %collective-permute-start.20 = (bf16[256,256]{1,0:T(8,128)(2,1)S(1)}, bf16[256,256]{1,0:T(8,128)(2,1)S(1)}, u32[]{:S(2)}, u32[]{:S(2)}) collective-permute-start(bf16[256,256]{1,0:T(8,128)(2,1)S(1)} %get-tuple-element.48), channel_id=1, source_target_pairs={{0,12},{2,14},{4,0},{6,2},{8,4},{10,6},{12,8},{14,10},{1,13},{3,15... | collective-permute-start | bytes 393224 | tf_op jit(solution)/shard_map/ppermute | solution.py:291
  105.8 6.2 %collective-permute-start.25 = (f32[192,128]{1,0:T(8,128)S(1)}, f32[192,128]{1,0:T(8,128)S(1)}, u32[]{:S(2)}, u32[]{:S(2)}) collective-permute-start(f32[192,128]{1,0:T(8,128)S(1)} %add.16), channel_id=1, source_target_pairs={{0,48},{32,16},{16,32},{48,0},{1,49},{33,17},{17,33},{49,1},{2,50}... | collective-permute-start | bytes 294920 | tf_op jit(solution)/shard_map/ppermute | solution.py:287
  123.0 6.8 %collective-permute-start.28 = (bf16[64,256]{1,0:T(8,128)(2,1)S(1)}, bf16[64,256]{1,0:T(8,128)(2,1)S(1)}, u32[]{:S(2)}, u32[]{:S(2)}) collective-permute-start(bf16[64,256]{1,0:T(8,128)(2,1)S(1)} %get-tuple-element.55), channel_id=1, source_target_pairs={{0,8},{4,12},{8,0},{12,4},{1,9},{5,13},{9,1},{13,5},{2,10},{6,14},... | collective-permute-start | bytes 98312 | tf_op jit(solution)/shard_map/ppermute | solution.py:392
  134.1 7.2 %collective-permute-start.35 = (bf16[4,64,256]{2,1,0:T(8,128)(2,1)S(1)}, bf16[4,64,256]{2,1,0:T(8,128)(2,1)S(1)}, u32[]{:S(2)}, u32[]{:S(2)}) collective-permute-start(bf16[4,64,256]{2,1,0:T(8,128)(2,1)S(1)} %pad_maximum_fusion.2.refs_0_), channel_id=1, source_target_pairs={{0,192},{64,128},{128,64},{192,0},{1,193},{65,129},{129,65},{193,1... | collective-permute-start | bytes 393224 | tf_op jit(solution)/shard_map/ppermute | solution.py:283
  135.2 7.8 %collective-permute-start.30 = (bf16[4,64,256]{2,1,0:T(8,128)(2,1)S(1)}, bf16[4,64,256]{2,1,0:T(8,128)(2,1)S(1)}, u32[]{:S(2)}, u32[]{:S(2)}) collective-permute-start(bf16[4,64,256]{2,1,0:T(8,128)(2,1)S(1)} %pad_maximum_fusion.2.refs_0_), channel_id=1, source_target_pairs={{0,32},{32,0},{1,33},{33,1},{2,34},{34,2},{3,35},{35,3},{4,36},{36... | collective-permute-start | bytes 393224 | tf_op jit(solution)/shard_map/ppermute | solution.py:295
  135.2 7.8 %collective-permute-start.32 = (bf16[4,64,256]{2,1,0:T(8,128)(2,1)S(1)}, bf16[4,64,256]{2,1,0:T(8,128)(2,1)S(1)}, u32[]{:S(2)}, u32[]{:S(2)}) collective-permute-start(bf16[4,64,256]{2,1,0:T(8,128)(2,1)S(1)} %collective-permute-done.31.refs_1_), channel_id=1, source_target_pairs={{0,32},{32,0},{1,33},{33,1},{2,34},{34,2},{3,35},{35,3},{4,36},{36... | collective-permute-start | bytes 393224 | tf_op jit(solution)/shard_map/ppermute | solution.py:295
  (15 other events, 63.6 us)
